TPU v7x, 32 devices: a whole 2x2x4 slice. The times are simulated.
32 devices in a mesh: rep: 4 (over y, core), shard: 8 (over z, x).
Axes of the slice: x: 2, y: 2, z: 4, core: 2. Of those that a mesh axis runs over, the one named last changes fastest.
Arguments:
- tokens: bfloat16 [16384, 1024], P(('rep', 'shard')), may hold values from -6 to 6
- state_in: bfloat16 [16, 512, 1024], P('rep', 'shard'), may hold values from -6 to 6
- gain_tok: bfloat16 [1024], P('shard'), may hold values from 0.5 to 1.5
- gain_state: bfloat16 [1024], P('shard'), may hold values from 0.5 to 1.5
- gain_mlp: bfloat16 [1024], P('shard'), may hold values from 0.5 to 1.5
- w_tok: bfloat16 [1024, 3072], P('shard'), may hold values from -0.1875 to 0.1875
- w_state: bfloat16 [1024, 3072], P('shard'), may hold values from -0.1875 to 0.1875
- w_out: bfloat16 [1024, 1024], P('shard'), may hold values from -3.5 to 3.5
- w_update: bfloat16 [1024, 1024], P('shard'), may hold values from -3.5 to 3.5
- gate_bias: bfloat16 [1024], P('shard'), may hold values from -3 to 3
- rel_bias: bfloat16 [8, 32], P('shard'), may hold values from -4 to 4
- w_up: bfloat16 [4096, 1024], P('shard'), may hold values from -0.1875 to 0.1875
- w_down: bfloat16 [4096, 1024], P('shard'), may hold values from -0.09375 to 0.09375
- d_out: bfloat16 [16384, 1024], P(('rep', 'shard')), may hold values from -6 to 6
- d_state_next: bfloat16 [16, 512, 1024], P('rep', 'shard'), may hold values from -6 to 6
Outputs:
- output: bfloat16 [16384, 1024], P(('rep', 'shard'))
- state_next: float32 [16, 512, 1024], P('rep', 'shard')
- grad_tokens: float32 [16384, 1024], P(('rep', 'shard'))
- grad_state_in: float32 [16, 512, 1024], P('rep', 'shard')
- grad_gain_tok: float32 [1024], P('shard')
- grad_gain_state: float32 [1024], P('shard')
- grad_gain_mlp: float32 [1024], P('shard')
- grad_w_tok: float32 [1024, 3072], P('shard')
- grad_w_state: float32 [1024, 3072], P('shard')
- grad_w_out: float32 [1024, 1024], P('shard')
- grad_w_update: float32 [1024, 1024], P('shard')
- grad_gate_bias: float32 [1024], P('shard')
- grad_rel_bias: float32 [8, 32], P('shard')
- grad_w_up: float32 [4096, 1024], P('shard')
- grad_w_down: float32 [4096, 1024], P('shard')
All inputs are finite; a program needn't handle non-finite values.
Results may differ from a plain program's by a relative error of at most 0.017.
Values may be sent and summed in bfloat16 or wider, within the bound.
No kernel may reach another device: no remote copies, remote signals or barrier semaphores. Data moves between devices by JAX's collectives and lax.ppermute only.
A program may use at most 320 MiB of HBM per device.

v0:
```python
import math

import jax
import jax.numpy as jnp
import numpy as np
from jax import lax
from jax.sharding import PartitionSpec as P

D = 1024
H = 8
BLK = 512
M = 512
NB = 32
REACH = 128
SEQ_BLOCKS = 2


eps = 1e-06
top_precision = lax.Precision.HIGHEST


def from_behind(shard, axis, by):
    count = lax.axis_size(axis)
    pairs = [(i, i + by) for i in range(count) if 0 <= i + by < count]
    return lax.ppermute(shard, axis, pairs)


def for_sending(shard):

    def short(part):
        return part.astype(jnp.bfloat16) if part.dtype == jnp.float32 else part

    return jax.tree.map(short, shard)


def bucket_table(block_len, bucket_count, reach_len):
    distance = np.arange(2 * block_len + 1)
    exact_count = bucket_count // 2
    log_ratio = np.log(np.maximum(distance, 1) / exact_count) / np.log(reach_len / exact_count)
    far_bucket = np.minimum(
        exact_count + np.floor(log_ratio * (bucket_count - exact_count)).astype(np.int64),
        bucket_count - 1,
    )
    return np.where(distance < exact_count, distance, far_bucket).astype(np.int32)


def position_terms():
    row_index = np.arange(BLK)[:, None]
    col_index = np.arange(2 * BLK)[None, :]
    distance = row_index + BLK - col_index
    allowed_pos = (distance >= 0) & (distance <= BLK)
    bucket_ids = bucket_table(BLK, NB, REACH)
    choose = (bucket_ids[BLK - np.arange(BLK + 1)][None, :] == np.arange(NB)[:, None]).astype(
        np.float32
    )
    return (allowed_pos, choose)


def toeplitz_bias(per_distance):
    head_count = per_distance.shape[0]
    padded = jnp.concatenate([per_distance, jnp.zeros((head_count, BLK), jnp.float32)], axis=1)
    repeated = jnp.tile(padded, (1, BLK))[:, : BLK * 2 * BLK]
    return repeated.reshape(head_count, BLK, 2 * BLK)


def diagonal_sums(grad_bias):
    head_count = grad_bias.shape[0]
    flattened = grad_bias.reshape(head_count, BLK * 2 * BLK)
    padded = jnp.concatenate([flattened, jnp.zeros((head_count, BLK), jnp.float32)], axis=1)
    padded = padded.reshape(head_count, BLK, 2 * BLK + 1)
    return jnp.sum(padded[:, :, : BLK + 1], axis=1)


def layer_norm(values, gain_vec):
    centered = values - jnp.mean(values, axis=-1, keepdims=True)
    variance = jnp.mean(centered * centered, axis=-1, keepdims=True)
    return centered * lax.rsqrt(variance + eps) * gain_vec


def gelu_exact(values):
    return jax.nn.gelu(values, approximate=False)


def matmul(first_op, second_op):
    return jnp.dot(first_op, second_op, preferred_element_type=jnp.float32)


def contract(first_op, second_op, first_dim, second_dim):
    return lax.dot_general(
        first_op,
        second_op,
        (((first_dim,), (second_dim,)), ((), ())),
        preferred_element_type=jnp.float32,
    )


def split_heads(values, head_count):
    return values.reshape(values.shape[0], head_count, values.shape[1] // head_count)


def attend_scores(queries, key_rows, pos_bias, allowed, head_count):
    score_scale = 1.0 / math.sqrt(queries.shape[1] // head_count)
    scores = (
        jnp.einsum(
            "qhd,khd->hqk",
            split_heads(queries, head_count),
            split_heads(key_rows, head_count),
            preferred_element_type=jnp.float32,
        )
        * score_scale
        + pos_bias
    )
    return (jnp.where(allowed, scores, -1e30), score_scale)


def attend_forward(queries, key_rows, values, pos_bias, allowed, head_count):
    scores, score_scale = attend_scores(queries, key_rows, pos_bias, allowed, head_count)
    largest = jnp.max(scores, axis=-1, keepdims=True)
    log_total = largest + jnp.log(jnp.sum(jnp.exp(scores - largest), axis=-1, keepdims=True))
    weights = jnp.exp(scores - log_total).astype(jnp.bfloat16)
    mixture = jnp.einsum(
        "hqk,khd->qhd", weights, split_heads(values, head_count), preferred_element_type=jnp.float32
    )
    return (mixture.reshape(queries.shape).astype(jnp.bfloat16), log_total)


def attend_backward(queries, key_rows, values, pos_bias, allowed, head_count, log_total, grad_mix):
    scores, score_scale = attend_scores(queries, key_rows, pos_bias, allowed, head_count)
    weights = jnp.exp(scores - log_total)
    grad_heads = split_heads(grad_mix, head_count)
    grad_weights = jnp.einsum(
        "qhd,khd->hqk",
        grad_heads,
        split_heads(values, head_count),
        preferred_element_type=jnp.float32,
    )
    inner_sum = jnp.sum(weights * grad_weights, axis=-1, keepdims=True)
    grad_scores = (weights * (grad_weights - inner_sum)).astype(jnp.bfloat16)
    grad_queries = (
        jnp.einsum(
            "hqk,khd->qhd",
            grad_scores,
            split_heads(key_rows, head_count),
            preferred_element_type=jnp.float32,
        )
        * score_scale
    )
    grad_keys = (
        jnp.einsum(
            "hqk,qhd->khd",
            grad_scores,
            split_heads(queries, head_count),
            preferred_element_type=jnp.float32,
        )
        * score_scale
    )
    grad_values = jnp.einsum(
        "hqk,qhd->khd", weights.astype(jnp.bfloat16), grad_heads, preferred_element_type=jnp.float32
    )
    return (
        grad_queries.reshape(queries.shape),
        grad_keys.reshape(key_rows.shape),
        grad_values.reshape(values.shape),
        grad_scores,
    )


def state_forward(memory, gain_state, w_state, w_update, gate_value, key_rows, values, head_count):
    normed = layer_norm(memory, gain_state).astype(jnp.bfloat16)
    projected = matmul(normed, w_state).astype(jnp.bfloat16)
    queries, own_keys, own_values = jnp.split(projected, 3, axis=1)
    mixture, log_total = attend_forward(
        queries,
        jnp.concatenate([own_keys, key_rows]),
        jnp.concatenate([own_values, values]),
        0.0,
        True,
        head_count,
    )
    update = matmul(mixture, w_update)
    return (gate_value * memory + (1.0 - gate_value) * update, own_keys, own_values)


def state_backward(
    memory,
    grad_next,
    grad_own_keys,
    grad_own_values,
    gain_state,
    w_state,
    w_update,
    gate_value,
    key_rows,
    values,
    head_count,
):
    mem_rows = memory.shape[0]
    normed_full, pull_norm = jax.vjp(layer_norm, memory, gain_state)
    normed = normed_full.astype(jnp.bfloat16)
    projected = matmul(normed, w_state).astype(jnp.bfloat16)
    queries, own_keys, own_values = jnp.split(projected, 3, axis=1)
    all_keys = jnp.concatenate([own_keys, key_rows])
    all_values = jnp.concatenate([own_values, values])
    mixture, log_total = attend_forward(queries, all_keys, all_values, 0.0, True, head_count)
    update = matmul(mixture, w_update)
    grad_update = ((1.0 - gate_value) * grad_next).astype(jnp.bfloat16)
    grad_gate = jnp.sum(grad_next * (memory - update), axis=0) * gate_value * (1.0 - gate_value)
    grad_mix = contract(grad_update, w_update, 1, 1).astype(jnp.bfloat16)
    grad_queries, grad_keys, grad_values, unused = attend_backward(
        queries, all_keys, all_values, 0.0, True, head_count, log_total, grad_mix
    )
    grad_proj = jnp.concatenate(
        [
            grad_queries,
            grad_keys[:mem_rows] + grad_own_keys,
            grad_values[:mem_rows] + grad_own_values,
        ],
        axis=1,
    ).astype(jnp.bfloat16)
    grad_normed = contract(grad_proj, w_state, 1, 1)
    grad_memory, grad_gain = pull_norm(grad_normed)
    return (
        gate_value * grad_next + grad_memory,
        grad_keys[mem_rows:],
        grad_values[mem_rows:],
        normed,
        grad_proj,
        mixture,
        grad_update,
        grad_gain,
        grad_gate,
    )


def regroup(grad_full, owners, groups):
    part_rows = grad_full.shape[0] // (owners * groups)
    shaped = grad_full.reshape((owners, groups, part_rows) + grad_full.shape[1:])
    return jnp.swapaxes(shaped, 0, 1).reshape(grad_full.shape)


def body(
    tokens,
    state_in,
    gain_tok,
    gain_state,
    gain_mlp,
    w_tok,
    w_state,
    w_out,
    w_update,
    gate_bias,
    rel_bias,
    w_up,
    w_down,
    d_out,
    d_state_next,
):
    head_count = H
    block_count = min(lax.axis_size("shard"), SEQ_BLOCKS)
    shard_pos = lax.axis_index("shard")
    position = shard_pos % block_count
    seq_slot = shard_pos // block_count
    (
        gain_tok_all,
        gain_state_all,
        gain_mlp_all,
        w_tok_all,
        w_state_all,
        w_out_all,
        w_update_all,
        gate_all,
        rel_all,
    ) = (
        lax.all_gather(gain_tok, "shard", axis=0, tiled=True),
        lax.all_gather(gain_state, "shard", axis=0, tiled=True),
        lax.all_gather(gain_mlp, "shard", axis=0, tiled=True),
        lax.all_gather(w_tok, "shard", axis=0, tiled=True),
        lax.all_gather(w_state, "shard", axis=0, tiled=True),
        lax.all_gather(w_out, "shard", axis=0, tiled=True),
        lax.all_gather(w_update, "shard", axis=0, tiled=True),
        lax.all_gather(gate_bias, "shard", axis=0, tiled=True),
        lax.all_gather(rel_bias, "shard", axis=0, tiled=True),
    )
    starts, next_grads = (
        lax.all_gather(state_in, "shard", axis=1, tiled=True),
        lax.all_gather(d_state_next, "shard", axis=1, tiled=True),
    )
    start_mine = lax.dynamic_index_in_dim(starts, seq_slot, 0, keepdims=False).astype(jnp.float32)
    next_grad_mine = lax.dynamic_index_in_dim(next_grads, seq_slot, 0, keepdims=False).astype(
        jnp.float32
    )
    gain_tok_full = gain_tok_all.astype(jnp.float32)
    gain_state_full = gain_state_all.astype(jnp.float32)
    gain_mlp_full = gain_mlp_all.astype(jnp.float32)
    gate_value = jax.nn.sigmoid(gate_all.astype(jnp.float32))
    token_rows = tokens.astype(jnp.float32)
    normed_full, pull_first = jax.vjp(layer_norm, token_rows, gain_tok_full)
    normed = normed_full.astype(jnp.bfloat16)
    projected = matmul(normed, w_tok_all).astype(jnp.bfloat16)
    queries, key_rows, values = jnp.split(projected, 3, axis=1)
    prev_keys, prev_values = from_behind((key_rows, values), "shard", 1)

    def run_state(memory):
        return state_forward(
            memory,
            gain_state_full,
            w_state_all,
            w_update_all,
            gate_value,
            key_rows,
            values,
            head_count,
        )

    def skip_state(memory):
        return (
            jnp.zeros_like(memory),
            jnp.zeros((memory.shape[0], D), jnp.bfloat16),
            jnp.zeros((memory.shape[0], D), jnp.bfloat16),
        )

    memory = start_mine
    kept_fwd = skip_state(memory)
    for turn_index in range(block_count):
        result = lax.cond(position == turn_index, run_state, skip_state, memory)
        kept_fwd = jax.tree.map(
            lambda fresh_one, older_one: jnp.where(position == turn_index, fresh_one, older_one),
            result,
            kept_fwd,
        )
        if turn_index + 1 < block_count:
            passed = from_behind(result[0].astype(jnp.bfloat16), "shard", 1).astype(jnp.float32)
            memory = jnp.where(position == turn_index + 1, passed, memory)
    new_memory, mem_keys, mem_values = kept_fwd
    allowed_pos, choose = position_terms()
    col_later = np.arange(2 * BLK)[None, :] >= BLK
    window = jnp.logical_and(allowed_pos, jnp.logical_or(col_later, position > 0))
    allowed = jnp.concatenate([jnp.ones((BLK, M), jnp.bool_), window], axis=1)
    per_distance = jnp.dot(rel_all.astype(jnp.float32), choose, precision=top_precision)
    pos_bias = jnp.concatenate(
        [jnp.zeros((head_count, BLK, M), jnp.float32), toeplitz_bias(per_distance)], axis=2
    )
    all_keys = jnp.concatenate([mem_keys, prev_keys, key_rows])
    all_values = jnp.concatenate([mem_values, prev_values, values])
    mixture, log_total = attend_forward(
        queries, all_keys, all_values, pos_bias, allowed, head_count
    )
    middle = token_rows + matmul(mixture, w_out_all)
    mlp_up, mlp_down = (
        lax.all_gather(w_up, "shard", axis=0, tiled=True),
        lax.all_gather(w_down, "shard", axis=0, tiled=True),
    )
    hidden_full, pull_mid = jax.vjp(layer_norm, middle, gain_mlp_full)
    hidden_in = hidden_full.astype(jnp.bfloat16)
    active_full, pull_gelu = jax.vjp(gelu_exact, contract(hidden_in, mlp_up, 1, 1))
    active = active_full.astype(jnp.bfloat16)
    output = middle + matmul(active, mlp_down)
    grad_active = contract(d_out, mlp_down, 1, 1)
    grad_w_down = contract(active, d_out, 0, 0)
    grad_up = pull_gelu(grad_active)[0].astype(jnp.bfloat16)
    grad_w_up = contract(grad_up, hidden_in, 0, 0)
    grad_hidden = matmul(grad_up, mlp_up)
    grad_middle_norm, grad_gain_mlp = pull_mid(grad_hidden)
    grad_middle = d_out.astype(jnp.float32) + grad_middle_norm
    grad_attn = grad_middle.astype(jnp.bfloat16)
    grad_w_out = contract(mixture, grad_attn, 0, 0)
    grad_mix = contract(grad_attn, w_out_all, 1, 1).astype(jnp.bfloat16)
    grad_queries, grad_keys, grad_values, grad_scores = attend_backward(
        queries, all_keys, all_values, pos_bias, allowed, head_count, log_total, grad_mix
    )
    grad_rel = jnp.dot(
        diagonal_sums(grad_scores[:, :, M:].astype(jnp.float32)), choose.T, precision=top_precision
    )
    recv_keys, recv_values = (
        from_behind(grad_keys[M : M + BLK].astype(jnp.bfloat16), "shard", -1).astype(jnp.float32),
        from_behind(grad_values[M : M + BLK].astype(jnp.bfloat16), "shard", -1).astype(jnp.float32),
    )
    grad_mem_keys = grad_keys[:M]
    grad_mem_values = grad_values[:M]

    def run_back(grad_next):
        return state_backward(
            memory,
            grad_next,
            grad_mem_keys,
            grad_mem_values,
            gain_state_full,
            w_state_all,
            w_update_all,
            gate_value,
            key_rows,
            values,
            head_count,
        )

    def skip_back(grad_next):
        mem_rows = grad_next.shape[0]
        return (
            jnp.zeros_like(grad_next),
            jnp.zeros((BLK, D), jnp.float32),
            jnp.zeros((BLK, D), jnp.float32),
            jnp.zeros((mem_rows, D), jnp.bfloat16),
            jnp.zeros((mem_rows, 3 * D), jnp.bfloat16),
            jnp.zeros((mem_rows, D), jnp.bfloat16),
            jnp.zeros((mem_rows, D), jnp.bfloat16),
            jnp.zeros((D,), jnp.float32),
            jnp.zeros((D,), jnp.float32),
        )

    grad_memory = jnp.where(position == block_count - 1, next_grad_mine, 0.0)
    kept_back = skip_back(grad_memory)
    for turn_index in reversed(range(block_count)):
        result = lax.cond(position == turn_index, run_back, skip_back, grad_memory)
        kept_back = jax.tree.map(
            lambda fresh_one, older_one: jnp.where(position == turn_index, fresh_one, older_one),
            result,
            kept_back,
        )
        if turn_index > 0:
            passed = from_behind(for_sending(result[0]), "shard", -1)
            grad_memory = jnp.where(position == turn_index - 1, passed, grad_memory)
    (
        grad_start,
        grad_tok_keys,
        grad_tok_values,
        mem_normed,
        mem_grad_proj,
        mem_mixture,
        mem_grad_update,
        grad_gain_state,
        grad_gate,
    ) = kept_back
    grad_w_state = contract(mem_normed, mem_grad_proj, 0, 0)
    grad_w_update = contract(mem_mixture, mem_grad_update, 0, 0)
    keys_total = grad_keys[M + BLK :] + recv_keys + grad_tok_keys
    values_total = grad_values[M + BLK :] + recv_values + grad_tok_values
    grad_proj = jnp.concatenate([grad_queries, keys_total, values_total], axis=1).astype(
        jnp.bfloat16
    )
    grad_w_tok = contract(normed, grad_proj, 0, 0)
    grad_normed = contract(grad_proj, w_tok_all, 1, 1)
    grad_rows_norm, grad_gain_tok = pull_first(grad_normed)
    grad_tokens = grad_middle + grad_rows_norm
    slot_hot = jnp.arange(starts.shape[0]) == seq_slot
    next_term = jnp.where(
        jnp.logical_and(slot_hot, position == block_count - 1)[:, None, None], new_memory[None], 0.0
    )
    start_term = jnp.where(
        jnp.logical_and(slot_hot, position == 0)[:, None, None], grad_start[None], 0.0
    )
    state_next, grad_state_in = (
        lax.psum_scatter(
            next_term.astype(jnp.bfloat16), "shard", scatter_dimension=1, tiled=True
        ).astype(jnp.float32),
        lax.psum_scatter(
            start_term.astype(jnp.bfloat16), "shard", scatter_dimension=1, tiled=True
        ).astype(jnp.float32),
    )
    owners = lax.axis_size("shard")
    groups = lax.axis_size("rep")
    spread = (
        lax.psum_scatter(
            regroup(grad_gain_tok, owners, groups),
            ("rep", "shard"),
            scatter_dimension=0,
            tiled=True,
        ),
        lax.psum_scatter(
            regroup(grad_gain_state, owners, groups),
            ("rep", "shard"),
            scatter_dimension=0,
            tiled=True,
        ),
        lax.psum_scatter(
            regroup(grad_gain_mlp, owners, groups),
            ("rep", "shard"),
            scatter_dimension=0,
            tiled=True,
        ),
        lax.psum_scatter(
            regroup(grad_w_tok, owners, groups), ("rep", "shard"), scatter_dimension=0, tiled=True
        ),
        lax.psum_scatter(
            regroup(grad_w_state, owners, groups), ("rep", "shard"), scatter_dimension=0, tiled=True
        ),
        lax.psum_scatter(
            regroup(grad_w_out, owners, groups), ("rep", "shard"), scatter_dimension=0, tiled=True
        ),
        lax.psum_scatter(
            regroup(grad_w_update, owners, groups),
            ("rep", "shard"),
            scatter_dimension=0,
            tiled=True,
        ),
        lax.psum_scatter(
            regroup(grad_gate, owners, groups), ("rep", "shard"), scatter_dimension=0, tiled=True
        ),
        lax.psum_scatter(
            regroup(grad_rel.reshape(-1), owners, groups),
            ("rep", "shard"),
            scatter_dimension=0,
            tiled=True,
        ),
        lax.psum_scatter(
            regroup(grad_w_up, owners, groups), ("rep", "shard"), scatter_dimension=0, tiled=True
        ),
        lax.psum_scatter(
            regroup(grad_w_down, owners, groups), ("rep", "shard"), scatter_dimension=0, tiled=True
        ),
    )
    pieces = (
        lax.all_gather(spread[0].astype(jnp.bfloat16), "rep", axis=0, tiled=True).astype(
            jnp.float32
        ),
        lax.all_gather(spread[1].astype(jnp.bfloat16), "rep", axis=0, tiled=True).astype(
            jnp.float32
        ),
        lax.all_gather(spread[2].astype(jnp.bfloat16), "rep", axis=0, tiled=True).astype(
            jnp.float32
        ),
        lax.all_gather(spread[3].astype(jnp.bfloat16), "rep", axis=0, tiled=True).astype(
            jnp.float32
        ),
        lax.all_gather(spread[4].astype(jnp.bfloat16), "rep", axis=0, tiled=True).astype(
            jnp.float32
        ),
        lax.all_gather(spread[5].astype(jnp.bfloat16), "rep", axis=0, tiled=True).astype(
            jnp.float32
        ),
        lax.all_gather(spread[6].astype(jnp.bfloat16), "rep", axis=0, tiled=True).astype(
            jnp.float32
        ),
        lax.all_gather(spread[7].astype(jnp.bfloat16), "rep", axis=0, tiled=True).astype(
            jnp.float32
        ),
        lax.all_gather(spread[8].astype(jnp.bfloat16), "rep", axis=0, tiled=True).astype(
            jnp.float32
        ),
        lax.all_gather(spread[9].astype(jnp.bfloat16), "rep", axis=0, tiled=True).astype(
            jnp.float32
        ),
        lax.all_gather(spread[10].astype(jnp.bfloat16), "rep", axis=0, tiled=True).astype(
            jnp.float32
        ),
    )
    rel_piece = pieces[8].reshape(head_count // owners, NB)
    return (
        output.astype(jnp.bfloat16),
        state_next,
        grad_tokens,
        grad_state_in,
        pieces[0],
        pieces[1],
        pieces[2],
        pieces[3],
        pieces[4],
        pieces[5],
        pieces[6],
        pieces[7],
        rel_piece,
        pieces[9],
        pieces[10],
    )


def solution(mesh):
    placed = (
        P(("rep", "shard"), None),
        P("rep", "shard", None),
        P("shard"),
        P("shard"),
        P("shard"),
        P("shard", None),
        P("shard", None),
        P("shard", None),
        P("shard", None),
        P("shard"),
        P("shard", None),
        P("shard", None),
        P("shard", None),
        P(("rep", "shard"), None),
        P("rep", "shard", None),
    )
    return jax.shard_map(
        body,
        mesh=mesh,
        in_specs=placed,
        out_specs=(
            P(("rep", "shard"), None),
            P("rep", "shard", None),
            P(("rep", "shard"), None),
            P("rep", "shard", None),
            P("shard"),
            P("shard"),
            P("shard"),
            P("shard", None),
            P("shard", None),
            P("shard", None),
            P("shard", None),
            P("shard"),
            P("shard", None),
            P("shard", None),
            P("shard", None),
        ),
        check_vma=False,
    )
```

profile of v0, /device:TPU:1, one launch (start us, length us, event | category | flops | bytes accessed | tf_op | source)
XLA Modules:
  0.0 2386.4 jit_solution(15404620387913708035)
XLA Ops:
  12.0 17.9 all-gather.2
  29.9 12.9 all-gather.1
  42.8 14.6 all-gather
  58.1 26.5 %all-gather.16.cloned.1.call-done = bf16[4,512,1024]{2,1,0:T(8,128)(2,1)} async-done(((bf16[4,64,1024]{2,1,0:T(8,128)(2,1)}), bf16[4,512,1024]{2,1,0:T(8,128)(2,1)}) %all-gather.16.cloned.1.call-update) | async-done | bytes 4194320 | tf_op jit(solution)/shard_map/all_gather | solution.py:285
  87.5 97.4 %all-gather.20.cloned.1.call-done = bf16[1024,3072]{1,0:T(8,128)(2,1)} async-done(((bf16[128,3072]{1,0:T(8,128)(2,1)}), bf16[1024,3072]{1,0:T(8,128)(2,1)}) %all-gather.20.cloned.1.call-update) | async-done | bytes 6291472 | tf_op jit(solution)/shard_map/all_gather | solution.py:277
  184.9 6.7 convolution_convert_fusion.8
  192.8 41.1 %all-gather.22.cloned.1.call-done = bf16[1024,1024]{1,0:T(8,128)(2,1)} async-done(((bf16[128,1024]{1,0:T(8,128)(2,1)}), bf16[1024,1024]{1,0:T(8,128)(2,1)}) %all-gather.22.cloned.1.call-update) | async-done | bytes 2097168 | tf_op jit(solution)/shard_map/all_gather | solution.py:280
  233.9 100.2 %all-gather.18.cloned.1.call-done = bf16[1024,3072]{1,0:T(8,128)(2,1)} async-done(((bf16[128,3072]{1,0:T(8,128)(2,1)}), bf16[1024,3072]{1,0:T(8,128)(2,1)}) %all-gather.18.cloned.1.call-update) | async-done | bytes 6291472 | tf_op jit(solution)/shard_map/all_gather | solution.py:278
  334.1 36.4 %conditional.4 = (bf16[512,1024]{1,0:T(8,128)(2,1)}, bf16[512,1024]{1,0:T(8,128)(2,1)}, bf16[512,1024]{1,0:T(8,128)(2,1)}) conditional(s32[]{:T(128)} %convert_element_type.279, () %tuple.41, (f32[1024]{0:T(1024)S(1)}, f32[512,1024]{1,0:T(8,128)}, f32[1024]{0:T(1024)S(1)}, bf16[1024,3072]{1,0:T(8,128)(2,1)}, bf16[512,1024]{1,0:T(8,128)(2,1)S(1)}, ...), branch_computations={%region_2.3_spmd, %region_3.8_spmd} | conditional | flops 6492780032 | bytes 101865528 | solution.py:325
  338.3 6.9 convolution_convert_fusion
  372.8 43.5 %all-gather.3 = bf16[8,1,32]{2,1,0:T(2,128)(2,1)S(1)} all-gather(bf16[1,1,32]{2,1,0:T(2,128)(2,1)S(1)} %bitcast.349), channel_id=1, replica_groups=mesh['rep'=4,'shard'=8] {'shard'}, dimensions={0}, use_global_device_ids=true | all-gather | bytes 576 | tf_op jit(solution)/shard_map/all_gather | solution.py:282
  421.5 46.0 %all-gather.4 = bf16[8,1,128]{2,1,0:T(2,128)(2,1)S(1)} all-gather(bf16[1,1,128]{2,1,0:T(2,128)(2,1)S(1)} %bitcast.350), channel_id=1, replica_groups=mesh['rep'=4,'shard'=8] {'shard'}, dimensions={0}, use_global_device_ids=true | all-gather | bytes 2304 | tf_op jit(solution)/shard_map/all_gather | solution.py:276
  467.5 7.7 tile.4
  475.2 25.3 %reshape.518 = f32[4198400]{0:T(1024)} reshape(f32[8,512,1025]{2,1,0:T(8,128)} %tile.4) | data formatting | bytes 33587200
  500.5 16.8 tile.10
  523.1 18.8 copy.390
  558.6 10.2 pad_maximum_fusion.8
  573.6 15.7 fusion.120
  589.3 11.2 exponential_reduce_fusion.4
  602.9 12.0 fusion.73
  620.5 12.0 fusion.106
  632.5 44.0 %all-gather.28.cloned.1.call-done = bf16[4096,1024]{1,0:T(8,128)(2,1)} async-done(((bf16[512,1024]{1,0:T(8,128)(2,1)}), bf16[4096,1024]{1,0:T(8,128)(2,1)}) %all-gather.28.cloned.1.call-update) | async-done | bytes 8388624 | tf_op jit(solution)/shard_map/all_gather | solution.py:351
  676.6 26.9 %add_convert_fusion = (bf16[512,4096]{1,0:T(8,128)(2,1)S(1)}, f32[512,4096]{1,0:T(8,128)}) fusion(f32[512,4096]{1,0:T(8,128)} %fusion.106, bf16[512,1024]{1,0:T(8,128)(2,1)S(1)} %copy-done.47, bf16[4096,1024]{1,0:T(8,128)(2,1)} %all-gather.28.cloned.1.call-done), kind=kOutput, calls=%fused_computation.141 | convolution fusion | flops 4445962240 | bytes 30408704 | tf_op jit(solution)/shard_map/dot_general | solution.py:89
  714.9 9.8 multiply_convert_fusion.13
  742.5 7.0 all-gather.30.cloned.1.call-done
  752.4 9.1 multiply_reduce_fusion.17
  772.0 10.6 convolution_bitcast_fusion.2
  789.4 18.0 multiply_reduce_fusion.16
  807.5 16.9 multiply_convert_fusion.12
  832.9 12.5 conditional.6
  848.8 174.2 %collective-permute-done.4 = bf16[512,1024]{1,0:T(8,128)(2,1)S(1)} collective-permute-done((bf16[512,1024]{1,0:T(8,128)(2,1)S(1)}, bf16[512,1024]{1,0:T(8,128)(2,1)S(1)}, u32[]{:S(2)}, u32[]{:S(2)}) %collective-permute-start.4) | collective-permute-done | bytes 1048608 | tf_op jit(solution)/shard_map/ppermute | solution.py:25
  1024.6 114.8 %conditional.7 = (f32[512,1024]{1,0:T(8,128)}, bf16[512,1024]{1,0:T(8,128)(2,1)}, bf16[512,3072]{0,1:T(8,128)(2,1)}, bf16[512,1024]{1,0:T(8,128)(2,1)S(1)}, f32[...) conditional(s32[]{:T(128)} %convert_element_type.279, () %tuple.44, ...), branch_computations={%region_33.34_spmd, %region_34.44_spmd} | conditional | flops 15157163008 | bytes 503607872 | solution.py:413
  1076.5 7.8 convolution_bitcast_fusion.1
  1090.9 12.4 multiply_reduce_fusion.10
  1103.3 12.3 multiply_convert_fusion.8
  1125.6 6.7 multiply_reduce_fusion.13
  1150.8 10.3 fusion.55
  1161.1 10.8 copy.303
  1185.8 9.9 multiply_convert_fusion.14
  1200.6 18.0 collective-permute-done.5
  1221.5 61.4 %collective-permute-done.3 = bf16[512,1024]{1,0:T(8,128)(2,1)} collective-permute-done((bf16[512,1024]{1,0:T(8,128)(2,1)}, bf16[512,1024]{1,0:T(8,128)(2,1)}, u32[]{:S(2)}, u32[]{:S(2)}) %collective-permute-start.3) | collective-permute-done | bytes 1048608 | tf_op jit(solution)/shard_map/ppermute | solution.py:25
  1285.9 7.0 fusion.79
  1292.8 10.8 copy.302
  1306.4 7.6 slice_bitcast_fusion.2
  1314.0 11.4 copy.349
  1325.4 8.9 concatenate.60
  1334.3 19.4 reshape.520
  1353.6 18.5 reshape.461
  1376.5 10.2 add_convert_fusion.3
  1388.5 7.2 fusion.71
  1398.6 52.3 %all-reduce.14 = (bf16[1024]{0:T(1024)(128)(2,1)S(1)}, bf16[1024]{0:T(1024)(128)(2,1)S(1)}, bf16[1024]{0:T(1024)(128)(2,1)S(1)}, bf16[1024]{0:T(1024)(128)(2,1)S(1)}, bf16[256]{0:T(256)(128)(2,1)S(1)}) all-reduce(f32[1024]{0:T(1024)S(1)} %reshape.446, ...), channel_id=4, replica_groups=mesh['rep'=4,'shard'=8] {'rep','shard'}, use_global_device_ids=true, to_apply=%region_48.49.clone | all-reduce | flops 4352 | bytes 26112
  1459.9 87.4 %reduce-scatter.23.cloned.1.call-done = f32[128,1024]{1,0:T(8,128)} async-done(((f32[4096,1024]{1,0:T(8,128)}), f32[128,1024]{1,0:T(8,128)}) %reduce-scatter.23.cloned.1.call-update) | async-done | bytes 524304 | tf_op jit(solution)/shard_map/reduce_scatter | solution.py:507
  1553.8 85.0 %reduce-scatter.9.cloned.1.call-done = bf16[4,64,1024]{2,1,0:T(8,128)(2,1)} async-done(((bf16[4,512,1024]{2,1,0:T(8,128)(2,1)}), bf16[4,64,1024]{2,1,0:T(8,128)(2,1)}) %reduce-scatter.9.cloned.1.call-update) | async-done | bytes 524304 | tf_op jit(solution)/shard_map/reduce_scatter | solution.py:452
  1640.9 137.2 %reduce-scatter.17.cloned.1.call-done = f32[32,1024]{1,0:T(8,128)} async-done(((f32[1024,1024]{1,0:T(8,128)}), f32[32,1024]{1,0:T(8,128)}) %reduce-scatter.17.cloned.1.call-update) | async-done | bytes 131088 | tf_op jit(solution)/shard_map/reduce_scatter | solution.py:486
  1779.0 12.7 all_gather.90
  1792.5 127.1 %reduce-scatter.19.cloned.1.call-done = f32[32,1024]{1,0:T(8,128)} async-done(((f32[1024,1024]{1,0:T(8,128)}), f32[32,1024]{1,0:T(8,128)}) %reduce-scatter.19.cloned.1.call-update) | async-done | bytes 131088 | tf_op jit(solution)/shard_map/reduce_scatter | solution.py:489
  1920.5 13.9 all_gather.91
  1935.2 82.3 %reduce-scatter.11.cloned.1.call-done = bf16[4,64,1024]{2,1,0:T(8,128)(2,1)} async-done(((bf16[4,512,1024]{2,1,0:T(8,128)(2,1)}), bf16[4,64,1024]{2,1,0:T(8,128)(2,1)}) %reduce-scatter.11.cloned.1.call-update) | async-done | bytes 524304 | tf_op jit(solution)/shard_map/reduce_scatter | solution.py:455
  2019.6 157.8 %reduce-scatter.15.cloned.1.call-done = f32[32,3072]{1,0:T(8,128)} async-done(((f32[1024,3072]{1,0:T(8,128)}), f32[32,3072]{1,0:T(8,128)}) %reduce-scatter.15.cloned.1.call-update) | async-done | bytes 393232 | tf_op jit(solution)/shard_map/reduce_scatter | solution.py:483
  2178.5 10.4 all_gather.89
  2190.1 148.7 %reduce-scatter.13.cloned.1.call-done = f32[32,3072]{1,0:T(8,128)} async-done(((f32[1024,3072]{1,0:T(8,128)}), f32[32,3072]{1,0:T(8,128)}) %reduce-scatter.13.cloned.1.call-update) | async-done | bytes 393232 | tf_op jit(solution)/shard_map/reduce_scatter | solution.py:480
  2339.9 10.4 all_gather.88
  2351.6 6.8 all-gather.32.cloned.1.call-done
  2361.2 15.4 all-gather.34.cloned.1.call-done
  (394 shorter events, 310.3 us)
Async XLA Ops:
  7.2 22.7 copy-start.85
  7.2 35.6 %copy-start.86 = (bf16[128]{0:T(256)(128)(2,1)S(1)}, bf16[128]{0:T(256)(128)(2,1)}, u32[]{:S(2)}) copy-start(bf16[128]{0:T(256)(128)(2,1)} %param.36) | copy-start | bytes 772
  7.2 50.2 %copy-start.5 = (bf16[512,1024]{1,0:T(8,128)(2,1)S(1)}, bf16[512,1024]{1,0:T(8,128)(2,1)}, u32[]{:S(2)}) copy-start(bf16[512,1024]{1,0:T(8,128)(2,1)} %param.27) | copy-start | bytes 3145732
  7.2 77.4 %all-gather.16.cloned.1.call-start = ((), (), s32[]{:S(2)}) async-start(), calls=%async_computation.8 | async-start | bytes 4718592 | tf_op jit(solution)/shard_map/all_gather | solution.py:285
  8.0 176.9 %all-gather.20.cloned.1.call-start = ((), (), s32[]{:S(2)}) async-start(), calls=%async_computation.10 | async-start | bytes 7077888 | tf_op jit(solution)/shard_map/all_gather | solution.py:277
  8.7 225.2 %all-gather.22.cloned.1.call-start = ((), (), s32[]{:S(2)}) async-start(), calls=%async_computation.11 | async-start | bytes 2359296 | tf_op jit(solution)/shard_map/all_gather | solution.py:280
  9.4 324.6 %all-gather.18.cloned.1.call-start = ((), (), s32[]{:S(2)}) async-start(), calls=%async_computation.9 | async-start | bytes 7077888 | tf_op jit(solution)/shard_map/all_gather | solution.py:278
  10.0 604.9 %all-gather.24.cloned.1.call-start = ((), (), s32[]{:S(2)}) async-start(), calls=%async_computation.12 | async-start | bytes 2359296 | tf_op jit(solution)/shard_map/all_gather | solution.py:279
  10.6 609.9 %all-gather.26.cloned.1.call-start = ((), (), s32[]{:S(2)}) async-start(), calls=%async_computation.13 | async-start | bytes 9437184 | tf_op jit(solution)/shard_map/all_gather | solution.py:350
  11.2 665.4 %all-gather.28.cloned.1.call-start = ((), (), s32[]{:S(2)}) async-start(), calls=%async_computation.14 | async-start | bytes 9437184 | tf_op jit(solution)/shard_map/all_gather | solution.py:351
  11.9 737.6 %all-gather.30.cloned.1.call-start = ((), (), s32[]{:S(2)}) async-start(), calls=%async_computation.16 | async-start | bytes 4718592 | tf_op jit(solution)/shard_map/all_gather | solution.py:286
  29.9 155.0 %copy-start.58 = (f32[8,1,128]{2,1,0:T(1,128)}, f32[8,1,128]{2,1,0:T(1,128)S(1)}, u32[]{:S(2)}) copy-start(f32[8,1,128]{2,1,0:T(1,128)S(1)} %convert_element_type.336) | copy-start | bytes 12292
  42.8 511.0 %copy-start.68 = (f32[8,1,128]{2,1,0:T(1,128)}, f32[8,1,128]{2,1,0:T(1,128)S(1)}, u32[]{:S(2)}) copy-start(f32[8,1,128]{2,1,0:T(1,128)S(1)} %convert_element_type.335) | copy-start | bytes 12292
  57.6 127.2 %copy-start.62 = (f32[512]{0:T(512)}, f32[512]{0:T(512)S(1)}, u32[]{:S(2)}) copy-start(f32[512]{0:T(512)S(1)} %broadcast_multiply_fusion.5) | copy-start | bytes 6148
  58.1 126.8 %copy-start.74 = (f32[512]{0:T(512)}, f32[512]{0:T(512)S(1)}, u32[]{:S(2)}) copy-start(f32[512]{0:T(512)S(1)} %fusion.70) | copy-start | bytes 6148
  58.1 126.8 %copy-start.66 = (f32[512]{0:T(512)}, f32[512]{0:T(512)S(1)}, u32[]{:S(2)}) copy-start(f32[512]{0:T(512)S(1)} %fusion.96) | copy-start | bytes 6148
  58.1 495.7 %copy-start.64 = (f32[1024]{0:T(1024)}, f32[1024]{0:T(1024)S(1)}, u32[]{:S(2)}) copy-start(f32[1024]{0:T(1024)S(1)} %bitcast_divide_fusion) | copy-start | bytes 12292
  192.8 365.8 %copy-start.7 = (bf16[512,1024]{1,0:T(8,128)(2,1)}, bf16[512,1024]{1,0:T(8,128)(2,1)S(1)}, u32[]{:S(2)}) copy-start(bf16[512,1024]{1,0:T(8,128)(2,1)S(1)} %get-tuple-element.343) | copy-start | bytes 3145732
  192.8 409.1 %copy-start.3 = (bf16[512,1024]{1,0:T(8,128)(2,1)}, bf16[512,1024]{1,0:T(8,128)(2,1)S(1)}, u32[]{:S(2)}) copy-start(bf16[512,1024]{1,0:T(8,128)(2,1)S(1)} %get-tuple-element.341) | copy-start | bytes 3145732
  334.1 38.7 %copy-start.87 = (bf16[1,32]{1,0:T(2,128)(2,1)S(1)}, bf16[1,32]{1,0:T(2,128)(2,1)}, u32[]{:S(2)}) copy-start(bf16[1,32]{1,0:T(2,128)(2,1)} %param.37) | copy-start | bytes 196
  334.1 87.2 %copy-start.70 = (f32[32,513]{1,0:T(8,128)S(1)}, f32[32,513]{1,0:T(8,128)}, u32[]{:S(2)}) copy-start(f32[32,513]{1,0:T(8,128)} %constant.239.clone) | copy-start | bytes 196996
  334.1 87.4 %copy-start.88 = (bf16[128]{0:T(256)(128)(2,1)S(1)}, bf16[128]{0:T(256)(128)(2,1)}, u32[]{:S(2)}) copy-start(bf16[128]{0:T(256)(128)(2,1)} %param.31) | copy-start | bytes 772
  361.3 5.3 copy-start.20
  370.4 180.1 %collective-permute-start = (bf16[512,1024]{1,0:T(8,128)(2,1)}, bf16[512,1024]{1,0:T(8,128)(2,1)}, u32[]{:S(2)}, u32[]{:S(2)}) collective-permute-start(bf16[512,1024]{1,0:T(8,128)(2,1)} %get-tuple-element.149), channel_id=1, source_target_pairs={{0,1},{1,2},{2,3},{3,4},{4,5},{5,6},{6,7},{8,9},{9,10},{10,11},{11... | collective-permute-start | bytes 3145736 | tf_op jit(solution)/shard_map/ppermute | solution.py:25
  372.7 1013.9 %reduce-scatter.21.cloned.1.call-start = ((), (), s32[]{:S(2)}) async-start(), calls=%async_computation.22 | async-start | bytes 17301504 | tf_op jit(solution)/shard_map/reduce_scatter | solution.py:504
  416.3 142.3 %collective-permute-start.2 = (bf16[512,1024]{1,0:T(8,128)(2,1)S(1)}, bf16[512,1024]{1,0:T(8,128)(2,1)}, u32[]{:S(2)}, u32[]{:S(2)}) collective-permute-start(bf16[512,1024]{1,0:T(8,128)(2,1)S(1)} %get-tuple-element.343), channel_id=1, source_target_pairs={{0,1},{1,2},{2,3},{3,4},{4,5},{5,6},{6,7},{8,9},{9,10},{10,11},{11... | collective-permute-start | bytes 3145736 | tf_op jit(solution)/shard_map/ppermute | solution.py:25
  517.3 5.8 slice-start
  523.1 18.8 copy-start.83
  523.1 18.9 copy-start.57
  543.2 58.7 %collective-permute-start.1 = (bf16[512,1024]{1,0:T(8,128)(2,1)S(1)}, bf16[512,1024]{1,0:T(8,128)(2,1)}, u32[]{:S(2)}, u32[]{:S(2)}) collective-permute-start(bf16[512,1024]{1,0:T(8,128)(2,1)S(1)} %get-tuple-element.341), channel_id=1, source_target_pairs={{0,1},{1,2},{2,3},{3,4},{4,5},{5,6},{6,7},{8,9},{9,10},{10,11},{11... | collective-permute-start | bytes 3145736 | tf_op jit(solution)/shard_map/ppermute | solution.py:25
  620.5 56.1 %copy-start.47 = (bf16[512,1024]{1,0:T(8,128)(2,1)S(1)}, bf16[512,1024]{1,0:T(8,128)(2,1)}, u32[]{:S(2)}) copy-start(bf16[512,1024]{1,0:T(8,128)(2,1)} %param.40) | copy-start | bytes 3145732
  632.5 70.9 %copy-start.18 = (f32[512,1024]{1,0:T(8,128)S(1)}, f32[512,1024]{1,0:T(8,128)}, u32[]{:S(2)}) copy-start(f32[512,1024]{1,0:T(8,128)} %copy-done.17) | copy-start | bytes 6291460
  714.7 832.7 %reduce-scatter.23.cloned.1.call-start = ((), (), s32[]{:S(2)}) async-start(), calls=%async_computation.24 | async-start | bytes 17301504 | tf_op jit(solution)/shard_map/reduce_scatter | solution.py:507
  737.5 901.3 %reduce-scatter.9.cloned.1.call-start = ((), (), s32[]{:S(2)}) async-start(), calls=%async_computation.15 | async-start | bytes 4718592 | tf_op jit(solution)/shard_map/reduce_scatter | solution.py:452
  742.2 1035.9 %reduce-scatter.17.cloned.1.call-start = ((), (), s32[]{:S(2)}) async-start(), calls=%async_computation.20 | async-start | bytes 4325376 | tf_op jit(solution)/shard_map/reduce_scatter | solution.py:486
  752.4 9.2 copy-start.77
  787.9 1131.7 %reduce-scatter.19.cloned.1.call-start = ((), (), s32[]{:S(2)}) async-start(), calls=%async_computation.21 | async-start | bytes 4325376 | tf_op jit(solution)/shard_map/reduce_scatter | solution.py:489
  807.5 16.9 copy-start.33
  845.4 179.2 %copy-start.53 = (bf16[512,1024]{1,0:T(8,128)(2,1)}, bf16[512,1024]{1,0:T(8,128)(2,1)S(1)}, u32[]{:S(2)}) copy-start(bf16[512,1024]{1,0:T(8,128)(2,1)S(1)} %get-tuple-element.164) | copy-start | bytes 3145732
  845.4 179.2 %copy-start.78 = (f32[1024]{0:T(1024)}, f32[1024]{0:T(1024)S(1)}, u32[]{:S(2)}) copy-start(f32[1024]{0:T(1024)S(1)} %get-tuple-element.172) | copy-start | bytes 12292
  845.4 179.2 %copy-start.80 = (f32[1024]{0:T(1024)}, f32[1024]{0:T(1024)S(1)}, u32[]{:S(2)}) copy-start(f32[1024]{0:T(1024)S(1)} %get-tuple-element.162) | copy-start | bytes 12292
  847.5 175.5 %collective-permute-start.4 = (bf16[512,1024]{1,0:T(8,128)(2,1)S(1)}, bf16[512,1024]{1,0:T(8,128)(2,1)S(1)}, u32[]{:S(2)}, u32[]{:S(2)}) collective-permute-start(bf16[512,1024]{1,0:T(8,128)(2,1)S(1)} %convert_element_type.306), channel_id=1, source_target_pairs={{1,0},{2,1},{3,2},{4,3},{5,4},{6,5},{7,6},{9,8},{10,9},{11,10},{12... | collective-permute-start | bytes 3145736 | tf_op jit(solution)/shard_map/ppermute | solution.py:25
  1051.7 6.2 copy-start.26
  1060.4 6.4 copy-start.1
  1060.4 6.4 copy-start.28
  1070.9 5.6 copy-start.36
  1103.3 12.3 copy-start.27
  1120.0 5.6 slice-start.3
  1144.4 873.1 %reduce-scatter.11.cloned.1.call-start = ((), (), s32[]{:S(2)}) async-start(), calls=%async_computation.17 | async-start | bytes 4718592 | tf_op jit(solution)/shard_map/reduce_scatter | solution.py:455
  1149.6 1027.8 %reduce-scatter.15.cloned.1.call-start = ((), (), s32[]{:S(2)}) async-start(), calls=%async_computation.19 | async-start | bytes 12976128 | tf_op jit(solution)/shard_map/reduce_scatter | solution.py:483
  1171.9 1166.9 %reduce-scatter.13.cloned.1.call-start = ((), (), s32[]{:S(2)}) async-start(), calls=%async_computation.18 | async-start | bytes 12976128 | tf_op jit(solution)/shard_map/reduce_scatter | solution.py:480
  1175.0 43.6 %collective-permute-start.5 = (bf16[512,1024]{1,0:T(8,128)(2,1)}, bf16[512,1024]{1,0:T(8,128)(2,1)}, u32[]{:S(2)}, u32[]{:S(2)}) collective-permute-start(bf16[512,1024]{1,0:T(8,128)(2,1)} %copy.318), channel_id=1, source_target_pairs={{1,0},{2,1},{3,2},{4,3},{5,4},{6,5},{7,6},{9,8},{10,9},{11,10},{12... | collective-permute-start | bytes 3145736 | tf_op jit(solution)/shard_map/ppermute | solution.py:25
  1179.0 6.8 copy-start.12
  1184.3 98.6 %collective-permute-start.3 = (bf16[512,1024]{1,0:T(8,128)(2,1)}, bf16[512,1024]{1,0:T(8,128)(2,1)}, u32[]{:S(2)}, u32[]{:S(2)}) collective-permute-start(bf16[512,1024]{1,0:T(8,128)(2,1)} %copy.316), channel_id=1, source_target_pairs={{1,0},{2,1},{3,2},{4,3},{5,4},{6,5},{7,6},{9,8},{10,9},{11,10},{12... | collective-permute-start | bytes 3145736 | tf_op jit(solution)/shard_map/ppermute | solution.py:25
  1195.7 22.9 copy-start.39
  1197.3 88.5 %copy-start.45 = (bf16[512,1024]{1,0:T(8,128)(2,1)}, bf16[512,1024]{1,0:T(8,128)(2,1)S(1)}, u32[]{:S(2)}) copy-start(bf16[512,1024]{1,0:T(8,128)(2,1)S(1)} %copy.314) | copy-start | bytes 3145732
  1218.6 64.3 %copy-start.40 = (f32[512,1024]{1,0:T(8,128)S(1)}, f32[512,1024]{1,0:T(8,128)}, u32[]{:S(2)}) copy-start(f32[512,1024]{1,0:T(8,128)} %copy.315) | copy-start | bytes 6291460
  1221.5 64.3 %copy-start.43 = (bf16[512,1024]{1,0:T(8,128)(2,1)}, bf16[512,1024]{1,0:T(8,128)(2,1)S(1)}, u32[]{:S(2)}) copy-start(bf16[512,1024]{1,0:T(8,128)(2,1)S(1)} %add_convert_fusion.1) | copy-start | bytes 3145732
  1285.9 7.0 copy-start.44
  1303.7 1054.7 %all-gather.32.cloned.1.call-start = ((), (), s32[]{:S(2)}) async-start(), calls=%async_computation.23 | async-start | bytes 1310720 | tf_op jit(solution)/shard_map/all_gather | solution.py:539
  1388.5 7.3 copy-start.75
  1388.5 988.1 %all-gather.34.cloned.1.call-start = ((), (), s32[]{:S(2)}) async-start(), calls=%async_computation.25 | async-start | bytes 1310720 | tf_op jit(solution)/shard_map/all_gather | solution.py:542
  1395.8 153.9 %copy-start.16 = (f32[512,1024]{1,0:T(8,128)S(1)}, f32[512,1024]{1,0:T(8,128)}, u32[]{:S(2)}) copy-start(f32[512,1024]{1,0:T(8,128)} %copy-done.15) | copy-start | bytes 6291460
  1395.8 153.9 %copy-start.73 = (f32[512]{0:T(512)S(1)}, f32[512]{0:T(512)}, u32[]{:S(2)}) copy-start(f32[512]{0:T(512)} %copy-done.72) | copy-start | bytes 6148
  (44 other events, 118.6 us)
Sparse Core Ops, SparseCore 0:
  10.2 74.3 all-gather.15
  86.8 97.9 all-gather.19
  187.0 46.8 all-gather.21
  235.9 98.0 all-gather.17
  336.0 46.8 all-gather.23
  384.9 146.2 all-gather.25
  533.4 143.1 all-gather.27
  678.8 70.7 all-gather.29
  751.9 379.4 reduce-scatter.20
  1133.5 413.8 reduce-scatter.22
  1551.0 87.7 reduce-scatter.8
  1641.0 137.0 reduce-scatter.16
  1780.5 139.1 reduce-scatter.18
  1923.5 93.9 reduce-scatter.10
  2023.4 154.0 reduce-scatter.14
  2184.4 154.4 reduce-scatter.12
  2340.8 17.5 all-gather.31
  2359.8 16.7 all-gather.33
where the time goes:
time: 2390 us
  waiting for transfers between devices  1420 us (59%)
  local copies, waits for them, and re-layouts  275 us (12%)
  matrix products  249 us (10%)
  blocking collectives  240 us (10%)
  other arithmetic  161 us (7%)
    ppermute x6, waiting for transfers between devices, from_behind(): return lax.ppermute(shard, axis, pairs)  254 us
    reduce_scatter x1, waiting for transfers between devices, body(): lax.psum_scatter(regroup(grad_w_state, owners, groups), ('rep', 'shard'),...  158 us
    reduce_scatter x1, waiting for transfers between devices, body(): lax.psum_scatter(regroup(grad_w_tok, owners, groups), ('rep', 'shard'), s...  149 us
    reduce_scatter x1, waiting for transfers between devices, body(): lax.psum_scatter(regroup(grad_w_out, owners, groups), ('rep', 'shard'), s...  137 us
    reduce_scatter x1, waiting for transfers between devices, body(): lax.psum_scatter(regroup(grad_w_update, owners, groups), ('rep', 'shard')...  127 us
    unnamed x151, local copies, waits for them, and re-layouts  100 us
    all_gather x1, waiting for transfers between devices, body(): lax.all_gather(w_state, 'shard', axis=0, tiled=True)  100 us
    all_gather x1, waiting for transfers between devices, body(): lax.all_gather(w_tok, 'shard', axis=0, tiled=True)  97.4 us
  transfers between devices with their start and end apart: 24, of which 18 were waited for; matrix products, arithmetic and copies ran while one was open for 27% of the time, Pallas kernels for 0%

commit v1 on v0

v1 whole, which is shorter than its diff:
```python
import functools
import math

import jax
import jax.numpy as jnp
import numpy as np
from jax import lax
from jax.experimental import pallas as pl
from jax.experimental.pallas import tpu as pltpu
from jax.sharding import Mesh
from jax.sharding import PartitionSpec as P


D = 1024
H = 8
HL = 4
DH = D // H
BLK = 512
M = 512
NB = 32
REACH = 128
HALF = 256
KEEP = HL * DH
NEG = -1e30
eps = 1e-06
SCALE = 1.0 / math.sqrt(DH)
BF = jnp.bfloat16
F32 = jnp.float32

AXIS_BITS = {"c": ("c", 1), "x": ("x", 1), "y": ("g", 1), "z1": ("s", 1), "z2": ("s", 2)}
VMEM_CAP = 56 * 1024 * 1024


def xch(value, bit):
    axis, mask = AXIS_BITS[bit]
    count = lax.axis_size(axis)
    return lax.ppermute(value, axis, [(i, i ^ mask) for i in range(count)])


def diag_send(value):
    return lax.ppermute(value, ("c", "x"), [(1, 2), (2, 1)])


def gather_bits(piece, order):
    held = piece
    for bit in order[:-1]:
        held = jnp.stack([held, xch(held, bit)])
    return held, xch(held, order[-1])


def reduce_bits(parts, order):
    for bit in order:
        got = xch(parts[1], bit)
        parts = (parts[0].astype(F32) + got.astype(F32)).astype(BF)
    return over_groups(parts)


def over_groups(part):
    groups = lax.axis_size("g")
    step = 2
    while step < groups:
        got = lax.ppermute(part, "g", [(i, i ^ step) for i in range(groups)])
        part = (part.astype(F32) + got.astype(F32)).astype(part.dtype)
        step *= 2
    return part


def untwist(value, bits):
    for axis, bit in enumerate(bits):
        value = jnp.where(bit == 1, jnp.flip(value, axis), value)
    return value


def mm(a, b):
    return jnp.dot(a, b, preferred_element_type=F32)


def mm_nt(a, b):
    return lax.dot_general(a, b, (((1,), (1,)), ((), ())), preferred_element_type=F32)


def mm_tn(a, b):
    return lax.dot_general(a, b, (((0,), (0,)), ((), ())), preferred_element_type=F32)


def norm_parts(values):
    centered = values - jnp.mean(values, axis=-1, keepdims=True)
    variance = jnp.mean(centered * centered, axis=-1, keepdims=True)
    rstd = lax.rsqrt(variance + eps)
    return centered * rstd, rstd


def norm_back(values, gain, grad):
    hat, rstd = norm_parts(values)
    g = grad * gain
    inner = g - jnp.mean(g, axis=-1, keepdims=True)
    inner = inner - hat * jnp.mean(g * hat, axis=-1, keepdims=True)
    return inner * rstd, grad * hat


def bucket_table(block_len, bucket_count, reach_len):
    distance = np.arange(2 * block_len + 1)
    exact = bucket_count // 2
    ratio = np.log(np.maximum(distance, 1) / exact) / np.log(reach_len / exact)
    far = np.minimum(
        exact + np.floor(ratio * (bucket_count - exact)).astype(np.int64), bucket_count - 1
    )
    return np.where(distance < exact, distance, far).astype(np.int32)


def slab_buckets():
    s = np.arange(8)[:, None]
    col = np.arange(BLK)[None, :]
    return bucket_table(BLK, NB, REACH)[(s - col) % BLK].reshape(-1)


def params(flops=0, moved=0, trans=0, grid=1):
    return dict(
        compiler_params=pltpu.CompilerParams(
            vmem_limit_bytes=VMEM_CAP, dimension_semantics=("arbitrary",) * grid
        ),
        cost_estimate=pl.CostEstimate(flops=flops, bytes_accessed=moved, transcendentals=trans),
    )


def full(shape, memory_space=None):
    return pl.BlockSpec(shape, lambda *_: (0,) * len(shape))


def pick_kernel(me, tok, st, *outs):
    c, y = me[0], me[3]
    for sub in range(3):
        for i in range(2):
            j = 6 * y + 2 * sub + i
            col = (j // HL) * D + (2 * (j % HL) + c) * DH
            src = pl.ds(pl.multiple_of(col, DH), DH)
            dst = slice(i * DH, (i + 1) * DH)
            outs[sub][0:DH, dst] = tok[:, src]
            outs[sub][DH : 2 * DH, dst] = st[:, src]


def pick_columns(me, w_tok, w_state):
    one = jax.ShapeDtypeStruct((2 * DH, 2 * DH), BF)
    return pl.pallas_call(
        pick_kernel,
        grid_spec=pltpu.PrefetchScalarGridSpec(
            num_scalar_prefetch=1,
            grid=(1,),
            in_specs=[full(w_tok.shape), full(w_state.shape)],
            out_specs=[full((2 * DH, 2 * DH))] * 3,
        ),
        out_shape=[one] * 3,
        name="pick",
        **params(moved=3 * 2**20),
    )(me, w_tok, w_state)


def lay_kernel(me, a0, a1, b0, b1, c0, c1, tok, st, small):
    q = pl.program_id(0)
    x0, y0 = me[1], me[3]
    low = lax.rem(q, 2) == 0
    c_val = jnp.where(low, c0[...], c1[...])
    for xr in range(2):
        for yr in range(2):
            va = (a0, a1)[xr][yr, 0, 0]
            vb = (b0, b1)[yr][0, xr, 0]
            vc = c_val[xr, yr, 0]
            rows = pl.ds(pl.multiple_of((x0 ^ xr) * DH, DH), DH)
            for sub, v in enumerate((va, vb, vc)):
                cols = pl.ds(pl.multiple_of((y0 ^ yr) * 768 + sub * 256, 256), 256)
                tok[rows, cols] = v[0:DH]
                st[rows, cols] = v[DH : 2 * DH]
        small[x0 ^ xr] = (a0, a1)[xr][0, 0, 0, 2 * DH : 2 * DH + 16]


def lay_tables(me, a, b, c):
    ra = a[0].shape[-2]
    a_spec = pl.BlockSpec((2, 1, 1, ra, 256), lambda q, me: (0, q % 2, q // 2, 0, 0))
    b_spec = pl.BlockSpec((1, 2, 1, 256, 256), lambda q, me: (q % 2, 0, q // 2, 0, 0))
    c_spec = pl.BlockSpec((2, 2, 1, 256, 256), lambda q, me: (0, 0, q // 2, 0, 0))
    w_spec = pl.BlockSpec((2 * DH, 3 * KEEP), lambda q, me: (q ^ me[2], 0))
    return pl.pallas_call(
        lay_kernel,
        grid_spec=pltpu.PrefetchScalarGridSpec(
            num_scalar_prefetch=1,
            grid=(4,),
            in_specs=[a_spec, a_spec, b_spec, b_spec, c_spec, c_spec],
            out_specs=[
                w_spec,
                w_spec,
                pl.BlockSpec((2, 16, 256), lambda q, me: (q ^ me[2], 0, 0)),
            ],
        ),
        out_shape=[
            jax.ShapeDtypeStruct((D, 3 * KEEP), BF),
            jax.ShapeDtypeStruct((D, 3 * KEEP), BF),
            jax.ShapeDtypeStruct((8, 16, 256), BF),
        ],
        name="lay",
        **params(moved=14 * 2**20),
    )(me, *a, *b, *c)


def lay_out_kernel(me, low, high, wo, wu):
    x0, z0, y0 = me[1], me[2], me[3]
    q = low.shape[3] // 2
    for xr in range(2):
        src = (low, high)[xr]
        for yr in range(2):
            for zr in range(4):
                v = src[yr, zr % 2, zr // 2]
                row = (z0 ^ zr) * DH + ((x0 ^ xr) * 2 + (y0 ^ yr)) * q
                rows = pl.ds(pl.multiple_of(row, q), q)
                wo[rows, :] = v[0:q]
                wu[rows, :] = v[q : 2 * q]


def lay_out_tables(me, low, high):
    one = jax.ShapeDtypeStruct((KEEP, D), BF)
    return pl.pallas_call(
        lay_out_kernel,
        grid_spec=pltpu.PrefetchScalarGridSpec(
            num_scalar_prefetch=1,
            grid=(1,),
            in_specs=[full(low.shape), full(high.shape)],
            out_specs=[full((KEEP, D))] * 2,
        ),
        out_shape=[one, one],
        name="lay_out",
        **params(moved=4 * 2**20),
    )(me, low, high)


def bias_kernel(base, out):
    slab = base[0]
    for a in range(0, 64, 2):
        two = jnp.concatenate(
            [pltpu.roll(slab, 8 * a, 1), pltpu.roll(slab, 8 * a + 8, 1)], axis=0
        )
        out[0, 8 * a : 8 * a + 16, :] = two.astype(BF)


def bias_tables(base):
    return pl.pallas_call(
        bias_kernel,
        grid=(HL,),
        in_specs=[pl.BlockSpec((1, 8, BLK), lambda h: (h, 0, 0))],
        out_specs=pl.BlockSpec((1, BLK, BLK), lambda h: (h, 0, 0)),
        out_shape=jax.ShapeDtypeStruct((HL, BLK, BLK), BF),
        name="bias",
        **params(moved=2 * 2**20),
    )(base)


def lower_mask():
    rows = lax.broadcasted_iota(jnp.int32, (HALF, HALF), 0)
    cols = lax.broadcasted_iota(jnp.int32, (HALF, HALF), 1)
    return rows >= cols


def head_lane(h):
    return lax.broadcasted_iota(jnp.int32, (HALF, DH), 1) == h


def window_scores(t, has_prev, qt, ko, kp, bias, rows, lower):
    near = bias[0, rows, rows].astype(F32)
    near_own = mm_nt(qt, ko[rows, :]) * SCALE
    if has_prev:
        near_prev = mm_nt(qt, kp[rows, :]) * SCALE
        s_near = jnp.where(lower, near_own, near_prev) + near
    else:
        s_near = jnp.where(lower, near_own + near, NEG)
    s_far = None
    if t == 1:
        s_far = mm_nt(qt, ko[0:HALF, :]) * SCALE + bias[0, rows, 0:HALF].astype(F32)
    elif has_prev:
        s_far = mm_nt(qt, kp[HALF:BLK, :]) * SCALE + bias[0, rows, HALF:BLK].astype(F32)
    s_edge = None
    if has_prev:
        pair = qt.astype(F32) * kp[rows, :].astype(F32)
        s_edge = jnp.sum(pair, axis=1, keepdims=True) * SCALE + bias[0, 0:1, 1:2].astype(F32)
    return s_near, s_far, s_edge


def tok_fwd_kernel(has_prev, *refs):
    if has_prev:
        q, km, vm, ko, vo, bias, kp, vp, out, logs = refs
    else:
        q, km, vm, ko, vo, bias, out, logs = refs
        kp = vp = None
    h = pl.program_id(0)
    lower = lower_mask()
    for t in range(2):
        rows = slice(t * HALF, (t + 1) * HALF)
        qt = q[rows, :]
        s_mem = mm_nt(qt, km[...]) * SCALE
        s_near, s_far, s_edge = window_scores(t, has_prev, qt, ko, kp, bias, rows, lower)
        top = jnp.maximum(
            jnp.max(s_mem, axis=1, keepdims=True), jnp.max(s_near, axis=1, keepdims=True)
        )
        if s_far is not None:
            top = jnp.maximum(top, jnp.max(s_far, axis=1, keepdims=True))
        if has_prev:
            top = jnp.maximum(top, s_edge)
        e_mem = jnp.exp(s_mem - top)
        e_near = jnp.exp(s_near - top)
        total = jnp.sum(e_mem, axis=1, keepdims=True) + jnp.sum(e_near, axis=1, keepdims=True)
        acc = mm(e_mem.astype(BF), vm[...])
        if has_prev:
            acc += mm(jnp.where(lower, e_near, 0.0).astype(BF), vo[rows, :])
            acc += mm(jnp.where(lower, 0.0, e_near).astype(BF), vp[rows, :])
            e_edge = jnp.exp(s_edge - top)
            total += e_edge
            acc += e_edge * vp[rows, :].astype(F32)
        else:
            acc += mm(e_near.astype(BF), vo[rows, :])
        if s_far is not None:
            e_far = jnp.exp(s_far - top)
            total += jnp.sum(e_far, axis=1, keepdims=True)
            v_far = vo[0:HALF, :] if t == 1 else vp[HALF:BLK, :]
            acc += mm(e_far.astype(BF), v_far)
        out[rows, :] = (acc / total).astype(BF)
        keep = jnp.where(h == 0, 0.0, logs[rows, :])
        logs[rows, :] = jnp.where(head_lane(h), top + jnp.log(total), keep)


def col(block, at):
    return pl.BlockSpec((BLK, DH), lambda h: (block, at * HL + h))


def tok_forward(block, proj, mem_proj, bias):
    has_prev = block > 0
    specs = [col(block, 0), col(0, 1), col(0, 2), col(block, 1), col(block, 2)]
    specs += [pl.BlockSpec((1, BLK, BLK), lambda h: (h, 0, 0))]
    ops = [proj, mem_proj, mem_proj, proj, proj, bias]
    if has_prev:
        specs += [col(block - 1, 1), col(block - 1, 2)]
        ops += [proj, proj]
    return pl.pallas_call(
        functools.partial(tok_fwd_kernel, has_prev),
        grid=(HL,),
        in_specs=specs,
        out_specs=[col(0, 0), full((BLK, DH))],
        out_shape=[
            jax.ShapeDtypeStruct((BLK, KEEP), BF),
            jax.ShapeDtypeStruct((BLK, DH), F32),
        ],
        name="tok_fwd",
        **params(flops=4 * BLK * 1280 * KEEP, moved=8 * 2**20, trans=HL * BLK * 1024),
    )(*ops)


def mem_fwd_kernel(q, ks, vs, ko, vo, out, logs):
    h = pl.program_id(0)
    for t in range(2):
        rows = slice(t * HALF, (t + 1) * HALF)
        qt = q[rows, :]
        s1 = mm_nt(qt, ks[...]) * SCALE
        s2 = mm_nt(qt, ko[...]) * SCALE
        top = jnp.maximum(jnp.max(s1, axis=1, keepdims=True), jnp.max(s2, axis=1, keepdims=True))
        e1 = jnp.exp(s1 - top)
        e2 = jnp.exp(s2 - top)
        total = jnp.sum(e1, axis=1, keepdims=True) + jnp.sum(e2, axis=1, keepdims=True)
        acc = mm(e1.astype(BF), vs[...]) + mm(e2.astype(BF), vo[...])
        out[rows, :] = (acc / total).astype(BF)
        keep = jnp.where(h == 0, 0.0, logs[rows, :])
        logs[rows, :] = jnp.where(head_lane(h), top + jnp.log(total), keep)


def mem_forward(block, proj, mem_proj):
    return pl.pallas_call(
        mem_fwd_kernel,
        grid=(HL,),
        in_specs=[col(0, 0), col(0, 1), col(0, 2), col(block, 1), col(block, 2)],
        out_specs=[col(0, 0), full((BLK, DH))],
        out_shape=[
            jax.ShapeDtypeStruct((BLK, KEEP), BF),
            jax.ShapeDtypeStruct((BLK, DH), F32),
        ],
        name="mem_fwd",
        **params(flops=4 * BLK * 1024 * KEEP, moved=4 * 2**20, trans=HL * BLK * 1024),
    )(mem_proj, mem_proj, mem_proj, proj, proj)


def head_cols(at, h):
    return pl.ds(pl.multiple_of((at * HL + h) * DH, DH), DH)


def mem_bwd_kernel(final, *refs):
    if final:
        q, ks, vs, ko, vo, do, logs, aks, avs, aq, ak, av, d_mem, d_tok, dks, dvs, dko, dvo = refs
    else:
        q, ks, vs, ko, vo, do, logs, d_mem, d_tok, dks, dvs, dko, dvo = refs
    h = pl.program_id(0)
    kind = BF if final else F32
    for t in range(2):
        rows = slice(t * HALF, (t + 1) * HALF)
        qt = q[rows, :]
        dt = do[rows, :]
        log_t = jnp.sum(jnp.where(head_lane(h), logs[rows, :], 0.0), axis=1, keepdims=True)
        p1 = jnp.exp(mm_nt(qt, ks[...]) * SCALE - log_t)
        p2 = jnp.exp(mm_nt(qt, ko[...]) * SCALE - log_t)
        w1 = mm_nt(dt, vs[...])
        w2 = mm_nt(dt, vo[...])
        inner = jnp.sum(p1 * w1, axis=1, keepdims=True) + jnp.sum(p2 * w2, axis=1, keepdims=True)
        g1 = (p1 * (w1 - inner)).astype(BF)
        g2 = (p2 * (w2 - inner)).astype(BF)
        dq = (mm(g1, ks[...]) + mm(g2, ko[...])) * SCALE
        d_mem[rows, head_cols(0, h)] = dq.astype(kind)
        terms = (
            (dks, mm_tn(g1, qt) * SCALE),
            (dko, mm_tn(g2, qt) * SCALE),
            (dvs, mm_tn(p1.astype(BF), dt)),
            (dvo, mm_tn(p2.astype(BF), dt)),
        )
        for ref, term in terms:
            if t == 0:
                ref[...] = term
            else:
                ref[...] += term
    if final:
        d_mem[:, head_cols(1, h)] = (dks[...] + aks[...]).astype(BF)
        d_mem[:, head_cols(2, h)] = (dvs[...] + avs[...]).astype(BF)
        d_tok[:, head_cols(0, h)] = aq[...].astype(BF)
        d_tok[:, head_cols(1, h)] = (dko[...] + ak[...]).astype(BF)
        d_tok[:, head_cols(2, h)] = (dvo[...] + av[...]).astype(BF)
    else:
        d_mem[:, head_cols(1, h)] = dks[...]
        d_mem[:, head_cols(2, h)] = dvs[...]
        d_tok[:, head_cols(0, h)] = dko[...]
        d_tok[:, head_cols(1, h)] = dvo[...]


def mem_backward(block, proj, mem_proj, grad_mix, logs, add_mem=None, add_tok=None):
    final = add_mem is not None
    specs = [col(0, 0), col(0, 1), col(0, 2), col(block, 1), col(block, 2), col(0, 0)]
    specs += [full((BLK, DH))]
    ops = [mem_proj, mem_proj, mem_proj, proj, proj, grad_mix, logs]
    if final:
        specs += [col(0, 0), col(0, 1), col(0, 0), col(0, 1), col(0, 2)]
        ops += [add_mem, add_mem, add_tok, add_tok, add_tok]
    kind = BF if final else F32
    wide = 3 * KEEP if final else 2 * KEEP
    return pl.pallas_call(
        functools.partial(mem_bwd_kernel, final),
        grid=(HL,),
        in_specs=specs,
        out_specs=[full((BLK, 3 * KEEP)), full((BLK, wide))],
        out_shape=[
            jax.ShapeDtypeStruct((BLK, 3 * KEEP), kind),
            jax.ShapeDtypeStruct((BLK, wide), kind),
        ],
        scratch_shapes=[pltpu.VMEM((BLK, DH), F32)] * 4,
        name="mem_bwd",
        **params(flops=10 * BLK * 1024 * KEEP, moved=9 * 2**20, trans=HL * BLK * 1024),
    )(*ops)


def tok_bwd_kernel(has_prev, *refs):
    if has_prev:
        q, km, vm, ko, vo, bias, do, logs, kp, vp, sq, sk, sv, ak, av = refs[:15]
        d_mem, d_tok, d_prev, rel, dkm, dvm, dko, dvo, dkp, dvp = refs[15:]
    else:
        q, km, vm, ko, vo, bias, do, logs, ak, av = refs[:10]
        d_mem, d_tok, rel, dkm, dvm, dko, dvo = refs[10:]
        kp = vp = None
    h = pl.program_id(0)
    lower = lower_mask()
    slab = jnp.zeros((8, BLK), F32)
    dko[...] = jnp.zeros_like(dko)
    dvo[...] = jnp.zeros_like(dvo)
    if has_prev:
        dkp[...] = jnp.zeros_like(dkp)
        dvp[...] = jnp.zeros_like(dvp)
    for t in range(2):
        rows = slice(t * HALF, (t + 1) * HALF)
        qt = q[rows, :]
        dt = do[rows, :]
        log_t = jnp.sum(jnp.where(head_lane(h), logs[rows, :], 0.0), axis=1, keepdims=True)
        p_mem = jnp.exp(mm_nt(qt, km[...]) * SCALE - log_t)
        s_near, s_far, s_edge = window_scores(t, has_prev, qt, ko, kp, bias, rows, lower)
        p_near = jnp.exp(s_near - log_t)
        w_mem = mm_nt(dt, vm[...])
        w_near = mm_nt(dt, vo[rows, :])
        inner = jnp.sum(p_mem * w_mem, axis=1, keepdims=True)
        if has_prev:
            w_near = jnp.where(lower, w_near, mm_nt(dt, vp[rows, :]))
            p_edge = jnp.exp(s_edge - log_t)
            v_edge = vp[rows, :].astype(F32)
            k_edge = kp[rows, :].astype(F32)
            w_edge = jnp.sum(dt.astype(F32) * v_edge, axis=1, keepdims=True)
            inner += p_edge * w_edge
        inner += jnp.sum(p_near * w_near, axis=1, keepdims=True)
        if s_far is not None:
            far = slice(0, HALF) if t == 1 else slice(HALF, BLK)
            k_far, v_far = (ko, vo) if t == 1 else (kp, vp)
            p_far = jnp.exp(s_far - log_t)
            w_far = mm_nt(dt, v_far[far, :])
            inner += jnp.sum(p_far * w_far, axis=1, keepdims=True)
        g_mem = (p_mem * (w_mem - inner)).astype(BF)
        g_near32 = p_near * (w_near - inner)
        g_near = g_near32.astype(BF)
        dq = mm(g_mem, km[...])
        zero = jnp.zeros((), BF)
        if has_prev:
            g_own = jnp.where(lower, g_near32, 0.0).astype(BF)
            g_prev = jnp.where(lower, 0.0, g_near32).astype(BF)
            p_own = jnp.where(lower, p_near, 0.0).astype(BF)
            p_prev = jnp.where(lower, 0.0, p_near).astype(BF)
            g_edge = (p_edge * (w_edge - inner)).astype(BF).astype(F32)
            p_edge16 = p_edge.astype(BF).astype(F32)
            dq += mm(g_prev, kp[rows, :]) + g_edge * k_edge
            dkp[rows, :] += mm_tn(g_prev, qt) + g_edge * qt.astype(F32)
            dvp[rows, :] += mm_tn(p_prev, dt) + p_edge16 * dt.astype(F32)
        else:
            g_own = g_near
            p_own = p_near.astype(BF)
        dq += mm(g_own, ko[rows, :])
        dko[rows, :] += mm_tn(g_own, qt)
        dvo[rows, :] += mm_tn(p_own, dt)
        g_far32 = jnp.zeros((HALF, HALF), F32)
        if s_far is not None:
            g_far = (p_far * (w_far - inner)).astype(BF)
            g_far32 = g_far.astype(F32)
            dq += mm(g_far, k_far[far, :])
            dk_far, dv_far = (dko, dvo) if t == 1 else (dkp, dvp)
            dk_far[far, :] += mm_tn(g_far, qt)
            dv_far[far, :] += mm_tn(p_far.astype(BF), dt)
        d_tok[rows, head_cols(0, h)] = (dq * SCALE).astype(d_tok.dtype)
        g_round = g_near.astype(F32)
        wide = [g_round, g_far32] if t == 0 else [g_far32, g_round]
        wide = jnp.concatenate(wide, axis=1)
        for a in range(HALF // 8):
            shift = (BLK - 8 * a - t * HALF) % BLK
            part = wide[8 * a : 8 * a + 8, :]
            slab = slab + (pltpu.roll(part, shift, 1) if shift else part)
        if has_prev:
            at = lax.broadcasted_iota(jnp.int32, (8, BLK), 0) * BLK
            at = at + lax.broadcasted_iota(jnp.int32, (8, BLK), 1)
            edge_sum = jnp.sum(g_edge, axis=0, keepdims=True)
            slab = slab + jnp.where(at == 1, edge_sum, 0.0)
        add_k = mm_tn(g_mem, qt)
        add_v = mm_tn(p_mem.astype(BF), dt)
        if t == 0:
            dkm[...] = add_k
            dvm[...] = add_v
        else:
            dkm[...] += add_k
            dvm[...] += add_v
    rel[0] = slab
    k_tok = dko[...] * SCALE + ak[...]
    v_tok = dvo[...] + av[...]
    d_tok[:, head_cols(1, h)] = k_tok.astype(d_tok.dtype)
    d_tok[:, head_cols(2, h)] = v_tok.astype(d_tok.dtype)
    if has_prev:
        d_mem[:, head_cols(0, h)] = sq[...].astype(BF)
        d_mem[:, head_cols(1, h)] = (dkm[...] * SCALE + sk[...]).astype(BF)
        d_mem[:, head_cols(2, h)] = (dvm[...] + sv[...]).astype(BF)
        d_prev[:, head_cols(0, h)] = dkp[...] * SCALE
        d_prev[:, head_cols(1, h)] = dvp[...]
    else:
        d_mem[:, head_cols(0, h)] = dkm[...] * SCALE
        d_mem[:, head_cols(1, h)] = dvm[...]


def tok_backward(block, proj, mem_proj, bias, grad_mix, logs, add_tok, add_mem=None):
    has_prev = block > 0
    specs = [col(block, 0), col(0, 1), col(0, 2), col(block, 1), col(block, 2)]
    specs += [pl.BlockSpec((1, BLK, BLK), lambda h: (h, 0, 0)), col(block, 0), full((BLK, DH))]
    ops = [proj, mem_proj, mem_proj, proj, proj, bias, grad_mix, logs]
    scratch = 4
    if has_prev:
        specs += [col(block - 1, 1), col(block - 1, 2), col(0, 0), col(0, 1), col(0, 2)]
        ops += [proj, proj, add_mem, add_mem, add_mem]
        scratch = 6
    specs += [col(0, 0), col(0, 1)]
    ops += [add_tok, add_tok]
    kind = BF if has_prev else F32
    rel_spec = pl.BlockSpec((1, 8, BLK), lambda h: (h, 0, 0))
    rel_shape = jax.ShapeDtypeStruct((HL, 8, BLK), F32)
    wide = 3 * KEEP if has_prev else 2 * KEEP
    out_specs = [full((BLK, wide)), full((BLK, 3 * KEEP))]
    out_shape = [
        jax.ShapeDtypeStruct((BLK, wide), kind),
        jax.ShapeDtypeStruct((BLK, 3 * KEEP), kind),
    ]
    if has_prev:
        out_specs.append(full((BLK, 2 * KEEP)))
        out_shape.append(jax.ShapeDtypeStruct((BLK, 2 * KEEP), F32))
    return pl.pallas_call(
        functools.partial(tok_bwd_kernel, has_prev),
        grid=(HL,),
        in_specs=specs,
        out_specs=out_specs + [rel_spec],
        out_shape=out_shape + [rel_shape],
        scratch_shapes=[pltpu.VMEM((BLK, DH), F32)] * scratch,
        name="tok_bwd",
        **params(flops=10 * BLK * 1280 * KEEP, moved=12 * 2**20, trans=HL * BLK * 1024),
    )(*ops)


def normal_parts(u):
    bell = jnp.exp(-0.5 * (u * u))
    t = 1.0 / (1.0 + (0.3275911 * math.sqrt(0.5)) * jnp.abs(u))
    poly = 1.061405429 * t - 1.453152027
    poly = poly * t + 1.421413741
    poly = poly * t - 0.284496736
    poly = poly * t + 0.254829592
    tail = (0.5 * poly) * (t * bell)
    return jnp.where(u >= 0, 1.0 - tail, tail), bell * (1.0 / math.sqrt(2.0 * math.pi))


def mlp_kernel(
    h0, h1, d0, d1, ua, ub, da, db, gu, gd, o0, o1, e0, e1, acc_o0, acc_o1, acc_e0, acc_e1
):
    t = pl.program_id(0)
    wu = jnp.where(t < 4, ua[...], ub[...])
    wd = jnp.where(lax.rem(t, 2) == 0, da[...], db[...])
    for r in range(2):
        h = (h0, h1)[r]
        d = (d0, d1)[r]
        acc_o = (acc_o0, acc_o1)[r]
        acc_e = (acc_e0, acc_e1)[r]
        u = mm_nt(h[...], wu)
        dg = mm_nt(d[...], wd)
        phi, pdf = normal_parts(u)
        g = (u * phi).astype(BF)
        du = (dg * (phi + u * pdf)).astype(BF)
        if r == 0:
            g_first, du_first = g, du
        o_term = mm(g, wd)
        e_term = mm(du, wu)

        @pl.when(t == 0)
        def _():
            acc_o[...] = o_term
            acc_e[...] = e_term

        @pl.when(t > 0)
        def _():
            acc_o[...] += o_term
            acc_e[...] += e_term

    gd[...] = (mm_tn(g_first, d0[...]) + mm_tn(g, d1[...])).astype(BF)
    gu[...] = (mm_tn(du_first, h0[...]) + mm_tn(du, h1[...])).astype(BF)

    @pl.when(t == 7)
    def _():
        o0[...] = acc_o0[...]
        o1[...] = acc_o1[...].astype(BF)
        e0[...] = acc_e0[...]
        e1[...] = acc_e1[...].astype(BF)


def mlp(h0, h1, d0, d1, ua, ub, da, db):
    act = full((BLK, D))
    tile = functools.partial(pl.BlockSpec, (HALF, D))
    return pl.pallas_call(
        mlp_kernel,
        grid=(8,),
        in_specs=[act] * 4
        + [
            tile(lambda t: (jnp.minimum(t, 3), 0)),
            tile(lambda t: (jnp.maximum(t - 4, 0), 0)),
            tile(lambda t: (t // 2, 0)),
            tile(lambda t: (t // 2, 0)),
        ],
        out_specs=[
            tile(lambda t: (((t // 2) % 2) * 4 + (t // 4) * 2 + t % 2, 0)),
            tile(lambda t: ((t // 4) * 4 + (t % 2) * 2 + (t // 2) % 2, 0)),
            act,
            act,
            act,
            act,
        ],
        out_shape=[
            jax.ShapeDtypeStruct((8 * HALF, D), BF),
            jax.ShapeDtypeStruct((8 * HALF, D), BF),
            jax.ShapeDtypeStruct((BLK, D), F32),
            jax.ShapeDtypeStruct((BLK, D), BF),
            jax.ShapeDtypeStruct((BLK, D), F32),
            jax.ShapeDtypeStruct((BLK, D), BF),
        ],
        scratch_shapes=[pltpu.VMEM((BLK, D), F32)] * 4,
        name="mlp",
        **params(flops=12 * D * D * 2 * D, moved=26 * 2**20, trans=4 * 2**20),
    )(h0, h1, d0, d1, ua, ub, da, db)


def proj_grad_kernel(me, xa, xb, sa, sb, pa, pb, ra, rb, out_a, out_b, out_c, tok, st):
    x0, y0 = me[1], me[3]
    tok[...] = mm_tn(xa[...], pa[...]) + mm_tn(xb[...], pb[...])
    st[...] = mm_tn(sa[...], ra[...]) + mm_tn(sb[...], rb[...])
    for xr in range(2):
        rows = pl.ds(pl.multiple_of((x0 ^ xr) * DH, DH), DH)
        for yr in range(2):
            dests = (out_a.at[xr, yr, 0, 0], out_b.at[yr, 0, xr, 0], out_c.at[0, xr, yr, 0])
            for sub, ref in enumerate(dests):
                cols = pl.ds(pl.multiple_of((y0 ^ yr) * 768 + sub * 256, 256), 256)
                ref[0:DH, :] = tok[rows, cols].astype(BF)
                ref[DH : 2 * DH, :] = st[rows, cols].astype(BF)


def proj_grads(me, xn, sn0, sn1, dp0, dp1, dr0, dr1):
    lhs = pl.BlockSpec((BLK, 2 * DH), lambda q, me: (0, q ^ me[2]))
    lhs1 = pl.BlockSpec((BLK, 2 * DH), lambda q, me: (1, q ^ me[2]))
    rhs = full((BLK, 3 * KEEP))
    shape = jax.ShapeDtypeStruct((2, 2, 2, 2, 2 * DH, 2 * DH), BF)
    tail = (2 * DH, 2 * DH)
    return pl.pallas_call(
        proj_grad_kernel,
        grid_spec=pltpu.PrefetchScalarGridSpec(
            num_scalar_prefetch=1,
            grid=(4,),
            in_specs=[lhs, lhs1, lhs, lhs, rhs, rhs, rhs, rhs],
            out_specs=[
                pl.BlockSpec((2, 2, 1, 1) + tail, lambda q, me: (0, 0, q % 2, q // 2, 0, 0)),
                pl.BlockSpec((2, 1, 2, 1) + tail, lambda q, me: (0, q % 2, 0, q // 2, 0, 0)),
                pl.BlockSpec((1, 2, 2, 1) + tail, lambda q, me: (q % 2, 0, 0, q // 2, 0, 0)),
            ],
            scratch_shapes=[pltpu.VMEM((2 * DH, 3 * KEEP), F32)] * 2,
        ),
        out_shape=[shape] * 3,
        name="proj_grad",
        **params(flops=4 * D * D * 3 * KEEP, moved=16 * 2**20),
    )(me, xn, xn, sn0, sn1, dp0, dp1, dr0, dr1)


def place_proj_kernel(me, p00, p01, p10, p11, tok, st):
    c0, y0 = me[0], me[3]
    for cr in range(2):
        for yr in range(2):
            src = ((p00, p01), (p10, p11))[cr][yr]
            for sub in range(3):
                for i in range(2):
                    j = 6 * (y0 ^ yr) + 2 * sub + i
                    at = (j // HL) * D + (2 * (j % HL) + (c0 ^ cr)) * DH
                    dst = pl.ds(pl.multiple_of(at, DH), DH)
                    cols = slice(i * DH, (i + 1) * DH)
                    tok[:, dst] = src[sub, 0:DH, cols].astype(F32)
                    st[:, dst] = src[sub, DH : 2 * DH, cols].astype(F32)


def place_proj(me, p00, p01, p10, p11):
    one = jax.ShapeDtypeStruct((DH, 3 * D), F32)
    return pl.pallas_call(
        place_proj_kernel,
        grid_spec=pltpu.PrefetchScalarGridSpec(
            num_scalar_prefetch=1,
            grid=(1,),
            in_specs=[full(p00.shape)] * 4,
            out_specs=[full((DH, 3 * D))] * 2,
        ),
        out_shape=[one, one],
        name="place_proj",
        **params(moved=5 * 2**20),
    )(me, p00, p01, p10, p11)


def place_mlp_kernel(me, p00, p01, p10, p11, up, down):
    c0, y0 = me[0], me[3]
    n = p00.shape[1]
    for cr in range(2):
        for yr in range(2):
            src = ((p00, p01), (p10, p11))[cr][yr]
            rows = pl.ds(pl.multiple_of(((c0 ^ cr) * 2 + (y0 ^ yr)) * n, n), n)
            up[rows, :] = src[0].astype(F32)
            down[rows, :] = src[1].astype(F32)


def place_mlp(me, p00, p01, p10, p11):
    one = jax.ShapeDtypeStruct((4 * p00.shape[1], D), F32)
    return pl.pallas_call(
        place_mlp_kernel,
        grid_spec=pltpu.PrefetchScalarGridSpec(
            num_scalar_prefetch=1,
            grid=(1,),
            in_specs=[full(p00.shape)] * 4,
            out_specs=[full(one.shape)] * 2,
        ),
        out_shape=[one, one],
        name="place_mlp",
        **params(moved=6 * 2**20),
    )(me, p00, p01, p10, p11)


def body(
    tokens,
    state_in,
    gain_tok,
    gain_state,
    gain_mlp,
    w_tok,
    w_state,
    w_out,
    w_update,
    gate_bias,
    rel_bias,
    w_up,
    w_down,
    d_out,
    d_state_next,
):
    c = lax.axis_index("c")
    x = lax.axis_index("x")
    z = lax.axis_index("s")
    y = lax.axis_index("g") % 2
    z1, z2 = z % 2, z // 2
    me = jnp.stack([c, x, z, y]).astype(jnp.int32)
    on_diag = c == x
    slots = state_in.shape[0]
    srows = state_in.shape[1]

    def cross(value):
        return jnp.where(on_diag, value, diag_send(value))

    def by_block(own, other):
        return jnp.where(c == 0, jnp.concatenate([own, other]), jnp.concatenate([other, own]))

    def my_half(rows):
        return lax.dynamic_slice_in_dim(rows, c * HALF, HALF, 0)

    def other_half(rows):
        return lax.dynamic_slice_in_dim(rows, (1 - c) * HALF, HALF, 0)

    def slot_rows(value):
        held = cross(value)
        parts = [lax.dynamic_index_in_dim(held, z, 0, keepdims=False)]
        for k in range(1, slots):
            send = lax.dynamic_index_in_dim(held, z ^ k, 0, keepdims=False)
            parts.append(lax.ppermute(send, "s", [(i, i ^ k) for i in range(slots)]))
        half = jnp.concatenate(parts)
        return by_block(half, xch(half, "c"))

    def owner_rows(half):
        parts = half.reshape(slots, srows, D)
        got = [parts[0]]
        for k in range(1, slots):
            got.append(lax.ppermute(parts[k], "s", [(i, i ^ k) for i in range(slots)]))
        stacked = jnp.stack(got).reshape(2, 2, srows, D)
        stacked = untwist(stacked, (z2, z1)).reshape(slots, srows, D)
        return cross(stacked).astype(F32)

    subs = pick_columns(me, w_tok, w_state)
    small = jnp.stack([gain_tok, gain_state, gain_mlp, gate_bias])
    small = jnp.concatenate([small, jnp.pad(rel_bias, ((0, 0), (0, DH - NB)))])
    small = jnp.pad(small, ((0, 11), (0, DH)))
    x_own = cross(tokens)
    x_oth = xch(x_own, "c")
    tab_a = gather_bits(jnp.concatenate([subs[0], small]), ("z2", "z1", "y", "x"))
    tab_b = gather_bits(subs[1], ("z2", "x", "z1", "y"))
    tab_c = gather_bits(subs[2], ("z2", "y", "x", "z1"))
    state0 = slot_rows(state_in).astype(F32)
    w_tok_l, w_state_l, small_all = lay_tables(me, tab_a, tab_b, tab_c)

    quarter = DH // 4
    at = (c * 2 + y) * quarter
    out_piece = cross(
        jnp.concatenate(
            [
                lax.dynamic_slice_in_dim(w_out, at, quarter, 0),
                lax.dynamic_slice_in_dim(w_update, at, quarter, 0),
            ]
        )
    )
    out_low, out_high = gather_bits(out_piece, ("z2", "z1", "y", "x"))
    wo, wu = lay_out_tables(me, out_low, out_high)
    hid = w_up.shape[0] // 4
    hid_at = (c * 2 + y) * hid
    up_a, up_b = gather_bits(
        lax.dynamic_slice_in_dim(w_up, hid_at, hid, 0), ("z2", "z1", "x", "y")
    )
    down_a, down_b = gather_bits(
        lax.dynamic_slice_in_dim(w_down, hid_at, hid, 0), ("z2", "x", "y", "z1")
    )
    d_own = cross(d_out)
    d_oth = xch(d_own, "c")
    ds2 = slot_rows(d_state_next).astype(F32)

    vectors = small_all[:, :4, :DH].transpose(1, 0, 2).reshape(4, D).astype(F32)
    g_tok, g_state, g_mlp = vectors[0], vectors[1], vectors[2]
    gate = jax.nn.sigmoid(vectors[3])
    rel_rows = small_all[:, 4, :NB].reshape(HL, 2, NB)
    rel_mine = lax.dynamic_index_in_dim(rel_rows, c, 1, keepdims=False)
    hot = jnp.asarray(slab_buckets())[None, :] == jnp.arange(NB, dtype=jnp.int32)[:, None]
    base = mm(rel_mine, hot.astype(BF)).reshape(HL, 8, BLK)
    bias = bias_tables(base)

    rows = by_block(x_own, x_oth).astype(F32)
    xn = (norm_parts(rows)[0] * g_tok).astype(BF)
    proj = mm(xn, w_tok_l).astype(BF)

    sn0 = (norm_parts(state0)[0] * g_state).astype(BF)
    r0 = mm(sn0, w_state_l).astype(BF)
    os0, log_s0 = mem_forward(0, proj, r0)
    zp0 = mm(os0, wu)
    zz0 = zp0 + xch(zp0.astype(BF), "c").astype(F32)
    state1 = gate * state0 + (1.0 - gate) * zz0
    sn1 = (norm_parts(state1)[0] * g_state).astype(BF)
    r1 = mm(sn1, w_state_l).astype(BF)

    ot0, log_t0 = tok_forward(0, proj, r0, bias)
    ot1, log_t1 = tok_forward(1, proj, r1, bias)
    part0, part1 = mm(ot0, wo), mm(ot1, wo)
    part_own = jnp.where(c == 0, part0, part1)
    part_oth = jnp.where(c == 0, part1, part0).astype(BF)
    mid = x_own.astype(F32) + part_own + xch(part_oth, "c").astype(F32)
    h_own = (norm_parts(mid)[0] * g_mlp).astype(BF)
    h_oth = xch(h_own, "c")

    os1, log_s1 = mem_forward(1, proj, r1)
    zp1 = mm(os1, wu)
    zz1 = my_half(zp1) + xch(other_half(zp1).astype(BF), "c").astype(F32)
    state1_half = my_half(state1)
    state2_half = gate * state1_half + (1.0 - gate) * zz1
    state_next = owner_rows(state2_half.astype(BF))

    dz1 = ((1.0 - gate) * ds2).astype(BF)
    dos1 = mm_nt(dz1, wu).astype(BF)
    dm1, dt1 = mem_backward(1, proj, r1, dos1, log_s1)

    gu, gd, o_own, o_oth, e_own, e_oth = mlp(
        h_own,
        h_oth,
        d_own,
        d_oth,
        up_a.reshape(-1, D),
        up_b.reshape(-1, D),
        down_a.reshape(-1, D),
        down_b.reshape(-1, D),
    )
    output = mid + o_own + xch(o_oth, "c").astype(F32)
    output = cross(output.astype(BF))
    gu = gu.reshape(2, 2, 2, 2, hid, D)
    gd = gd.reshape(2, 2, 2, 2, hid, D)
    gu = reduce_bits(gu, ("x", "y", "z1", "z2"))
    gd = reduce_bits(gd, ("y", "z1", "x", "z2"))

    dh = e_own + xch(e_oth, "c").astype(F32)
    back, gain_rows = norm_back(mid, g_mlp, dh)
    grad_g_mlp = jnp.sum(gain_rows, axis=0)
    dmid = d_own.astype(F32) + back
    da_own = dmid.astype(BF)
    da = by_block(da_own, xch(da_own, "c"))
    dot_all = mm_nt(da, wo).astype(BF)
    grad_wo = mm_tn(ot0, da[:BLK]) + mm_tn(ot1, da[BLK:])

    dr1, dp1, dprev, rel1 = tok_backward(1, proj, r1, bias, dot_all, log_t1, dt1, dm1)
    dsn1p = mm_nt(dr1, w_state_l)
    dsn1 = dsn1p + xch(dsn1p.astype(BF), "c").astype(F32)
    back1, gain1 = norm_back(state1, g_state, dsn1)
    ds1 = gate * ds2 + back1
    dz0 = ((1.0 - gate) * ds1).astype(BF)
    dos0 = mm_nt(dz0, wu).astype(BF)
    dm0, dt0, rel0 = tok_backward(0, proj, r0, bias, dot_all, log_t0, dprev)
    dr0, dp0 = mem_backward(0, proj, r0, dos0, log_s0, dm0, dt0)

    subs = proj_grads(me, xn, sn0, sn1, dp0, dp1, dr0, dr1)
    ga = reduce_bits(subs[0], ("x", "y", "z1", "z2"))
    gb = reduce_bits(subs[1], ("y", "z1", "x", "z2"))
    gc = reduce_bits(subs[2], ("z1", "x", "y", "z2"))
    grad_wu = mm_tn(os0, dz0) + mm_tn(os1, dz1)

    dsn0p = mm_nt(dr0, w_state_l)
    dsn0 = my_half(dsn0p) + xch(other_half(dsn0p).astype(BF), "c").astype(F32)
    back0, gain0 = norm_back(my_half(state0), g_state, dsn0)
    grad_state = owner_rows((gate * my_half(ds1) + back0).astype(BF))
    grad_g_state = jnp.sum(my_half(gain1) + gain0, axis=0)
    gate_rows = my_half(ds2) * (state1_half - zz1) + my_half(ds1) * my_half(state0 - zz0)
    grad_gate = jnp.sum(gate_rows, axis=0) * gate * (1.0 - gate)

    dxn0, dxn1 = mm_nt(dp0, w_tok_l), mm_nt(dp1, w_tok_l)
    dxn_own = jnp.where(c == 0, dxn0, dxn1)
    dxn_oth = jnp.where(c == 0, dxn1, dxn0).astype(BF)
    dxn = dxn_own + xch(dxn_oth, "c").astype(F32)
    back_x, gain_x = norm_back(x_own.astype(F32), g_tok, dxn)
    grad_g_tok = jnp.sum(gain_x, axis=0)
    grad_tokens = cross((dmid + back_x).astype(BF)).astype(F32)

    rel_sum = (rel0 + rel1).reshape(HL, 8 * BLK)
    grad_rel = lax.dot_general(
        rel_sum,
        hot.astype(F32),
        (((1,), (1,)), ((), ())),
        precision=lax.Precision.HIGHEST,
        preferred_element_type=F32,
    )
    both = jnp.stack([grad_rel, jnp.zeros_like(grad_rel)], axis=1)
    both = jnp.where(c == 0, both, jnp.flip(both, 1)).reshape(1, H * NB)
    vec = jnp.stack([grad_g_tok, grad_g_state, grad_g_mlp, grad_gate])
    vec = jnp.concatenate([vec, jnp.pad(both, ((0, 3), (0, D - H * NB)))])
    for bit in ("c", "x", "y", "z1", "z2"):
        vec = vec + xch(vec, bit)
    vec = over_groups(vec)
    spot = z * 2 + x
    own = lax.dynamic_slice_in_dim(vec[:4], spot * DH, DH, 1)
    rel_own = lax.dynamic_slice_in_dim(vec[4:5], spot * NB, NB, 1)

    outs = jnp.stack([grad_wo, grad_wu]).astype(BF).reshape(2, 2, 2, 2, 2, quarter, D)
    spots = {"z2": z2, "z1": z1, "x": x, "y": y}
    names = ["z2", "z1", "x", "y"]
    for bit in ("z1", "y", "x", "z2"):
        axis = names.index(bit) + 1
        names.remove(bit)
        keep = lax.dynamic_index_in_dim(outs, spots[bit], axis, keepdims=False)
        send = lax.dynamic_index_in_dim(outs, 1 - spots[bit], axis, keepdims=False)
        outs = (keep.astype(F32) + xch(send, bit).astype(F32)).astype(BF)
    outs = over_groups(outs)
    outs = jnp.stack([outs, xch(outs, "y")])
    outs = jnp.stack([outs, xch(outs, "x")])
    outs = untwist(outs, (x, y)).transpose(2, 0, 1, 3, 4).reshape(2, DH, D)
    outs = jnp.where(on_diag, outs, xch(outs, "c")).astype(F32)

    def spread(part):
        other = xch(part, "y")
        return part, other, xch(part, "c"), xch(other, "c")

    grad_up, grad_down = place_mlp(me, *spread(jnp.stack([gu, gd])))
    grad_tok_w, grad_state_w = place_proj(me, *spread(jnp.stack([ga, gb, gc])))

    return (
        output,
        state_next,
        grad_tokens,
        grad_state,
        own[0],
        own[1],
        own[2],
        grad_tok_w,
        grad_state_w,
        outs[0],
        outs[1],
        own[3],
        rel_own,
        grad_up,
        grad_down,
    )


def solution(mesh):
    reps, shards = mesh.devices.shape
    grid = Mesh(mesh.devices.reshape(reps // 2, 2, shards // 2, 2), ("g", "c", "s", "x"))
    rep, shard = ("g", "c"), ("s", "x")
    every = rep + shard
    by_token = P(every, None)
    by_state = P(rep, shard, None)
    line = P(shard)
    table = P(shard, None)
    params_spec = (line, line, line, table, table, table, table, line, table, table, table)
    return jax.shard_map(
        body,
        mesh=grid,
        in_specs=(by_token, by_state) + params_spec + (by_token, by_state),
        out_specs=(by_token, by_state, by_token, by_state) + params_spec,
        check_vma=False,
    )
```

time: 2390 us -> 769 us (0.32)
  waiting for transfers between devices: 1420 us -> 297 us
  local copies, waits for them, and re-layouts: 275 us -> 35 us
  blocking collectives: 240 us -> 0 us
  matrix products: 249 us -> 54.1 us
  Pallas kernels: 0 us -> 172 us
  starting transfers between devices: 17.9 us -> 122 us
  other arithmetic: 161 us -> 78.9 us
    reduce_scatter x8 -> x0, waiting for transfers between devices: 826 us -> none  [the longest x1 158 us: body(): lax.psum_scatter(regroup(grad_w_state, owners, groups), ('rep', 'shard'),...]
    all_gather x10 -> x0, waiting for transfers between devices: 338 us -> none  [the longest x1 100 us: body(): lax.all_gather(w_state, 'shard', axis=0, tiled=True)]
    dot_general x36 -> x20, matrix products: 249 us -> 54.1 us  [the longest x7 23.9 us: mm_nt(): lax.dot_general(a, b, (((1,), (1,)), ((), ())), preferred_element_type=F32)]
    all_gather x9 -> x0, blocking collectives: 182 us -> none  [the longest x1 46 us: body(): lax.all_gather(gain_mlp, 'shard', axis=0, tiled=True)]
    pallas_call x0 -> x16, Pallas kernels: none -> 172 us  [the longest x1 50.6 us: mlp(): pl.pallas_call(mlp_kernel, grid=(8,), in_specs=[act] * 4 + [tile(lambda t...]
    ppermute x6 -> x97, starting transfers between devices: 16.2 us -> 122 us  [the longest x76 69.9 us: xch(): return lax.ppermute(value, axis, [(i, i ^ mask) for i in range(count)])]
    unnamed x151 -> x194, local copies, waits for them, and re-layouts: 100 us -> 12.4 us
    unnamed x2 -> x0, blocking collectives: 57.8 us -> none
  transfers between devices with their start and end apart: 24 -> 97, of which waited for: 18 -> 45; matrix products, arithmetic and copies ran while one was open for 27% -> 20% of each run, Pallas kernels for 0% -> 23%
where the time goes in v1:
time: 769 us; the launch traced here: 761 us
  waiting for transfers between devices  297 us (39%)
  Pallas kernels  172 us (22%)
  starting transfers between devices  122 us (16%)
  other arithmetic  78.9 us (10%)
  matrix products  54.1 us (7%)
  local copies, waits for them, and re-layouts  35 us (5%)
    ppermute x76, waiting for transfers between devices, xch(): return lax.ppermute(value, axis, [(i, i ^ mask) for i in range(count)])  243 us
    ppermute x76, starting transfers between devices, xch(): return lax.ppermute(value, axis, [(i, i ^ mask) for i in range(count)])  69.9 us
    pallas_call x1, Pallas kernels, mlp(): pl.pallas_call(mlp_kernel, grid=(8,), in_specs=[act] * 4 + [tile(lambda t...  50.6 us
    ppermute x9, starting transfers between devices, diag_send(): return lax.ppermute(value, ('c', 'x'), [(1, 2), (2, 1)])  32.6 us
    pallas_call x2, Pallas kernels, tok_backward(): pl.pallas_call(functools.partial(tok_bwd_kernel, has_prev), grid=(HL,), i...  28.8 us
    pallas_call x2, Pallas kernels, mem_backward(): pl.pallas_call(functools.partial(mem_bwd_kernel, final), grid=(HL,), in_s...  24.3 us
    dot_general x7, matrix products, mm_nt(): lax.dot_general(a, b, (((1,), (1,)), ((), ())), preferred_element_type=F32)  23.9 us
    ppermute x6, waiting for transfers between devices, slot_rows(): parts.append(lax.ppermute(send, 's', [(i, i ^ k) for i in range(slots)]))  22.4 us
  transfers between devices with their start and end apart: 97, of which 45 were waited for; matrix products, arithmetic and copies ran while one was open for 20% of the time, Pallas kernels for 23%

profile of v1, /device:TPU:1, one launch (start us, length us, event | category | flops | bytes accessed | tf_op | source)
XLA Modules:
  0.0 761.4 jit_solution(7594941154170889979)
XLA Ops:
  0.7 4.6 collective-permute-start.14
  5.9 2.9 pick.1
  21.0 3.8 collective-permute-done.19
  34.2 12.8 %collective-permute-done.29 = bf16[128,1024]{1,0:T(8,128)(2,1)S(1)} collective-permute-done((bf16[128,1024]{1,0:T(8,128)(2,1)S(1)}, bf16[128,1024]{1,0:T(8,128)(2,1)S(1)}, u32[]{:S(2)}, u32[]{:S(2)}) %collective-permute-start.29) | collective-permute-done | bytes 262176 | tf_op jit(solution)/shard_map/ppermute | solution.py:37
  47.1 6.9 collective-permute-done.33
  59.2 3.2 collective-permute-done.7
  72.3 3.6 collective-permute-done.15
  80.9 14.0 %collective-permute-done.46 = bf16[64,1024]{1,0:T(8,128)(2,1)S(1)} collective-permute-done((bf16[64,1024]{1,0:T(8,128)(2,1)S(1)}, bf16[64,1024]{1,0:T(8,128)(2,1)S(1)}, u32[]{:S(2)}, u32[]{:S(2)}) %collective-permute-start.46) | collective-permute-done | bytes 131104 | tf_op jit(solution)/shard_map/ppermute | solution.py:831
  96.3 3.3 collective-permute-done.48
  102.5 4.3 collective-permute-done.34
  110.6 7.4 collective-permute-done.12
  118.0 4.2 collective-permute-start.27
  127.0 15.9 %collective-permute-done.27 = bf16[512,1024]{1,0:T(8,128)(2,1)S(1)} collective-permute-done((bf16[512,1024]{1,0:T(8,128)(2,1)S(1)}, bf16[512,1024]{1,0:T(8,128)(2,1)S(1)}, u32[]{:S(2)}, u32[]{:S(2)}) %collective-permute-start.27) | collective-permute-done | bytes 1048608 | tf_op jit(solution)/shard_map/ppermute | solution.py:41
  148.5 8.4 %collective-permute-done.13.c1 = bf16[2,2,2,256,256]{4,3,2,1,0:T(8,128)(2,1)S(1)} collective-permute-done((bf16[2,2,2,256,256]{4,3,2,1,0:T(8,128)(2,1)S(1)}, bf16[2,2,2,256,256]{4,3,2,1,0:T(8,128)(2,1)S(1)}, u32[]{:S(2)}, u32[]{:S(2)}) %collective-permute-start.13) | collective-permute-done | bytes 1048608 | tf_op jit(solution)/shard_map/ppermute | solution.py:37
  156.9 13.9 %collective-permute-done.9.b1 = bf16[2,2,2,256,256]{4,3,2,1,0:T(8,128)(2,1)S(1)} collective-permute-done((bf16[2,2,2,256,256]{4,3,2,1,0:T(8,128)(2,1)S(1)}, bf16[2,2,2,256,256]{4,3,2,1,0:T(8,128)(2,1)S(1)}, u32[]{:S(2)}, u32[]{:S(2)}) %collective-permute-start.9) | collective-permute-done | bytes 1048608 | tf_op jit(solution)/shard_map/ppermute | solution.py:37
  172.0 12.3 %collective-permute-done.5.a1 = bf16[2,2,2,272,256]{4,3,2,1,0:T(8,128)(2,1)S(1)} collective-permute-done((bf16[2,2,2,272,256]{4,3,2,1,0:T(8,128)(2,1)S(1)}, bf16[2,2,2,272,256]{4,3,2,1,0:T(8,128)(2,1)S(1)}, u32[]{:S(2)}, u32[]{:S(2)}) %collective-permute-start.5) | collective-permute-done | bytes 1114144 | tf_op jit(solution)/shard_map/ppermute | solution.py:37
  185.3 4.9 collective-permute-start.28
  190.3 7.1 lay.1
  198.5 5.2 convolution_convert_fusion.2.refs_1_.refs_2_.q.ks.vs.refs_0_
  209.3 4.9 convolution_convert_fusion.refs_0_.refs_3_.refs_4_.ko.vo.refs_6_.refs_7_.refs_8_.refs_9_
  214.2 6.8 mem_fwd.2
  222.0 3.7 lay_out.1
  230.0 3.2 bias.1.refs_5_
  233.3 7.4 tok_fwd.2
  240.7 3.1 fusion.100
  248.6 2.9 convolution_convert_fusion.1.refs_1_.refs_2_.q.ks.vs.refs_0_
  251.5 8.3 %tok_fwd.3 = (bf16[512,512]{1,0:T(8,128)(2,1)}, f32[512,128]{1,0:T(8,128)}) custom-call(bf16[1024,1536]{1,0:T(8,128)(2,1)} %convolution_convert_fusion.refs_0_.refs_3_.refs_4_.ko.vo.refs_6_.refs_7_.refs_8_.refs_9_, bf16[512,1536]{1,0:T(8,128)(2,1)} %convolution_convert_fusion.1.refs_1_.refs_2_.q.ks.vs.refs_0_, ...), custom_call_target="tpu_custom_call" | custom-call | flops 1342177280 | bytes 8388608 | tf_op jit(solution)/shard_map/tok_fwd/pallas_call | solution.py:339
  264.2 3.1 pad_maximum_fusion
  276.9 6.7 mem_fwd.3
  290.1 25.9 %collective-permute-done.32 = bf16[2,2,2,128,1024]{4,3,2,1,0:T(8,128)(2,1)} collective-permute-done((bf16[2,2,2,128,1024]{4,3,2,1,0:T(8,128)(2,1)}, bf16[2,2,2,128,1024]{4,3,2,1,0:T(8,128)(2,1)}, u32[]{:S(2)}, u32[]{:S(2)}) %collective-permute-start.32) | collective-permute-done | bytes 2097184 | tf_op jit(solution)/shard_map/ppermute | solution.py:37
  316.0 3.7 collective-permute-done.36
  319.7 50.6 %mlp.1 = (bf16[2048,1024]{1,0:T(8,128)(2,1)}, bf16[2048,1024]{1,0:T(8,128)(2,1)}, f32[512,1024]{1,0:T(8,128)}, bf16[512,1024]{1,0:T(8,128)(2,1)}, f32[512,1024]{1,0:T(8,128)}, /*index=5*/bf16[512,1024]{1,0:T(8,128)(2,1)}) custom-call(bf16[512,1024]{1,0:T(8,128)(2,1)} %multiply_convert_fusion.2.h0, bf16[512,1024]{1,0:T(8,128)(2,1)} %collective-permute-done.26.h1, ...), custom_call_target="tpu_custom_call" | custom-call | flops 25769803776 | bytes 27262976 | tf_op jit(solution)/shard_map/mlp/pallas_call | solution.py:658
  371.6 4.0 fusion.95
  375.5 12.0 %mem_bwd.2 = (f32[512,1536]{1,0:T(8,128)}, f32[512,1024]{1,0:T(8,128)}) custom-call(bf16[512,1536]{1,0:T(8,128)(2,1)} %convolution_convert_fusion.1.refs_1_.refs_2_.q.ks.vs.refs_0_, bf16[512,1536]{1,0:T(8,128)(2,1)} %convolution_convert_fusion.1.refs_1_.refs_2_.q.ks.vs.refs_0_, bf16[512,1536]{1,0:T(8,128)(2,1)} %convolution_convert_fusion.1.refs_1_.refs_2_.q.ks.vs.refs_0_, ...), custom_call_target="tpu_custom_call" | custom-call | flops 2684354560 | bytes 9437184 | tf_op jit(solution)/shard_map/mem_bwd/pallas_call | solution.py:444
  392.8 3.7 fusion.90
  397.3 3.3 collective-permute-start.38
  400.6 22.5 %collective-permute-done.86 = bf16[2,2,2,128,1024]{4,3,2,1,0:T(8,128)(2,1)} collective-permute-done((bf16[2,2,2,128,1024]{4,3,2,1,0:T(8,128)(2,1)}, bf16[2,2,2,128,1024]{4,3,2,1,0:T(8,128)(2,1)}, u32[]{:S(2)}, u32[]{:S(2)}) %collective-permute-start.86) | collective-permute-done | bytes 2097184 | tf_op jit(solution)/shard_map/ppermute | solution.py:37
  426.8 10.3 %collective-permute-done.90 = bf16[2,2,2,128,1024]{4,3,2,1,0:T(8,128)(2,1)S(1)} collective-permute-done((bf16[2,2,2,128,1024]{4,3,2,1,0:T(8,128)(2,1)S(1)}, bf16[2,2,2,128,1024]{4,3,2,1,0:T(8,128)(2,1)S(1)}, u32[]{:S(2)}, u32[]{:S(2)}) %collective-permute-start.90) | collective-permute-done | bytes 2097184 | tf_op jit(solution)/shard_map/ppermute | solution.py:37
  443.3 16.4 %tok_bwd.2 = (bf16[512,1536]{1,0:T(8,128)(2,1)}, bf16[512,1536]{1,0:T(8,128)(2,1)}, f32[512,1024]{1,0:T(8,128)}, f32[4,8,512]{2,1,0:T(8,128)}) custom-call(bf16[1024,1536]{1,0:T(8,128)(2,1)} %convolution_convert_fusion.refs_0_.refs_3_.refs_4_.ko.vo.refs_6_.refs_7_.refs_8_.refs_9_, ...), custom_call_target="tpu_custom_call" | custom-call | flops 3355443200 | bytes 12582912 | tf_op jit(solution)/shard_map/tok_bwd/pallas_call | solution.py:590
  459.7 5.8 fusion.99
  467.9 12.4 %tok_bwd.3 = (f32[512,1024]{1,0:T(8,128)}, f32[512,1536]{1,0:T(8,128)}, f32[4,8,512]{2,1,0:T(8,128)}) custom-call(bf16[1024,1536]{1,0:T(8,128)(2,1)} %convolution_convert_fusion.refs_0_.refs_3_.refs_4_.ko.vo.refs_6_.refs_7_.refs_8_.refs_9_, bf16[512,1536]{1,0:T(8,128)(2,1)} %convolution_convert_fusion.2.refs_1_.refs_2_.q.ks.vs.refs_0_, ...), custom_call_target="tpu_custom_call" | custom-call | flops 3355443200 | bytes 12582912 | tf_op jit(solution)/shard_map/tok_bwd/pallas_call | solution.py:590
  486.2 2.9 add_convert_fusion.1
  505.3 12.3 %mem_bwd.3 = (bf16[512,1536]{1,0:T(8,128)(2,1)}, bf16[512,1536]{1,0:T(8,128)(2,1)}) custom-call(bf16[512,1536]{1,0:T(8,128)(2,1)} %convolution_convert_fusion.2.refs_1_.refs_2_.q.ks.vs.refs_0_, bf16[512,1536]{1,0:T(8,128)(2,1)} %convolution_convert_fusion.2.refs_1_.refs_2_.q.ks.vs.refs_0_, ...), custom_call_target="tpu_custom_call" | custom-call | flops 2684354560 | bytes 9437184 | tf_op jit(solution)/shard_map/mem_bwd/pallas_call | solution.py:444
  517.6 5.6 fusion.102
  523.2 13.6 %proj_grad.1 = (bf16[2,2,2,2,256,256]{5,4,3,2,1,0:T(8,128)(2,1)}, bf16[2,2,2,2,256,256]{5,4,3,2,1,0:T(8,128)(2,1)}, bf16[2,2,2,2,256,256]{5,4,3,2,1,0:T(8,128)(2,1)}) custom-call(s32[4]{0:T(128)} %pad_add_fusion.me, bf16[1024,1024]{1,0:T(8,128)(2,1)} %copy-done.48, bf16[1024,1024]{1,0:T(8,128)(2,1)} %copy-done.48, bf16[512,1024]{1,0:T(8,128)(2,1)} %copy-done.68, ...), custom_call_target="tpu_custom_call" | custom-call | flops 6442450944 | bytes 16777216 | tf_op jit(solution)/shard_map/proj_grad/pallas_call | solution.py:710
  540.8 5.3 select_convert_fusion
  569.1 3.2 collective-permute-start.52
  572.3 6.6 collective-permute-done.41
  583.8 12.8 %collective-permute-done.89 = bf16[128,1024]{1,0:T(8,128)(2,1)S(1)} collective-permute-done((bf16[128,1024]{1,0:T(8,128)(2,1)S(1)}, bf16[128,1024]{1,0:T(8,128)(2,1)S(1)}, u32[]{:S(2)}, u32[]{:S(2)}) %collective-permute-start.89) | collective-permute-done | bytes 262176 | tf_op jit(solution)/shard_map/ppermute | solution.py:37
  599.3 5.7 collective-permute-done.93
  605.9 4.3 collective-permute-start.58
  614.9 5.1 collective-permute-done.68
  624.0 5.0 collective-permute-done.72
  652.0 13.3 %collective-permute-done.65 = bf16[2,2,256,256]{3,2,1,0:T(8,128)(2,1)S(1)} collective-permute-done((bf16[2,2,256,256]{3,2,1,0:T(8,128)(2,1)S(1)}, bf16[2,2,256,256]{3,2,1,0:T(8,128)(2,1)S(1)}, u32[]{:S(2)}, u32[]{:S(2)}) %collective-permute-start.65) | collective-permute-done | bytes 524320 | tf_op jit(solution)/shard_map/ppermute | solution.py:37
  666.9 6.5 collective-permute-start.53
  674.5 20.8 %collective-permute-done.81 = bf16[2,2,32,1024]{3,2,1,0:T(8,128)(2,1)S(1)} collective-permute-done((bf16[2,2,32,1024]{3,2,1,0:T(8,128)(2,1)S(1)}, bf16[2,2,32,1024]{3,2,1,0:T(8,128)(2,1)S(1)}, u32[]{:S(2)}, u32[]{:S(2)}) %collective-permute-start.81) | collective-permute-done | bytes 262176 | tf_op jit(solution)/shard_map/ppermute | solution.py:37
  697.7 5.1 collective-permute-done.70
  705.7 10.9 %collective-permute-done.67 = bf16[256,256]{1,0:T(8,128)(2,1)S(1)} collective-permute-done((bf16[256,256]{1,0:T(8,128)(2,1)S(1)}, bf16[256,256]{1,0:T(8,128)(2,1)S(1)}, u32[]{:S(2)}, u32[]{:S(2)}) %collective-permute-start.67) | collective-permute-done | bytes 131104 | tf_op jit(solution)/shard_map/ppermute | solution.py:37
  719.1 8.6 %collective-permute-done.71 = bf16[256,256]{1,0:T(8,128)(2,1)S(1)} collective-permute-done((bf16[256,256]{1,0:T(8,128)(2,1)S(1)}, bf16[256,256]{1,0:T(8,128)(2,1)S(1)}, u32[]{:S(2)}, u32[]{:S(2)}) %collective-permute-start.71) | collective-permute-done | bytes 131104 | tf_op jit(solution)/shard_map/ppermute | solution.py:37
  728.2 3.9 collective-permute-done.83
  732.2 3.1 collective-permute-start.84
  735.8 4.6 collective-permute-done.84
  748.4 4.4 place_mlp.1
  755.8 4.3 place_proj.1
  (539 shorter events, 230.7 us)
Async XLA Ops:
  0.7 63.0 %collective-permute-start.14 = (bf16[4,64,1024]{2,1,0:T(8,128)(2,1)}, bf16[4,64,1024]{2,1,0:T(8,128)(2,1)S(1)}, u32[]{:S(2)}, u32[]{:S(2)}) collective-permute-start(bf16[4,64,1024]{2,1,0:T(8,128)(2,1)} %param.17), channel_id=1, source_target_pairs={{1,8},{8,1},{3,10},{10,3},{5,12},{12,5},{7,14},{14,7},{17,24},{24,... | collective-permute-start | bytes 1572872 | tf_op jit(solution)/shard_map/ppermute | solution.py:41
  8.8 19.5 %collective-permute-start.10 = (bf16[256,256]{1,0:T(8,128)(2,1)}, bf16[256,256]{1,0:T(8,128)(2,1)}, u32[]{:S(2)}, u32[]{:S(2)}) collective-permute-start(bf16[256,256]{1,0:T(8,128)(2,1)} %get-tuple-element.57), channel_id=1, source_target_pairs={{0,4},{2,6},{4,0},{6,2},{1,5},{3,7},{5,1},{7,3},{8,12},{10,14},{12... | collective-permute-start | bytes 393224 | tf_op jit(solution)/shard_map/ppermute | solution.py:37
  11.1 18.3 %collective-permute-start.6 = (bf16[256,256]{1,0:T(8,128)(2,1)}, bf16[256,256]{1,0:T(8,128)(2,1)}, u32[]{:S(2)}, u32[]{:S(2)}) collective-permute-start(bf16[256,256]{1,0:T(8,128)(2,1)} %get-tuple-element.56), channel_id=1, source_target_pairs={{0,4},{2,6},{4,0},{6,2},{1,5},{3,7},{5,1},{7,3},{8,12},{10,14},{12... | collective-permute-start | bytes 393224 | tf_op jit(solution)/shard_map/ppermute | solution.py:37
  14.1 18.7 %collective-permute-start.2 = (bf16[272,256]{1,0:T(8,128)(2,1)}, bf16[272,256]{1,0:T(8,128)(2,1)S(1)}, u32[]{:S(2)}, u32[]{:S(2)}) collective-permute-start(bf16[272,256]{1,0:T(8,128)(2,1)} %get-tuple-element.184), channel_id=1, source_target_pairs={{0,4},{2,6},{4,0},{6,2},{1,5},{3,7},{5,1},{7,3},{8,12},{10,14},{12... | collective-permute-start | bytes 417800 | tf_op jit(solution)/shard_map/ppermute | solution.py:37
  24.8 100.5 %collective-permute-start = (bf16[512,1024]{1,0:T(8,128)(2,1)}, bf16[512,1024]{1,0:T(8,128)(2,1)S(1)}, u32[]{:S(2)}, u32[]{:S(2)}) collective-permute-start(bf16[512,1024]{1,0:T(8,128)(2,1)} %param.16), channel_id=1, source_target_pairs={{1,8},{8,1},{3,10},{10,3},{5,12},{12,5},{7,14},{14,7},{17,24},{24,... | collective-permute-start | bytes 3145736 | tf_op jit(solution)/shard_map/ppermute | solution.py:41
  28.3 18.7 %collective-permute-start.29 = (bf16[128,1024]{1,0:T(8,128)(2,1)S(1)}, bf16[128,1024]{1,0:T(8,128)(2,1)S(1)}, u32[]{:S(2)}, u32[]{:S(2)}) collective-permute-start(bf16[128,1024]{1,0:T(8,128)(2,1)S(1)} %constant_dynamic-slice_fusion.3), channel_id=1, source_target_pairs={{0,4},{2,6},{4,0},{6,2},{1,5},{3,7},{5,1},{7,3},{8,12},{10,14},{12... | collective-permute-start | bytes 786440 | tf_op jit(solution)/shard_map/ppermute | solution.py:37
  29.4 24.6 %collective-permute-start.33 = (bf16[128,1024]{1,0:T(8,128)(2,1)S(1)}, bf16[128,1024]{1,0:T(8,128)(2,1)S(1)}, u32[]{:S(2)}, u32[]{:S(2)}) collective-permute-start(bf16[128,1024]{1,0:T(8,128)(2,1)S(1)} %constant_dynamic-slice_fusion.2), channel_id=1, source_target_pairs={{0,4},{2,6},{4,0},{6,2},{1,5},{3,7},{5,1},{7,3},{8,12},{10,14},{12... | collective-permute-start | bytes 786440 | tf_op jit(solution)/shard_map/ppermute | solution.py:37
  32.8 23.7 %collective-permute-start.11 = (bf16[2,256,256]{2,1,0:T(8,128)(2,1)S(1)}, bf16[2,256,256]{2,1,0:T(8,128)(2,1)S(1)}, u32[]{:S(2)}, u32[]{:S(2)}) collective-permute-start(bf16[2,256,256]{2,1,0:T(8,128)(2,1)S(1)} %get-tuple-element.180), channel_id=1, source_target_pairs={{0,16},{16,0},{1,17},{17,1},{2,18},{18,2},{3,19},{19,3},{4,20},{20... | collective-permute-start | bytes 786440 | tf_op jit(solution)/shard_map/ppermute | solution.py:37
  72.2 27.5 %collective-permute-start.30 = (bf16[2,128,1024]{2,1,0:T(8,128)(2,1)S(1)}, bf16[2,128,1024]{2,1,0:T(8,128)(2,1)S(1)}, u32[]{:S(2)}, u32[]{:S(2)}) collective-permute-start(bf16[2,128,1024]{2,1,0:T(8,128)(2,1)S(1)} %get-tuple-element.161), channel_id=1, source_target_pairs={{0,2},{2,0},{4,6},{6,4},{1,3},{3,1},{5,7},{7,5},{8,10},{10,8},{12,... | collective-permute-start | bytes 1572872 | tf_op jit(solution)/shard_map/ppermute | solution.py:37
  75.9 19.0 %collective-permute-start.46 = (bf16[64,1024]{1,0:T(8,128)(2,1)S(1)}, bf16[64,1024]{1,0:T(8,128)(2,1)S(1)}, u32[]{:S(2)}, u32[]{:S(2)}) collective-permute-start(bf16[64,1024]{1,0:T(8,128)(2,1)S(1)} %get-tuple-element.153), channel_id=1, source_target_pairs={{0,2},{2,0},{4,6},{6,4},{1,3},{3,1},{5,7},{7,5},{8,10},{10,8},{12,... | collective-permute-start | bytes 393224 | tf_op jit(solution)/shard_map/ppermute | solution.py:831
  75.9 19.0 %collective-permute-start.47 = (bf16[64,1024]{1,0:T(8,128)(2,1)S(1)}, bf16[64,1024]{1,0:T(8,128)(2,1)S(1)}, u32[]{:S(2)}, u32[]{:S(2)}) collective-permute-start(bf16[64,1024]{1,0:T(8,128)(2,1)S(1)} %get-tuple-element.152), channel_id=1, source_target_pairs={{0,4},{2,6},{4,0},{6,2},{1,5},{3,7},{5,1},{7,3},{8,12},{10,14},{12... | collective-permute-start | bytes 393224 | tf_op jit(solution)/shard_map/ppermute | solution.py:831
  80.0 19.7 %collective-permute-start.48 = (bf16[64,1024]{1,0:T(8,128)(2,1)S(1)}, bf16[64,1024]{1,0:T(8,128)(2,1)S(1)}, u32[]{:S(2)}, u32[]{:S(2)}) collective-permute-start(bf16[64,1024]{1,0:T(8,128)(2,1)S(1)} %get-tuple-element.151), channel_id=1, source_target_pairs={{0,6},{2,4},{4,2},{6,0},{1,7},{3,5},{5,3},{7,1},{8,14},{10,12},{12... | collective-permute-start | bytes 393224 | tf_op jit(solution)/shard_map/ppermute | solution.py:831
  94.9 23.2 %collective-permute-start.12 = (bf16[2,2,256,256]{3,2,1,0:T(8,128)(2,1)S(1)}, bf16[2,2,256,256]{3,2,1,0:T(8,128)(2,1)S(1)}, u32[]{:S(2)}, u32[]{:S(2)}) collective-permute-start(bf16[2,2,256,256]{3,2,1,0:T(8,128)(2,1)S(1)} %get-tuple-element.170), channel_id=1, source_target_pairs={{0,1},{1,0},{2,3},{3,2},{4,5},{5,4},{6,7},{7,6},{8,9},{9,8},{10,11... | collective-permute-start | bytes 1572872 | tf_op jit(solution)/shard_map/ppermute | solution.py:37
  99.6 22.7 %collective-permute-start.8 = (bf16[2,2,256,256]{3,2,1,0:T(8,128)(2,1)S(1)}, bf16[2,2,256,256]{3,2,1,0:T(8,128)(2,1)S(1)}, u32[]{:S(2)}, u32[]{:S(2)}) collective-permute-start(bf16[2,2,256,256]{3,2,1,0:T(8,128)(2,1)S(1)} %get-tuple-element.172), channel_id=1, source_target_pairs={{0,2},{2,0},{4,6},{6,4},{1,3},{3,1},{5,7},{7,5},{8,10},{10,8},{12,... | collective-permute-start | bytes 1572872 | tf_op jit(solution)/shard_map/ppermute | solution.py:37
  99.7 22.8 %collective-permute-start.4 = (bf16[2,2,272,256]{3,2,1,0:T(8,128)(2,1)S(1)}, bf16[2,2,272,256]{3,2,1,0:T(8,128)(2,1)S(1)}, u32[]{:S(2)}, u32[]{:S(2)}) collective-permute-start(bf16[2,2,272,256]{3,2,1,0:T(8,128)(2,1)S(1)} %get-tuple-element.144), channel_id=1, source_target_pairs={{0,16},{16,0},{1,17},{17,1},{2,18},{18,2},{3,19},{19,3},{4,20},{20... | collective-permute-start | bytes 1671176 | tf_op jit(solution)/shard_map/ppermute | solution.py:37
  106.8 17.4 %collective-permute-start.22 = (bf16[2,2,64,1024]{3,2,1,0:T(8,128)(2,1)S(1)}, bf16[2,2,64,1024]{3,2,1,0:T(8,128)(2,1)S(1)}, u32[]{:S(2)}, u32[]{:S(2)}) collective-permute-start(bf16[2,2,64,1024]{3,2,1,0:T(8,128)(2,1)S(1)} %get-tuple-element.163), channel_id=1, source_target_pairs={{0,16},{16,0},{1,17},{17,1},{2,18},{18,2},{3,19},{19,3},{4,20},{20... | collective-permute-start | bytes 1572872 | tf_op jit(solution)/shard_map/ppermute | solution.py:37
  118.0 24.8 %collective-permute-start.27 = (bf16[512,1024]{1,0:T(8,128)(2,1)S(1)}, bf16[512,1024]{1,0:T(8,128)(2,1)S(1)}, u32[]{:S(2)}, u32[]{:S(2)}) collective-permute-start(bf16[512,1024]{1,0:T(8,128)(2,1)S(1)} %copy-done.67), channel_id=1, source_target_pairs={{1,8},{8,1},{3,10},{10,3},{5,12},{12,5},{7,14},{14,7},{17,24},{24,... | collective-permute-start | bytes 3145736 | tf_op jit(solution)/shard_map/ppermute | solution.py:41
  122.4 21.6 %collective-permute-start.18 = (bf16[256,1024]{1,0:T(8,128)(2,1)S(1)}, bf16[256,1024]{1,0:T(8,128)(2,1)S(1)}, u32[]{:S(2)}, u32[]{:S(2)}) collective-permute-start(bf16[256,1024]{1,0:T(8,128)(2,1)S(1)} %pad_maximum_fusion.11), channel_id=1, source_target_pairs={{0,8},{8,0},{1,9},{9,1},{2,10},{10,2},{3,11},{11,3},{4,12},{12,4},... | collective-permute-start | bytes 1572872 | tf_op jit(solution)/shard_map/ppermute | solution.py:37
  122.6 23.8 %collective-permute-start.49 = (bf16[256,1024]{1,0:T(8,128)(2,1)S(1)}, bf16[256,1024]{1,0:T(8,128)(2,1)S(1)}, u32[]{:S(2)}, u32[]{:S(2)}) collective-permute-start(bf16[256,1024]{1,0:T(8,128)(2,1)S(1)} %pad_maximum_fusion.16), channel_id=1, source_target_pairs={{0,8},{8,0},{1,9},{9,1},{2,10},{10,2},{3,11},{11,3},{4,12},{12,4},... | collective-permute-start | bytes 1572872 | tf_op jit(solution)/shard_map/ppermute | solution.py:37
  124.2 140.0 %collective-permute-start.31 = (bf16[2,2,128,1024]{3,2,1,0:T(8,128)(2,1)}, bf16[2,2,128,1024]{3,2,1,0:T(8,128)(2,1)}, u32[]{:S(2)}, u32[]{:S(2)}) collective-permute-start(bf16[2,2,128,1024]{3,2,1,0:T(8,128)(2,1)} %get-tuple-element.142), channel_id=1, source_target_pairs={{0,1},{1,0},{2,3},{3,2},{4,5},{5,4},{6,7},{7,6},{8,9},{9,8},{10,11... | collective-permute-start | bytes 3145736 | tf_op jit(solution)/shard_map/ppermute | solution.py:37
  125.3 144.4 %collective-permute-start.35 = (bf16[2,2,128,1024]{3,2,1,0:T(8,128)(2,1)}, bf16[2,2,128,1024]{3,2,1,0:T(8,128)(2,1)}, u32[]{:S(2)}, u32[]{:S(2)}) collective-permute-start(bf16[2,2,128,1024]{3,2,1,0:T(8,128)(2,1)} %get-tuple-element.140), channel_id=1, source_target_pairs={{0,16},{16,0},{1,17},{17,1},{2,18},{18,2},{3,19},{19,3},{4,20},{20... | collective-permute-start | bytes 3145736 | tf_op jit(solution)/shard_map/ppermute | solution.py:37
  142.9 14.1 %collective-permute-start.13 = (bf16[2,2,2,256,256]{4,3,2,1,0:T(8,128)(2,1)S(1)}, bf16[2,2,2,256,256]{4,3,2,1,0:T(8,128)(2,1)S(1)}, u32[]{:S(2)}, u32[]{:S(2)}) collective-permute-start(bf16[2,2,2,256,256]{4,3,2,1,0:T(8,128)(2,1)S(1)} %pad_maximum_fusion.4.c0), channel_id=1, source_target_pairs={{0,2},{2,0},{4,6},{6,4},{1,3},{3,1},{5,7},{7,5},{8,10},{10,8},{12,... | collective-permute-start | bytes 3145736 | tf_op jit(solution)/shard_map/ppermute | solution.py:37
  144.0 26.9 %collective-permute-start.9 = (bf16[2,2,2,256,256]{4,3,2,1,0:T(8,128)(2,1)S(1)}, bf16[2,2,2,256,256]{4,3,2,1,0:T(8,128)(2,1)S(1)}, u32[]{:S(2)}, u32[]{:S(2)}) collective-permute-start(bf16[2,2,2,256,256]{4,3,2,1,0:T(8,128)(2,1)S(1)} %pad_maximum_fusion.3.b0), channel_id=1, source_target_pairs={{0,16},{16,0},{1,17},{17,1},{2,18},{18,2},{3,19},{19,3},{4,20},{20... | collective-permute-start | bytes 3145736 | tf_op jit(solution)/shard_map/ppermute | solution.py:37
  146.4 37.9 %collective-permute-start.5 = (bf16[2,2,2,272,256]{4,3,2,1,0:T(8,128)(2,1)S(1)}, bf16[2,2,2,272,256]{4,3,2,1,0:T(8,128)(2,1)S(1)}, u32[]{:S(2)}, u32[]{:S(2)}) collective-permute-start(bf16[2,2,2,272,256]{4,3,2,1,0:T(8,128)(2,1)S(1)} %pad_maximum_fusion.2.a0), channel_id=1, source_target_pairs={{0,1},{1,0},{2,3},{3,2},{4,5},{5,4},{6,7},{7,6},{8,9},{9,8},{10,11... | collective-permute-start | bytes 3342344 | tf_op jit(solution)/shard_map/ppermute | solution.py:37
  156.9 46.8 %collective-permute-start.1 = (bf16[512,1024]{1,0:T(8,128)(2,1)S(1)}, bf16[512,1024]{1,0:T(8,128)(2,1)S(1)}, u32[]{:S(2)}, u32[]{:S(2)}) collective-permute-start(bf16[512,1024]{1,0:T(8,128)(2,1)S(1)} %get-tuple-element.113), channel_id=1, source_target_pairs={{0,8},{8,0},{1,9},{9,1},{2,10},{10,2},{3,11},{11,3},{4,12},{12,4},... | collective-permute-start | bytes 3145736 | tf_op jit(solution)/shard_map/ppermute | solution.py:37
  170.8 50.2 %collective-permute-start.23 = (bf16[2,2,2,64,1024]{4,3,2,1,0:T(8,128)(2,1)}, bf16[2,2,2,64,1024]{4,3,2,1,0:T(8,128)(2,1)S(1)}, u32[]{:S(2)}, u32[]{:S(2)}) collective-permute-start(bf16[2,2,2,64,1024]{4,3,2,1,0:T(8,128)(2,1)} %pad_maximum_fusion.5.low), channel_id=1, source_target_pairs={{0,1},{1,0},{2,3},{3,2},{4,5},{5,4},{6,7},{7,6},{8,9},{9,8},{10,11... | collective-permute-start | bytes 3145736 | tf_op jit(solution)/shard_map/ppermute | solution.py:37
  185.3 104.7 %collective-permute-start.28 = (bf16[512,1024]{1,0:T(8,128)(2,1)}, bf16[512,1024]{1,0:T(8,128)(2,1)}, u32[]{:S(2)}, u32[]{:S(2)}) collective-permute-start(bf16[512,1024]{1,0:T(8,128)(2,1)} %broadcast_select_fusion.3.d0), channel_id=1, source_target_pairs={{0,8},{8,0},{1,9},{9,1},{2,10},{10,2},{3,11},{11,3},{4,12},{12,4},... | collective-permute-start | bytes 3145736 | tf_op jit(solution)/shard_map/ppermute | solution.py:37
  227.6 16.2 %collective-permute-start.24 = (bf16[512,1024]{1,0:T(8,128)(2,1)S(1)}, bf16[512,1024]{1,0:T(8,128)(2,1)S(1)}, u32[]{:S(2)}, u32[]{:S(2)}) collective-permute-start(bf16[512,1024]{1,0:T(8,128)(2,1)S(1)} %get-tuple-element.192), channel_id=1, source_target_pairs={{0,8},{8,0},{1,9},{9,1},{2,10},{10,2},{3,11},{11,3},{4,12},{12,4},... | collective-permute-start | bytes 3145736 | tf_op jit(solution)/shard_map/ppermute | solution.py:37
  267.4 48.6 %collective-permute-start.32 = (bf16[2,2,2,128,1024]{4,3,2,1,0:T(8,128)(2,1)}, bf16[2,2,2,128,1024]{4,3,2,1,0:T(8,128)(2,1)}, u32[]{:S(2)}, u32[]{:S(2)}) collective-permute-start(bf16[2,2,2,128,1024]{4,3,2,1,0:T(8,128)(2,1)} %pad_maximum_fusion), channel_id=1, source_target_pairs={{0,16},{16,0},{1,17},{17,1},{2,18},{18,2},{3,19},{19,3},{4,20},{20... | collective-permute-start | bytes 6291464 | tf_op jit(solution)/shard_map/ppermute | solution.py:37
  272.5 47.2 %collective-permute-start.36 = (bf16[2,2,2,128,1024]{4,3,2,1,0:T(8,128)(2,1)}, bf16[2,2,2,128,1024]{4,3,2,1,0:T(8,128)(2,1)}, u32[]{:S(2)}, u32[]{:S(2)}) collective-permute-start(bf16[2,2,2,128,1024]{4,3,2,1,0:T(8,128)(2,1)} %pad_maximum_fusion.1), channel_id=1, source_target_pairs={{0,2},{2,0},{4,6},{6,4},{1,3},{3,1},{5,7},{7,5},{8,10},{10,8},{12,... | collective-permute-start | bytes 6291464 | tf_op jit(solution)/shard_map/ppermute | solution.py:37
  275.1 44.7 %collective-permute-start.26 = (bf16[512,1024]{1,0:T(8,128)(2,1)}, bf16[512,1024]{1,0:T(8,128)(2,1)}, u32[]{:S(2)}, u32[]{:S(2)}) collective-permute-start(bf16[512,1024]{1,0:T(8,128)(2,1)} %multiply_convert_fusion.2.h0), channel_id=1, source_target_pairs={{0,8},{8,0},{1,9},{9,1},{2,10},{10,2},{3,11},{11,3},{4,12},{12,4},... | collective-permute-start | bytes 3145736 | tf_op jit(solution)/shard_map/ppermute | solution.py:37
  287.8 264.6 %collective-permute-start.39 = (bf16[256,1024]{1,0:T(8,128)(2,1)}, bf16[256,1024]{1,0:T(8,128)(2,1)}, u32[]{:S(2)}, u32[]{:S(2)}) collective-permute-start(bf16[256,1024]{1,0:T(8,128)(2,1)} %dynamic-slice_convert_fusion.1), channel_id=1, source_target_pairs={{0,8},{8,0},{1,9},{9,1},{2,10},{10,2},{3,11},{11,3},{4,12},{12,4},... | collective-permute-start | bytes 1572872 | tf_op jit(solution)/shard_map/ppermute | solution.py:37
  370.4 20.1 %collective-permute-start.44 = (bf16[512,1024]{1,0:T(8,128)(2,1)}, bf16[512,1024]{1,0:T(8,128)(2,1)}, u32[]{:S(2)}, u32[]{:S(2)}) collective-permute-start(bf16[512,1024]{1,0:T(8,128)(2,1)} %get-tuple-element.70), channel_id=1, source_target_pairs={{0,8},{8,0},{1,9},{9,1},{2,10},{10,2},{3,11},{11,3},{4,12},{12,4},... | collective-permute-start | bytes 3145736 | tf_op jit(solution)/shard_map/ppermute | solution.py:37
  375.5 47.6 %collective-permute-start.86 = (bf16[2,2,2,128,1024]{4,3,2,1,0:T(8,128)(2,1)}, bf16[2,2,2,128,1024]{4,3,2,1,0:T(8,128)(2,1)}, u32[]{:S(2)}, u32[]{:S(2)}) collective-permute-start(bf16[2,2,2,128,1024]{4,3,2,1,0:T(8,128)(2,1)} %bitcast.131), channel_id=1, source_target_pairs={{0,1},{1,0},{2,3},{3,2},{4,5},{5,4},{6,7},{7,6},{8,9},{9,8},{10,11... | collective-permute-start | bytes 6291464 | tf_op jit(solution)/shard_map/ppermute | solution.py:37
  390.4 46.8 %collective-permute-start.90 = (bf16[2,2,2,128,1024]{4,3,2,1,0:T(8,128)(2,1)S(1)}, bf16[2,2,2,128,1024]{4,3,2,1,0:T(8,128)(2,1)S(1)}, u32[]{:S(2)}, u32[]{:S(2)}) collective-permute-start(bf16[2,2,2,128,1024]{4,3,2,1,0:T(8,128)(2,1)S(1)} %bitcast.348), channel_id=1, source_target_pairs={{0,16},{16,0},{1,17},{17,1},{2,18},{18,2},{3,19},{19,3},{4,20},{20... | collective-permute-start | bytes 6291464 | tf_op jit(solution)/shard_map/ppermute | solution.py:37
  396.6 43.3 %collective-permute-start.50 = (bf16[512,1024]{1,0:T(8,128)(2,1)S(1)}, bf16[512,1024]{1,0:T(8,128)(2,1)S(1)}, u32[]{:S(2)}, u32[]{:S(2)}) collective-permute-start(bf16[512,1024]{1,0:T(8,128)(2,1)S(1)} %get-tuple-element.117), channel_id=1, source_target_pairs={{0,8},{8,0},{1,9},{9,1},{2,10},{10,2},{3,11},{11,3},{4,12},{12,4},... | collective-permute-start | bytes 3145736 | tf_op jit(solution)/shard_map/ppermute | solution.py:37
  397.3 84.4 %collective-permute-start.38 = (bf16[512,1024]{1,0:T(8,128)(2,1)}, bf16[512,1024]{1,0:T(8,128)(2,1)}, u32[]{:S(2)}, u32[]{:S(2)}) collective-permute-start(bf16[512,1024]{1,0:T(8,128)(2,1)} %get-tuple-element.135), channel_id=1, source_target_pairs={{1,8},{8,1},{3,10},{10,3},{5,12},{12,5},{7,14},{14,7},{17,24},{24,... | collective-permute-start | bytes 3145736 | tf_op jit(solution)/shard_map/ppermute | solution.py:41
  426.8 62.3 %collective-permute-start.87 = (bf16[2,2,128,1024]{3,2,1,0:T(8,128)(2,1)}, bf16[2,2,128,1024]{3,2,1,0:T(8,128)(2,1)}, u32[]{:S(2)}, u32[]{:S(2)}) collective-permute-start(bf16[2,2,128,1024]{3,2,1,0:T(8,128)(2,1)} %slice_bitcast_fusion.2), channel_id=1, source_target_pairs={{0,16},{16,0},{1,17},{17,1},{2,18},{18,2},{3,19},{19,3},{4,20},{20... | collective-permute-start | bytes 3145736 | tf_op jit(solution)/shard_map/ppermute | solution.py:37
  439.8 53.8 %collective-permute-start.91 = (bf16[2,2,128,1024]{3,2,1,0:T(8,128)(2,1)}, bf16[2,2,128,1024]{3,2,1,0:T(8,128)(2,1)}, u32[]{:S(2)}, u32[]{:S(2)}) collective-permute-start(bf16[2,2,128,1024]{3,2,1,0:T(8,128)(2,1)} %slice_bitcast_fusion), channel_id=1, source_target_pairs={{0,2},{2,0},{4,6},{6,4},{1,3},{3,1},{5,7},{7,5},{8,10},{10,8},{12,... | collective-permute-start | bytes 3145736 | tf_op jit(solution)/shard_map/ppermute | solution.py:37
  465.5 32.0 %collective-permute-start.51 = (bf16[512,1024]{1,0:T(8,128)(2,1)}, bf16[512,1024]{1,0:T(8,128)(2,1)}, u32[]{:S(2)}, u32[]{:S(2)}) collective-permute-start(bf16[512,1024]{1,0:T(8,128)(2,1)} %get-tuple-element.196), channel_id=1, source_target_pairs={{0,8},{8,0},{1,9},{9,1},{2,10},{10,2},{3,11},{11,3},{4,12},{12,4},... | collective-permute-start | bytes 3145736 | tf_op jit(solution)/shard_map/ppermute | solution.py:37
  492.1 56.0 %collective-permute-start.88 = (bf16[2,128,1024]{2,1,0:T(8,128)(2,1)}, bf16[2,128,1024]{2,1,0:T(8,128)(2,1)}, u32[]{:S(2)}, u32[]{:S(2)}) collective-permute-start(bf16[2,128,1024]{2,1,0:T(8,128)(2,1)} %slice_bitcast_fusion.9), channel_id=1, source_target_pairs={{0,2},{2,0},{4,6},{6,4},{1,3},{3,1},{5,7},{7,5},{8,10},{10,8},{12,... | collective-permute-start | bytes 1572872 | tf_op jit(solution)/shard_map/ppermute | solution.py:37
  496.2 54.9 %collective-permute-start.92 = (bf16[2,128,1024]{2,1,0:T(8,128)(2,1)}, bf16[2,128,1024]{2,1,0:T(8,128)(2,1)}, u32[]{:S(2)}, u32[]{:S(2)}) collective-permute-start(bf16[2,128,1024]{2,1,0:T(8,128)(2,1)} %slice_bitcast_fusion.7), channel_id=1, source_target_pairs={{0,1},{1,0},{2,3},{3,2},{4,5},{5,4},{6,7},{7,6},{8,9},{9,8},{10,11... | collective-permute-start | bytes 1572872 | tf_op jit(solution)/shard_map/ppermute | solution.py:37
  505.1 128.2 %collective-permute-start.79 = (bf16[2,2,2,2,32,1024]{5,4,3,2,1,0:T(8,128)(2,1)}, bf16[2,2,2,2,32,1024]{5,4,3,2,1,0:T(8,128)(2,1)}, u32[]{:S(2)}, u32[]{:S(2)}) collective-permute-start(bf16[2,2,2,2,32,1024]{5,4,3,2,1,0:T(8,128)(2,1)} %fusion.27), channel_id=1, source_target_pairs={{0,2},{2,0},{4,6},{6,4},{1,3},{3,1},{5,7},{7,5},{8,10},{10,8},{12,... | collective-permute-start | bytes 3145736 | tf_op jit(solution)/shard_map/ppermute | solution.py:37
  538.3 73.4 %collective-permute-start.64 = (bf16[2,2,2,256,256]{4,3,2,1,0:T(8,128)(2,1)S(1)}, bf16[2,2,2,256,256]{4,3,2,1,0:T(8,128)(2,1)S(1)}, u32[]{:S(2)}, u32[]{:S(2)}) collective-permute-start(bf16[2,2,2,256,256]{4,3,2,1,0:T(8,128)(2,1)S(1)} %slice_bitcast_fusion.6), channel_id=1, source_target_pairs={{0,1},{1,0},{2,3},{3,2},{4,5},{5,4},{6,7},{7,6},{8,9},{9,8},{10,11... | collective-permute-start | bytes 3145736 | tf_op jit(solution)/shard_map/ppermute | solution.py:37
  562.7 16.3 %collective-permute-start.41 = (bf16[64,1024]{1,0:T(8,128)(2,1)S(1)}, bf16[64,1024]{1,0:T(8,128)(2,1)S(1)}, u32[]{:S(2)}, u32[]{:S(2)}) collective-permute-start(bf16[64,1024]{1,0:T(8,128)(2,1)S(1)} %get-tuple-element.156), channel_id=1, source_target_pairs={{0,4},{2,6},{4,0},{6,2},{1,5},{3,7},{5,1},{7,3},{8,12},{10,14},{12... | collective-permute-start | bytes 393224 | tf_op jit(solution)/shard_map/ppermute | solution.py:839
  569.1 36.8 %collective-permute-start.52 = (bf16[512,1024]{1,0:T(8,128)(2,1)S(1)}, bf16[512,1024]{1,0:T(8,128)(2,1)S(1)}, u32[]{:S(2)}, u32[]{:S(2)}) collective-permute-start(bf16[512,1024]{1,0:T(8,128)(2,1)S(1)} %copy-done.85), channel_id=1, source_target_pairs={{0,8},{8,0},{1,9},{9,1},{2,10},{10,2},{3,11},{11,3},{4,12},{12,4},... | collective-permute-start | bytes 3145736 | tf_op jit(solution)/shard_map/ppermute | solution.py:37
  579.0 17.6 %collective-permute-start.89 = (bf16[128,1024]{1,0:T(8,128)(2,1)S(1)}, bf16[128,1024]{1,0:T(8,128)(2,1)S(1)}, u32[]{:S(2)}, u32[]{:S(2)}) collective-permute-start(bf16[128,1024]{1,0:T(8,128)(2,1)S(1)} %slice_bitcast_fusion.21), channel_id=1, source_target_pairs={{0,4},{2,6},{4,0},{6,2},{1,5},{3,7},{5,1},{7,3},{8,12},{10,14},{12... | collective-permute-start | bytes 786440 | tf_op jit(solution)/shard_map/ppermute | solution.py:37
  580.6 24.4 %collective-permute-start.93 = (bf16[128,1024]{1,0:T(8,128)(2,1)S(1)}, bf16[128,1024]{1,0:T(8,128)(2,1)S(1)}, u32[]{:S(2)}, u32[]{:S(2)}) collective-permute-start(bf16[128,1024]{1,0:T(8,128)(2,1)S(1)} %slice_bitcast_fusion.19), channel_id=1, source_target_pairs={{0,4},{2,6},{4,0},{6,2},{1,5},{3,7},{5,1},{7,3},{8,12},{10,14},{12... | collective-permute-start | bytes 786440 | tf_op jit(solution)/shard_map/ppermute | solution.py:37
  596.6 23.4 %collective-permute-start.68 = (bf16[2,2,2,256,256]{4,3,2,1,0:T(8,128)(2,1)}, bf16[2,2,2,256,256]{4,3,2,1,0:T(8,128)(2,1)}, u32[]{:S(2)}, u32[]{:S(2)}) collective-permute-start(bf16[2,2,2,256,256]{4,3,2,1,0:T(8,128)(2,1)} %slice_bitcast_fusion.5), channel_id=1, source_target_pairs={{0,16},{16,0},{1,17},{17,1},{2,18},{18,2},{3,19},{19,3},{4,20},{20... | collective-permute-start | bytes 3145736 | tf_op jit(solution)/shard_map/ppermute | solution.py:37
  605.0 23.9 %collective-permute-start.72 = (bf16[2,2,2,256,256]{4,3,2,1,0:T(8,128)(2,1)}, bf16[2,2,2,256,256]{4,3,2,1,0:T(8,128)(2,1)}, u32[]{:S(2)}, u32[]{:S(2)}) collective-permute-start(bf16[2,2,2,256,256]{4,3,2,1,0:T(8,128)(2,1)} %slice_bitcast_fusion.4), channel_id=1, source_target_pairs={{0,2},{2,0},{4,6},{6,4},{1,3},{3,1},{5,7},{7,5},{8,10},{10,8},{12,... | collective-permute-start | bytes 3145736 | tf_op jit(solution)/shard_map/ppermute | solution.py:37
  605.9 38.2 %collective-permute-start.58 = (bf16[4,64,1024]{2,1,0:T(8,128)(2,1)}, bf16[4,64,1024]{2,1,0:T(8,128)(2,1)}, u32[]{:S(2)}, u32[]{:S(2)}) collective-permute-start(bf16[4,64,1024]{2,1,0:T(8,128)(2,1)} %bitcast.75), channel_id=1, source_target_pairs={{1,8},{8,1},{3,10},{10,3},{5,12},{12,5},{7,14},{14,7},{17,24},{24,... | collective-permute-start | bytes 1572872 | tf_op jit(solution)/shard_map/ppermute | solution.py:41
  611.6 36.2 %collective-permute-start.43 = (bf16[4,64,1024]{2,1,0:T(8,128)(2,1)}, bf16[4,64,1024]{2,1,0:T(8,128)(2,1)}, u32[]{:S(2)}, u32[]{:S(2)}) collective-permute-start(bf16[4,64,1024]{2,1,0:T(8,128)(2,1)} %bitcast.65), channel_id=1, source_target_pairs={{1,8},{8,1},{3,10},{10,3},{5,12},{12,5},{7,14},{14,7},{17,24},{24,... | collective-permute-start | bytes 1572872 | tf_op jit(solution)/shard_map/ppermute | solution.py:41
  620.0 46.9 %collective-permute-start.94 = (bf16[2,128,1024]{2,1,0:T(8,128)(2,1)}, bf16[2,128,1024]{2,1,0:T(8,128)(2,1)S(1)}, u32[]{:S(2)}, u32[]{:S(2)}) collective-permute-start(bf16[2,128,1024]{2,1,0:T(8,128)(2,1)} %pad_maximum_fusion.19.p00), channel_id=1, source_target_pairs={{0,16},{16,0},{1,17},{17,1},{2,18},{18,2},{3,19},{19,3},{4,20},{20... | collective-permute-start | bytes 1572872 | tf_op jit(solution)/shard_map/ppermute | solution.py:37
  629.0 114.5 %collective-permute-start.95 = (bf16[2,128,1024]{2,1,0:T(8,128)(2,1)S(1)}, bf16[2,128,1024]{2,1,0:T(8,128)(2,1)S(1)}, u32[]{:S(2)}, u32[]{:S(2)}) collective-permute-start(bf16[2,128,1024]{2,1,0:T(8,128)(2,1)S(1)} %copy-done.53), channel_id=1, source_target_pairs={{0,8},{8,0},{1,9},{9,1},{2,10},{10,2},{3,11},{11,3},{4,12},{12,4},... | collective-permute-start | bytes 1572872 | tf_op jit(solution)/shard_map/ppermute | solution.py:37
  644.1 29.3 %collective-permute-start.80 = (bf16[2,2,2,32,1024]{4,3,2,1,0:T(8,128)(2,1)S(1)}, bf16[2,2,2,32,1024]{4,3,2,1,0:T(8,128)(2,1)S(1)}, u32[]{:S(2)}, u32[]{:S(2)}) collective-permute-start(bf16[2,2,2,32,1024]{4,3,2,1,0:T(8,128)(2,1)S(1)} %dynamic-slice_bitcast_fusion), channel_id=1, source_target_pairs={{0,16},{16,0},{1,17},{17,1},{2,18},{18,2},{3,19},{19,3},{4,20},{20... | collective-permute-start | bytes 1572872 | tf_op jit(solution)/shard_map/ppermute | solution.py:37
  644.1 21.2 %collective-permute-start.65 = (bf16[2,2,256,256]{3,2,1,0:T(8,128)(2,1)S(1)}, bf16[2,2,256,256]{3,2,1,0:T(8,128)(2,1)S(1)}, u32[]{:S(2)}, u32[]{:S(2)}) collective-permute-start(bf16[2,2,256,256]{3,2,1,0:T(8,128)(2,1)S(1)} %slice_bitcast_fusion.17), channel_id=1, source_target_pairs={{0,16},{16,0},{1,17},{17,1},{2,18},{18,2},{3,19},{19,3},{4,20},{20... | collective-permute-start | bytes 1572872 | tf_op jit(solution)/shard_map/ppermute | solution.py:37
  651.6 22.1 %collective-permute-start.69 = (bf16[2,2,256,256]{3,2,1,0:T(8,128)(2,1)S(1)}, bf16[2,2,256,256]{3,2,1,0:T(8,128)(2,1)S(1)}, u32[]{:S(2)}, u32[]{:S(2)}) collective-permute-start(bf16[2,2,256,256]{3,2,1,0:T(8,128)(2,1)S(1)} %slice_bitcast_fusion.15), channel_id=1, source_target_pairs={{0,2},{2,0},{4,6},{6,4},{1,3},{3,1},{5,7},{7,5},{8,10},{10,8},{12,... | collective-permute-start | bytes 1572872 | tf_op jit(solution)/shard_map/ppermute | solution.py:37
  666.9 85.9 %collective-permute-start.53 = (bf16[512,1024]{1,0:T(8,128)(2,1)S(1)}, bf16[512,1024]{1,0:T(8,128)(2,1)S(1)}, u32[]{:S(2)}, u32[]{:S(2)}) collective-permute-start(bf16[512,1024]{1,0:T(8,128)(2,1)S(1)} %fusion.16), channel_id=1, source_target_pairs={{1,8},{8,1},{3,10},{10,3},{5,12},{12,5},{7,14},{14,7},{17,24},{24,... | collective-permute-start | bytes 3145736 | tf_op jit(solution)/shard_map/ppermute | solution.py:41
  673.4 74.2 %collective-permute-start.96 = (bf16[2,128,1024]{2,1,0:T(8,128)(2,1)S(1)}, bf16[2,128,1024]{2,1,0:T(8,128)(2,1)S(1)}, u32[]{:S(2)}, u32[]{:S(2)}) collective-permute-start(bf16[2,128,1024]{2,1,0:T(8,128)(2,1)S(1)} %collective-permute-done.94.p01), channel_id=1, source_target_pairs={{0,8},{8,0},{1,9},{9,1},{2,10},{10,2},{3,11},{11,3},{4,12},{12,4},... | collective-permute-start | bytes 1572872 | tf_op jit(solution)/shard_map/ppermute | solution.py:37
  673.7 21.6 %collective-permute-start.81 = (bf16[2,2,32,1024]{3,2,1,0:T(8,128)(2,1)S(1)}, bf16[2,2,32,1024]{3,2,1,0:T(8,128)(2,1)S(1)}, u32[]{:S(2)}, u32[]{:S(2)}) collective-permute-start(bf16[2,2,32,1024]{3,2,1,0:T(8,128)(2,1)S(1)} %dynamic-slice_bitcast_fusion.1), channel_id=1, source_target_pairs={{0,1},{1,0},{2,3},{3,2},{4,5},{5,4},{6,7},{7,6},{8,9},{9,8},{10,11... | collective-permute-start | bytes 786440 | tf_op jit(solution)/shard_map/ppermute | solution.py:37
  674.3 23.0 %collective-permute-start.66 = (bf16[2,256,256]{2,1,0:T(8,128)(2,1)S(1)}, bf16[2,256,256]{2,1,0:T(8,128)(2,1)S(1)}, u32[]{:S(2)}, u32[]{:S(2)}) collective-permute-start(bf16[2,256,256]{2,1,0:T(8,128)(2,1)S(1)} %slice_bitcast_fusion.27), channel_id=1, source_target_pairs={{0,2},{2,0},{4,6},{6,4},{1,3},{3,1},{5,7},{7,5},{8,10},{10,8},{12,... | collective-permute-start | bytes 786440 | tf_op jit(solution)/shard_map/ppermute | solution.py:37
  702.9 13.8 %collective-permute-start.82 = (bf16[2,32,1024]{2,1,0:T(8,128)(2,1)S(1)}, bf16[2,32,1024]{2,1,0:T(8,128)(2,1)S(1)}, u32[]{:S(2)}, u32[]{:S(2)}) collective-permute-start(bf16[2,32,1024]{2,1,0:T(8,128)(2,1)S(1)} %dynamic-slice_bitcast_fusion.2), channel_id=1, source_target_pairs={{0,4},{2,6},{4,0},{6,2},{1,5},{3,7},{5,1},{7,3},{8,12},{10,14},{12... | collective-permute-start | bytes 393224 | tf_op jit(solution)/shard_map/ppermute | solution.py:37
  716.6 18.6 %collective-permute-start.75 = (bf16[256,256]{1,0:T(8,128)(2,1)S(1)}, bf16[256,256]{1,0:T(8,128)(2,1)S(1)}, u32[]{:S(2)}, u32[]{:S(2)}) collective-permute-start(bf16[256,256]{1,0:T(8,128)(2,1)S(1)} %slice_bitcast_fusion.29), channel_id=1, source_target_pairs={{0,4},{2,6},{4,0},{6,2},{1,5},{3,7},{5,1},{7,3},{8,12},{10,14},{12... | collective-permute-start | bytes 393224 | tf_op jit(solution)/shard_map/ppermute | solution.py:37
  740.8 19.2 %collective-permute-start.85 = (bf16[2,128,1024]{2,1,0:T(8,128)(2,1)S(1)}, bf16[2,128,1024]{2,1,0:T(8,128)(2,1)S(1)}, u32[]{:S(2)}, u32[]{:S(2)}) collective-permute-start(bf16[2,128,1024]{2,1,0:T(8,128)(2,1)S(1)} %bitcast.345), channel_id=1, source_target_pairs={{0,8},{8,0},{1,9},{9,1},{2,10},{10,2},{3,11},{11,3},{4,12},{12,4},... | collective-permute-start | bytes 1572872 | tf_op jit(solution)/shard_map/ppermute | solution.py:37
  (121 other events, 973.4 us)

commit v2 on v1

--- a/solution.py
+++ b/solution.py
@@ -27,8 +27,11 @@
 BF = jnp.bfloat16
 F32 = jnp.float32
 
-AXIS_BITS = {"c": ("c", 1), "x": ("x", 1), "y": ("g", 1), "z1": ("s", 1), "z2": ("s", 2)}
-VMEM_CAP = 56 * 1024 * 1024
+AXIS_BITS = {"c": ("c", 1), "x": ("x", 1), "y": ("y", 1), "z1": ("s", 1), "z2": ("s", 2)}
+VMEM_MLP = 44
+VMEM_GRADS = 56
+VMEM_MOST = 18
+COST_CUT = 10
 
 
 def xch(value, bit):
@@ -41,28 +44,20 @@
     return lax.ppermute(value, ("c", "x"), [(1, 2), (2, 1)])
 
 
-def gather_bits(piece, order):
-    held = piece
-    for bit in order[:-1]:
-        held = jnp.stack([held, xch(held, bit)])
-    return held, xch(held, order[-1])
-
-
-def reduce_bits(parts, order):
-    for bit in order:
-        got = xch(parts[1], bit)
-        parts = (parts[0].astype(F32) + got.astype(F32)).astype(BF)
-    return over_groups(parts)
-
-
 def over_groups(part):
-    groups = lax.axis_size("g")
-    step = 2
+    groups = lax.axis_size("h")
+    step = 1
     while step < groups:
-        got = lax.ppermute(part, "g", [(i, i ^ step) for i in range(groups)])
+        got = lax.ppermute(part, "h", [(i, i ^ step) for i in range(groups)])
         part = (part.astype(F32) + got.astype(F32)).astype(part.dtype)
         step *= 2
     return part
+
+
+def fence(values, done):
+    leaves, tree = jax.tree.flatten(values)
+    tied = lax.optimization_barrier(tuple(leaves) + tuple(jax.tree.leaves(done)))
+    return jax.tree.unflatten(tree, tied[: len(leaves)])
 
 
 def untwist(value, bits):
@@ -114,17 +109,21 @@
     return bucket_table(BLK, NB, REACH)[(s - col) % BLK].reshape(-1)
 
 
-def params(flops=0, moved=0, trans=0, grid=1):
+def params(flops=0, moved=0, trans=0, grid=1, vmem=VMEM_MOST):
     return dict(
         compiler_params=pltpu.CompilerParams(
-            vmem_limit_bytes=VMEM_CAP, dimension_semantics=("arbitrary",) * grid
+            vmem_limit_bytes=vmem * 2**20, dimension_semantics=("arbitrary",) * grid
         ),
-        cost_estimate=pl.CostEstimate(flops=flops, bytes_accessed=moved, transcendentals=trans),
+        cost_estimate=pl.CostEstimate(
+            flops=flops // COST_CUT, bytes_accessed=moved // COST_CUT, transcendentals=0
+        ),
     )
 
 
 def full(shape, memory_space=None):
-    return pl.BlockSpec(shape, lambda *_: (0,) * len(shape))
+    return pl.BlockSpec(
+        shape, lambda *_: (0,) * len(shape), pipeline_mode=pl.Buffered(buffer_count=1)
+    )
 
 
 def pick_kernel(me, tok, st, *outs):
@@ -204,11 +203,11 @@
 def lay_out_kernel(me, low, high, wo, wu):
     x0, z0, y0 = me[1], me[2], me[3]
     q = low.shape[3] // 2
-    for xr in range(2):
-        src = (low, high)[xr]
-        for yr in range(2):
+    for yr in range(2):
+        src = (low, high)[yr]
+        for xr in range(2):
             for zr in range(4):
-                v = src[yr, zr % 2, zr // 2]
+                v = src[xr, zr % 2, zr // 2]
                 row = (z0 ^ zr) * DH + ((x0 ^ xr) * 2 + (y0 ^ yr)) * q
                 rows = pl.ds(pl.multiple_of(row, q), q)
                 wo[rows, :] = v[0:q]
@@ -610,178 +609,439 @@
     return jnp.where(u >= 0, 1.0 - tail, tail), bell * (1.0 / math.sqrt(2.0 * math.pi))
 
 
-def mlp_kernel(
-    h0, h1, d0, d1, ua, ub, da, db, gu, gd, o0, o1, e0, e1, acc_o0, acc_o1, acc_e0, acc_e1
-):
+MAIN = 96
+REST = DH - MAIN
+TILE = 4 * DH
+
+
+def mlp_kernel(h0, h1, d0, d1, u0, u1, w0, w1, *refs):
+    a_keep, a_send, b_keep, b_send, c_keep, c_send, o0, o1, e0, e1 = refs[:10]
+    accs = refs[10:]
     t = pl.program_id(0)
-    wu = jnp.where(t < 4, ua[...], ub[...])
-    wd = jnp.where(lax.rem(t, 2) == 0, da[...], db[...])
+    in_x, in_y = t // 2, lax.rem(t, 2)
+
+    @pl.when(t == 0)
+    def _():
+        for ref in accs:
+            ref[...] = jnp.zeros_like(ref)
+
+    wu = jnp.where(in_y == 0, u0[...], u1[...])
+    wd = jnp.concatenate([w0[...], w1[...]], axis=0)
+    kept = []
     for r in range(2):
         h = (h0, h1)[r]
         d = (d0, d1)[r]
-        acc_o = (acc_o0, acc_o1)[r]
-        acc_e = (acc_e0, acc_e1)[r]
         u = mm_nt(h[...], wu)
         dg = mm_nt(d[...], wd)
         phi, pdf = normal_parts(u)
         g = (u * phi).astype(BF)
         du = (dg * (phi + u * pdf)).astype(BF)
-        if r == 0:
-            g_first, du_first = g, du
-        o_term = mm(g, wd)
-        e_term = mm(du, wu)
-
-        @pl.when(t == 0)
+        accs[r][...] += mm(g, wd)
+        accs[2 + r][...] += mm(du, wu)
+        kept.append((g, du))
+    gd = (mm_tn(kept[0][0], d0[...]) + mm_tn(kept[1][0], d1[...])).astype(BF)
+    gu = (mm_tn(kept[0][1], h0[...]) + mm_tn(kept[1][1], h1[...])).astype(BF)
+    gd, gu = gd.reshape(4, DH, D), gu.reshape(4, DH, D)
+    for z1 in range(2):
+        side = (c_keep, c_send)[z1]
+        for z2 in range(2):
+            side[0, 0, z2, 0:REST, :] = gu[2 * z1 + z2, MAIN:, :]
+            side[0, 0, z2, REST:, :] = gd[2 * z1 + z2, MAIN:, :]
+    for bit in range(2):
+
+        @pl.when(in_x == bit)
         def _():
-            acc_o[...] = o_term
-            acc_e[...] = e_term
-
-        @pl.when(t > 0)
+            for z in range(4):
+                (a_keep, a_send)[bit][0, z // 2, z % 2] = gu[z, 0:MAIN, :]
+
+        @pl.when(in_y == bit)
         def _():
-            acc_o[...] += o_term
-            acc_e[...] += e_term
-
-    gd[...] = (mm_tn(g_first, d0[...]) + mm_tn(g, d1[...])).astype(BF)
-    gu[...] = (mm_tn(du_first, h0[...]) + mm_tn(du, h1[...])).astype(BF)
-
-    @pl.when(t == 7)
+            for z in range(4):
+                (b_keep, b_send)[bit][z // 2, 0, z % 2] = gd[z, 0:MAIN, :]
+
+    @pl.when(t == pl.num_programs(0) - 1)
     def _():
-        o0[...] = acc_o0[...]
-        o1[...] = acc_o1[...].astype(BF)
-        e0[...] = acc_e0[...]
-        e1[...] = acc_e1[...].astype(BF)
-
-
-def mlp(h0, h1, d0, d1, ua, ub, da, db):
+        o0[...] = accs[0][...]
+        o1[...] = accs[1][...].astype(BF)
+        e0[...] = accs[2][...]
+        e1[...] = accs[3][...].astype(BF)
+
+
+def mlp(h0, h1, d0, d1, u0, u1, w0, w1):
     act = full((BLK, D))
-    tile = functools.partial(pl.BlockSpec, (HALF, D))
+    up0 = pl.BlockSpec((TILE, D), lambda t: (t // 2, 0))
+    up1 = pl.BlockSpec((TILE, D), lambda t: (t // 2, 0))
+    down = pl.BlockSpec((TILE // 2, D), lambda t: ((t % 2) * 2 + t // 2, 0))
+    tail = (MAIN, D)
+    a_keep = pl.BlockSpec((1, 2, 2) + tail, lambda t: (jnp.minimum(t, 1), 0, 0, 0, 0))
+    a_send = pl.BlockSpec((1, 2, 2) + tail, lambda t: (jnp.maximum(t - 2, 0), 0, 0, 0, 0))
+    b_keep = pl.BlockSpec((2, 1, 2) + tail, lambda t: (0, t // 2, 0, 0, 0))
+    b_send = pl.BlockSpec((2, 1, 2) + tail, lambda t: (0, t // 3, 0, 0, 0))
+    c_spec = pl.BlockSpec((1, 1, 2, 2 * REST, D), lambda t: (t // 2, t % 2, 0, 0, 0))
+    big_shape = jax.ShapeDtypeStruct((2, 2, 2, MAIN, D), BF)
+    rest_shape = jax.ShapeDtypeStruct((2, 2, 2, 2 * REST, D), BF)
     return pl.pallas_call(
         mlp_kernel,
-        grid=(8,),
-        in_specs=[act] * 4
+        grid=(4,),
+        in_specs=[act] * 4 + [up0, up1, down, down],
+        out_specs=[a_keep, a_send, b_keep, b_send, c_spec, c_spec] + [act] * 4,
+        scratch_shapes=[pltpu.VMEM((BLK, D), F32)] * 4,
+        out_shape=[big_shape] * 4
+        + [rest_shape] * 2
         + [
-            tile(lambda t: (jnp.minimum(t, 3), 0)),
-            tile(lambda t: (jnp.maximum(t - 4, 0), 0)),
-            tile(lambda t: (t // 2, 0)),
-            tile(lambda t: (t // 2, 0)),
-        ],
-        out_specs=[
-            tile(lambda t: (((t // 2) % 2) * 4 + (t // 4) * 2 + t % 2, 0)),
-            tile(lambda t: ((t // 4) * 4 + (t % 2) * 2 + (t // 2) % 2, 0)),
-            act,
-            act,
-            act,
-            act,
-        ],
-        out_shape=[
-            jax.ShapeDtypeStruct((8 * HALF, D), BF),
-            jax.ShapeDtypeStruct((8 * HALF, D), BF),
             jax.ShapeDtypeStruct((BLK, D), F32),
             jax.ShapeDtypeStruct((BLK, D), BF),
             jax.ShapeDtypeStruct((BLK, D), F32),
             jax.ShapeDtypeStruct((BLK, D), BF),
         ],
-        scratch_shapes=[pltpu.VMEM((BLK, D), F32)] * 4,
         name="mlp",
-        **params(flops=12 * D * D * 2 * D, moved=26 * 2**20, trans=4 * 2**20),
-    )(h0, h1, d0, d1, ua, ub, da, db)
-
-
-def proj_grad_kernel(me, xa, xb, sa, sb, pa, pb, ra, rb, out_a, out_b, out_c, tok, st):
+        **params(flops=12 * D * D * 2 * D, moved=26 * 2**20, vmem=VMEM_MLP),
+    )(h0, h1, d0, d1, u0, u1, w0, w1)
+
+
+def halves_kernel(*refs):
+    count = len(refs) // 4
+    for keep, got, out_keep, out_send in zip(
+        refs[:count], refs[count : 2 * count], refs[2 * count :: 2], refs[2 * count + 1 :: 2]
+    ):
+        out_keep[...] = (keep[0].astype(F32) + got[0].astype(F32)).astype(BF)
+        out_send[...] = (keep[1].astype(F32) + got[1].astype(F32)).astype(BF)
+
+
+def add_halves(keeps, gots):
+    shapes = [k.shape for k in keeps]
+    flat = [k.reshape(2, -1, k.shape[-1]) for k in keeps]
+    flat_got = [g.reshape(2, -1, g.shape[-1]) for g in gots]
+    steps = 4
+    while any((k.shape[1] // steps) % 16 or k.shape[1] % steps for k in flat):
+        steps //= 2
+    ins, outs, out_shapes = [], [], []
+    for k in flat:
+        rows, width = k.shape[1] // steps, k.shape[2]
+        ins.append(pl.BlockSpec((2, rows, width), lambda t: (0, t, 0)))
+        outs += [pl.BlockSpec((rows, width), lambda t: (t, 0))] * 2
+        out_shapes += [jax.ShapeDtypeStruct(k.shape[1:], BF)] * 2
+    done = pl.pallas_call(
+        halves_kernel,
+        grid=(steps,),
+        in_specs=ins * 2,
+        out_specs=outs,
+        out_shape=out_shapes,
+        name="halves",
+        **params(),
+    )(*flat, *flat_got)
+    done = [d.reshape(sh[1:]) for d, sh in zip(done, [s for s in shapes for _ in range(2)])]
+    return done[0::2], done[1::2]
+
+
+def eight_rows(values):
+    return jnp.sum(values.reshape(-1, 8, values.shape[-1]), axis=0)
+
+
+def mid_back_kernel(mid, gain, e_own, e_got, d_own, o_own, o_got, dmid, da, out, gsum):
+    rows = mid[...]
+    back, gain_rows = norm_back(rows, gain[...], e_own[...] + e_got[...].astype(F32))
+    total = d_own[...].astype(F32) + back
+    dmid[...] = total
+    da[...] = total.astype(BF)
+    out[...] = (rows + o_own[...] + o_got[...].astype(F32)).astype(BF)
+
+    @pl.when(pl.program_id(0) == 0)
+    def _():
+        gsum[...] = jnp.zeros_like(gsum)
+
+    gsum[...] += eight_rows(gain_rows)
+
+
+def mid_back(mid, gain, e_own, e_got, d_own, o_own, o_got):
+    row = pl.BlockSpec((DH, D), lambda t: (t, 0))
+    return pl.pallas_call(
+        mid_back_kernel,
+        grid=(BLK // DH,),
+        in_specs=[row, full((1, D))] + [row] * 5,
+        out_specs=[row, row, row, full((8, D))],
+        out_shape=[
+            jax.ShapeDtypeStruct((BLK, D), F32),
+            jax.ShapeDtypeStruct((BLK, D), BF),
+            jax.ShapeDtypeStruct((BLK, D), BF),
+            jax.ShapeDtypeStruct((8, D), F32),
+        ],
+        name="mid_back",
+        **params(vmem=VMEM_GRADS),
+    )(mid, gain, e_own, e_got, d_own, o_own, o_got)
+
+
+def out_back_kernel(me, own, oth, wo, ot0, ot1, dot_all, grad):
+    first = me[0] == 0
+    da0 = jnp.where(first, own[...], oth[...])
+    da1 = jnp.where(first, oth[...], own[...])
+    dot_all[0:BLK, :] = mm_nt(da0, wo[...]).astype(BF)
+    dot_all[BLK:, :] = mm_nt(da1, wo[...]).astype(BF)
+    grad[...] = (mm_tn(ot0[...], da0) + mm_tn(ot1[...], da1)).astype(BF)
+
+
+def out_back(me, own, oth, wo, ot0, ot1):
+    return pl.pallas_call(
+        out_back_kernel,
+        grid_spec=pltpu.PrefetchScalarGridSpec(
+            num_scalar_prefetch=1,
+            grid=(1,),
+            in_specs=[full((BLK, D))] * 2 + [full((KEEP, D))] + [full((BLK, KEEP))] * 2,
+            out_specs=[full((2 * BLK, KEEP)), full((KEEP, D))],
+        ),
+        out_shape=[
+            jax.ShapeDtypeStruct((2 * BLK, KEEP), BF),
+            jax.ShapeDtypeStruct((KEEP, D), BF),
+        ],
+        name="out_back",
+        **params(vmem=VMEM_GRADS),
+    )(me, own, oth, wo, ot0, ot1)
+
+
+def proj_back_kernel(me, a, b, w, own, oth):
+    first = me[0] == 0
+    own[...] = mm_nt(jnp.where(first, a[...], b[...]), w[...])
+    oth[...] = mm_nt(jnp.where(first, b[...], a[...]), w[...]).astype(BF)
+
+
+def proj_both_kernel(me, a, b, w, own, oth):
+    term = mm_nt(a[...], w[...])
+    own[...] = term
+    oth[...] = term.astype(BF)
+
+
+def proj_back(me, a, b, w):
+    kernel = proj_both_kernel if b is None else proj_back_kernel
+    rows = a.shape[0] // 2 if b is a else a.shape[0]
+    side = 1 if b is a else 0
+    return pl.pallas_call(
+        kernel,
+        grid_spec=pltpu.PrefetchScalarGridSpec(
+            num_scalar_prefetch=1,
+            grid=(4,),
+            in_specs=[
+                pl.BlockSpec((rows, 3 * KEEP), lambda t, me: (0, 0)),
+                pl.BlockSpec((rows, 3 * KEEP), lambda t, me: (side, 0)),
+                pl.BlockSpec((D // 4, 3 * KEEP), lambda t, me: (t, 0)),
+            ],
+            out_specs=[pl.BlockSpec((rows, D // 4), lambda t, me: (0, t))] * 2,
+        ),
+        out_shape=[
+            jax.ShapeDtypeStruct((rows, D), F32),
+            jax.ShapeDtypeStruct((rows, D), BF),
+        ],
+        name="proj_back",
+        **params(),
+    )(me, a, a if b is None else b, w)
+
+
+def state_back_kernel(me, *refs):
+    state1, gain, own, got, ds2, gate, wu, os0, os1, dz1, zz1, state0, zz0 = refs[:13]
+    ds1, dos0, grad_wu, gate_sum, acc = refs[13:]
+    t = pl.program_id(0)
+    last = ds2[...]
+    back = norm_back(state1[...], gain[...], own[...] + got[...].astype(F32))[0]
+    total = gate[...] * last + back
+    ds1[...] = total
+    dz0 = ((1.0 - gate[...]) * total).astype(BF)
+    dos0[...] = mm_nt(dz0, wu[...]).astype(BF)
+
+    @pl.when(t == 0)
+    def _():
+        acc[...] = jnp.zeros_like(acc)
+        gate_sum[...] = jnp.zeros_like(gate_sum)
+
+    acc[...] += mm_tn(os0[...], dz0) + mm_tn(os1[...], dz1[...])
+
+    @pl.when(t // 2 == me[0])
+    def _():
+        terms = last * (state1[...] - zz1[...]) + total * (state0[...] - zz0[...])
+        gate_sum[...] += eight_rows(terms)
+
+    @pl.when(t == 3)
+    def _():
+        grad_wu[...] = acc[...].astype(BF)
+
+
+def state_back(me, state1, gain, own, got, ds2, gate, wu, os0, os1, dz1, zz1, state0, zz0):
+    row = pl.BlockSpec((DH, D), lambda t, me: (t, 0))
+    head = pl.BlockSpec((DH, KEEP), lambda t, me: (t, 0))
+    half = pl.BlockSpec((DH, D), lambda t, me: (t % 2, 0))
+    line = full((1, D))
+    return pl.pallas_call(
+        state_back_kernel,
+        grid_spec=pltpu.PrefetchScalarGridSpec(
+            num_scalar_prefetch=1,
+            grid=(4,),
+            in_specs=[row, line, row, row, row, line, full((KEEP, D)), head, head, row, half]
+            + [row, row],
+            out_specs=[row, head, full((KEEP, D)), full((8, D))],
+            scratch_shapes=[pltpu.VMEM((KEEP, D), F32)],
+        ),
+        out_shape=[
+            jax.ShapeDtypeStruct((BLK, D), F32),
+            jax.ShapeDtypeStruct((BLK, KEEP), BF),
+            jax.ShapeDtypeStruct((KEEP, D), BF),
+            jax.ShapeDtypeStruct((8, D), F32),
+        ],
+        name="state_back",
+        **params(vmem=VMEM_GRADS),
+    )(me, state1, gain, own, got, ds2, gate, wu, os0, os1, dz1, zz1, state0, zz0)
+
+
+def row_back_kernel(me, values, gain, own, got, scale, base, out):
+    back = norm_back(values[...].astype(F32), gain[...], own[...] + got[...].astype(F32))[0]
+    out[...] = (scale[...] * base[...] + back).astype(BF)
+
+
+def row_back(me, values, gain, own, got, scale, base):
+    count = own.shape[0] // DH
+    skip = values.shape[0] // DH - count
+    row = pl.BlockSpec((DH, D), lambda t, me: (t, 0))
+    mine = pl.BlockSpec((DH, D), lambda t, me: (me[0] * skip + t, 0))
+    return pl.pallas_call(
+        row_back_kernel,
+        grid_spec=pltpu.PrefetchScalarGridSpec(
+            num_scalar_prefetch=1,
+            grid=(count,),
+            in_specs=[mine, full((1, D)), row, row, full((1, D)), mine],
+            out_specs=row,
+        ),
+        out_shape=jax.ShapeDtypeStruct(own.shape, BF),
+        name="row_back",
+        **params(vmem=VMEM_GRADS),
+    )(me, values, gain, own, got, scale, base)
+
+
+def proj_grad_kernel(me, *refs):
+    xa, xb, sa, sb, pa, pb, ra, rb, small = refs[:9]
+    a_keep, a_send, b_keep, b_send, c_keep, c_send, tok, st = refs[9:]
     x0, y0 = me[1], me[3]
+    in_z = lax.rem(pl.program_id(0), 2)
     tok[...] = mm_tn(xa[...], pa[...]) + mm_tn(xb[...], pb[...])
     st[...] = mm_tn(sa[...], ra[...]) + mm_tn(sb[...], rb[...])
+
+    def write(ref, xr, yr, sub):
+        rows = pl.ds(pl.multiple_of((x0 ^ xr) * DH, DH), DH)
+        cols = pl.ds(pl.multiple_of((y0 ^ yr) * 768 + sub * 256, 256), 256)
+        ref[0:DH, :] = tok[rows, cols].astype(BF)
+        ref[DH : 2 * DH, :] = st[rows, cols].astype(BF)
+
     for xr in range(2):
-        rows = pl.ds(pl.multiple_of((x0 ^ xr) * DH, DH), DH)
         for yr in range(2):
-            dests = (out_a.at[xr, yr, 0, 0], out_b.at[yr, 0, xr, 0], out_c.at[0, xr, yr, 0])
-            for sub, ref in enumerate(dests):
-                cols = pl.ds(pl.multiple_of((y0 ^ yr) * 768 + sub * 256, 256), 256)
-                ref[0:DH, :] = tok[rows, cols].astype(BF)
-                ref[DH : 2 * DH, :] = st[rows, cols].astype(BF)
-
-
-def proj_grads(me, xn, sn0, sn1, dp0, dp1, dr0, dr1):
+            write((a_keep, a_send)[xr].at[yr, 0, 0], xr, yr, 0)
+            (a_keep, a_send)[xr][yr, 0, 0, 2 * DH :, :] = small[x0 ^ xr, y0 ^ yr]
+            write((b_keep, b_send)[yr].at[0, xr, 0], xr, yr, 1)
+    for zb in range(2):
+
+        @pl.when(in_z == zb)
+        def _():
+            for xr in range(2):
+                for yr in range(2):
+                    write((c_keep, c_send)[zb].at[xr, yr, 0], xr, yr, 2)
+
+
+def proj_grads(me, xn, sn0, sn1, dp0, dp1, dr0, dr1, small):
     lhs = pl.BlockSpec((BLK, 2 * DH), lambda q, me: (0, q ^ me[2]))
     lhs1 = pl.BlockSpec((BLK, 2 * DH), lambda q, me: (1, q ^ me[2]))
     rhs = full((BLK, 3 * KEEP))
-    shape = jax.ShapeDtypeStruct((2, 2, 2, 2, 2 * DH, 2 * DH), BF)
+    shape = jax.ShapeDtypeStruct((2, 2, 2, 2 * DH, 2 * DH), BF)
+    tall = jax.ShapeDtypeStruct((2, 2, 2, 2 * DH + 16, 2 * DH), BF)
     tail = (2 * DH, 2 * DH)
+    a_tail = (2 * DH + 16, 2 * DH)
+    a_spec = pl.BlockSpec((2, 1, 1) + a_tail, lambda q, me: (0, q % 2, q // 2, 0, 0))
+    small_spec = pl.BlockSpec((2, 2, 16, 256), lambda q, me: (q ^ me[2], 0, 0, 0))
+    b_spec = pl.BlockSpec((1, 2, 1) + tail, lambda q, me: (q % 2, 0, q // 2, 0, 0))
+    c_spec = pl.BlockSpec((2, 2, 1) + tail, lambda q, me: (0, 0, q // 2, 0, 0))
     return pl.pallas_call(
         proj_grad_kernel,
         grid_spec=pltpu.PrefetchScalarGridSpec(
             num_scalar_prefetch=1,
             grid=(4,),
-            in_specs=[lhs, lhs1, lhs, lhs, rhs, rhs, rhs, rhs],
-            out_specs=[
-                pl.BlockSpec((2, 2, 1, 1) + tail, lambda q, me: (0, 0, q % 2, q // 2, 0, 0)),
-                pl.BlockSpec((2, 1, 2, 1) + tail, lambda q, me: (0, q % 2, 0, q // 2, 0, 0)),
-                pl.BlockSpec((1, 2, 2, 1) + tail, lambda q, me: (q % 2, 0, 0, q // 2, 0, 0)),
-            ],
+            in_specs=[lhs, lhs1, lhs, lhs, rhs, rhs, rhs, rhs, small_spec],
+            out_specs=[a_spec, a_spec, b_spec, b_spec, c_spec, c_spec],
             scratch_shapes=[pltpu.VMEM((2 * DH, 3 * KEEP), F32)] * 2,
         ),
-        out_shape=[shape] * 3,
+        out_shape=[tall] * 2 + [shape] * 4,
         name="proj_grad",
-        **params(flops=4 * D * D * 3 * KEEP, moved=16 * 2**20),
-    )(me, xn, xn, sn0, sn1, dp0, dp1, dr0, dr1)
-
-
-def place_proj_kernel(me, p00, p01, p10, p11, tok, st):
+        **params(flops=4 * D * D * 3 * KEEP, moved=16 * 2**20, vmem=VMEM_GRADS),
+    )(me, xn, xn, sn0, sn1, dp0, dp1, dr0, dr1, small)
+
+
+def place_proj_kernel(me, p0, p1, w_tok, w_state, tok, st, gain_tok, gain_st, small):
     c0, y0 = me[0], me[3]
+    starts = (0, 2 * DH + 16, 4 * DH + 16)
     for cr in range(2):
         for yr in range(2):
-            src = ((p00, p01), (p10, p11))[cr][yr]
+            src = (p0, p1)[cr].at[yr]
             for sub in range(3):
                 for i in range(2):
                     j = 6 * (y0 ^ yr) + 2 * sub + i
                     at = (j // HL) * D + (2 * (j % HL) + (c0 ^ cr)) * DH
                     dst = pl.ds(pl.multiple_of(at, DH), DH)
                     cols = slice(i * DH, (i + 1) * DH)
-                    tok[:, dst] = src[sub, 0:DH, cols].astype(F32)
-                    st[:, dst] = src[sub, DH : 2 * DH, cols].astype(F32)
-
-
-def place_proj(me, p00, p01, p10, p11):
+                    row = starts[sub]
+                    tok[:, dst] = src[row : row + DH, cols].astype(F32)
+                    st[:, dst] = src[row + DH : row + 2 * DH, cols].astype(F32)
+    for yr in range(2):
+        first = p0[yr, 2 * DH : 2 * DH + 16, :].astype(F32)
+        small[y0 ^ yr] = first + p1[yr, 2 * DH : 2 * DH + 16, :].astype(F32)
+    ones = jnp.ones((8, 3 * D), F32)
+    for out, grad, weight in ((gain_tok, tok, w_tok), (gain_st, st, w_state)):
+        out[...] = lax.dot_general(
+            ones,
+            grad[...] * weight[...].astype(F32),
+            (((1,), (1,)), ((), ())),
+            precision=lax.Precision.HIGHEST,
+            preferred_element_type=F32,
+        )
+
+
+def place_proj(me, p0, p1, w_tok, w_state):
     one = jax.ShapeDtypeStruct((DH, 3 * D), F32)
+    line = jax.ShapeDtypeStruct((8, DH), F32)
     return pl.pallas_call(
         place_proj_kernel,
         grid_spec=pltpu.PrefetchScalarGridSpec(
             num_scalar_prefetch=1,
             grid=(1,),
-            in_specs=[full(p00.shape)] * 4,
-            out_specs=[full((DH, 3 * D))] * 2,
+            in_specs=[full(p0.shape)] * 2 + [full(w_tok.shape)] * 2,
+            out_specs=[full((DH, 3 * D))] * 2 + [full((8, DH))] * 2 + [full((2, 16, 256))],
         ),
-        out_shape=[one, one],
+        out_shape=[one, one, line, line, jax.ShapeDtypeStruct((2, 16, 256), F32)],
         name="place_proj",
         **params(moved=5 * 2**20),
-    )(me, p00, p01, p10, p11)
-
-
-def place_mlp_kernel(me, p00, p01, p10, p11, up, down):
+    )(me, p0, p1, w_tok, w_state)
+
+
+def place_mlp_kernel(me, p0, p1, up, down):
     c0, y0 = me[0], me[3]
-    n = p00.shape[1]
     for cr in range(2):
         for yr in range(2):
-            src = ((p00, p01), (p10, p11))[cr][yr]
-            rows = pl.ds(pl.multiple_of(((c0 ^ cr) * 2 + (y0 ^ yr)) * n, n), n)
-            up[rows, :] = src[0].astype(F32)
-            down[rows, :] = src[1].astype(F32)
-
-
-def place_mlp(me, p00, p01, p10, p11):
-    one = jax.ShapeDtypeStruct((4 * p00.shape[1], D), F32)
+            src = (p0, p1)[cr].at[yr]
+            row = ((c0 ^ cr) * 2 + (y0 ^ yr)) * DH
+            big = pl.ds(pl.multiple_of(row, DH), MAIN)
+            rest = pl.ds(pl.multiple_of(row + MAIN, REST), REST)
+            up[big, :] = src[0:MAIN].astype(F32)
+            down[big, :] = src[MAIN : 2 * MAIN].astype(F32)
+            up[rest, :] = src[2 * MAIN : 2 * MAIN + REST].astype(F32)
+            down[rest, :] = src[2 * MAIN + REST :].astype(F32)
+
+
+def place_mlp(me, p0, p1):
+    one = jax.ShapeDtypeStruct((2 * p0.shape[1], D), F32)
     return pl.pallas_call(
         place_mlp_kernel,
         grid_spec=pltpu.PrefetchScalarGridSpec(
             num_scalar_prefetch=1,
             grid=(1,),
-            in_specs=[full(p00.shape)] * 4,
+            in_specs=[full(p0.shape)] * 2,
             out_specs=[full(one.shape)] * 2,
         ),
         out_shape=[one, one],
         name="place_mlp",
         **params(moved=6 * 2**20),
-    )(me, p00, p01, p10, p11)
+    )(me, p0, p1)
 
 
 def body(
@@ -804,15 +1064,15 @@
     c = lax.axis_index("c")
     x = lax.axis_index("x")
     z = lax.axis_index("s")
-    y = lax.axis_index("g") % 2
+    y = lax.axis_index("y")
     z1, z2 = z % 2, z // 2
     me = jnp.stack([c, x, z, y]).astype(jnp.int32)
     on_diag = c == x
     slots = state_in.shape[0]
     srows = state_in.shape[1]
 
-    def cross(value):
-        return jnp.where(on_diag, value, diag_send(value))
+    def pick(value, got):
+        return jnp.where(on_diag, value, got)
 
     def by_block(own, other):
         return jnp.where(c == 0, jnp.concatenate([own, other]), jnp.concatenate([other, own]))
@@ -823,160 +1083,202 @@
     def other_half(rows):
         return lax.dynamic_slice_in_dim(rows, (1 - c) * HALF, HALF, 0)
 
-    def slot_rows(value):
-        held = cross(value)
-        parts = [lax.dynamic_index_in_dim(held, z, 0, keepdims=False)]
-        for k in range(1, slots):
-            send = lax.dynamic_index_in_dim(held, z ^ k, 0, keepdims=False)
-            parts.append(lax.ppermute(send, "s", [(i, i ^ k) for i in range(slots)]))
-        half = jnp.concatenate(parts)
-        return by_block(half, xch(half, "c"))
-
-    def owner_rows(half):
-        parts = half.reshape(slots, srows, D)
-        got = [parts[0]]
-        for k in range(1, slots):
-            got.append(lax.ppermute(parts[k], "s", [(i, i ^ k) for i in range(slots)]))
-        stacked = jnp.stack(got).reshape(2, 2, srows, D)
-        stacked = untwist(stacked, (z2, z1)).reshape(slots, srows, D)
-        return cross(stacked).astype(F32)
+    def to_slot(value, k):
+        return lax.ppermute(value, "s", [(i, i ^ k) for i in range(slots)])
+
+    def slot(value, k):
+        return lax.dynamic_index_in_dim(value, z ^ k, 0, keepdims=False)
+
+    def slot_order(parts):
+        stacked = jnp.stack(parts).reshape(2, 2, srows, D)
+        return untwist(stacked, (z2, z1)).reshape(slots, srows, D)
+
+    def half_sum(part, got):
+        return (part.astype(F32) + got.astype(F32)).astype(BF)
+
+    def slot_spread(value):
+        return [value[0]] + [to_slot(value[k], k) for k in range(1, slots)]
 
     subs = pick_columns(me, w_tok, w_state)
     small = jnp.stack([gain_tok, gain_state, gain_mlp, gate_bias])
     small = jnp.concatenate([small, jnp.pad(rel_bias, ((0, 0), (0, DH - NB)))])
     small = jnp.pad(small, ((0, 11), (0, DH)))
-    x_own = cross(tokens)
-    x_oth = xch(x_own, "c")
-    tab_a = gather_bits(jnp.concatenate([subs[0], small]), ("z2", "z1", "y", "x"))
-    tab_b = gather_bits(subs[1], ("z2", "x", "z1", "y"))
-    tab_c = gather_bits(subs[2], ("z2", "y", "x", "z1"))
-    state0 = slot_rows(state_in).astype(F32)
-    w_tok_l, w_state_l, small_all = lay_tables(me, tab_a, tab_b, tab_c)
-
+    ha, hb, hc = jnp.concatenate([subs[0], small]), subs[1], subs[2]
+    got = [xch(hc, "z2"), xch(hb, "z2"), xch(ha, "z2"), diag_send(state_in), diag_send(tokens)]
     quarter = DH // 4
     at = (c * 2 + y) * quarter
-    out_piece = cross(
-        jnp.concatenate(
-            [
-                lax.dynamic_slice_in_dim(w_out, at, quarter, 0),
-                lax.dynamic_slice_in_dim(w_update, at, quarter, 0),
-            ]
-        )
-    )
-    out_low, out_high = gather_bits(out_piece, ("z2", "z1", "y", "x"))
-    wo, wu = lay_out_tables(me, out_low, out_high)
+    ho = jnp.concatenate(
+        [
+            lax.dynamic_slice_in_dim(w_out, at, quarter, 0),
+            lax.dynamic_slice_in_dim(w_update, at, quarter, 0),
+        ]
+    )
+
+    gc, gb, ga, g_states, g_tokens, ho = fence(got + [ho], got[:4])
+    ha, hb, hc = jnp.stack([ha, ga]), jnp.stack([hb, gb]), jnp.stack([hc, gc])
+    got = [xch(ha, "z1"), xch(hb, "x"), xch(hc, "y")]
+    states = pick(state_in, g_states)
+    half = [slot(states, 0), to_slot(slot(states, 2), 2)]
+    g_piece = diag_send(ho)
+
+    ga, gb, gc, half, g_piece, g_tokens = fence(
+        got + [half, g_piece, g_tokens], got + [half, g_piece, g_tokens]
+    )
+    ha, hb, hc = jnp.stack([ha, ga]), jnp.stack([hb, gb]), jnp.stack([hc, gc])
+    got = [xch(ha, "y"), xch(hb, "z1"), xch(hc, "x")]
+    half = half + [to_slot(slot(states, 3), 3)]
+    x_own = pick(tokens, g_tokens)
+    x_oth = xch(x_own, "c")
+    ho = pick(ho, g_piece)
+
+    ga, gb, gc, half, ho, x_own, x_oth = fence(
+        got + [half, ho, x_own, x_oth], got + [half, x_oth]
+    )
+    half = half[:1] + [to_slot(slot(states, 1), 1)] + half[1:]
+    ha, hb, hc = jnp.stack([ha, ga]), jnp.stack([hb, gb]), jnp.stack([hc, gc])
+    got = [xch(ha, "x"), xch(hb, "y"), xch(hc, "z1")]
+    half = jnp.concatenate(half)
+    state0 = by_block(half, xch(half, "c")).astype(F32)
+    rows = by_block(x_own, x_oth).astype(F32)
+    x_hat = norm_parts(rows)[0]
+    s_hat = norm_parts(state0)[0]
+    go = xch(ho, "z2")
+
     hid = w_up.shape[0] // 4
     hid_at = (c * 2 + y) * hid
-    up_a, up_b = gather_bits(
-        lax.dynamic_slice_in_dim(w_up, hid_at, hid, 0), ("z2", "z1", "x", "y")
-    )
-    down_a, down_b = gather_bits(
-        lax.dynamic_slice_in_dim(w_down, hid_at, hid, 0), ("z2", "x", "y", "z1")
-    )
-    d_own = cross(d_out)
-    d_oth = xch(d_own, "c")
-    ds2 = slot_rows(d_state_next).astype(F32)
-
+    hu = lax.dynamic_slice_in_dim(w_up, hid_at, hid, 0)
+    hd = lax.dynamic_slice_in_dim(w_down, hid_at, hid, 0)
+    got, go, hu, hd, x_hat, s_hat, d_out, d_state_next = fence(
+        (got, go, hu, hd, x_hat, s_hat, d_out, d_state_next), (got, x_hat, s_hat)
+    )
+    ho = jnp.stack([ho, go])
+    go = xch(ho, "z1")
+    gm = [xch(hu, "z2"), xch(hd, "z2")]
+    g_states = diag_send(d_state_next)
+    w_tok_l, w_state_l, small_all = lay_tables(me, (ha, got[0]), (hb, got[1]), (hc, got[2]))
     vectors = small_all[:, :4, :DH].transpose(1, 0, 2).reshape(4, D).astype(F32)
     g_tok, g_state, g_mlp = vectors[0], vectors[1], vectors[2]
     gate = jax.nn.sigmoid(vectors[3])
+    xn = (x_hat * g_tok).astype(BF)
+    proj = mm(xn, w_tok_l).astype(BF)
+
+    go, gm, g_states, proj, small_all = fence(
+        (go, gm, g_states, proj, small_all), (go, g_states, proj)
+    )
+    ho = jnp.stack([ho, go])
+    go = xch(ho, "x")
+    d_states = pick(d_state_next, g_states)
+    sn0 = (s_hat * g_state).astype(BF)
+    r0 = mm(sn0, w_state_l).astype(BF)
     rel_rows = small_all[:, 4, :NB].reshape(HL, 2, NB)
     rel_mine = lax.dynamic_index_in_dim(rel_rows, c, 1, keepdims=False)
     hot = jnp.asarray(slab_buckets())[None, :] == jnp.arange(NB, dtype=jnp.int32)[:, None]
     base = mm(rel_mine, hot.astype(BF)).reshape(HL, 8, BLK)
     bias = bias_tables(base)
 
-    rows = by_block(x_own, x_oth).astype(F32)
-    xn = (norm_parts(rows)[0] * g_tok).astype(BF)
-    proj = mm(xn, w_tok_l).astype(BF)
-
-    sn0 = (norm_parts(state0)[0] * g_state).astype(BF)
-    r0 = mm(sn0, w_state_l).astype(BF)
+    go, gm, r0, bias, d_states = fence((go, gm, r0, bias, d_states), (go, gm, r0, bias))
+    ho = jnp.stack([ho, go])
+    go = xch(ho, "y")
+    hu, hd = jnp.stack([hu, gm[0]]), jnp.stack([hd, gm[1]])
+    gm = [xch(hu, "z1"), xch(hd, "x")]
     os0, log_s0 = mem_forward(0, proj, r0)
+    ot0, log_t0 = tok_forward(0, proj, r0, bias)
+
+    go, gm, os0, ot0, d_states = fence((go, gm, os0, ot0, d_states), (go, gm, os0, ot0))
+    wo, wu = lay_out_tables(me, ho, go)
+    hu, hd = jnp.stack([hu, gm[0]]), jnp.stack([hd, gm[1]])
+    gm = [xch(hu, "x"), xch(hd, "y")]
+    d_half = [slot(d_states, 0)] + [to_slot(slot(d_states, k), k) for k in range(1, slots)]
     zp0 = mm(os0, wu)
     zz0 = zp0 + xch(zp0.astype(BF), "c").astype(F32)
     state1 = gate * state0 + (1.0 - gate) * zz0
     sn1 = (norm_parts(state1)[0] * g_state).astype(BF)
     r1 = mm(sn1, w_state_l).astype(BF)
-
-    ot0, log_t0 = tok_forward(0, proj, r0, bias)
     ot1, log_t1 = tok_forward(1, proj, r1, bias)
+
+    gm, ot1, r1, d_out, d_half = fence((gm, ot1, r1, d_out, d_half), (gm, ot1, d_half))
+    hu, hd = jnp.stack([hu, gm[0]]), jnp.stack([hd, gm[1]])
+    gm = [xch(hu, "y"), xch(hd, "z1")]
+    d_half = jnp.concatenate(d_half)
+    ds2 = by_block(d_half, xch(d_half, "c")).astype(F32)
+    d_own = pick(d_out, diag_send(d_out))
+    d_oth = xch(d_own, "c")
     part0, part1 = mm(ot0, wo), mm(ot1, wo)
     part_own = jnp.where(c == 0, part0, part1)
     part_oth = jnp.where(c == 0, part1, part0).astype(BF)
     mid = x_own.astype(F32) + part_own + xch(part_oth, "c").astype(F32)
     h_own = (norm_parts(mid)[0] * g_mlp).astype(BF)
     h_oth = xch(h_own, "c")
-
     os1, log_s1 = mem_forward(1, proj, r1)
     zp1 = mm(os1, wu)
     zz1 = my_half(zp1) + xch(other_half(zp1).astype(BF), "c").astype(F32)
     state1_half = my_half(state1)
-    state2_half = gate * state1_half + (1.0 - gate) * zz1
-    state_next = owner_rows(state2_half.astype(BF))
-
+    state2_half = (gate * state1_half + (1.0 - gate) * zz1).astype(BF)
     dz1 = ((1.0 - gate) * ds2).astype(BF)
     dos1 = mm_nt(dz1, wu).astype(BF)
     dm1, dt1 = mem_backward(1, proj, r1, dos1, log_s1)
 
-    gu, gd, o_own, o_oth, e_own, e_oth = mlp(
+    gm, h_own, h_oth, d_own, d_oth, state2_half = fence(
+        (gm, h_own, h_oth, d_own, d_oth, state2_half),
+        (gm, h_own, h_oth, d_own, d_oth, state2_half, dm1),
+    )
+    out_rows = slot_spread(state2_half.reshape(slots, srows, D))
+    ma, ma_out, mb, mb_out, mc, mc_out, o_own, o_oth, e_own, e_oth = mlp(
         h_own,
         h_oth,
         d_own,
         d_oth,
-        up_a.reshape(-1, D),
-        up_b.reshape(-1, D),
-        down_a.reshape(-1, D),
-        down_b.reshape(-1, D),
-    )
-    output = mid + o_own + xch(o_oth, "c").astype(F32)
-    output = cross(output.astype(BF))
-    gu = gu.reshape(2, 2, 2, 2, hid, D)
-    gd = gd.reshape(2, 2, 2, 2, hid, D)
-    gu = reduce_bits(gu, ("x", "y", "z1", "z2"))
-    gd = reduce_bits(gd, ("y", "z1", "x", "z2"))
-
-    dh = e_own + xch(e_oth, "c").astype(F32)
-    back, gain_rows = norm_back(mid, g_mlp, dh)
+        hu.reshape(-1, D),
+        gm[0].reshape(-1, D),
+        hd.reshape(-1, D),
+        gm[1].reshape(-1, D),
+    )
+
+    out_rows, ma_out, mb_out, mc_out, o_oth, e_oth = fence(
+        (out_rows, ma_out, mb_out, mc_out, o_oth, e_oth), (out_rows, o_oth, e_oth)
+    )
+    got = [xch(ma_out, "x"), xch(mb_out, "y"), xch(mc_out, "z1")]
+    state_next = slot_order(out_rows)
+    e_got, o_got = xch(e_oth, "c"), xch(o_oth, "c")
+    dmid, da_own, output, gain_rows = mid_back(
+        mid, g_mlp[None], e_own, e_got, d_own, o_own, o_got
+    )
+    dot_all, grad_wo = out_back(me, da_own, xch(da_own, "c"), wo, ot0, ot1)
+    dr1, dp1, dprev, rel1 = tok_backward(1, proj, r1, bias, dot_all, log_t1, dt1, dm1)
+
+    got, dr1, dprev, output, state_next = fence(
+        (got, dr1, dprev, output, state_next), (got, dr1, dprev, output)
+    )
+    (ma, mb, mc), sends = add_halves((ma, mb, mc), got)
+    got = [xch(s, b) for s, b in zip(sends, ("y", "z1", "x"))]
+    got += [diag_send(output), diag_send(state_next)]
+    dsn1, dsn1_send = proj_back(me, dr1, None, w_state_l)
+    dsn1_got = xch(dsn1_send, "c")
+    dm0, dt0, rel0 = tok_backward(0, proj, r0, bias, dot_all, log_t0, dprev)
+
+    got, dm0, dt0, dsn1, dsn1_got = fence((got, dm0, dt0, dsn1, dsn1_got), (got, dm0, dsn1_got))
+    output = pick(output, got[3])
+    state_next = pick(state_next, got[4]).astype(F32)
+    (ma, mb, mc), sends = add_halves((ma, mb, mc), got[:3])
+    got = [xch(s, b) for s, b in zip(sends, ("z1", "x", "y"))]
+    ds1, dos0, grad_wu, gate_rows = state_back(
+        me,
+        state1,
+        g_state[None],
+        dsn1,
+        dsn1_got,
+        ds2,
+        gate[None],
+        wu,
+        os0,
+        os1,
+        dz1,
+        zz1,
+        state0,
+        zz0,
+    )
+    grad_gate = jnp.sum(gate_rows, axis=0) * gate * (1.0 - gate)
     grad_g_mlp = jnp.sum(gain_rows, axis=0)
-    dmid = d_own.astype(F32) + back
-    da_own = dmid.astype(BF)
-    da = by_block(da_own, xch(da_own, "c"))
-    dot_all = mm_nt(da, wo).astype(BF)
-    grad_wo = mm_tn(ot0, da[:BLK]) + mm_tn(ot1, da[BLK:])
-
-    dr1, dp1, dprev, rel1 = tok_backward(1, proj, r1, bias, dot_all, log_t1, dt1, dm1)
-    dsn1p = mm_nt(dr1, w_state_l)
-    dsn1 = dsn1p + xch(dsn1p.astype(BF), "c").astype(F32)
-    back1, gain1 = norm_back(state1, g_state, dsn1)
-    ds1 = gate * ds2 + back1
-    dz0 = ((1.0 - gate) * ds1).astype(BF)
-    dos0 = mm_nt(dz0, wu).astype(BF)
-    dm0, dt0, rel0 = tok_backward(0, proj, r0, bias, dot_all, log_t0, dprev)
-    dr0, dp0 = mem_backward(0, proj, r0, dos0, log_s0, dm0, dt0)
-
-    subs = proj_grads(me, xn, sn0, sn1, dp0, dp1, dr0, dr1)
-    ga = reduce_bits(subs[0], ("x", "y", "z1", "z2"))
-    gb = reduce_bits(subs[1], ("y", "z1", "x", "z2"))
-    gc = reduce_bits(subs[2], ("z1", "x", "y", "z2"))
-    grad_wu = mm_tn(os0, dz0) + mm_tn(os1, dz1)
-
-    dsn0p = mm_nt(dr0, w_state_l)
-    dsn0 = my_half(dsn0p) + xch(other_half(dsn0p).astype(BF), "c").astype(F32)
-    back0, gain0 = norm_back(my_half(state0), g_state, dsn0)
-    grad_state = owner_rows((gate * my_half(ds1) + back0).astype(BF))
-    grad_g_state = jnp.sum(my_half(gain1) + gain0, axis=0)
-    gate_rows = my_half(ds2) * (state1_half - zz1) + my_half(ds1) * my_half(state0 - zz0)
-    grad_gate = jnp.sum(gate_rows, axis=0) * gate * (1.0 - gate)
-
-    dxn0, dxn1 = mm_nt(dp0, w_tok_l), mm_nt(dp1, w_tok_l)
-    dxn_own = jnp.where(c == 0, dxn0, dxn1)
-    dxn_oth = jnp.where(c == 0, dxn1, dxn0).astype(BF)
-    dxn = dxn_own + xch(dxn_oth, "c").astype(F32)
-    back_x, gain_x = norm_back(x_own.astype(F32), g_tok, dxn)
-    grad_g_tok = jnp.sum(gain_x, axis=0)
-    grad_tokens = cross((dmid + back_x).astype(BF)).astype(F32)
-
     rel_sum = (rel0 + rel1).reshape(HL, 8 * BLK)
     grad_rel = lax.dot_general(
         rel_sum,
@@ -986,52 +1288,119 @@
         preferred_element_type=F32,
     )
     both = jnp.stack([grad_rel, jnp.zeros_like(grad_rel)], axis=1)
-    both = jnp.where(c == 0, both, jnp.flip(both, 1)).reshape(1, H * NB)
-    vec = jnp.stack([grad_g_tok, grad_g_state, grad_g_mlp, grad_gate])
-    vec = jnp.concatenate([vec, jnp.pad(both, ((0, 3), (0, D - H * NB)))])
-    for bit in ("c", "x", "y", "z1", "z2"):
-        vec = vec + xch(vec, bit)
-    vec = over_groups(vec)
-    spot = z * 2 + x
-    own = lax.dynamic_slice_in_dim(vec[:4], spot * DH, DH, 1)
-    rel_own = lax.dynamic_slice_in_dim(vec[4:5], spot * NB, NB, 1)
-
+    both = jnp.where(c == 0, both, jnp.flip(both, 1)).reshape(H, NB)
+    first = jnp.concatenate([grad_g_mlp.reshape(H, DH), jnp.pad(both, ((0, 0), (0, DH - NB)))], 1)
+    second = jnp.pad(grad_gate.reshape(H, DH), ((0, 0), (0, DH)))
+    small_sums = jnp.stack([first, second], axis=1)[:, :, None, :].astype(BF)
+    small_sums = jnp.pad(small_sums, ((0, 0), (0, 0), (0, 15), (0, 0)))
     outs = jnp.stack([grad_wo, grad_wu]).astype(BF).reshape(2, 2, 2, 2, 2, quarter, D)
+
+    got, dos0, outs = fence((got, dos0, outs), (got, dos0, outs))
+    (ma, mb, mc), sends = add_halves((ma, mb, mc), got)
+    got_m = [xch(s, "z2") for s in sends]
+    names = ["z2", "z1", "x", "y"]
     spots = {"z2": z2, "z1": z1, "x": x, "y": y}
-    names = ["z2", "z1", "x", "y"]
-    for bit in ("z1", "y", "x", "z2"):
+
+    def split_outs(value, bit):
         axis = names.index(bit) + 1
         names.remove(bit)
-        keep = lax.dynamic_index_in_dim(outs, spots[bit], axis, keepdims=False)
-        send = lax.dynamic_index_in_dim(outs, 1 - spots[bit], axis, keepdims=False)
-        outs = (keep.astype(F32) + xch(send, bit).astype(F32)).astype(BF)
-    outs = over_groups(outs)
+        keep = lax.dynamic_index_in_dim(value, spots[bit], axis, keepdims=False)
+        send = lax.dynamic_index_in_dim(value, 1 - spots[bit], axis, keepdims=False)
+        return keep, send
+
+    keep_o, send_o = split_outs(outs, "y")
+    got_o = xch(send_o, "y")
+    dr0, dp0 = mem_backward(0, proj, r0, dos0, log_s0, dm0, dt0)
+
+    got_o, got_m, dr0, dp0, xn, sn0, sn1 = fence(
+        (got_o, got_m, dr0, dp0, xn, sn0, sn1), (got_o, got_m, dr0, dp0)
+    )
+    mlp_part = [half_sum(h, g) for h, g in zip((ma, mb, mc), got_m)]
+    mlp_part = over_groups(jnp.concatenate(mlp_part))
+    got_m = xch(mlp_part, "y")
+    keep_o, send_o = split_outs(half_sum(keep_o, got_o), "x")
+    got_o = xch(send_o, "x")
+    ha, ha_out, hb, hb_out, hc, hc_out = proj_grads(
+        me, xn, sn0, sn1, dp0, dp1, dr0, dr1, small_sums
+    )
+
+    got_o, got_m, ha_out, hb_out, hc_out, dr0, dp0 = fence(
+        (got_o, got_m, ha_out, hb_out, hc_out, dr0, dp0), (got_o, got_m, ha_out)
+    )
+    both_m = jnp.stack([mlp_part, got_m])
+    got_c = xch(both_m, "c")
+    got = [xch(ha_out, "x"), xch(hb_out, "y"), xch(hc_out, "z1")]
+    dxn, dxn_send = proj_back(me, dp0, dp1, w_tok_l)
+    dxn_got = xch(dxn_send, "c")
+    dsn0, dsn0_send = proj_back(me, dr0, dr0, w_state_l)
+    dsn0_got = xch(dsn0_send, "c")
+
+    got, got_o, dxn_got, dsn0_got = fence(
+        (got, got_o, dxn_got, dsn0_got), (got, got_o, dxn_got, dsn0_got)
+    )
+    (ha, hb, hc), sends = add_halves((ha, hb, hc), got)
+    got = [xch(s, b) for s, b in zip(sends, ("y", "z1", "x"))]
+    keep_o, send_o = split_outs(half_sum(keep_o, got_o), "z1")
+    got_o = xch(send_o, "z1")
+    one = jnp.ones((1, D), F32)
+    grad_tokens = row_back(me, x_own, g_tok[None], dxn, dxn_got, one, dmid)
+
+    got, got_o, grad_tokens, dsn0_got = fence(
+        (got, got_o, grad_tokens, dsn0_got), (got, got_o, grad_tokens)
+    )
+    (ha, hb, hc), sends = add_halves((ha, hb, hc), got)
+    got = [xch(s, b) for s, b in zip(sends, ("z1", "x", "y"))]
+    keep_o, send_o = split_outs(half_sum(keep_o, got_o), "z2")
+    got_o = xch(send_o, "z2")
+    grad_state = row_back(me, state0, g_state[None], dsn0, dsn0_got, gate[None], ds1)
+    grad_state = grad_state.reshape(slots, srows, D)
+
+    got, got_o, grad_state, grad_tokens = fence(
+        (got, got_o, grad_state, grad_tokens), (got, got_o, grad_state)
+    )
+    (ha, hb, hc), sends = add_halves((ha, hb, hc), got)
+    got = [xch(s, "z2") for s in sends]
+    got_t = diag_send(grad_tokens)
+    outs = over_groups(half_sum(keep_o, got_o))
     outs = jnp.stack([outs, xch(outs, "y")])
+    grad_up, grad_down = place_mlp(me, both_m, got_c)
+
+    got, got_t, outs, grad_state, grad_up = fence(
+        (got, got_t, outs, grad_state, grad_up), (got, got_t, outs, grad_up)
+    )
+    part = over_groups(jnp.concatenate([half_sum(h, g) for h, g in zip((ha, hb, hc), got)]))
+    got_y = xch(part, "y")
+    grad_rows = slot_spread(grad_state)
     outs = jnp.stack([outs, xch(outs, "x")])
+    grad_tokens = pick(grad_tokens, got_t).astype(F32)
+
+    got_y, grad_rows, outs = fence((got_y, grad_rows, outs), (got_y, grad_rows, outs))
+    both_t = jnp.stack([part, got_y])
+    got_p = xch(both_t, "c")
+    grad_state = slot_order(grad_rows)
+    grad_state = pick(grad_state, diag_send(grad_state)).astype(F32)
     outs = untwist(outs, (x, y)).transpose(2, 0, 1, 3, 4).reshape(2, DH, D)
-    outs = jnp.where(on_diag, outs, xch(outs, "c")).astype(F32)
-
-    def spread(part):
-        other = xch(part, "y")
-        return part, other, xch(part, "c"), xch(other, "c")
-
-    grad_up, grad_down = place_mlp(me, *spread(jnp.stack([gu, gd])))
-    grad_tok_w, grad_state_w = place_proj(me, *spread(jnp.stack([ga, gb, gc])))
+    outs = pick(outs, xch(outs, "c")).astype(F32)
+    grad_tok_w, grad_state_w, rows_tok, rows_st, small = place_proj(
+        me, both_t, got_p, w_tok, w_state
+    )
+    grad_g_tok = rows_tok[0] / gain_tok.astype(F32)
+    grad_g_state = rows_st[0] / gain_state.astype(F32)
 
     return (
         output,
         state_next,
         grad_tokens,
         grad_state,
-        own[0],
-        own[1],
-        own[2],
+        grad_g_tok,
+        grad_g_state,
+        small[0, 0, :DH],
         grad_tok_w,
         grad_state_w,
         outs[0],
         outs[1],
-        own[3],
-        rel_own,
+        small[1, 0, :DH],
+        small[0, 0:1, DH : DH + NB],
         grad_up,
         grad_down,
     )
@@ -1039,8 +1408,8 @@
 
 def solution(mesh):
     reps, shards = mesh.devices.shape
-    grid = Mesh(mesh.devices.reshape(reps // 2, 2, shards // 2, 2), ("g", "c", "s", "x"))
-    rep, shard = ("g", "c"), ("s", "x")
+    grid = Mesh(mesh.devices.reshape(reps // 4, 2, 2, shards // 2, 2), ("h", "y", "c", "s", "x"))
+    rep, shard = ("h", "y", "c"), ("s", "x")
     every = rep + shard
     by_token = P(every, None)
     by_state = P(rep, shard, None)

time: 769 us -> 567 us (0.74)
  waiting for transfers between devices: 297 us -> 131 us
  matrix products: 54.1 us -> 13.8 us
  other arithmetic: 78.9 us -> 49.9 us
  Pallas kernels: 172 us -> 189 us
  local copies, waits for them, and re-layouts: 35 us -> 48.1 us
    ppermute x76 -> x73, waiting for transfers between devices: 243 us -> 105 us  [xch(): return lax.ppermute(value, axis, [(i, i ^ mask) for i in range(count)])]
    pallas_call x1 -> x15, Pallas kernels: 50.6 us -> 99.5 us  [the longest x1 38.3 us: mlp(): pl.pallas_call(mlp_kernel, grid=(4,), in_specs=[act] * 4 + [up0, up1, dow...]
    unnamed x194 -> x306, local copies, waits for them, and re-layouts: 12.4 us -> 39.2 us
    dot_general x7 -> x1, matrix products: 23.9 us -> 0.74 us  [mm_nt(): lax.dot_general(a, b, (((1,), (1,)), ((), ())), preferred_element_type=F32)]
    ppermute x12, waiting for transfers between devices: 33.5 us -> 12.8 us  [to_slot(): return lax.ppermute(value, 's', [(i, i ^ k) for i in range(slots)])]
    convert_element_type x30 -> x19, other arithmetic: 33.2 us -> 14 us  [the longest x10 3.13 us: half_sum(): return (part.astype(F32) + got.astype(F32)).astype(BF)]
    dot_general x8, matrix products: 22 us -> 11.9 us  [mm(): return jnp.dot(a, b, preferred_element_type=F32)]
    dot_general x4 -> x0, matrix products: 7.8 us -> none  [mm_tn(): lax.dot_general(a, b, (((0,), (0,)), ((), ())), preferred_element_type=F32)]
  transfers between devices with their start and end apart: 97 -> 94, of which waited for: 45 -> 33; matrix products, arithmetic and copies ran while one was open for 20% -> 12% of each run, Pallas kernels for 23% -> 31%
where the time goes in v2:
time: 567 us; the launch traced here: 560 us
  Pallas kernels  189 us (33%)
  waiting for transfers between devices  131 us (23%)
  starting transfers between devices  124 us (22%)
  other arithmetic  49.9 us (9%)
  local copies, waits for them, and re-layouts  48.1 us (8%)
  matrix products  13.8 us (2%)
    ppermute x73, waiting for transfers between devices, xch(): return lax.ppermute(value, axis, [(i, i ^ mask) for i in range(count)])  105 us
    ppermute x73, starting transfers between devices, xch(): return lax.ppermute(value, axis, [(i, i ^ mask) for i in range(count)])  71.3 us
    unnamed x306, local copies, waits for them, and re-layouts  39.2 us
    ppermute x9, starting transfers between devices, diag_send(): return lax.ppermute(value, ('c', 'x'), [(1, 2), (2, 1)])  38.9 us
    pallas_call x1, Pallas kernels, mlp(): pl.pallas_call(mlp_kernel, grid=(4,), in_specs=[act] * 4 + [up0, up1, dow...  38.3 us
    pallas_call x2, Pallas kernels, tok_backward(): pl.pallas_call(functools.partial(tok_bwd_kernel, has_prev), grid=(HL,), i...  22.7 us
    pallas_call x2, Pallas kernels, mem_backward(): pl.pallas_call(functools.partial(mem_bwd_kernel, final), grid=(HL,), in_s...  18.5 us
    ppermute x12, starting transfers between devices, to_slot(): return lax.ppermute(value, 's', [(i, i ^ k) for i in range(slots)])  14.3 us
  transfers between devices with their start and end apart: 94, of which 33 were waited for; matrix products, arithmetic and copies ran while one was open for 12% of the time, Pallas kernels for 31%

profile of v2, /device:TPU:1, one launch (start us, length us, event | category | flops | bytes accessed | tf_op | source)
XLA Modules:
  0.0 559.7 jit_solution(15782618743312513101)
XLA Ops:
  0.6 4.5 collective-permute-start.4
  10.1 2.4 collective-permute-start
  17.3 6.4 %collective-permute-done = bf16[256,256]{1,0:T(8,128)(2,1)S(1)} collective-permute-done((bf16[256,256]{1,0:T(8,128)(2,1)S(1)}, bf16[256,256]{1,0:T(8,128)(2,1)S(1)}, u32[]{:S(2)}, u32[]{:S(2)}) %collective-permute-start) | collective-permute-done | bytes 131104 | tf_op jit(solution)/shard_map/ppermute | solution.py:40
  32.1 2.6 collective-permute-start.8
  34.7 4.7 collective-permute-start.9
  39.5 2.6 collective-permute-done.9
  51.4 11.5 %collective-permute-done.13 = bf16[64,1024]{1,0:T(8,128)(2,1)S(1)} collective-permute-done((bf16[64,1024]{1,0:T(8,128)(2,1)}, bf16[64,1024]{1,0:T(8,128)(2,1)S(1)}, u32[]{:S(2)}, u32[]{:S(2)}) %collective-permute-start.13) | collective-permute-done | bytes 131104 | tf_op jit(solution)/shard_map/ppermute | solution.py:1087
  71.2 2.5 fusion.2
  73.9 2.5 collective-permute-start.20
  80.6 12.3 %collective-permute-done.18 = bf16[64,1024]{1,0:T(8,128)(2,1)S(1)} collective-permute-done((bf16[64,1024]{1,0:T(8,128)(2,1)S(1)}, bf16[64,1024]{1,0:T(8,128)(2,1)S(1)}, u32[]{:S(2)}, u32[]{:S(2)}) %collective-permute-start.18) | collective-permute-done | bytes 131104 | tf_op jit(solution)/shard_map/ppermute | solution.py:40
  98.0 6.2 %collective-permute-start.24 = (bf16[4,64,1024]{2,1,0:T(8,128)(2,1)S(1)}, bf16[4,64,1024]{2,1,0:T(8,128)(2,1)S(1)}, u32[]{:S(2)}, u32[]{:S(2)}) collective-permute-start(bf16[4,64,1024]{2,1,0:T(8,128)(2,1)S(1)} %copy-done.124), channel_id=1, source_target_pairs={{1,8},{8,1},{3,10},{10,3},{5,12},{12,5},{7,14},{14,7},{17,24},{24,... | collective-permute-start | bytes 1572872 | tf_op jit(solution)/shard_map/ppermute | solution.py:44
  107.8 3.6 convolution_convert_fusion.ko.vo.refs_0_.refs_3_.refs_4_.refs_6_.refs_7_.refs_8_.refs_9_
  113.6 5.6 collective-permute-done.23
  121.1 8.6 %collective-permute-done.25 = bf16[2,2,64,1024]{3,2,1,0:T(8,128)(2,1)S(1)} collective-permute-done((bf16[2,2,64,1024]{3,2,1,0:T(8,128)(2,1)S(1)}, bf16[2,2,64,1024]{3,2,1,0:T(8,128)(2,1)S(1)}, u32[]{:S(2)}, u32[]{:S(2)}) %collective-permute-start.25) | collective-permute-done | bytes 524320 | tf_op jit(solution)/shard_map/ppermute | solution.py:40
  132.0 5.4 mem_fwd.2
  137.5 5.2 tok_fwd.2
  142.7 7.9 %collective-permute-done.26.high = bf16[2,2,2,64,1024]{4,3,2,1,0:T(8,128)(2,1)S(1)} collective-permute-done((bf16[2,2,2,64,1024]{4,3,2,1,0:T(8,128)(2,1)S(1)}, bf16[2,2,2,64,1024]{4,3,2,1,0:T(8,128)(2,1)S(1)}, u32[]{:S(2)}, u32[]{:S(2)}) %collective-permute-start.26) | collective-permute-done | bytes 1048608 | tf_op jit(solution)/shard_map/ppermute | solution.py:40
  151.3 2.4 fusion.49
  153.7 4.9 collective-permute-start.31
  161.3 2.8 collective-permute-start.33
  165.7 3.0 fusion.46
  173.3 7.0 %tok_fwd.3 = (bf16[512,512]{1,0:T(8,128)(2,1)S(1)}, f32[512,128]{1,0:T(8,128)S(1)}) custom-call(bf16[1024,1536]{1,0:T(8,128)(2,1)S(1)} %convolution_convert_fusion.ko.vo.refs_0_.refs_3_.refs_4_.refs_6_.refs_7_.refs_8_.refs_9_, bf16[512,1536]{1,0:T(8,128)(2,1)S(1)} %convolution_convert_fusion.1.refs_1_.refs_2_.q.ks.vs.refs_0_, ...), custom_call_target="tpu_custom_call" | custom-call | flops 134217728 | bytes 838860 | tf_op jit(solution)/shard_map/tok_fwd/pallas_call | solution.py:338
  181.1 3.9 collective-permute-done.29
  188.9 3.8 collective-permute-start.39
  192.9 5.4 mem_fwd.3
  202.7 2.8 collective-permute-done.39
  208.3 8.8 %mem_bwd.2 = (f32[512,1536]{1,0:T(8,128)S(1)}, f32[512,1024]{1,0:T(8,128)S(1)}) custom-call(bf16[512,1536]{1,0:T(8,128)(2,1)S(1)} %convolution_convert_fusion.1.refs_1_.refs_2_.q.ks.vs.refs_0_, bf16[512,1536]{1,0:T(8,128)(2,1)S(1)} %convolution_convert_fusion.1.refs_1_.refs_2_.q.ks.vs.refs_0_, ...), custom_call_target="tpu_custom_call" | custom-call | flops 268435456 | bytes 943718 | tf_op jit(solution)/shard_map/mem_bwd/pallas_call | solution.py:443
  220.6 10.8 %collective-permute-done.35 = bf16[2,2,2,128,1024]{4,3,2,1,0:T(8,128)(2,1)S(1)} collective-permute-done((bf16[2,2,2,128,1024]{4,3,2,1,0:T(8,128)(2,1)S(1)}, bf16[2,2,2,128,1024]{4,3,2,1,0:T(8,128)(2,1)S(1)}, u32[]{:S(2)}, u32[]{:S(2)}) %collective-permute-start.35) | collective-permute-done | bytes 2097184 | tf_op jit(solution)/shard_map/ppermute | solution.py:40
  232.8 3.1 collective-permute-start.44
  236.3 38.3 %mlp.1 = (bf16[2,2,2,96,1024]{4,3,2,1,0:T(8,128)(2,1)S(1)}, bf16[2,2,2,96,1024]{4,3,2,1,0:T(8,128)(2,1)}, bf16[2,2,2,96,1024]{4,3,2,1,0:T(8,128)(2,1)}, bf16[2,2...) custom-call(bf16[512,1024]{1,0:T(8,128)(2,1)S(1)} %multiply_convert_, ...), custom_call_target="tpu_custom_call" | custom-call | flops 2576980480 | bytes 2726297 | tf_op jit(solution)/shard_map/mlp/pallas_call | solution.py:683
  277.4 2.8 collective-permute-start.49
  284.9 6.8 %mid_back.1 = (f32[512,1024]{1,0:T(8,128)}, bf16[512,1024]{1,0:T(8,128)(2,1)}, bf16[512,1024]{1,0:T(8,128)(2,1)}, f32[8,1024]{1,0:T(8,128)}) custom-call(f32[512,1024]{1,0:T(8,128)} %copy-done.84, f32[1,1024]{1,0:T(1,128)} %get-tuple-element.574.gain, f32[512,1024]{1,0:T(8,128)} %get-tuple-element.348.e_own, bf16[512,1024]{1,0:T(8,128)(2,1)} %copy-done.110, ...), custom_call_target="tpu_custom_call" | custom-call | tf_op jit(solution)/shard_map/mid_back/pallas_call | solution.py:758
  294.8 6.4 %out_back.1 = (bf16[1024,512]{1,0:T(8,128)(2,1)}, bf16[512,1024]{1,0:T(8,128)(2,1)}) custom-call(s32[4]{0:T(128)} %copy-done.75, bf16[512,1024]{1,0:T(8,128)(2,1)} %get-tuple-element.352.own, bf16[512,1024]{1,0:T(8,128)(2,1)} %collective-permute-done.51.oth, bf16[512,1024]{1,0:T(8,128)(2,1)} %copy-done.22, bf16[512,512]{1,0:T(8,128)(2,1)} %copy-done.43, ...), custom_call_target="tpu_custom_call" | custom-call | tf_op jit(solution)/shard_map/out_back/pallas_call | solution.py:784
  305.9 13.2 %tok_bwd.2 = (bf16[512,1536]{1,0:T(8,128)(2,1)S(1)}, bf16[512,1536]{1,0:T(8,128)(2,1)S(1)}, f32[512,1024]{1,0:T(8,128)S(1)}, f32[4,8,512]{2,1,0:T(8,128)S(1)}) custom-call(bf16[1024,1536]{1,0:T(8,128)(2,1)S(1)} %convolution_convert_fusion.ko.vo.refs_0_.refs_3_.refs_4_.refs_6_.refs_7_.refs_8_.refs_9_, bf16[512,1536]{1,0:T(8,128)(2,1)S(1)} %copy-done.1, ...), custom_call_target="tpu_custom_call" | custom-call | flops 335544320 | bytes 1258291 | tf_op jit(solution)/shard_map/tok_bwd/pallas_call | solution.py:589
  320.3 4.2 halves.6
  326.0 2.8 collective-permute-start.55
  328.8 3.2 proj_back.3
  334.1 3.7 collective-permute-done.54
  337.8 5.1 collective-permute-start.56
  342.9 9.6 %tok_bwd.3 = (f32[512,1024]{1,0:T(8,128)S(1)}, f32[512,1536]{1,0:T(8,128)S(1)}, f32[4,8,512]{2,1,0:T(8,128)S(1)}) custom-call(bf16[1024,1536]{1,0:T(8,128)(2,1)S(1)} %convolution_convert_fusion.ko.vo.refs_0_.refs_3_.refs_4_.refs_6_.refs_7_.refs_8_.refs_9_, bf16[512,1536]{1,0:T(8,128)(2,1)S(1)} %copy-done.3, bf16[512,1536]{1,0:T(8,128)(2,1)S(1)} %copy-done.3, ...), custom_call_target="tpu_custom_call" | custom-call | flops 335544320 | bytes 1258291 | tf_op jit(solution)/shard_map/tok_bwd/pallas_call | solution.py:589
  360.8 12.5 %state_back.1 = (f32[512,1024]{1,0:T(8,128)}, bf16[512,512]{1,0:T(8,128)(2,1)}, bf16[512,1024]{1,0:T(8,128)(2,1)}, f32[8,1024]{1,0:T(8,128)}) custom-call(s32[4]{0:T(128)} %copy-done.75, f32[512,1024]{1,0:T(8,128)} %copy-done.81, f32[1,1024]{1,0:T(1,128)} %get-tuple-element.573.refs_1_.gain, f32[512,1024]{1,0:T(8,128)} %copy-done.41, ...), custom_call_target="tpu_custom_call" | custom-call | tf_op jit(solution)/shard_map/state_back/pallas_call | solution.py:871
  392.5 9.7 %mem_bwd.3 = (bf16[512,1536]{1,0:T(8,128)(2,1)S(1)}, bf16[512,1536]{1,0:T(8,128)(2,1)S(1)}) custom-call(bf16[512,1536]{1,0:T(8,128)(2,1)S(1)} %copy-done.4, bf16[512,1536]{1,0:T(8,128)(2,1)S(1)} %copy-done.4, bf16[512,1536]{1,0:T(8,128)(2,1)S(1)} %copy-done.4, ...), custom_call_target="tpu_custom_call" | custom-call | flops 268435456 | bytes 943718 | tf_op jit(solution)/shard_map/mem_bwd/pallas_call | solution.py:443
  402.2 7.4 %collective-permute-done.64 = bf16[64,1024]{1,0:T(8,128)(2,1)S(1)} collective-permute-done((bf16[64,1024]{1,0:T(8,128)(2,1)S(1)}, bf16[64,1024]{1,0:T(8,128)(2,1)S(1)}, u32[]{:S(2)}, u32[]{:S(2)}) %collective-permute-start.64) | collective-permute-done | bytes 131104 | tf_op jit(solution)/shard_map/ppermute | solution.py:40
  415.5 14.3 %proj_grad.1 = (bf16[2,2,2,272,256]{4,3,2,1,0:T(8,128)(2,1)}, bf16[2,2,2,272,256]{4,3,2,1,0:T(8,128)(2,1)}, bf16[2,2,2,256,256]{4,3,2,1,0:T(8,128)(2,1)}, bf16[2...) custom-call(s32[4]{0:T(128)} %copy-done.75, ...), custom_call_target="tpu_custom_call" | custom-call | flops 644245120 | bytes 1677721 | tf_op jit(solution)/shard_map/proj_grad/pallas_call | solution.py:956
  432.4 5.4 proj_back.4
  439.8 3.3 proj_back.5
  446.1 7.4 %collective-permute-done.68 = bf16[2,2,2,256,256]{4,3,2,1,0:T(8,128)(2,1)} collective-permute-done((bf16[2,2,2,256,256]{4,3,2,1,0:T(8,128)(2,1)}, bf16[2,2,2,256,256]{4,3,2,1,0:T(8,128)(2,1)}, u32[]{:S(2)}, u32[]{:S(2)}) %collective-permute-start.68) | collective-permute-done | bytes 1048608 | tf_op jit(solution)/shard_map/ppermute | solution.py:40
  457.6 4.0 halves.9
  468.0 3.7 collective-permute-start.85
  472.2 6.0 %row_back.2 = bf16[512,1024]{1,0:T(8,128)(2,1)} custom-call(s32[4]{0:T(128)} %copy-done.75, bf16[512,1024]{1,0:T(8,128)(2,1)} %copy-done.82, f32[1,1024]{1,0:T(1,128)} %get-tuple-element.572.gain, f32[512,1024]{1,0:T(8,128)} %copy-done.40, bf16[512,1024]{1,0:T(8,128)(2,1)} %collective-permute-done.70.got, f32[1,1024]{1,0:T(1,128)} %broadcast.130.scale, ...), custom_call_target="tpu_custom_call" | custom-call | tf_op jit(solution)/shard_map/row_back/pallas_call | solution.py:902
  478.2 2.7 collective-permute-done.75
  487.7 3.2 collective-permute-start.79
  490.9 3.8 row_back.3
  495.4 8.0 %collective-permute-start.83 = (bf16[512,1024]{1,0:T(8,128)(2,1)}, bf16[512,1024]{1,0:T(8,128)(2,1)}, u32[]{:S(2)}, u32[]{:S(2)}) collective-permute-start(bf16[512,1024]{1,0:T(8,128)(2,1)} %row_back.2), channel_id=1, source_target_pairs={{1,8},{8,1},{3,10},{10,3},{5,12},{12,5},{7,14},{14,7},{17,24},{24,... | collective-permute-start | bytes 3145736 | tf_op jit(solution)/shard_map/ppermute | solution.py:44
  503.5 2.4 broadcast_select_fusion.1
  512.0 2.8 place_mlp.1
  515.5 8.0 %collective-permute-done.81 = bf16[256,256]{1,0:T(8,128)(2,1)S(1)} collective-permute-done((bf16[256,256]{1,0:T(8,128)(2,1)S(1)}, bf16[256,256]{1,0:T(8,128)(2,1)S(1)}, u32[]{:S(2)}, u32[]{:S(2)}) %collective-permute-start.81) | collective-permute-done | bytes 131104 | tf_op jit(solution)/shard_map/ppermute | solution.py:40
  523.5 2.7 collective-permute-done.82
  527.0 2.5 collective-permute-start.88
  530.6 2.7 select_convert_fusion.1
  533.2 3.6 collective-permute-done.90
  538.4 2.7 collective-permute-start.93
  544.8 7.2 %collective-permute-done.91 = bf16[4,64,1024]{2,1,0:T(8,128)(2,1)S(1)} collective-permute-done((bf16[4,64,1024]{2,1,0:T(8,128)(2,1)S(1)}, bf16[4,64,1024]{2,1,0:T(8,128)(2,1)S(1)}, u32[]{:S(2)}, u32[]{:S(2)}) %collective-permute-start.91) | collective-permute-done | bytes 524320 | tf_op jit(solution)/shard_map/ppermute | solution.py:44
  553.0 4.4 place_proj.1
  (593 shorter events, 176.9 us)
Async XLA Ops:
  0.6 26.8 %collective-permute-start.4 = (bf16[512,1024]{1,0:T(8,128)(2,1)}, bf16[512,1024]{1,0:T(8,128)(2,1)S(1)}, u32[]{:S(2)}, u32[]{:S(2)}) collective-permute-start(bf16[512,1024]{1,0:T(8,128)(2,1)} %param.16), channel_id=1, source_target_pairs={{1,8},{8,1},{3,10},{10,3},{5,12},{12,5},{7,14},{14,7},{17,24},{24,... | collective-permute-start | bytes 3145736 | tf_op jit(solution)/shard_map/ppermute | solution.py:44
  5.2 22.3 %collective-permute-start.3 = (bf16[4,64,1024]{2,1,0:T(8,128)(2,1)}, bf16[4,64,1024]{2,1,0:T(8,128)(2,1)S(1)}, u32[]{:S(2)}, u32[]{:S(2)}) collective-permute-start(bf16[4,64,1024]{2,1,0:T(8,128)(2,1)} %param.17), channel_id=1, source_target_pairs={{1,8},{8,1},{3,10},{10,3},{5,12},{12,5},{7,14},{14,7},{17,24},{24,... | collective-permute-start | bytes 1572872 | tf_op jit(solution)/shard_map/ppermute | solution.py:44
  10.1 13.6 %collective-permute-start = (bf16[256,256]{1,0:T(8,128)(2,1)S(1)}, bf16[256,256]{1,0:T(8,128)(2,1)S(1)}, u32[]{:S(2)}, u32[]{:S(2)}) collective-permute-start(bf16[256,256]{1,0:T(8,128)(2,1)S(1)} %get-tuple-element.261), channel_id=1, source_target_pairs={{0,4},{2,6},{4,0},{6,2},{1,5},{3,7},{5,1},{7,3},{8,12},{10,14},{12... | collective-permute-start | bytes 393224 | tf_op jit(solution)/shard_map/ppermute | solution.py:40
  12.5 13.4 %collective-permute-start.1 = (bf16[256,256]{1,0:T(8,128)(2,1)S(1)}, bf16[256,256]{1,0:T(8,128)(2,1)S(1)}, u32[]{:S(2)}, u32[]{:S(2)}) collective-permute-start(bf16[256,256]{1,0:T(8,128)(2,1)S(1)} %get-tuple-element.262), channel_id=1, source_target_pairs={{0,4},{2,6},{4,0},{6,2},{1,5},{3,7},{5,1},{7,3},{8,12},{10,14},{12... | collective-permute-start | bytes 393224 | tf_op jit(solution)/shard_map/ppermute | solution.py:40
  14.0 13.4 %collective-permute-start.2 = (bf16[272,256]{1,0:T(8,128)(2,1)S(1)}, bf16[272,256]{1,0:T(8,128)(2,1)S(1)}, u32[]{:S(2)}, u32[]{:S(2)}) collective-permute-start(bf16[272,256]{1,0:T(8,128)(2,1)S(1)} %get-tuple-element.569), channel_id=1, source_target_pairs={{0,4},{2,6},{4,0},{6,2},{1,5},{3,7},{5,1},{7,3},{8,12},{10,14},{12... | collective-permute-start | bytes 417800 | tf_op jit(solution)/shard_map/ppermute | solution.py:40
  27.5 14.6 %collective-permute-start.5 = (bf16[2,272,256]{2,1,0:T(8,128)(2,1)S(1)}, bf16[2,272,256]{2,1,0:T(8,128)(2,1)S(1)}, u32[]{:S(2)}, u32[]{:S(2)}) collective-permute-start(bf16[2,272,256]{2,1,0:T(8,128)(2,1)S(1)} %get-tuple-element.561), channel_id=1, source_target_pairs={{0,2},{2,0},{4,6},{6,4},{1,3},{3,1},{5,7},{7,5},{8,10},{10,8},{12,... | collective-permute-start | bytes 835592 | tf_op jit(solution)/shard_map/ppermute | solution.py:40
  28.6 13.5 %collective-permute-start.6 = (bf16[2,256,256]{2,1,0:T(8,128)(2,1)S(1)}, bf16[2,256,256]{2,1,0:T(8,128)(2,1)S(1)}, u32[]{:S(2)}, u32[]{:S(2)}) collective-permute-start(bf16[2,256,256]{2,1,0:T(8,128)(2,1)S(1)} %get-tuple-element.567), channel_id=1, source_target_pairs={{0,1},{1,0},{2,3},{3,2},{4,5},{5,4},{6,7},{7,6},{8,9},{9,8},{10,11... | collective-permute-start | bytes 786440 | tf_op jit(solution)/shard_map/ppermute | solution.py:40
  42.9 20.0 %collective-permute-start.14 = (bf16[512,1024]{1,0:T(8,128)(2,1)S(1)}, bf16[512,1024]{1,0:T(8,128)(2,1)S(1)}, u32[]{:S(2)}, u32[]{:S(2)}) collective-permute-start(bf16[512,1024]{1,0:T(8,128)(2,1)S(1)} %broadcast_select_fusion.3.values), channel_id=1, source_target_pairs={{0,8},{8,0},{1,9},{9,1},{2,10},{10,2},{3,11},{11,3},{4,12},{12,4},... | collective-permute-start | bytes 3145736 | tf_op jit(solution)/shard_map/ppermute | solution.py:40
  44.0 18.9 %collective-permute-start.10 = (bf16[2,2,272,256]{3,2,1,0:T(8,128)(2,1)}, bf16[2,2,272,256]{3,2,1,0:T(8,128)(2,1)}, u32[]{:S(2)}, u32[]{:S(2)}) collective-permute-start(bf16[2,2,272,256]{3,2,1,0:T(8,128)(2,1)} %get-tuple-element.525), channel_id=1, source_target_pairs={{0,16},{16,0},{1,17},{17,1},{2,18},{18,2},{3,19},{19,3},{4,20},{20... | collective-permute-start | bytes 1671176 | tf_op jit(solution)/shard_map/ppermute | solution.py:40
  45.1 17.8 %collective-permute-start.11 = (bf16[2,2,256,256]{3,2,1,0:T(8,128)(2,1)}, bf16[2,2,256,256]{3,2,1,0:T(8,128)(2,1)}, u32[]{:S(2)}, u32[]{:S(2)}) collective-permute-start(bf16[2,2,256,256]{3,2,1,0:T(8,128)(2,1)} %get-tuple-element.557), channel_id=1, source_target_pairs={{0,2},{2,0},{4,6},{6,4},{1,3},{3,1},{5,7},{7,5},{8,10},{10,8},{12,... | collective-permute-start | bytes 1572872 | tf_op jit(solution)/shard_map/ppermute | solution.py:40
  46.9 16.0 %collective-permute-start.12 = (bf16[2,2,256,256]{3,2,1,0:T(8,128)(2,1)}, bf16[2,2,256,256]{3,2,1,0:T(8,128)(2,1)}, u32[]{:S(2)}, u32[]{:S(2)}) collective-permute-start(bf16[2,2,256,256]{3,2,1,0:T(8,128)(2,1)} %get-tuple-element.555), channel_id=1, source_target_pairs={{0,1},{1,0},{2,3},{3,2},{4,5},{5,4},{6,7},{7,6},{8,9},{9,8},{10,11... | collective-permute-start | bytes 1572872 | tf_op jit(solution)/shard_map/ppermute | solution.py:40
  64.2 29.8 %collective-permute-start.15 = (bf16[2,2,2,272,256]{4,3,2,1,0:T(8,128)(2,1)S(1)}, bf16[2,2,2,272,256]{4,3,2,1,0:T(8,128)(2,1)S(1)}, u32[]{:S(2)}, u32[]{:S(2)}) collective-permute-start(bf16[2,2,2,272,256]{4,3,2,1,0:T(8,128)(2,1)S(1)} %pad_maximum_fusion.3.a0), channel_id=1, source_target_pairs={{0,1},{1,0},{2,3},{3,2},{4,5},{5,4},{6,7},{7,6},{8,9},{9,8},{10,11... | collective-permute-start | bytes 3342344 | tf_op jit(solution)/shard_map/ppermute | solution.py:40
  65.6 27.4 %collective-permute-start.16 = (bf16[2,2,2,256,256]{4,3,2,1,0:T(8,128)(2,1)S(1)}, bf16[2,2,2,256,256]{4,3,2,1,0:T(8,128)(2,1)S(1)}, u32[]{:S(2)}, u32[]{:S(2)}) collective-permute-start(bf16[2,2,2,256,256]{4,3,2,1,0:T(8,128)(2,1)S(1)} %pad_maximum_fusion.4.b0), channel_id=1, source_target_pairs={{0,16},{16,0},{1,17},{17,1},{2,18},{18,2},{3,19},{19,3},{4,20},{20... | collective-permute-start | bytes 3145736 | tf_op jit(solution)/shard_map/ppermute | solution.py:40
  68.1 25.9 %collective-permute-start.17 = (bf16[2,2,2,256,256]{4,3,2,1,0:T(8,128)(2,1)S(1)}, bf16[2,2,2,256,256]{4,3,2,1,0:T(8,128)(2,1)S(1)}, u32[]{:S(2)}, u32[]{:S(2)}) collective-permute-start(bf16[2,2,2,256,256]{4,3,2,1,0:T(8,128)(2,1)S(1)} %pad_maximum_fusion.5.c0), channel_id=1, source_target_pairs={{0,2},{2,0},{4,6},{6,4},{1,3},{3,1},{5,7},{7,5},{8,10},{10,8},{12,... | collective-permute-start | bytes 3145736 | tf_op jit(solution)/shard_map/ppermute | solution.py:40
  69.6 23.4 %collective-permute-start.18 = (bf16[64,1024]{1,0:T(8,128)(2,1)S(1)}, bf16[64,1024]{1,0:T(8,128)(2,1)S(1)}, u32[]{:S(2)}, u32[]{:S(2)}) collective-permute-start(bf16[64,1024]{1,0:T(8,128)(2,1)S(1)} %broadcast_select_fusion.6), channel_id=1, source_target_pairs={{0,4},{2,6},{4,0},{6,2},{1,5},{3,7},{5,1},{7,3},{8,12},{10,14},{12... | collective-permute-start | bytes 393224 | tf_op jit(solution)/shard_map/ppermute | solution.py:40
  94.0 19.5 %collective-permute-start.21 = (bf16[2,64,1024]{2,1,0:T(8,128)(2,1)S(1)}, bf16[2,64,1024]{2,1,0:T(8,128)(2,1)S(1)}, u32[]{:S(2)}, u32[]{:S(2)}) collective-permute-start(bf16[2,64,1024]{2,1,0:T(8,128)(2,1)S(1)} %get-tuple-element.563), channel_id=1, source_target_pairs={{0,2},{2,0},{4,6},{6,4},{1,3},{3,1},{5,7},{7,5},{8,10},{10,8},{12,... | collective-permute-start | bytes 786440 | tf_op jit(solution)/shard_map/ppermute | solution.py:40
  95.7 17.9 %collective-permute-start.22 = (bf16[128,1024]{1,0:T(8,128)(2,1)S(1)}, bf16[128,1024]{1,0:T(8,128)(2,1)S(1)}, u32[]{:S(2)}, u32[]{:S(2)}) collective-permute-start(bf16[128,1024]{1,0:T(8,128)(2,1)S(1)} %get-tuple-element.285), channel_id=1, source_target_pairs={{0,4},{2,6},{4,0},{6,2},{1,5},{3,7},{5,1},{7,3},{8,12},{10,14},{12... | collective-permute-start | bytes 786440 | tf_op jit(solution)/shard_map/ppermute | solution.py:40
  96.2 22.9 %collective-permute-start.23 = (bf16[128,1024]{1,0:T(8,128)(2,1)S(1)}, bf16[128,1024]{1,0:T(8,128)(2,1)S(1)}, u32[]{:S(2)}, u32[]{:S(2)}) collective-permute-start(bf16[128,1024]{1,0:T(8,128)(2,1)S(1)} %get-tuple-element.287), channel_id=1, source_target_pairs={{0,4},{2,6},{4,0},{6,2},{1,5},{3,7},{5,1},{7,3},{8,12},{10,14},{12... | collective-permute-start | bytes 786440 | tf_op jit(solution)/shard_map/ppermute | solution.py:40
  98.0 21.1 %collective-permute-start.24 = (bf16[4,64,1024]{2,1,0:T(8,128)(2,1)S(1)}, bf16[4,64,1024]{2,1,0:T(8,128)(2,1)S(1)}, u32[]{:S(2)}, u32[]{:S(2)}) collective-permute-start(bf16[4,64,1024]{2,1,0:T(8,128)(2,1)S(1)} %copy-done.124), channel_id=1, source_target_pairs={{1,8},{8,1},{3,10},{10,3},{5,12},{12,5},{7,14},{14,7},{17,24},{24,... | collective-permute-start | bytes 1572872 | tf_op jit(solution)/shard_map/ppermute | solution.py:44
  129.8 20.8 %collective-permute-start.26 = (bf16[2,2,2,64,1024]{4,3,2,1,0:T(8,128)(2,1)S(1)}, bf16[2,2,2,64,1024]{4,3,2,1,0:T(8,128)(2,1)S(1)}, u32[]{:S(2)}, u32[]{:S(2)}) collective-permute-start(bf16[2,2,2,64,1024]{4,3,2,1,0:T(8,128)(2,1)S(1)} %pad_maximum_fusion.6.low), channel_id=1, source_target_pairs={{0,16},{16,0},{1,17},{17,1},{2,18},{18,2},{3,19},{19,3},{4,20},{20... | collective-permute-start | bytes 3145736 | tf_op jit(solution)/shard_map/ppermute | solution.py:40
  160.1 24.8 %collective-permute-start.29 = (bf16[2,2,128,1024]{3,2,1,0:T(8,128)(2,1)S(1)}, bf16[2,2,128,1024]{3,2,1,0:T(8,128)(2,1)S(1)}, u32[]{:S(2)}, u32[]{:S(2)}) collective-permute-start(bf16[2,2,128,1024]{3,2,1,0:T(8,128)(2,1)S(1)} %get-tuple-element.523), channel_id=1, source_target_pairs={{0,1},{1,0},{2,3},{3,2},{4,5},{5,4},{6,7},{7,6},{8,9},{9,8},{10,11... | collective-permute-start | bytes 3145736 | tf_op jit(solution)/shard_map/ppermute | solution.py:40
  160.4 24.6 %collective-permute-start.30 = (bf16[2,2,128,1024]{3,2,1,0:T(8,128)(2,1)S(1)}, bf16[2,2,128,1024]{3,2,1,0:T(8,128)(2,1)S(1)}, u32[]{:S(2)}, u32[]{:S(2)}) collective-permute-start(bf16[2,2,128,1024]{3,2,1,0:T(8,128)(2,1)S(1)} %get-tuple-element.521), channel_id=1, source_target_pairs={{0,16},{16,0},{1,17},{17,1},{2,18},{18,2},{3,19},{19,3},{4,20},{20... | collective-permute-start | bytes 3145736 | tf_op jit(solution)/shard_map/ppermute | solution.py:40
  161.2 19.8 %collective-permute-start.32 = (bf16[64,1024]{1,0:T(8,128)(2,1)S(1)}, bf16[64,1024]{1,0:T(8,128)(2,1)S(1)}, u32[]{:S(2)}, u32[]{:S(2)}) collective-permute-start(bf16[64,1024]{1,0:T(8,128)(2,1)S(1)} %get-tuple-element.540), channel_id=1, source_target_pairs={{0,2},{2,0},{4,6},{6,4},{1,3},{3,1},{5,7},{7,5},{8,10},{10,8},{12,... | collective-permute-start | bytes 393224 | tf_op jit(solution)/shard_map/ppermute | solution.py:1087
  161.3 19.8 %collective-permute-start.33 = (bf16[64,1024]{1,0:T(8,128)(2,1)S(1)}, bf16[64,1024]{1,0:T(8,128)(2,1)S(1)}, u32[]{:S(2)}, u32[]{:S(2)}) collective-permute-start(bf16[64,1024]{1,0:T(8,128)(2,1)S(1)} %get-tuple-element.539), channel_id=1, source_target_pairs={{0,4},{2,6},{4,0},{6,2},{1,5},{3,7},{5,1},{7,3},{8,12},{10,14},{12... | collective-permute-start | bytes 393224 | tf_op jit(solution)/shard_map/ppermute | solution.py:1087
  164.8 16.2 %collective-permute-start.34 = (bf16[64,1024]{1,0:T(8,128)(2,1)S(1)}, bf16[64,1024]{1,0:T(8,128)(2,1)S(1)}, u32[]{:S(2)}, u32[]{:S(2)}) collective-permute-start(bf16[64,1024]{1,0:T(8,128)(2,1)S(1)} %get-tuple-element.538), channel_id=1, source_target_pairs={{0,6},{2,4},{4,2},{6,0},{1,7},{3,5},{5,3},{7,1},{8,14},{10,12},{12... | collective-permute-start | bytes 393224 | tf_op jit(solution)/shard_map/ppermute | solution.py:1087
  185.2 46.2 %collective-permute-start.35 = (bf16[2,2,2,128,1024]{4,3,2,1,0:T(8,128)(2,1)S(1)}, bf16[2,2,2,128,1024]{4,3,2,1,0:T(8,128)(2,1)S(1)}, u32[]{:S(2)}, u32[]{:S(2)}) collective-permute-start(bf16[2,2,2,128,1024]{4,3,2,1,0:T(8,128)(2,1)S(1)} %pad_maximum_fusion), channel_id=1, source_target_pairs={{0,16},{16,0},{1,17},{17,1},{2,18},{18,2},{3,19},{19,3},{4,20},{20... | collective-permute-start | bytes 6291464 | tf_op jit(solution)/shard_map/ppermute | solution.py:40
  186.5 46.1 %collective-permute-start.36 = (bf16[2,2,2,128,1024]{4,3,2,1,0:T(8,128)(2,1)S(1)}, bf16[2,2,2,128,1024]{4,3,2,1,0:T(8,128)(2,1)S(1)}, u32[]{:S(2)}, u32[]{:S(2)}) collective-permute-start(bf16[2,2,2,128,1024]{4,3,2,1,0:T(8,128)(2,1)S(1)} %pad_maximum_fusion.1), channel_id=1, source_target_pairs={{0,2},{2,0},{4,6},{6,4},{1,3},{3,1},{5,7},{7,5},{8,10},{10,8},{12,... | collective-permute-start | bytes 6291464 | tf_op jit(solution)/shard_map/ppermute | solution.py:40
  188.9 16.5 %collective-permute-start.39 = (bf16[512,1024]{1,0:T(8,128)(2,1)S(1)}, bf16[512,1024]{1,0:T(8,128)(2,1)S(1)}, u32[]{:S(2)}, u32[]{:S(2)}) collective-permute-start(bf16[512,1024]{1,0:T(8,128)(2,1)S(1)} %copy-done.113), channel_id=1, source_target_pairs={{1,8},{8,1},{3,10},{10,3},{5,12},{12,5},{7,14},{14,7},{17,24},{24,... | collective-permute-start | bytes 3145736 | tf_op jit(solution)/shard_map/ppermute | solution.py:44
  199.2 19.3 %collective-permute-start.41 = (bf16[256,1024]{1,0:T(8,128)(2,1)S(1)}, bf16[256,1024]{1,0:T(8,128)(2,1)S(1)}, u32[]{:S(2)}, u32[]{:S(2)}) collective-permute-start(bf16[256,1024]{1,0:T(8,128)(2,1)S(1)} %dynamic-slice_convert_fusion), channel_id=1, source_target_pairs={{0,8},{8,0},{1,9},{9,1},{2,10},{10,2},{3,11},{11,3},{4,12},{12,4},... | collective-permute-start | bytes 1572872 | tf_op jit(solution)/shard_map/ppermute | solution.py:40
  202.2 18.4 %collective-permute-start.38 = (bf16[512,1024]{1,0:T(8,128)(2,1)S(1)}, bf16[512,1024]{1,0:T(8,128)(2,1)S(1)}, u32[]{:S(2)}, u32[]{:S(2)}) collective-permute-start(bf16[512,1024]{1,0:T(8,128)(2,1)S(1)} %multiply_convert_fusion.2.h0), channel_id=1, source_target_pairs={{0,8},{8,0},{1,9},{9,1},{2,10},{10,2},{3,11},{11,3},{4,12},{12,4},... | collective-permute-start | bytes 3145736 | tf_op jit(solution)/shard_map/ppermute | solution.py:40
  205.6 15.0 %collective-permute-start.40 = (bf16[512,1024]{1,0:T(8,128)(2,1)S(1)}, bf16[512,1024]{1,0:T(8,128)(2,1)S(1)}, u32[]{:S(2)}, u32[]{:S(2)}) collective-permute-start(bf16[512,1024]{1,0:T(8,128)(2,1)S(1)} %broadcast_select_fusion.2.d0.d_own), channel_id=1, source_target_pairs={{0,8},{8,0},{1,9},{9,1},{2,10},{10,2},{3,11},{11,3},{4,12},{12,4},... | collective-permute-start | bytes 3145736 | tf_op jit(solution)/shard_map/ppermute | solution.py:40
  232.7 44.0 %collective-permute-start.43 = (bf16[64,1024]{1,0:T(8,128)(2,1)S(1)}, bf16[64,1024]{1,0:T(8,128)(2,1)S(1)}, u32[]{:S(2)}, u32[]{:S(2)}) collective-permute-start(bf16[64,1024]{1,0:T(8,128)(2,1)S(1)} %get-tuple-element.534), channel_id=1, source_target_pairs={{0,2},{2,0},{4,6},{6,4},{1,3},{3,1},{5,7},{7,5},{8,10},{10,8},{12,... | collective-permute-start | bytes 393224 | tf_op jit(solution)/shard_map/ppermute | solution.py:1087
  232.8 43.9 %collective-permute-start.44 = (bf16[64,1024]{1,0:T(8,128)(2,1)S(1)}, bf16[64,1024]{1,0:T(8,128)(2,1)S(1)}, u32[]{:S(2)}, u32[]{:S(2)}) collective-permute-start(bf16[64,1024]{1,0:T(8,128)(2,1)S(1)} %get-tuple-element.533), channel_id=1, source_target_pairs={{0,4},{2,6},{4,0},{6,2},{1,5},{3,7},{5,1},{7,3},{8,12},{10,14},{12... | collective-permute-start | bytes 393224 | tf_op jit(solution)/shard_map/ppermute | solution.py:1087
  235.9 40.8 %collective-permute-start.45 = (bf16[64,1024]{1,0:T(8,128)(2,1)S(1)}, bf16[64,1024]{1,0:T(8,128)(2,1)S(1)}, u32[]{:S(2)}, u32[]{:S(2)}) collective-permute-start(bf16[64,1024]{1,0:T(8,128)(2,1)S(1)} %get-tuple-element.532), channel_id=1, source_target_pairs={{0,6},{2,4},{4,2},{6,0},{1,7},{3,5},{5,3},{7,1},{8,14},{10,12},{12... | collective-permute-start | bytes 393224 | tf_op jit(solution)/shard_map/ppermute | solution.py:1087
  280.2 40.1 %collective-permute-start.46 = (bf16[2,2,2,96,1024]{4,3,2,1,0:T(8,128)(2,1)}, bf16[2,2,2,96,1024]{4,3,2,1,0:T(8,128)(2,1)}, u32[]{:S(2)}, u32[]{:S(2)}) collective-permute-start(bf16[2,2,2,96,1024]{4,3,2,1,0:T(8,128)(2,1)} %get-tuple-element.345), channel_id=1, source_target_pairs={{0,1},{1,0},{2,3},{3,2},{4,5},{5,4},{6,7},{7,6},{8,9},{9,8},{10,11... | collective-permute-start | bytes 4718600 | tf_op jit(solution)/shard_map/ppermute | solution.py:40
  281.5 38.8 %collective-permute-start.47 = (bf16[2,2,2,96,1024]{4,3,2,1,0:T(8,128)(2,1)}, bf16[2,2,2,96,1024]{4,3,2,1,0:T(8,128)(2,1)}, u32[]{:S(2)}, u32[]{:S(2)}) collective-permute-start(bf16[2,2,2,96,1024]{4,3,2,1,0:T(8,128)(2,1)} %get-tuple-element.346), channel_id=1, source_target_pairs={{0,16},{16,0},{1,17},{17,1},{2,18},{18,2},{3,19},{19,3},{4,20},{20... | collective-permute-start | bytes 4718600 | tf_op jit(solution)/shard_map/ppermute | solution.py:40
  292.2 28.1 %collective-permute-start.48 = (bf16[2,2,2,64,1024]{4,3,2,1,0:T(8,128)(2,1)}, bf16[2,2,2,64,1024]{4,3,2,1,0:T(8,128)(2,1)}, u32[]{:S(2)}, u32[]{:S(2)}) collective-permute-start(bf16[2,2,2,64,1024]{4,3,2,1,0:T(8,128)(2,1)} %get-tuple-element.347), channel_id=1, source_target_pairs={{0,2},{2,0},{4,6},{6,4},{1,3},{3,1},{5,7},{7,5},{8,10},{10,8},{12,... | collective-permute-start | bytes 3145736 | tf_op jit(solution)/shard_map/ppermute | solution.py:40
  326.0 29.2 %collective-permute-start.55 = (bf16[512,1024]{1,0:T(8,128)(2,1)S(1)}, bf16[512,1024]{1,0:T(8,128)(2,1)S(1)}, u32[]{:S(2)}, u32[]{:S(2)}) collective-permute-start(bf16[512,1024]{1,0:T(8,128)(2,1)S(1)} %copy-done.114), channel_id=1, source_target_pairs={{1,8},{8,1},{3,10},{10,3},{5,12},{12,5},{7,14},{14,7},{17,24},{24,... | collective-permute-start | bytes 3145736 | tf_op jit(solution)/shard_map/ppermute | solution.py:44
  332.0 23.2 %collective-permute-start.57 = (bf16[512,1024]{1,0:T(8,128)(2,1)S(1)}, bf16[512,1024]{1,0:T(8,128)(2,1)S(1)}, u32[]{:S(2)}, u32[]{:S(2)}) collective-permute-start(bf16[512,1024]{1,0:T(8,128)(2,1)S(1)} %get-tuple-element.380), channel_id=1, source_target_pairs={{0,8},{8,0},{1,9},{9,1},{2,10},{10,2},{3,11},{11,3},{4,12},{12,4},... | collective-permute-start | bytes 3145736 | tf_op jit(solution)/shard_map/ppermute | solution.py:40
  332.1 23.1 %collective-permute-start.52 = (bf16[2,2,96,1024]{3,2,1,0:T(8,128)(2,1)S(1)}, bf16[2,2,96,1024]{3,2,1,0:T(8,128)(2,1)S(1)}, u32[]{:S(2)}, u32[]{:S(2)}) collective-permute-start(bf16[2,2,96,1024]{3,2,1,0:T(8,128)(2,1)S(1)} %bitcast.275), channel_id=1, source_target_pairs={{0,16},{16,0},{1,17},{17,1},{2,18},{18,2},{3,19},{19,3},{4,20},{20... | collective-permute-start | bytes 2359304 | tf_op jit(solution)/shard_map/ppermute | solution.py:40
  332.7 22.5 %collective-permute-start.53 = (bf16[2,2,96,1024]{3,2,1,0:T(8,128)(2,1)S(1)}, bf16[2,2,96,1024]{3,2,1,0:T(8,128)(2,1)S(1)}, u32[]{:S(2)}, u32[]{:S(2)}) collective-permute-start(bf16[2,2,96,1024]{3,2,1,0:T(8,128)(2,1)S(1)} %bitcast.274), channel_id=1, source_target_pairs={{0,2},{2,0},{4,6},{6,4},{1,3},{3,1},{5,7},{7,5},{8,10},{10,8},{12,... | collective-permute-start | bytes 2359304 | tf_op jit(solution)/shard_map/ppermute | solution.py:40
  337.8 17.4 %collective-permute-start.56 = (bf16[4,64,1024]{2,1,0:T(8,128)(2,1)S(1)}, bf16[4,64,1024]{2,1,0:T(8,128)(2,1)S(1)}, u32[]{:S(2)}, u32[]{:S(2)}) collective-permute-start(bf16[4,64,1024]{2,1,0:T(8,128)(2,1)S(1)} %bitcast.284), channel_id=1, source_target_pairs={{1,8},{8,1},{3,10},{10,3},{5,12},{12,5},{7,14},{14,7},{17,24},{24,... | collective-permute-start | bytes 1572872 | tf_op jit(solution)/shard_map/ppermute | solution.py:44
  358.9 15.9 %collective-permute-start.58 = (bf16[2,96,1024]{2,1,0:T(8,128)(2,1)}, bf16[2,96,1024]{2,1,0:T(8,128)(2,1)}, u32[]{:S(2)}, u32[]{:S(2)}) collective-permute-start(bf16[2,96,1024]{2,1,0:T(8,128)(2,1)} %bitcast.86), channel_id=1, source_target_pairs={{0,2},{2,0},{4,6},{6,4},{1,3},{3,1},{5,7},{7,5},{8,10},{10,8},{12,... | collective-permute-start | bytes 1179656 | tf_op jit(solution)/shard_map/ppermute | solution.py:40
  360.3 14.5 %collective-permute-start.59 = (bf16[2,96,1024]{2,1,0:T(8,128)(2,1)}, bf16[2,96,1024]{2,1,0:T(8,128)(2,1)}, u32[]{:S(2)}, u32[]{:S(2)}) collective-permute-start(bf16[2,96,1024]{2,1,0:T(8,128)(2,1)} %bitcast.87), channel_id=1, source_target_pairs={{0,1},{1,0},{2,3},{3,2},{4,5},{5,4},{6,7},{7,6},{8,9},{9,8},{10,11... | collective-permute-start | bytes 1179656 | tf_op jit(solution)/shard_map/ppermute | solution.py:40
  360.3 14.5 %collective-permute-start.60 = (bf16[2,64,1024]{2,1,0:T(8,128)(2,1)}, bf16[2,64,1024]{2,1,0:T(8,128)(2,1)}, u32[]{:S(2)}, u32[]{:S(2)}) collective-permute-start(bf16[2,64,1024]{2,1,0:T(8,128)(2,1)} %bitcast.88), channel_id=1, source_target_pairs={{0,16},{16,0},{1,17},{17,1},{2,18},{18,2},{3,19},{19,3},{4,20},{20... | collective-permute-start | bytes 786440 | tf_op jit(solution)/shard_map/ppermute | solution.py:40
  377.1 32.5 %collective-permute-start.61 = (bf16[2,2,2,2,32,1024]{5,4,3,2,1,0:T(8,128)(2,1)}, bf16[2,2,2,2,32,1024]{5,4,3,2,1,0:T(8,128)(2,1)}, u32[]{:S(2)}, u32[]{:S(2)}) collective-permute-start(bf16[2,2,2,2,32,1024]{5,4,3,2,1,0:T(8,128)(2,1)} %dynamic-slice_bitcast_fusion), channel_id=1, source_target_pairs={{0,16},{16,0},{1,17},{17,1},{2,18},{18,2},{3,19},{19,3},{4,20},{20... | collective-permute-start | bytes 3145736 | tf_op jit(solution)/shard_map/ppermute | solution.py:40
  384.5 25.1 %collective-permute-start.62 = (bf16[96,1024]{1,0:T(8,128)(2,1)S(1)}, bf16[96,1024]{1,0:T(8,128)(2,1)S(1)}, u32[]{:S(2)}, u32[]{:S(2)}) collective-permute-start(bf16[96,1024]{1,0:T(8,128)(2,1)S(1)} %get-tuple-element.404), channel_id=1, source_target_pairs={{0,4},{2,6},{4,0},{6,2},{1,5},{3,7},{5,1},{7,3},{8,12},{10,14},{12... | collective-permute-start | bytes 589832 | tf_op jit(solution)/shard_map/ppermute | solution.py:40
  386.6 23.0 %collective-permute-start.63 = (bf16[96,1024]{1,0:T(8,128)(2,1)S(1)}, bf16[96,1024]{1,0:T(8,128)(2,1)S(1)}, u32[]{:S(2)}, u32[]{:S(2)}) collective-permute-start(bf16[96,1024]{1,0:T(8,128)(2,1)S(1)} %get-tuple-element.405), channel_id=1, source_target_pairs={{0,4},{2,6},{4,0},{6,2},{1,5},{3,7},{5,1},{7,3},{8,12},{10,14},{12... | collective-permute-start | bytes 589832 | tf_op jit(solution)/shard_map/ppermute | solution.py:40
  386.9 22.7 %collective-permute-start.64 = (bf16[64,1024]{1,0:T(8,128)(2,1)S(1)}, bf16[64,1024]{1,0:T(8,128)(2,1)S(1)}, u32[]{:S(2)}, u32[]{:S(2)}) collective-permute-start(bf16[64,1024]{1,0:T(8,128)(2,1)S(1)} %get-tuple-element.406), channel_id=1, source_target_pairs={{0,4},{2,6},{4,0},{6,2},{1,5},{3,7},{5,1},{7,3},{8,12},{10,14},{12... | collective-permute-start | bytes 393224 | tf_op jit(solution)/shard_map/ppermute | solution.py:40
  411.4 18.4 %collective-permute-start.65 = (bf16[2,2,2,32,1024]{4,3,2,1,0:T(8,128)(2,1)S(1)}, bf16[2,2,2,32,1024]{4,3,2,1,0:T(8,128)(2,1)S(1)}, u32[]{:S(2)}, u32[]{:S(2)}) collective-permute-start(bf16[2,2,2,32,1024]{4,3,2,1,0:T(8,128)(2,1)S(1)} %dynamic-slice_bitcast_fusion.1), channel_id=1, source_target_pairs={{0,1},{1,0},{2,3},{3,2},{4,5},{5,4},{6,7},{7,6},{8,9},{9,8},{10,11... | collective-permute-start | bytes 1572872 | tf_op jit(solution)/shard_map/ppermute | solution.py:40
  414.2 15.6 %collective-permute-start.66 = (bf16[256,1024]{1,0:T(8,128)(2,1)S(1)}, bf16[256,1024]{1,0:T(8,128)(2,1)}, u32[]{:S(2)}, u32[]{:S(2)}) collective-permute-start(bf16[256,1024]{1,0:T(8,128)(2,1)S(1)} %get-tuple-element.531), channel_id=1, source_target_pairs={{0,16},{16,0},{1,17},{17,1},{2,18},{18,2},{3,19},{19,3},{4,20},{20... | collective-permute-start | bytes 1572872 | tf_op jit(solution)/shard_map/ppermute | solution.py:40
  430.6 24.5 %collective-permute-start.67 = (bf16[2,2,2,272,256]{4,3,2,1,0:T(8,128)(2,1)}, bf16[2,2,2,272,256]{4,3,2,1,0:T(8,128)(2,1)S(1)}, u32[]{:S(2)}, u32[]{:S(2)}) collective-permute-start(bf16[2,2,2,272,256]{4,3,2,1,0:T(8,128)(2,1)} %get-tuple-element.436), channel_id=1, source_target_pairs={{0,1},{1,0},{2,3},{3,2},{4,5},{5,4},{6,7},{7,6},{8,9},{9,8},{10,11... | collective-permute-start | bytes 3342344 | tf_op jit(solution)/shard_map/ppermute | solution.py:40
  430.6 22.9 %collective-permute-start.68 = (bf16[2,2,2,256,256]{4,3,2,1,0:T(8,128)(2,1)}, bf16[2,2,2,256,256]{4,3,2,1,0:T(8,128)(2,1)}, u32[]{:S(2)}, u32[]{:S(2)}) collective-permute-start(bf16[2,2,2,256,256]{4,3,2,1,0:T(8,128)(2,1)} %get-tuple-element.437), channel_id=1, source_target_pairs={{0,16},{16,0},{1,17},{17,1},{2,18},{18,2},{3,19},{19,3},{4,20},{20... | collective-permute-start | bytes 3145736 | tf_op jit(solution)/shard_map/ppermute | solution.py:40
  431.5 22.6 %collective-permute-start.69 = (bf16[2,2,2,256,256]{4,3,2,1,0:T(8,128)(2,1)}, bf16[2,2,2,256,256]{4,3,2,1,0:T(8,128)(2,1)}, u32[]{:S(2)}, u32[]{:S(2)}) collective-permute-start(bf16[2,2,2,256,256]{4,3,2,1,0:T(8,128)(2,1)} %get-tuple-element.438), channel_id=1, source_target_pairs={{0,2},{2,0},{4,6},{6,4},{1,3},{3,1},{5,7},{7,5},{8,10},{10,8},{12,... | collective-permute-start | bytes 3145736 | tf_op jit(solution)/shard_map/ppermute | solution.py:40
  437.9 16.3 %collective-permute-start.70 = (bf16[512,1024]{1,0:T(8,128)(2,1)}, bf16[512,1024]{1,0:T(8,128)(2,1)}, u32[]{:S(2)}, u32[]{:S(2)}) collective-permute-start(bf16[512,1024]{1,0:T(8,128)(2,1)} %get-tuple-element.441), channel_id=1, source_target_pairs={{0,8},{8,0},{1,9},{9,1},{2,10},{10,2},{3,11},{11,3},{4,12},{12,4},... | collective-permute-start | bytes 3145736 | tf_op jit(solution)/shard_map/ppermute | solution.py:40
  463.2 17.7 %collective-permute-start.72 = (bf16[2,2,272,256]{3,2,1,0:T(8,128)(2,1)}, bf16[2,2,272,256]{3,2,1,0:T(8,128)(2,1)}, u32[]{:S(2)}, u32[]{:S(2)}) collective-permute-start(bf16[2,2,272,256]{3,2,1,0:T(8,128)(2,1)} %bitcast.114), channel_id=1, source_target_pairs={{0,16},{16,0},{1,17},{17,1},{2,18},{18,2},{3,19},{19,3},{4,20},{20... | collective-permute-start | bytes 1671176 | tf_op jit(solution)/shard_map/ppermute | solution.py:40
  464.1 16.7 %collective-permute-start.73 = (bf16[2,2,256,256]{3,2,1,0:T(8,128)(2,1)}, bf16[2,2,256,256]{3,2,1,0:T(8,128)(2,1)}, u32[]{:S(2)}, u32[]{:S(2)}) collective-permute-start(bf16[2,2,256,256]{3,2,1,0:T(8,128)(2,1)} %bitcast.115), channel_id=1, source_target_pairs={{0,2},{2,0},{4,6},{6,4},{1,3},{3,1},{5,7},{7,5},{8,10},{10,8},{12,... | collective-permute-start | bytes 1572872 | tf_op jit(solution)/shard_map/ppermute | solution.py:40
  465.8 15.1 %collective-permute-start.74 = (bf16[2,2,256,256]{3,2,1,0:T(8,128)(2,1)}, bf16[2,2,256,256]{3,2,1,0:T(8,128)(2,1)}, u32[]{:S(2)}, u32[]{:S(2)}) collective-permute-start(bf16[2,2,256,256]{3,2,1,0:T(8,128)(2,1)} %bitcast.116), channel_id=1, source_target_pairs={{0,1},{1,0},{2,3},{3,2},{4,5},{5,4},{6,7},{7,6},{8,9},{9,8},{10,11... | collective-permute-start | bytes 1572872 | tf_op jit(solution)/shard_map/ppermute | solution.py:40
  466.1 14.8 %collective-permute-start.75 = (bf16[2,2,32,1024]{3,2,1,0:T(8,128)(2,1)S(1)}, bf16[2,2,32,1024]{3,2,1,0:T(8,128)(2,1)}, u32[]{:S(2)}, u32[]{:S(2)}) collective-permute-start(bf16[2,2,32,1024]{3,2,1,0:T(8,128)(2,1)S(1)} %dynamic-slice_bitcast_fusion.2), channel_id=1, source_target_pairs={{0,2},{2,0},{4,6},{6,4},{1,3},{3,1},{5,7},{7,5},{8,10},{10,8},{12,... | collective-permute-start | bytes 786440 | tf_op jit(solution)/shard_map/ppermute | solution.py:40
  468.0 42.0 %collective-permute-start.85 = (bf16[2,256,1024]{2,1,0:T(8,128)(2,1)S(1)}, bf16[2,256,1024]{2,1,0:T(8,128)(2,1)S(1)}, u32[]{:S(2)}, u32[]{:S(2)}) collective-permute-start(bf16[2,256,1024]{2,1,0:T(8,128)(2,1)S(1)} %pad_maximum_fusion.9.p0), channel_id=1, source_target_pairs={{0,8},{8,0},{1,9},{9,1},{2,10},{10,2},{3,11},{11,3},{4,12},{12,4},... | collective-permute-start | bytes 3145736 | tf_op jit(solution)/shard_map/ppermute | solution.py:40
  495.4 30.7 %collective-permute-start.83 = (bf16[512,1024]{1,0:T(8,128)(2,1)}, bf16[512,1024]{1,0:T(8,128)(2,1)}, u32[]{:S(2)}, u32[]{:S(2)}) collective-permute-start(bf16[512,1024]{1,0:T(8,128)(2,1)} %row_back.2), channel_id=1, source_target_pairs={{1,8},{8,1},{3,10},{10,3},{5,12},{12,5},{7,14},{14,7},{17,24},{24,... | collective-permute-start | bytes 3145736 | tf_op jit(solution)/shard_map/ppermute | solution.py:44
  506.1 20.0 %collective-permute-start.80 = (bf16[272,256]{1,0:T(8,128)(2,1)S(1)}, bf16[272,256]{1,0:T(8,128)(2,1)S(1)}, u32[]{:S(2)}, u32[]{:S(2)}) collective-permute-start(bf16[272,256]{1,0:T(8,128)(2,1)S(1)} %get-tuple-element.476), channel_id=1, source_target_pairs={{0,4},{2,6},{4,0},{6,2},{1,5},{3,7},{5,1},{7,3},{8,12},{10,14},{12... | collective-permute-start | bytes 417800 | tf_op jit(solution)/shard_map/ppermute | solution.py:40
  507.5 15.9 %collective-permute-start.81 = (bf16[256,256]{1,0:T(8,128)(2,1)S(1)}, bf16[256,256]{1,0:T(8,128)(2,1)S(1)}, u32[]{:S(2)}, u32[]{:S(2)}) collective-permute-start(bf16[256,256]{1,0:T(8,128)(2,1)S(1)} %get-tuple-element.477), channel_id=1, source_target_pairs={{0,4},{2,6},{4,0},{6,2},{1,5},{3,7},{5,1},{7,3},{8,12},{10,14},{12... | collective-permute-start | bytes 393224 | tf_op jit(solution)/shard_map/ppermute | solution.py:40
  508.5 17.6 %collective-permute-start.82 = (bf16[256,256]{1,0:T(8,128)(2,1)S(1)}, bf16[256,256]{1,0:T(8,128)(2,1)S(1)}, u32[]{:S(2)}, u32[]{:S(2)}) collective-permute-start(bf16[256,256]{1,0:T(8,128)(2,1)S(1)} %get-tuple-element.478), channel_id=1, source_target_pairs={{0,4},{2,6},{4,0},{6,2},{1,5},{3,7},{5,1},{7,3},{8,12},{10,14},{12... | collective-permute-start | bytes 393224 | tf_op jit(solution)/shard_map/ppermute | solution.py:40
  (174 other events, 1460.7 us)

commit v3 on v2

--- a/solution.py
+++ b/solution.py
@@ -200,33 +200,32 @@
     )(me, *a, *b, *c)
 
 
-def lay_out_kernel(me, low, high, wo, wu):
+def lay_out_kernel(last, me, low, high, out):
     x0, z0, y0 = me[1], me[2], me[3]
-    q = low.shape[3] // 2
+    q = low.shape[3]
     for yr in range(2):
-        src = (low, high)[yr]
         for xr in range(2):
             for zr in range(4):
-                v = src[xr, zr % 2, zr // 2]
                 row = (z0 ^ zr) * DH + ((x0 ^ xr) * 2 + (y0 ^ yr)) * q
-                rows = pl.ds(pl.multiple_of(row, q), q)
-                wo[rows, :] = v[0:q]
-                wu[rows, :] = v[q : 2 * q]
-
-
-def lay_out_tables(me, low, high):
-    one = jax.ShapeDtypeStruct((KEEP, D), BF)
-    return pl.pallas_call(
-        lay_out_kernel,
+                if last == "y":
+                    v = (low, high)[yr][zr % 2, xr, zr // 2]
+                else:
+                    v = (low, high)[zr % 2][yr, xr, zr // 2]
+                out[pl.ds(pl.multiple_of(row, q), q), :] = v
+
+
+def lay_out_table(last, me, low, high):
+    return pl.pallas_call(
+        functools.partial(lay_out_kernel, last),
         grid_spec=pltpu.PrefetchScalarGridSpec(
             num_scalar_prefetch=1,
             grid=(1,),
             in_specs=[full(low.shape), full(high.shape)],
-            out_specs=[full((KEEP, D))] * 2,
+            out_specs=full((KEEP, D)),
         ),
-        out_shape=[one, one],
+        out_shape=jax.ShapeDtypeStruct((KEEP, D), BF),
         name="lay_out",
-        **params(moved=4 * 2**20),
+        **params(moved=2 * 2**20),
     )(me, low, high)
 
 
@@ -614,7 +613,7 @@
 TILE = 4 * DH
 
 
-def mlp_kernel(h0, h1, d0, d1, u0, u1, w0, w1, *refs):
+def mlp_kernel(h0, h1, d0, d1, u0, u1, w0, w1, r0, r1, *refs):
     a_keep, a_send, b_keep, b_send, c_keep, c_send, o0, o1, e0, e1 = refs[:10]
     accs = refs[10:]
     t = pl.program_id(0)
@@ -625,8 +624,11 @@
         for ref in accs:
             ref[...] = jnp.zeros_like(ref)
 
-    wu = jnp.where(in_y == 0, u0[...], u1[...])
-    wd = jnp.concatenate([w0[...], w1[...]], axis=0)
+    rest = jnp.where(in_x == 0, r0[...], r1[...]).reshape(4, 2 * REST, D)
+    wu = jnp.where(in_y == 0, u0[...], u1[...]).reshape(4 * MAIN, D)
+    wu = jnp.concatenate([wu, rest[:, 0:REST].reshape(4 * REST, D)], axis=0)
+    wd = [w0[...].reshape(2 * MAIN, D), w1[...].reshape(2 * MAIN, D)]
+    wd = jnp.concatenate(wd + [rest[:, REST:].reshape(4 * REST, D)], axis=0)
     kept = []
     for r in range(2):
         h = (h0, h1)[r]
@@ -641,37 +643,38 @@
         kept.append((g, du))
     gd = (mm_tn(kept[0][0], d0[...]) + mm_tn(kept[1][0], d1[...])).astype(BF)
     gu = (mm_tn(kept[0][1], h0[...]) + mm_tn(kept[1][1], h1[...])).astype(BF)
-    gd, gu = gd.reshape(4, DH, D), gu.reshape(4, DH, D)
+    gd_rest, gu_rest = (v[4 * MAIN :].reshape(4, REST, D) for v in (gd, gu))
+    gd, gu = (v[0 : 4 * MAIN].reshape(4, MAIN, D) for v in (gd, gu))
     for z1 in range(2):
         side = (c_keep, c_send)[z1]
         for z2 in range(2):
-            side[0, 0, z2, 0:REST, :] = gu[2 * z1 + z2, MAIN:, :]
-            side[0, 0, z2, REST:, :] = gd[2 * z1 + z2, MAIN:, :]
+            side[0, 0, z2, 0:REST, :] = gu_rest[2 * z1 + z2]
+            side[0, 0, z2, REST:, :] = gd_rest[2 * z1 + z2]
     for bit in range(2):
 
         @pl.when(in_x == bit)
         def _():
             for z in range(4):
-                (a_keep, a_send)[bit][0, z // 2, z % 2] = gu[z, 0:MAIN, :]
+                (a_keep, a_send)[bit][0, z // 2, z % 2] = gu[z]
 
         @pl.when(in_y == bit)
         def _():
             for z in range(4):
-                (b_keep, b_send)[bit][z // 2, 0, z % 2] = gd[z, 0:MAIN, :]
+                (b_keep, b_send)[bit][z // 2, 0, z % 2] = gd[z]
 
     @pl.when(t == pl.num_programs(0) - 1)
     def _():
-        o0[...] = accs[0][...]
-        o1[...] = accs[1][...].astype(BF)
-        e0[...] = accs[2][...]
-        e1[...] = accs[3][...].astype(BF)
-
-
-def mlp(h0, h1, d0, d1, u0, u1, w0, w1):
+        for ref, acc in zip((o0, o1, e0, e1), accs):
+            ref[...] = acc[...].astype(BF)
+
+
+def mlp(h0, h1, d0, d1, u0, u1, w0, w1, r0, r1):
     act = full((BLK, D))
-    up0 = pl.BlockSpec((TILE, D), lambda t: (t // 2, 0))
-    up1 = pl.BlockSpec((TILE, D), lambda t: (t // 2, 0))
-    down = pl.BlockSpec((TILE // 2, D), lambda t: ((t % 2) * 2 + t // 2, 0))
+    up = pl.BlockSpec((1, 2, 2, MAIN, D), lambda t: (t // 2, 0, 0, 0, 0))
+    down = pl.BlockSpec((1, 1, 2, MAIN, D), lambda t: (t % 2, t // 2, 0, 0, 0))
+    rest_block = (2, 1, 2, 2 * REST, D)
+    rest0 = pl.BlockSpec(rest_block, lambda t: (0, jnp.minimum(t, 1), 0, 0, 0))
+    rest1 = pl.BlockSpec(rest_block, lambda t: (0, jnp.maximum(t - 2, 0), 0, 0, 0))
     tail = (MAIN, D)
     a_keep = pl.BlockSpec((1, 2, 2) + tail, lambda t: (jnp.minimum(t, 1), 0, 0, 0, 0))
     a_send = pl.BlockSpec((1, 2, 2) + tail, lambda t: (jnp.maximum(t - 2, 0), 0, 0, 0, 0))
@@ -683,20 +686,15 @@
     return pl.pallas_call(
         mlp_kernel,
         grid=(4,),
-        in_specs=[act] * 4 + [up0, up1, down, down],
+        in_specs=[act] * 4 + [up, up, down, down, rest0, rest1],
         out_specs=[a_keep, a_send, b_keep, b_send, c_spec, c_spec] + [act] * 4,
         scratch_shapes=[pltpu.VMEM((BLK, D), F32)] * 4,
         out_shape=[big_shape] * 4
         + [rest_shape] * 2
-        + [
-            jax.ShapeDtypeStruct((BLK, D), F32),
-            jax.ShapeDtypeStruct((BLK, D), BF),
-            jax.ShapeDtypeStruct((BLK, D), F32),
-            jax.ShapeDtypeStruct((BLK, D), BF),
-        ],
+        + [jax.ShapeDtypeStruct((BLK, D), BF)] * 4,
         name="mlp",
         **params(flops=12 * D * D * 2 * D, moved=26 * 2**20, vmem=VMEM_MLP),
-    )(h0, h1, d0, d1, u0, u1, w0, w1)
+    )(h0, h1, d0, d1, u0, u1, w0, w1, r0, r1)
 
 
 def halves_kernel(*refs):
@@ -740,11 +738,13 @@
 
 def mid_back_kernel(mid, gain, e_own, e_got, d_own, o_own, o_got, dmid, da, out, gsum):
     rows = mid[...]
-    back, gain_rows = norm_back(rows, gain[...], e_own[...] + e_got[...].astype(F32))
+    back, gain_rows = norm_back(
+        rows, gain[...], e_own[...].astype(F32) + e_got[...].astype(F32)
+    )
     total = d_own[...].astype(F32) + back
     dmid[...] = total
     da[...] = total.astype(BF)
-    out[...] = (rows + o_own[...] + o_got[...].astype(F32)).astype(BF)
+    out[...] = (rows + o_own[...].astype(F32) + o_got[...].astype(F32)).astype(BF)
 
     @pl.when(pl.program_id(0) == 0)
     def _():
@@ -800,22 +800,32 @@
 
 def proj_back_kernel(me, a, b, w, own, oth):
     first = me[0] == 0
-    own[...] = mm_nt(jnp.where(first, a[...], b[...]), w[...])
+    own[...] = mm_nt(jnp.where(first, a[...], b[...]), w[...]).astype(BF)
     oth[...] = mm_nt(jnp.where(first, b[...], a[...]), w[...]).astype(BF)
 
 
-def proj_both_kernel(me, a, b, w, own, oth):
-    term = mm_nt(a[...], w[...])
-    own[...] = term
-    oth[...] = term.astype(BF)
+def proj_one_kernel(a, w, own):
+    own[...] = mm_nt(a[...], w[...]).astype(BF)
+
+
+def proj_one(a, w):
+    rows = a.shape[0]
+    return pl.pallas_call(
+        proj_one_kernel,
+        grid=(4,),
+        in_specs=[full(a.shape), pl.BlockSpec((D // 4, 3 * KEEP), lambda t: (t, 0))],
+        out_specs=pl.BlockSpec((rows, D // 4), lambda t: (0, t)),
+        out_shape=jax.ShapeDtypeStruct((rows, D), BF),
+        name="proj_one",
+        **params(),
+    )(a, w)
 
 
 def proj_back(me, a, b, w):
-    kernel = proj_both_kernel if b is None else proj_back_kernel
     rows = a.shape[0] // 2 if b is a else a.shape[0]
     side = 1 if b is a else 0
     return pl.pallas_call(
-        kernel,
+        proj_back_kernel,
         grid_spec=pltpu.PrefetchScalarGridSpec(
             num_scalar_prefetch=1,
             grid=(4,),
@@ -826,21 +836,20 @@
             ],
             out_specs=[pl.BlockSpec((rows, D // 4), lambda t, me: (0, t))] * 2,
         ),
-        out_shape=[
-            jax.ShapeDtypeStruct((rows, D), F32),
-            jax.ShapeDtypeStruct((rows, D), BF),
-        ],
+        out_shape=[jax.ShapeDtypeStruct((rows, D), BF)] * 2,
         name="proj_back",
         **params(),
-    )(me, a, a if b is None else b, w)
+    )(me, a, b, w)
 
 
 def state_back_kernel(me, *refs):
     state1, gain, own, got, ds2, gate, wu, os0, os1, dz1, zz1, state0, zz0 = refs[:13]
     ds1, dos0, grad_wu, gate_sum, acc = refs[13:]
     t = pl.program_id(0)
-    last = ds2[...]
-    back = norm_back(state1[...], gain[...], own[...] + got[...].astype(F32))[0]
+    last = ds2[...].astype(F32)
+    back = norm_back(
+        state1[...], gain[...], own[...].astype(F32) + got[...].astype(F32)
+    )[0]
     total = gate[...] * last + back
     ds1[...] = total
     dz0 = ((1.0 - gate[...]) * total).astype(BF)
@@ -855,7 +864,8 @@
 
     @pl.when(t // 2 == me[0])
     def _():
-        terms = last * (state1[...] - zz1[...]) + total * (state0[...] - zz0[...])
+        step = state0[...].astype(F32) - zz0[...].astype(F32)
+        terms = last * (state1[...] - zz1[...].astype(F32)) + total * step
         gate_sum[...] += eight_rows(terms)
 
     @pl.when(t == 3)
@@ -890,7 +900,9 @@
 
 
 def row_back_kernel(me, values, gain, own, got, scale, base, out):
-    back = norm_back(values[...].astype(F32), gain[...], own[...] + got[...].astype(F32))[0]
+    back = norm_back(
+        values[...].astype(F32), gain[...], own[...].astype(F32) + got[...].astype(F32)
+    )[0]
     out[...] = (scale[...] * base[...] + back).astype(BF)
 
 
@@ -1130,30 +1142,40 @@
     x_own = pick(tokens, g_tokens)
     x_oth = xch(x_own, "c")
     ho = pick(ho, g_piece)
-
-    ga, gb, gc, half, ho, x_own, x_oth = fence(
-        got + [half, ho, x_own, x_oth], got + [half, x_oth]
+    hid = w_up.shape[0] // 4
+    hid_at = (c * 2 + y) * hid
+    hu = lax.dynamic_slice_in_dim(w_up, hid_at, hid, 0)
+    hd = lax.dynamic_slice_in_dim(w_down, hid_at, hid, 0)
+    hm = jnp.concatenate([hu[:MAIN], hd[:MAIN], hu[MAIN:], hd[MAIN:]])
+
+    def three(value):
+        return value[:MAIN], value[MAIN : 2 * MAIN], value[2 * MAIN :]
+
+    def stacks(held, got):
+        return [jnp.stack([h, g]) for h, g in zip(held, got)]
+
+    def sends(held, bits):
+        return [xch(h, b) for h, b in zip(held, bits)]
+
+    ga, gb, gc, half, ho, x_own, x_oth, hm = fence(
+        got + [half, ho, x_own, x_oth, hm], got + [half, x_oth]
     )
     half = half[:1] + [to_slot(slot(states, 1), 1)] + half[1:]
     ha, hb, hc = jnp.stack([ha, ga]), jnp.stack([hb, gb]), jnp.stack([hc, gc])
     got = [xch(ha, "x"), xch(hb, "y"), xch(hc, "z1")]
     half = jnp.concatenate(half)
-    state0 = by_block(half, xch(half, "c")).astype(F32)
+    state0 = by_block(half, xch(half, "c"))
     rows = by_block(x_own, x_oth).astype(F32)
     x_hat = norm_parts(rows)[0]
-    s_hat = norm_parts(state0)[0]
+    s_hat = norm_parts(state0.astype(F32))[0]
     go = xch(ho, "z2")
 
-    hid = w_up.shape[0] // 4
-    hid_at = (c * 2 + y) * hid
-    hu = lax.dynamic_slice_in_dim(w_up, hid_at, hid, 0)
-    hd = lax.dynamic_slice_in_dim(w_down, hid_at, hid, 0)
-    got, go, hu, hd, x_hat, s_hat, d_out, d_state_next = fence(
-        (got, go, hu, hd, x_hat, s_hat, d_out, d_state_next), (got, x_hat, s_hat)
+    got, go, hm, x_hat, s_hat, d_out, d_state_next = fence(
+        (got, go, hm, x_hat, s_hat, d_out, d_state_next), (got, x_hat, s_hat)
     )
     ho = jnp.stack([ho, go])
-    go = xch(ho, "z1")
-    gm = [xch(hu, "z2"), xch(hd, "z2")]
+    gm = xch(hm, "z2")
+    go = xch(ho, "x")
     g_states = diag_send(d_state_next)
     w_tok_l, w_state_l, small_all = lay_tables(me, (ha, got[0]), (hb, got[1]), (hc, got[2]))
     vectors = small_all[:, :4, :DH].transpose(1, 0, 2).reshape(4, D).astype(F32)
@@ -1162,12 +1184,12 @@
     xn = (x_hat * g_tok).astype(BF)
     proj = mm(xn, w_tok_l).astype(BF)
 
-    go, gm, g_states, proj, small_all = fence(
-        (go, gm, g_states, proj, small_all), (go, g_states, proj)
-    )
+    go, g_states, proj, small_all = fence((go, g_states, proj, small_all), (go, proj))
     ho = jnp.stack([ho, go])
-    go = xch(ho, "x")
+    tu, to = ho[:, :, quarter:], ho[:, :, :quarter]
+    gt, go = xch(tu, "z1"), xch(to, "y")
     d_states = pick(d_state_next, g_states)
+    d_rows = [slot(d_states, 0)] + [to_slot(slot(d_states, k), k) for k in (1, 2)]
     sn0 = (s_hat * g_state).astype(BF)
     r0 = mm(sn0, w_state_l).astype(BF)
     rel_rows = small_all[:, 4, :NB].reshape(HL, 2, NB)
@@ -1175,34 +1197,41 @@
     hot = jnp.asarray(slab_buckets())[None, :] == jnp.arange(NB, dtype=jnp.int32)[:, None]
     base = mm(rel_mine, hot.astype(BF)).reshape(HL, 8, BLK)
     bias = bias_tables(base)
-
-    go, gm, r0, bias, d_states = fence((go, gm, r0, bias, d_states), (go, gm, r0, bias))
-    ho = jnp.stack([ho, go])
-    go = xch(ho, "y")
-    hu, hd = jnp.stack([hu, gm[0]]), jnp.stack([hd, gm[1]])
-    gm = [xch(hu, "z1"), xch(hd, "x")]
     os0, log_s0 = mem_forward(0, proj, r0)
+
+    gt, go, gm, r0, os0, bias, d_states, d_rows = fence(
+        (gt, go, gm, r0, os0, bias, d_states, d_rows), (gt, gm, os0, bias)
+    )
+    d_rows = d_rows + [to_slot(slot(d_states, 3), 3)]
+    tu = jnp.stack([tu, gt])
+    gt = xch(tu, "y")
+    hm = stacks(three(hm), three(gm))
+    gm = sends(hm, ("z1", "x", "y"))
+    to = jnp.stack([to, go])
     ot0, log_t0 = tok_forward(0, proj, r0, bias)
 
-    go, gm, os0, ot0, d_states = fence((go, gm, os0, ot0, d_states), (go, gm, os0, ot0))
-    wo, wu = lay_out_tables(me, ho, go)
-    hu, hd = jnp.stack([hu, gm[0]]), jnp.stack([hd, gm[1]])
-    gm = [xch(hu, "x"), xch(hd, "y")]
-    d_half = [slot(d_states, 0)] + [to_slot(slot(d_states, k), k) for k in range(1, slots)]
+    to, gt, gm, os0, ot0, d_half = fence((to, gt, gm, os0, ot0, d_rows), (gt, os0, ot0))
+    wu = lay_out_table("y", me, tu, gt)
+    hm = stacks(hm, gm)
+    gm = sends(hm, ("x", "y", "z1"))
+    go = xch(to, "z1")
     zp0 = mm(os0, wu)
     zz0 = zp0 + xch(zp0.astype(BF), "c").astype(F32)
-    state1 = gate * state0 + (1.0 - gate) * zz0
+    zz0_kept = zz0.astype(BF)
+    state1 = gate * state0.astype(F32) + (1.0 - gate) * zz0
     sn1 = (norm_parts(state1)[0] * g_state).astype(BF)
     r1 = mm(sn1, w_state_l).astype(BF)
     ot1, log_t1 = tok_forward(1, proj, r1, bias)
 
-    gm, ot1, r1, d_out, d_half = fence((gm, ot1, r1, d_out, d_half), (gm, ot1, d_half))
-    hu, hd = jnp.stack([hu, gm[0]]), jnp.stack([hd, gm[1]])
-    gm = [xch(hu, "y"), xch(hd, "z1")]
+    gm, go, ot1, r1, d_out, d_half = fence(
+        (gm, go, ot1, r1, d_out, d_half), (gm, ot1, d_half)
+    )
+    wo = lay_out_table("z", me, to, go)
+    hm = stacks(hm, gm)
+    gm = sends(hm, ("y", "z1", "x"))
     d_half = jnp.concatenate(d_half)
-    ds2 = by_block(d_half, xch(d_half, "c")).astype(F32)
-    d_own = pick(d_out, diag_send(d_out))
-    d_oth = xch(d_own, "c")
+    ds2 = by_block(d_half, xch(d_half, "c"))
+    g_dout = diag_send(d_out)
     part0, part1 = mm(ot0, wo), mm(ot1, wo)
     part_own = jnp.where(c == 0, part0, part1)
     part_oth = jnp.where(c == 0, part1, part0).astype(BF)
@@ -1214,24 +1243,27 @@
     zz1 = my_half(zp1) + xch(other_half(zp1).astype(BF), "c").astype(F32)
     state1_half = my_half(state1)
     state2_half = (gate * state1_half + (1.0 - gate) * zz1).astype(BF)
-    dz1 = ((1.0 - gate) * ds2).astype(BF)
+    dz1 = ((1.0 - gate) * ds2.astype(F32)).astype(BF)
     dos1 = mm_nt(dz1, wu).astype(BF)
     dm1, dt1 = mem_backward(1, proj, r1, dos1, log_s1)
 
-    gm, h_own, h_oth, d_own, d_oth, state2_half = fence(
-        (gm, h_own, h_oth, d_own, d_oth, state2_half),
-        (gm, h_own, h_oth, d_own, d_oth, state2_half, dm1),
-    )
+    gm, h_own, h_oth, g_dout, state2_half = fence(
+        (gm, h_own, h_oth, g_dout, state2_half), (gm, h_own, h_oth, g_dout, state2_half, dm1)
+    )
+    d_own = pick(d_out, g_dout)
+    d_oth = xch(d_own, "c")
     out_rows = slot_spread(state2_half.reshape(slots, srows, D))
     ma, ma_out, mb, mb_out, mc, mc_out, o_own, o_oth, e_own, e_oth = mlp(
         h_own,
         h_oth,
         d_own,
         d_oth,
-        hu.reshape(-1, D),
-        gm[0].reshape(-1, D),
-        hd.reshape(-1, D),
-        gm[1].reshape(-1, D),
+        hm[0],
+        gm[0],
+        hm[1],
+        gm[1],
+        hm[2],
+        gm[2],
     )
 
     out_rows, ma_out, mb_out, mc_out, o_oth, e_oth = fence(
@@ -1252,8 +1284,8 @@
     (ma, mb, mc), sends = add_halves((ma, mb, mc), got)
     got = [xch(s, b) for s, b in zip(sends, ("y", "z1", "x"))]
     got += [diag_send(output), diag_send(state_next)]
-    dsn1, dsn1_send = proj_back(me, dr1, None, w_state_l)
-    dsn1_got = xch(dsn1_send, "c")
+    dsn1 = proj_one(dr1, w_state_l)
+    dsn1_got = xch(dsn1, "c")
     dm0, dt0, rel0 = tok_backward(0, proj, r0, bias, dot_all, log_t0, dprev)
 
     got, dm0, dt0, dsn1, dsn1_got = fence((got, dm0, dt0, dsn1, dsn1_got), (got, dm0, dsn1_got))
@@ -1273,9 +1305,9 @@
         os0,
         os1,
         dz1,
-        zz1,
+        zz1.astype(BF),
         state0,
-        zz0,
+        zz0_kept,
     )
     grad_gate = jnp.sum(gate_rows, axis=0) * gate * (1.0 - gate)
     grad_g_mlp = jnp.sum(gain_rows, axis=0)
@@ -1374,7 +1406,7 @@
     outs = jnp.stack([outs, xch(outs, "x")])
     grad_tokens = pick(grad_tokens, got_t).astype(F32)
 
-    got_y, grad_rows, outs = fence((got_y, grad_rows, outs), (got_y, grad_rows, outs))
+    got_y, grad_rows, outs = fence((got_y, grad_rows, outs), (got_y,))
     both_t = jnp.stack([part, got_y])
     got_p = xch(both_t, "c")
     grad_state = slot_order(grad_rows)

time: 567 us -> 561 us (0.989)
  starting transfers between devices: 124 us -> 112 us
    ppermute x73 -> x77, starting transfers between devices: 71.3 us -> 62.1 us  [xch(): return lax.ppermute(value, axis, [(i, i ^ mask) for i in range(count)])]
    ppermute x73 -> x77, waiting for transfers between devices: 105 us -> 103 us  [xch(): return lax.ppermute(value, axis, [(i, i ^ mask) for i in range(count)])]
    unnamed x306 -> x338, local copies, waits for them, and re-layouts: 39.2 us -> 38.2 us
    pallas_call x5 -> x6, Pallas kernels: 50.9 us -> 50.1 us  [the longest x1 37.5 us: mlp(): pl.pallas_call(mlp_kernel, grid=(4,), in_specs=[act] * 4 + [up, up, down,...]
  transfers between devices with their start and end apart: 94 -> 98, of which waited for: 33 -> 33; matrix products, arithmetic and copies ran while one was open for 12% -> 13% of each run, Pallas kernels for 31% -> 31%
where the time goes in v3:
time: 561 us; the launch traced here: 553 us
  Pallas kernels  187 us (33%)
  waiting for transfers between devices  134 us (24%)
  starting transfers between devices  112 us (20%)
  other arithmetic  54.2 us (10%)
  local copies, waits for them, and re-layouts  48.8 us (9%)
  matrix products  13.8 us (2%)
    ppermute x77, waiting for transfers between devices, xch(): return lax.ppermute(value, axis, [(i, i ^ mask) for i in range(count)])  103 us
    ppermute x77, starting transfers between devices, xch(): return lax.ppermute(value, axis, [(i, i ^ mask) for i in range(count)])  62.1 us
    unnamed x338, local copies, waits for them, and re-layouts  38.2 us
    pallas_call x1, Pallas kernels, mlp(): pl.pallas_call(mlp_kernel, grid=(4,), in_specs=[act] * 4 + [up, up, down,...  37.5 us
    ppermute x9, starting transfers between devices, diag_send(): return lax.ppermute(value, ('c', 'x'), [(1, 2), (2, 1)])  36.6 us
    pallas_call x2, Pallas kernels, tok_backward(): pl.pallas_call(functools.partial(tok_bwd_kernel, has_prev), grid=(HL,), i...  22.6 us
    pallas_call x2, Pallas kernels, mem_backward(): pl.pallas_call(functools.partial(mem_bwd_kernel, final), grid=(HL,), in_s...  18.9 us
    ppermute x12, waiting for transfers between devices, to_slot(): return lax.ppermute(value, 's', [(i, i ^ k) for i in range(slots)])  16 us
  transfers between devices with their start and end apart: 98, of which 33 were waited for; matrix products, arithmetic and copies ran while one was open for 13% of the time, Pallas kernels for 31%

profile of v3, /device:TPU:1, one launch (start us, length us, event | category | flops | bytes accessed | tf_op | source)
XLA Modules:
  0.0 552.9 jit_solution(16439734784768750855)
XLA Ops:
  0.6 4.5 collective-permute-start.4
  10.1 2.4 collective-permute-start
  14.0 2.4 collective-permute-start.2
  17.3 6.4 %collective-permute-done = bf16[256,256]{1,0:T(8,128)(2,1)S(1)} collective-permute-done((bf16[256,256]{1,0:T(8,128)(2,1)S(1)}, bf16[256,256]{1,0:T(8,128)(2,1)S(1)}, u32[]{:S(2)}, u32[]{:S(2)}) %collective-permute-start) | collective-permute-done | bytes 131104 | tf_op jit(solution)/shard_map/ppermute | solution.py:40
  33.4 2.5 collective-permute-start.8
  35.9 4.8 collective-permute-start.9
  58.9 7.9 %collective-permute-done.13 = bf16[64,1024]{1,0:T(8,128)(2,1)S(1)} collective-permute-done((bf16[64,1024]{1,0:T(8,128)(2,1)}, bf16[64,1024]{1,0:T(8,128)(2,1)S(1)}, u32[]{:S(2)}, u32[]{:S(2)}) %collective-permute-start.13) | collective-permute-done | bytes 131104 | tf_op jit(solution)/shard_map/ppermute | solution.py:1099
  75.4 2.5 fusion.2
  78.0 2.5 collective-permute-start.20
  83.6 13.4 %collective-permute-done.18 = bf16[64,1024]{1,0:T(8,128)(2,1)S(1)} collective-permute-done((bf16[64,1024]{1,0:T(8,128)(2,1)S(1)}, bf16[64,1024]{1,0:T(8,128)(2,1)S(1)}, u32[]{:S(2)}, u32[]{:S(2)}) %collective-permute-start.18) | collective-permute-done | bytes 131104 | tf_op jit(solution)/shard_map/ppermute | solution.py:40
  99.3 5.2 collective-permute-start.22
  107.0 2.4 collective-permute-start.25
  110.0 3.6 convolution_convert_fusion.ko.vo.refs_0_.refs_3_.refs_4_.refs_6_.refs_7_.refs_8_.refs_9_
  119.7 5.4 mem_fwd.2
  125.8 10.2 %collective-permute-done.25 = bf16[256,1024]{1,0:T(8,128)(2,1)S(1)} collective-permute-done((bf16[256,1024]{1,0:T(8,128)(2,1)S(1)}, bf16[256,1024]{1,0:T(8,128)(2,1)S(1)}, u32[]{:S(2)}, u32[]{:S(2)}) %collective-permute-start.25) | collective-permute-done | bytes 524320 | tf_op jit(solution)/shard_map/ppermute | solution.py:40
  136.0 2.9 collective-permute-done.26
  143.1 5.2 tok_fwd.2
  149.2 2.6 collective-permute-done.32
  151.8 6.5 %collective-permute-done.31 = bf16[2,64,1024]{2,1,0:T(8,128)(2,1)S(1)} collective-permute-done((bf16[2,64,1024]{2,1,0:T(8,128)(2,1)S(1)}, bf16[2,64,1024]{2,1,0:T(8,128)(2,1)S(1)}, u32[]{:S(2)}, u32[]{:S(2)}) %collective-permute-start.31) | collective-permute-done | bytes 262176 | tf_op jit(solution)/shard_map/ppermute | solution.py:40
  159.0 2.4 fusion.57
  166.5 2.8 fusion.53
  173.8 6.8 %tok_fwd.3 = (bf16[512,512]{1,0:T(8,128)(2,1)S(1)}, f32[512,128]{1,0:T(8,128)S(1)}) custom-call(bf16[1024,1536]{1,0:T(8,128)(2,1)S(1)} %convolution_convert_fusion.ko.vo.refs_0_.refs_3_.refs_4_.refs_6_.refs_7_.refs_8_.refs_9_, bf16[512,1536]{1,0:T(8,128)(2,1)S(1)} %convolution_convert_fusion.1.refs_1_.refs_2_.q.ks.vs.refs_0_, ...), custom_call_target="tpu_custom_call" | custom-call | flops 134217728 | bytes 838860 | tf_op jit(solution)/shard_map/tok_fwd/pallas_call | solution.py:337
  180.7 8.7 %collective-permute-done.36.high = bf16[2,2,2,32,1024]{4,3,2,1,0:T(8,128)(2,1)S(1)} collective-permute-done((bf16[2,2,2,32,1024]{4,3,2,1,0:T(8,128)(2,1)S(1)}, bf16[2,2,2,32,1024]{4,3,2,1,0:T(8,128)(2,1)S(1)}, u32[]{:S(2)}, u32[]{:S(2)}) %collective-permute-start.36) | collective-permute-done | bytes 524320 | tf_op jit(solution)/shard_map/ppermute | solution.py:40
  197.3 5.4 mem_fwd.3
  204.1 2.5 collective-permute-start.43
  211.8 9.2 %mem_bwd.2 = (f32[512,1536]{1,0:T(8,128)S(1)}, f32[512,1024]{1,0:T(8,128)S(1)}) custom-call(bf16[512,1536]{1,0:T(8,128)(2,1)S(1)} %convolution_convert_fusion.1.refs_1_.refs_2_.q.ks.vs.refs_0_, bf16[512,1536]{1,0:T(8,128)(2,1)S(1)} %convolution_convert_fusion.1.refs_1_.refs_2_.q.ks.vs.refs_0_, ...), custom_call_target="tpu_custom_call" | custom-call | flops 268435456 | bytes 943718 | tf_op jit(solution)/shard_map/mem_bwd/pallas_call | solution.py:442
  222.4 5.3 collective-permute-done.43
  230.1 2.4 collective-permute-start.48
  233.5 37.5 %mlp.1 = (bf16[2,2,2,96,1024]{4,3,2,1,0:T(8,128)(2,1)}, bf16[2,2,2,96,1024]{4,3,2,1,0:T(8,128)(2,1)}, bf16[2,2,2,96,1024]{4,3,2,1,0:T(8,128)(2,1)}, bf16[2,2,2,9...) custom-call(bf16[512,1024]{1,0:T(8,128)(2,1)S(1)} %multiply_convert_, ...), custom_call_target="tpu_custom_call" | custom-call | flops 2576980480 | bytes 2726297 | tf_op jit(solution)/shard_map/mlp/pallas_call | solution.py:686
  279.3 6.4 %mid_back.1 = (f32[512,1024]{1,0:T(8,128)}, bf16[512,1024]{1,0:T(8,128)(2,1)}, bf16[512,1024]{1,0:T(8,128)(2,1)}, f32[8,1024]{1,0:T(8,128)}) custom-call(f32[512,1024]{1,0:T(8,128)} %copy-done.86, f32[1,1024]{1,0:T(1,128)} %get-tuple-element.591.gain, bf16[512,1024]{1,0:T(8,128)(2,1)} %copy-done.53, bf16[512,1024]{1,0:T(8,128)(2,1)} %copy-done.118, ...), custom_call_target="tpu_custom_call" | custom-call | tf_op jit(solution)/shard_map/mid_back/pallas_call | solution.py:758
  288.8 6.4 %out_back.1 = (bf16[1024,512]{1,0:T(8,128)(2,1)}, bf16[512,1024]{1,0:T(8,128)(2,1)}) custom-call(s32[4]{0:T(128)} %copy-done.76, bf16[512,1024]{1,0:T(8,128)(2,1)} %get-tuple-element.364.own, bf16[512,1024]{1,0:T(8,128)(2,1)} %collective-permute-done.55.oth, bf16[512,1024]{1,0:T(8,128)(2,1)} %copy-done.14, bf16[512,512]{1,0:T(8,128)(2,1)} %copy-done.41, ...), custom_call_target="tpu_custom_call" | custom-call | tf_op jit(solution)/shard_map/out_back/pallas_call | solution.py:784
  300.0 13.2 %tok_bwd.2 = (bf16[512,1536]{1,0:T(8,128)(2,1)S(1)}, bf16[512,1536]{1,0:T(8,128)(2,1)S(1)}, f32[512,1024]{1,0:T(8,128)S(1)}, f32[4,8,512]{2,1,0:T(8,128)S(1)}) custom-call(bf16[1024,1536]{1,0:T(8,128)(2,1)S(1)} %convolution_convert_fusion.ko.vo.refs_0_.refs_3_.refs_4_.refs_6_.refs_7_.refs_8_.refs_9_, bf16[512,1536]{1,0:T(8,128)(2,1)S(1)} %copy-done.1, ...), custom_call_target="tpu_custom_call" | custom-call | flops 335544320 | bytes 1258291 | tf_op jit(solution)/shard_map/tok_bwd/pallas_call | solution.py:588
  314.4 4.2 halves.6
  320.8 2.5 collective-permute-start.59
  323.3 2.5 proj_one.1.refs_2_
  327.5 5.2 collective-permute-done.58
  332.7 5.1 collective-permute-start.60
  337.8 9.4 %tok_bwd.3 = (f32[512,1024]{1,0:T(8,128)S(1)}, f32[512,1536]{1,0:T(8,128)S(1)}, f32[4,8,512]{2,1,0:T(8,128)S(1)}) custom-call(bf16[1024,1536]{1,0:T(8,128)(2,1)S(1)} %convolution_convert_fusion.ko.vo.refs_0_.refs_3_.refs_4_.refs_6_.refs_7_.refs_8_.refs_9_, bf16[512,1536]{1,0:T(8,128)(2,1)S(1)} %copy-done.3, bf16[512,1536]{1,0:T(8,128)(2,1)S(1)} %copy-done.3, ...), custom_call_target="tpu_custom_call" | custom-call | flops 335544320 | bytes 1258291 | tf_op jit(solution)/shard_map/tok_bwd/pallas_call | solution.py:588
  349.9 2.2 halves.7
  355.1 11.7 %state_back.1 = (f32[512,1024]{1,0:T(8,128)}, bf16[512,512]{1,0:T(8,128)(2,1)}, bf16[512,1024]{1,0:T(8,128)(2,1)}, f32[8,1024]{1,0:T(8,128)}) custom-call(s32[4]{0:T(128)} %copy-done.76, f32[512,1024]{1,0:T(8,128)} %copy-done.81, f32[1,1024]{1,0:T(1,128)} %get-tuple-element.590.refs_1_.gain, bf16[512,1024]{1,0:T(8,128)(2,1)} %copy-done.33, ...), custom_call_target="tpu_custom_call" | custom-call | tf_op jit(solution)/shard_map/state_back/pallas_call | solution.py:881
  378.3 2.4 collective-permute-start.67
  384.2 9.7 %mem_bwd.3 = (bf16[512,1536]{1,0:T(8,128)(2,1)S(1)}, bf16[512,1536]{1,0:T(8,128)(2,1)S(1)}) custom-call(bf16[512,1536]{1,0:T(8,128)(2,1)S(1)} %copy-done.4, bf16[512,1536]{1,0:T(8,128)(2,1)S(1)} %copy-done.4, bf16[512,1536]{1,0:T(8,128)(2,1)S(1)} %copy-done.4, ...), custom_call_target="tpu_custom_call" | custom-call | flops 268435456 | bytes 943718 | tf_op jit(solution)/shard_map/mem_bwd/pallas_call | solution.py:442
  394.0 10.3 %collective-permute-done.68 = bf16[64,1024]{1,0:T(8,128)(2,1)S(1)} collective-permute-done((bf16[64,1024]{1,0:T(8,128)(2,1)S(1)}, bf16[64,1024]{1,0:T(8,128)(2,1)S(1)}, u32[]{:S(2)}, u32[]{:S(2)}) %collective-permute-start.68) | collective-permute-done | bytes 131104 | tf_op jit(solution)/shard_map/ppermute | solution.py:40
  409.7 14.3 %proj_grad.1 = (bf16[2,2,2,272,256]{4,3,2,1,0:T(8,128)(2,1)}, bf16[2,2,2,272,256]{4,3,2,1,0:T(8,128)(2,1)}, bf16[2,2,2,256,256]{4,3,2,1,0:T(8,128)(2,1)}, bf16[2...) custom-call(s32[4]{0:T(128)} %copy-done.76, ...), custom_call_target="tpu_custom_call" | custom-call | flops 644245120 | bytes 1677721 | tf_op jit(solution)/shard_map/proj_grad/pallas_call | solution.py:968
  426.0 5.4 proj_back.2
  433.1 3.4 proj_back.3
  439.3 9.1 %collective-permute-done.72 = bf16[2,2,2,256,256]{4,3,2,1,0:T(8,128)(2,1)} collective-permute-done((bf16[2,2,2,256,256]{4,3,2,1,0:T(8,128)(2,1)}, bf16[2,2,2,256,256]{4,3,2,1,0:T(8,128)(2,1)}, u32[]{:S(2)}, u32[]{:S(2)}) %collective-permute-start.72) | collective-permute-done | bytes 1048608 | tf_op jit(solution)/shard_map/ppermute | solution.py:40
  452.5 4.0 halves.9
  462.3 3.4 collective-permute-start.89
  466.3 5.8 %row_back.2 = bf16[512,1024]{1,0:T(8,128)(2,1)} custom-call(s32[4]{0:T(128)} %copy-done.76, bf16[512,1024]{1,0:T(8,128)(2,1)} %copy-done.84, f32[1,1024]{1,0:T(1,128)} %get-tuple-element.589.gain, bf16[512,1024]{1,0:T(8,128)(2,1)} %copy-done.49, bf16[512,1024]{1,0:T(8,128)(2,1)} %collective-permute-done.74.got, f32[1,1024]{1,0:T(1,128)} %broadcast.130.scale, ...), custom_call_target="tpu_custom_call" | custom-call | tf_op jit(solution)/shard_map/row_back/pallas_call | solution.py:914
  472.1 4.4 collective-permute-done.79
  481.7 3.6 row_back.3
  487.9 8.3 %collective-permute-start.87 = (bf16[512,1024]{1,0:T(8,128)(2,1)}, bf16[512,1024]{1,0:T(8,128)(2,1)}, u32[]{:S(2)}, u32[]{:S(2)}) collective-permute-start(bf16[512,1024]{1,0:T(8,128)(2,1)} %row_back.2), channel_id=1, source_target_pairs={{1,8},{8,1},{3,10},{10,3},{5,12},{12,5},{7,14},{14,7},{17,24},{24,... | collective-permute-start | bytes 3145736 | tf_op jit(solution)/shard_map/ppermute | solution.py:44
  496.3 2.4 broadcast_select_fusion.2
  499.0 2.4 collective-permute-start.85
  503.8 2.8 place_mlp.1
  506.8 9.7 %collective-permute-done.85 = bf16[256,256]{1,0:T(8,128)(2,1)S(1)} collective-permute-done((bf16[256,256]{1,0:T(8,128)(2,1)S(1)}, bf16[256,256]{1,0:T(8,128)(2,1)S(1)}, u32[]{:S(2)}, u32[]{:S(2)}) %collective-permute-start.85) | collective-permute-done | bytes 131104 | tf_op jit(solution)/shard_map/ppermute | solution.py:40
  516.4 2.8 collective-permute-done.86
  521.1 2.5 collective-permute-start.93
  523.6 2.7 select_convert_fusion.1
  526.3 3.6 collective-permute-done.94
  531.4 2.7 collective-permute-start.97
  537.7 7.2 %collective-permute-done.95 = bf16[4,64,1024]{2,1,0:T(8,128)(2,1)S(1)} collective-permute-done((bf16[4,64,1024]{2,1,0:T(8,128)(2,1)S(1)}, bf16[4,64,1024]{2,1,0:T(8,128)(2,1)S(1)}, u32[]{:S(2)}, u32[]{:S(2)}) %collective-permute-start.95) | collective-permute-done | bytes 524320 | tf_op jit(solution)/shard_map/ppermute | solution.py:44
  546.0 4.4 place_proj.1
  (644 shorter events, 177.0 us)
Async XLA Ops:
  0.6 26.8 %collective-permute-start.4 = (bf16[512,1024]{1,0:T(8,128)(2,1)}, bf16[512,1024]{1,0:T(8,128)(2,1)S(1)}, u32[]{:S(2)}, u32[]{:S(2)}) collective-permute-start(bf16[512,1024]{1,0:T(8,128)(2,1)} %param.16), channel_id=1, source_target_pairs={{1,8},{8,1},{3,10},{10,3},{5,12},{12,5},{7,14},{14,7},{17,24},{24,... | collective-permute-start | bytes 3145736 | tf_op jit(solution)/shard_map/ppermute | solution.py:44
  5.2 22.3 %collective-permute-start.3 = (bf16[4,64,1024]{2,1,0:T(8,128)(2,1)}, bf16[4,64,1024]{2,1,0:T(8,128)(2,1)S(1)}, u32[]{:S(2)}, u32[]{:S(2)}) collective-permute-start(bf16[4,64,1024]{2,1,0:T(8,128)(2,1)} %param.17), channel_id=1, source_target_pairs={{1,8},{8,1},{3,10},{10,3},{5,12},{12,5},{7,14},{14,7},{17,24},{24,... | collective-permute-start | bytes 1572872 | tf_op jit(solution)/shard_map/ppermute | solution.py:44
  27.5 15.9 %collective-permute-start.5 = (bf16[2,272,256]{2,1,0:T(8,128)(2,1)S(1)}, bf16[2,272,256]{2,1,0:T(8,128)(2,1)S(1)}, u32[]{:S(2)}, u32[]{:S(2)}) collective-permute-start(bf16[2,272,256]{2,1,0:T(8,128)(2,1)S(1)} %get-tuple-element.576), channel_id=1, source_target_pairs={{0,2},{2,0},{4,6},{6,4},{1,3},{3,1},{5,7},{7,5},{8,10},{10,8},{12,... | collective-permute-start | bytes 835592 | tf_op jit(solution)/shard_map/ppermute | solution.py:40
  29.3 14.0 %collective-permute-start.6 = (bf16[2,256,256]{2,1,0:T(8,128)(2,1)S(1)}, bf16[2,256,256]{2,1,0:T(8,128)(2,1)S(1)}, u32[]{:S(2)}, u32[]{:S(2)}) collective-permute-start(bf16[2,256,256]{2,1,0:T(8,128)(2,1)S(1)} %get-tuple-element.584), channel_id=1, source_target_pairs={{0,1},{1,0},{2,3},{3,2},{4,5},{5,4},{6,7},{7,6},{8,9},{9,8},{10,11... | collective-permute-start | bytes 786440 | tf_op jit(solution)/shard_map/ppermute | solution.py:40
  45.0 21.8 %collective-permute-start.14 = (bf16[512,1024]{1,0:T(8,128)(2,1)S(1)}, bf16[512,1024]{1,0:T(8,128)(2,1)S(1)}, u32[]{:S(2)}, u32[]{:S(2)}) collective-permute-start(bf16[512,1024]{1,0:T(8,128)(2,1)S(1)} %broadcast_select_fusion.4.values), channel_id=1, source_target_pairs={{0,8},{8,0},{1,9},{9,1},{2,10},{10,2},{3,11},{11,3},{4,12},{12,4},... | collective-permute-start | bytes 3145736 | tf_op jit(solution)/shard_map/ppermute | solution.py:40
  47.1 19.7 %collective-permute-start.10 = (bf16[2,2,272,256]{3,2,1,0:T(8,128)(2,1)}, bf16[2,2,272,256]{3,2,1,0:T(8,128)(2,1)}, u32[]{:S(2)}, u32[]{:S(2)}) collective-permute-start(bf16[2,2,272,256]{3,2,1,0:T(8,128)(2,1)} %get-tuple-element.535), channel_id=1, source_target_pairs={{0,16},{16,0},{1,17},{17,1},{2,18},{18,2},{3,19},{19,3},{4,20},{20... | collective-permute-start | bytes 1671176 | tf_op jit(solution)/shard_map/ppermute | solution.py:40
  49.3 17.6 %collective-permute-start.11 = (bf16[2,2,256,256]{3,2,1,0:T(8,128)(2,1)}, bf16[2,2,256,256]{3,2,1,0:T(8,128)(2,1)}, u32[]{:S(2)}, u32[]{:S(2)}) collective-permute-start(bf16[2,2,256,256]{3,2,1,0:T(8,128)(2,1)} %get-tuple-element.568), channel_id=1, source_target_pairs={{0,2},{2,0},{4,6},{6,4},{1,3},{3,1},{5,7},{7,5},{8,10},{10,8},{12,... | collective-permute-start | bytes 1572872 | tf_op jit(solution)/shard_map/ppermute | solution.py:40
  52.0 14.8 %collective-permute-start.12 = (bf16[2,2,256,256]{3,2,1,0:T(8,128)(2,1)}, bf16[2,2,256,256]{3,2,1,0:T(8,128)(2,1)}, u32[]{:S(2)}, u32[]{:S(2)}) collective-permute-start(bf16[2,2,256,256]{3,2,1,0:T(8,128)(2,1)} %get-tuple-element.566), channel_id=1, source_target_pairs={{0,1},{1,0},{2,3},{3,2},{4,5},{5,4},{6,7},{7,6},{8,9},{9,8},{10,11... | collective-permute-start | bytes 1572872 | tf_op jit(solution)/shard_map/ppermute | solution.py:40
  68.1 30.0 %collective-permute-start.15 = (bf16[2,2,2,272,256]{4,3,2,1,0:T(8,128)(2,1)S(1)}, bf16[2,2,2,272,256]{4,3,2,1,0:T(8,128)(2,1)S(1)}, u32[]{:S(2)}, u32[]{:S(2)}) collective-permute-start(bf16[2,2,2,272,256]{4,3,2,1,0:T(8,128)(2,1)S(1)} %pad_maximum_fusion.3.a0), channel_id=1, source_target_pairs={{0,1},{1,0},{2,3},{3,2},{4,5},{5,4},{6,7},{7,6},{8,9},{9,8},{10,11... | collective-permute-start | bytes 3342344 | tf_op jit(solution)/shard_map/ppermute | solution.py:40
  69.7 27.4 %collective-permute-start.16 = (bf16[2,2,2,256,256]{4,3,2,1,0:T(8,128)(2,1)S(1)}, bf16[2,2,2,256,256]{4,3,2,1,0:T(8,128)(2,1)S(1)}, u32[]{:S(2)}, u32[]{:S(2)}) collective-permute-start(bf16[2,2,2,256,256]{4,3,2,1,0:T(8,128)(2,1)S(1)} %pad_maximum_fusion.4.b0), channel_id=1, source_target_pairs={{0,16},{16,0},{1,17},{17,1},{2,18},{18,2},{3,19},{19,3},{4,20},{20... | collective-permute-start | bytes 3145736 | tf_op jit(solution)/shard_map/ppermute | solution.py:40
  72.2 25.9 %collective-permute-start.17 = (bf16[2,2,2,256,256]{4,3,2,1,0:T(8,128)(2,1)S(1)}, bf16[2,2,2,256,256]{4,3,2,1,0:T(8,128)(2,1)S(1)}, u32[]{:S(2)}, u32[]{:S(2)}) collective-permute-start(bf16[2,2,2,256,256]{4,3,2,1,0:T(8,128)(2,1)S(1)} %pad_maximum_fusion.5.c0), channel_id=1, source_target_pairs={{0,2},{2,0},{4,6},{6,4},{1,3},{3,1},{5,7},{7,5},{8,10},{10,8},{12,... | collective-permute-start | bytes 3145736 | tf_op jit(solution)/shard_map/ppermute | solution.py:40
  73.7 23.4 %collective-permute-start.18 = (bf16[64,1024]{1,0:T(8,128)(2,1)S(1)}, bf16[64,1024]{1,0:T(8,128)(2,1)S(1)}, u32[]{:S(2)}, u32[]{:S(2)}) collective-permute-start(bf16[64,1024]{1,0:T(8,128)(2,1)S(1)} %broadcast_select_fusion.7), channel_id=1, source_target_pairs={{0,4},{2,6},{4,0},{6,2},{1,5},{3,7},{5,1},{7,3},{8,12},{10,14},{12... | collective-permute-start | bytes 393224 | tf_op jit(solution)/shard_map/ppermute | solution.py:40
  98.2 17.7 %collective-permute-start.21 = (bf16[2,64,1024]{2,1,0:T(8,128)(2,1)S(1)}, bf16[2,64,1024]{2,1,0:T(8,128)(2,1)S(1)}, u32[]{:S(2)}, u32[]{:S(2)}) collective-permute-start(bf16[2,64,1024]{2,1,0:T(8,128)(2,1)S(1)} %get-tuple-element.579), channel_id=1, source_target_pairs={{0,1},{1,0},{2,3},{3,2},{4,5},{5,4},{6,7},{7,6},{8,9},{9,8},{10,11... | collective-permute-start | bytes 786440 | tf_op jit(solution)/shard_map/ppermute | solution.py:40
  99.3 16.6 %collective-permute-start.22 = (bf16[4,64,1024]{2,1,0:T(8,128)(2,1)S(1)}, bf16[4,64,1024]{2,1,0:T(8,128)(2,1)S(1)}, u32[]{:S(2)}, u32[]{:S(2)}) collective-permute-start(bf16[4,64,1024]{2,1,0:T(8,128)(2,1)S(1)} %copy-done.133), channel_id=1, source_target_pairs={{1,8},{8,1},{3,10},{10,3},{5,12},{12,5},{7,14},{14,7},{17,24},{24,... | collective-permute-start | bytes 1572872 | tf_op jit(solution)/shard_map/ppermute | solution.py:44
  107.0 29.0 %collective-permute-start.25 = (bf16[256,1024]{1,0:T(8,128)(2,1)S(1)}, bf16[256,1024]{1,0:T(8,128)(2,1)S(1)}, u32[]{:S(2)}, u32[]{:S(2)}) collective-permute-start(bf16[256,1024]{1,0:T(8,128)(2,1)S(1)} %pad_maximum_fusion.14), channel_id=1, source_target_pairs={{0,4},{2,6},{4,0},{6,2},{1,5},{3,7},{5,1},{7,3},{8,12},{10,14},{12... | collective-permute-start | bytes 1572872 | tf_op jit(solution)/shard_map/ppermute | solution.py:40
  115.9 23.0 %collective-permute-start.23 = (bf16[2,2,32,1024]{3,2,1,0:T(8,128)(2,1)S(1)}, bf16[2,2,32,1024]{3,2,1,0:T(8,128)(2,1)S(1)}, u32[]{:S(2)}, u32[]{:S(2)}) collective-permute-start(bf16[2,2,32,1024]{3,2,1,0:T(8,128)(2,1)S(1)} %get-tuple-element.558), channel_id=1, source_target_pairs={{0,2},{2,0},{4,6},{6,4},{1,3},{3,1},{5,7},{7,5},{8,10},{10,8},{12,... | collective-permute-start | bytes 786440 | tf_op jit(solution)/shard_map/ppermute | solution.py:40
  116.4 22.5 %collective-permute-start.24 = (bf16[2,2,32,1024]{3,2,1,0:T(8,128)(2,1)S(1)}, bf16[2,2,32,1024]{3,2,1,0:T(8,128)(2,1)S(1)}, u32[]{:S(2)}, u32[]{:S(2)}) collective-permute-start(bf16[2,2,32,1024]{3,2,1,0:T(8,128)(2,1)S(1)} %get-tuple-element.557), channel_id=1, source_target_pairs={{0,16},{16,0},{1,17},{17,1},{2,18},{18,2},{3,19},{19,3},{4,20},{20... | collective-permute-start | bytes 786440 | tf_op jit(solution)/shard_map/ppermute | solution.py:40
  116.8 22.1 %collective-permute-start.26 = (bf16[64,1024]{1,0:T(8,128)(2,1)S(1)}, bf16[64,1024]{1,0:T(8,128)(2,1)S(1)}, u32[]{:S(2)}, u32[]{:S(2)}) collective-permute-start(bf16[64,1024]{1,0:T(8,128)(2,1)S(1)} %get-tuple-element.555), channel_id=1, source_target_pairs={{0,2},{2,0},{4,6},{6,4},{1,3},{3,1},{5,7},{7,5},{8,10},{10,8},{12,... | collective-permute-start | bytes 393224 | tf_op jit(solution)/shard_map/ppermute | solution.py:1099
  117.9 21.0 %collective-permute-start.27 = (bf16[64,1024]{1,0:T(8,128)(2,1)S(1)}, bf16[64,1024]{1,0:T(8,128)(2,1)S(1)}, u32[]{:S(2)}, u32[]{:S(2)}) collective-permute-start(bf16[64,1024]{1,0:T(8,128)(2,1)S(1)} %get-tuple-element.554), channel_id=1, source_target_pairs={{0,4},{2,6},{4,0},{6,2},{1,5},{3,7},{5,1},{7,3},{8,12},{10,14},{12... | collective-permute-start | bytes 393224 | tf_op jit(solution)/shard_map/ppermute | solution.py:1099
  139.0 19.3 %collective-permute-start.28 = (bf16[2,2,2,32,1024]{4,3,2,1,0:T(8,128)(2,1)S(1)}, bf16[2,2,2,32,1024]{4,3,2,1,0:T(8,128)(2,1)S(1)}, u32[]{:S(2)}, u32[]{:S(2)}) collective-permute-start(bf16[2,2,2,32,1024]{4,3,2,1,0:T(8,128)(2,1)S(1)} %pad_maximum_fusion.17.low), channel_id=1, source_target_pairs={{0,16},{16,0},{1,17},{17,1},{2,18},{18,2},{3,19},{19,3},{4,20},{20... | collective-permute-start | bytes 1572872 | tf_op jit(solution)/shard_map/ppermute | solution.py:40
  140.1 18.2 %collective-permute-start.29 = (bf16[2,96,1024]{2,1,0:T(8,128)(2,1)S(1)}, bf16[2,96,1024]{2,1,0:T(8,128)(2,1)S(1)}, u32[]{:S(2)}, u32[]{:S(2)}) collective-permute-start(bf16[2,96,1024]{2,1,0:T(8,128)(2,1)S(1)} %get-tuple-element.574), channel_id=1, source_target_pairs={{0,2},{2,0},{4,6},{6,4},{1,3},{3,1},{5,7},{7,5},{8,10},{10,8},{12,... | collective-permute-start | bytes 1179656 | tf_op jit(solution)/shard_map/ppermute | solution.py:40
  140.9 17.4 %collective-permute-start.30 = (bf16[2,96,1024]{2,1,0:T(8,128)(2,1)S(1)}, bf16[2,96,1024]{2,1,0:T(8,128)(2,1)S(1)}, u32[]{:S(2)}, u32[]{:S(2)}) collective-permute-start(bf16[2,96,1024]{2,1,0:T(8,128)(2,1)S(1)} %get-tuple-element.572), channel_id=1, source_target_pairs={{0,1},{1,0},{2,3},{3,2},{4,5},{5,4},{6,7},{7,6},{8,9},{9,8},{10,11... | collective-permute-start | bytes 1179656 | tf_op jit(solution)/shard_map/ppermute | solution.py:40
  141.7 16.6 %collective-permute-start.31 = (bf16[2,64,1024]{2,1,0:T(8,128)(2,1)S(1)}, bf16[2,64,1024]{2,1,0:T(8,128)(2,1)S(1)}, u32[]{:S(2)}, u32[]{:S(2)}) collective-permute-start(bf16[2,64,1024]{2,1,0:T(8,128)(2,1)S(1)} %get-tuple-element.578), channel_id=1, source_target_pairs={{0,16},{16,0},{1,17},{17,1},{2,18},{18,2},{3,19},{19,3},{4,20},{20... | collective-permute-start | bytes 786440 | tf_op jit(solution)/shard_map/ppermute | solution.py:40
  164.3 25.1 %collective-permute-start.33 = (bf16[2,2,96,1024]{3,2,1,0:T(8,128)(2,1)S(1)}, bf16[2,2,96,1024]{3,2,1,0:T(8,128)(2,1)S(1)}, u32[]{:S(2)}, u32[]{:S(2)}) collective-permute-start(bf16[2,2,96,1024]{3,2,1,0:T(8,128)(2,1)S(1)} %get-tuple-element.533), channel_id=1, source_target_pairs={{0,1},{1,0},{2,3},{3,2},{4,5},{5,4},{6,7},{7,6},{8,9},{9,8},{10,11... | collective-permute-start | bytes 2359304 | tf_op jit(solution)/shard_map/ppermute | solution.py:40
  164.5 24.9 %collective-permute-start.34 = (bf16[2,2,96,1024]{3,2,1,0:T(8,128)(2,1)S(1)}, bf16[2,2,96,1024]{3,2,1,0:T(8,128)(2,1)S(1)}, u32[]{:S(2)}, u32[]{:S(2)}) collective-permute-start(bf16[2,2,96,1024]{3,2,1,0:T(8,128)(2,1)S(1)} %get-tuple-element.531), channel_id=1, source_target_pairs={{0,16},{16,0},{1,17},{17,1},{2,18},{18,2},{3,19},{19,3},{4,20},{20... | collective-permute-start | bytes 2359304 | tf_op jit(solution)/shard_map/ppermute | solution.py:40
  164.9 15.8 %collective-permute-start.35 = (bf16[2,2,64,1024]{3,2,1,0:T(8,128)(2,1)S(1)}, bf16[2,2,64,1024]{3,2,1,0:T(8,128)(2,1)S(1)}, u32[]{:S(2)}, u32[]{:S(2)}) collective-permute-start(bf16[2,2,64,1024]{3,2,1,0:T(8,128)(2,1)S(1)} %get-tuple-element.549), channel_id=1, source_target_pairs={{0,2},{2,0},{4,6},{6,4},{1,3},{3,1},{5,7},{7,5},{8,10},{10,8},{12,... | collective-permute-start | bytes 1572872 | tf_op jit(solution)/shard_map/ppermute | solution.py:40
  165.4 24.1 %collective-permute-start.36 = (bf16[2,2,2,32,1024]{4,3,2,1,0:T(8,128)(2,1)S(1)}, bf16[2,2,2,32,1024]{4,3,2,1,0:T(8,128)(2,1)S(1)}, u32[]{:S(2)}, u32[]{:S(2)}) collective-permute-start(bf16[2,2,2,32,1024]{4,3,2,1,0:T(8,128)(2,1)S(1)} %copy-done.44), channel_id=1, source_target_pairs={{0,2},{2,0},{4,6},{6,4},{1,3},{3,1},{5,7},{7,5},{8,10},{10,8},{12,... | collective-permute-start | bytes 1572872 | tf_op jit(solution)/shard_map/ppermute | solution.py:40
  189.6 38.2 %collective-permute-start.38 = (bf16[2,2,2,96,1024]{4,3,2,1,0:T(8,128)(2,1)S(1)}, bf16[2,2,2,96,1024]{4,3,2,1,0:T(8,128)(2,1)S(1)}, u32[]{:S(2)}, u32[]{:S(2)}) collective-permute-start(bf16[2,2,2,96,1024]{4,3,2,1,0:T(8,128)(2,1)S(1)} %pad_maximum_fusion.1.u0), channel_id=1, source_target_pairs={{0,16},{16,0},{1,17},{17,1},{2,18},{18,2},{3,19},{19,3},{4,20},{20... | collective-permute-start | bytes 4718600 | tf_op jit(solution)/shard_map/ppermute | solution.py:40
  191.1 36.7 %collective-permute-start.39 = (bf16[2,2,2,96,1024]{4,3,2,1,0:T(8,128)(2,1)S(1)}, bf16[2,2,2,96,1024]{4,3,2,1,0:T(8,128)(2,1)S(1)}, u32[]{:S(2)}, u32[]{:S(2)}) collective-permute-start(bf16[2,2,2,96,1024]{4,3,2,1,0:T(8,128)(2,1)S(1)} %pad_maximum_fusion.2.w0), channel_id=1, source_target_pairs={{0,2},{2,0},{4,6},{6,4},{1,3},{3,1},{5,7},{7,5},{8,10},{10,8},{12,... | collective-permute-start | bytes 4718600 | tf_op jit(solution)/shard_map/ppermute | solution.py:40
  191.6 30.9 %collective-permute-start.40 = (bf16[2,2,2,64,1024]{4,3,2,1,0:T(8,128)(2,1)S(1)}, bf16[2,2,2,64,1024]{4,3,2,1,0:T(8,128)(2,1)S(1)}, u32[]{:S(2)}, u32[]{:S(2)}) collective-permute-start(bf16[2,2,2,64,1024]{4,3,2,1,0:T(8,128)(2,1)S(1)} %pad_maximum_fusion.6.r0), channel_id=1, source_target_pairs={{0,1},{1,0},{2,3},{3,2},{4,5},{5,4},{6,7},{7,6},{8,9},{9,8},{10,11... | collective-permute-start | bytes 3145736 | tf_op jit(solution)/shard_map/ppermute | solution.py:40
  204.1 23.6 %collective-permute-start.43 = (bf16[512,1024]{1,0:T(8,128)(2,1)S(1)}, bf16[512,1024]{1,0:T(8,128)(2,1)S(1)}, u32[]{:S(2)}, u32[]{:S(2)}) collective-permute-start(bf16[512,1024]{1,0:T(8,128)(2,1)S(1)} %copy-done.121), channel_id=1, source_target_pairs={{1,8},{8,1},{3,10},{10,3},{5,12},{12,5},{7,14},{14,7},{17,24},{24,... | collective-permute-start | bytes 3145736 | tf_op jit(solution)/shard_map/ppermute | solution.py:44
  208.8 19.0 %collective-permute-start.42 = (bf16[512,1024]{1,0:T(8,128)(2,1)S(1)}, bf16[512,1024]{1,0:T(8,128)(2,1)S(1)}, u32[]{:S(2)}, u32[]{:S(2)}) collective-permute-start(bf16[512,1024]{1,0:T(8,128)(2,1)S(1)} %multiply_convert_fusion.2.h0), channel_id=1, source_target_pairs={{0,8},{8,0},{1,9},{9,1},{2,10},{10,2},{3,11},{11,3},{4,12},{12,4},... | collective-permute-start | bytes 3145736 | tf_op jit(solution)/shard_map/ppermute | solution.py:40
  228.9 45.0 %collective-permute-start.46 = (bf16[64,1024]{1,0:T(8,128)(2,1)S(1)}, bf16[64,1024]{1,0:T(8,128)(2,1)S(1)}, u32[]{:S(2)}, u32[]{:S(2)}) collective-permute-start(bf16[64,1024]{1,0:T(8,128)(2,1)S(1)} %get-tuple-element.544), channel_id=1, source_target_pairs={{0,2},{2,0},{4,6},{6,4},{1,3},{3,1},{5,7},{7,5},{8,10},{10,8},{12,... | collective-permute-start | bytes 393224 | tf_op jit(solution)/shard_map/ppermute | solution.py:1099
  230.1 43.8 %collective-permute-start.47 = (bf16[64,1024]{1,0:T(8,128)(2,1)S(1)}, bf16[64,1024]{1,0:T(8,128)(2,1)S(1)}, u32[]{:S(2)}, u32[]{:S(2)}) collective-permute-start(bf16[64,1024]{1,0:T(8,128)(2,1)S(1)} %get-tuple-element.543), channel_id=1, source_target_pairs={{0,4},{2,6},{4,0},{6,2},{1,5},{3,7},{5,1},{7,3},{8,12},{10,14},{12... | collective-permute-start | bytes 393224 | tf_op jit(solution)/shard_map/ppermute | solution.py:1099
  230.1 43.9 %collective-permute-start.48 = (bf16[64,1024]{1,0:T(8,128)(2,1)S(1)}, bf16[64,1024]{1,0:T(8,128)(2,1)S(1)}, u32[]{:S(2)}, u32[]{:S(2)}) collective-permute-start(bf16[64,1024]{1,0:T(8,128)(2,1)S(1)} %get-tuple-element.542), channel_id=1, source_target_pairs={{0,6},{2,4},{4,2},{6,0},{1,7},{3,5},{5,3},{7,1},{8,14},{10,12},{12... | collective-permute-start | bytes 393224 | tf_op jit(solution)/shard_map/ppermute | solution.py:1099
  274.6 39.6 %collective-permute-start.50 = (bf16[2,2,2,96,1024]{4,3,2,1,0:T(8,128)(2,1)}, bf16[2,2,2,96,1024]{4,3,2,1,0:T(8,128)(2,1)}, u32[]{:S(2)}, u32[]{:S(2)}) collective-permute-start(bf16[2,2,2,96,1024]{4,3,2,1,0:T(8,128)(2,1)} %get-tuple-element.357), channel_id=1, source_target_pairs={{0,1},{1,0},{2,3},{3,2},{4,5},{5,4},{6,7},{7,6},{8,9},{9,8},{10,11... | collective-permute-start | bytes 4718600 | tf_op jit(solution)/shard_map/ppermute | solution.py:40
  276.7 37.6 %collective-permute-start.51 = (bf16[2,2,2,96,1024]{4,3,2,1,0:T(8,128)(2,1)}, bf16[2,2,2,96,1024]{4,3,2,1,0:T(8,128)(2,1)}, u32[]{:S(2)}, u32[]{:S(2)}) collective-permute-start(bf16[2,2,2,96,1024]{4,3,2,1,0:T(8,128)(2,1)} %get-tuple-element.358), channel_id=1, source_target_pairs={{0,16},{16,0},{1,17},{17,1},{2,18},{18,2},{3,19},{19,3},{4,20},{20... | collective-permute-start | bytes 4718600 | tf_op jit(solution)/shard_map/ppermute | solution.py:40
  286.2 28.1 %collective-permute-start.52 = (bf16[2,2,2,64,1024]{4,3,2,1,0:T(8,128)(2,1)}, bf16[2,2,2,64,1024]{4,3,2,1,0:T(8,128)(2,1)}, u32[]{:S(2)}, u32[]{:S(2)}) collective-permute-start(bf16[2,2,2,64,1024]{4,3,2,1,0:T(8,128)(2,1)} %get-tuple-element.359), channel_id=1, source_target_pairs={{0,2},{2,0},{4,6},{6,4},{1,3},{3,1},{5,7},{7,5},{8,10},{10,8},{12,... | collective-permute-start | bytes 3145736 | tf_op jit(solution)/shard_map/ppermute | solution.py:40
  318.6 14.1 %collective-permute-start.58 = (bf16[2,2,64,1024]{3,2,1,0:T(8,128)(2,1)S(1)}, bf16[2,2,64,1024]{3,2,1,0:T(8,128)(2,1)S(1)}, u32[]{:S(2)}, u32[]{:S(2)}) collective-permute-start(bf16[2,2,64,1024]{3,2,1,0:T(8,128)(2,1)S(1)} %bitcast.287), channel_id=1, source_target_pairs={{0,1},{1,0},{2,3},{3,2},{4,5},{5,4},{6,7},{7,6},{8,9},{9,8},{10,11... | collective-permute-start | bytes 1572872 | tf_op jit(solution)/shard_map/ppermute | solution.py:40
  320.8 29.1 %collective-permute-start.59 = (bf16[512,1024]{1,0:T(8,128)(2,1)S(1)}, bf16[512,1024]{1,0:T(8,128)(2,1)S(1)}, u32[]{:S(2)}, u32[]{:S(2)}) collective-permute-start(bf16[512,1024]{1,0:T(8,128)(2,1)S(1)} %copy-done.122), channel_id=1, source_target_pairs={{1,8},{8,1},{3,10},{10,3},{5,12},{12,5},{7,14},{14,7},{17,24},{24,... | collective-permute-start | bytes 3145736 | tf_op jit(solution)/shard_map/ppermute | solution.py:44
  325.9 24.0 %collective-permute-start.61 = (bf16[512,1024]{1,0:T(8,128)(2,1)S(1)}, bf16[512,1024]{1,0:T(8,128)(2,1)S(1)}, u32[]{:S(2)}, u32[]{:S(2)}) collective-permute-start(bf16[512,1024]{1,0:T(8,128)(2,1)S(1)} %proj_one.1.refs_2_), channel_id=1, source_target_pairs={{0,8},{8,0},{1,9},{9,1},{2,10},{10,2},{3,11},{11,3},{4,12},{12,4},... | collective-permute-start | bytes 3145736 | tf_op jit(solution)/shard_map/ppermute | solution.py:40
  326.0 23.9 %collective-permute-start.56 = (bf16[2,2,96,1024]{3,2,1,0:T(8,128)(2,1)S(1)}, bf16[2,2,96,1024]{3,2,1,0:T(8,128)(2,1)S(1)}, u32[]{:S(2)}, u32[]{:S(2)}) collective-permute-start(bf16[2,2,96,1024]{3,2,1,0:T(8,128)(2,1)S(1)} %bitcast.286), channel_id=1, source_target_pairs={{0,16},{16,0},{1,17},{17,1},{2,18},{18,2},{3,19},{19,3},{4,20},{20... | collective-permute-start | bytes 2359304 | tf_op jit(solution)/shard_map/ppermute | solution.py:40
  326.3 23.5 %collective-permute-start.57 = (bf16[2,2,96,1024]{3,2,1,0:T(8,128)(2,1)S(1)}, bf16[2,2,96,1024]{3,2,1,0:T(8,128)(2,1)S(1)}, u32[]{:S(2)}, u32[]{:S(2)}) collective-permute-start(bf16[2,2,96,1024]{3,2,1,0:T(8,128)(2,1)S(1)} %bitcast.285), channel_id=1, source_target_pairs={{0,2},{2,0},{4,6},{6,4},{1,3},{3,1},{5,7},{7,5},{8,10},{10,8},{12,... | collective-permute-start | bytes 2359304 | tf_op jit(solution)/shard_map/ppermute | solution.py:40
  332.7 17.1 %collective-permute-start.60 = (bf16[4,64,1024]{2,1,0:T(8,128)(2,1)S(1)}, bf16[4,64,1024]{2,1,0:T(8,128)(2,1)S(1)}, u32[]{:S(2)}, u32[]{:S(2)}) collective-permute-start(bf16[4,64,1024]{2,1,0:T(8,128)(2,1)S(1)} %bitcast.293), channel_id=1, source_target_pairs={{1,8},{8,1},{3,10},{10,3},{5,12},{12,5},{7,14},{14,7},{17,24},{24,... | collective-permute-start | bytes 1572872 | tf_op jit(solution)/shard_map/ppermute | solution.py:44
  353.6 14.7 %collective-permute-start.62 = (bf16[2,96,1024]{2,1,0:T(8,128)(2,1)}, bf16[2,96,1024]{2,1,0:T(8,128)(2,1)}, u32[]{:S(2)}, u32[]{:S(2)}) collective-permute-start(bf16[2,96,1024]{2,1,0:T(8,128)(2,1)} %bitcast.90), channel_id=1, source_target_pairs={{0,2},{2,0},{4,6},{6,4},{1,3},{3,1},{5,7},{7,5},{8,10},{10,8},{12,... | collective-permute-start | bytes 1179656 | tf_op jit(solution)/shard_map/ppermute | solution.py:40
  370.6 33.6 %collective-permute-start.65 = (bf16[2,2,2,2,32,1024]{5,4,3,2,1,0:T(8,128)(2,1)}, bf16[2,2,2,2,32,1024]{5,4,3,2,1,0:T(8,128)(2,1)}, u32[]{:S(2)}, u32[]{:S(2)}) collective-permute-start(bf16[2,2,2,2,32,1024]{5,4,3,2,1,0:T(8,128)(2,1)} %dynamic-slice_bitcast_fusion), channel_id=1, source_target_pairs={{0,16},{16,0},{1,17},{17,1},{2,18},{18,2},{3,19},{19,3},{4,20},{20... | collective-permute-start | bytes 3145736 | tf_op jit(solution)/shard_map/ppermute | solution.py:40
  378.2 26.0 %collective-permute-start.66 = (bf16[96,1024]{1,0:T(8,128)(2,1)S(1)}, bf16[96,1024]{1,0:T(8,128)(2,1)S(1)}, u32[]{:S(2)}, u32[]{:S(2)}) collective-permute-start(bf16[96,1024]{1,0:T(8,128)(2,1)S(1)} %get-tuple-element.414), channel_id=1, source_target_pairs={{0,4},{2,6},{4,0},{6,2},{1,5},{3,7},{5,1},{7,3},{8,12},{10,14},{12... | collective-permute-start | bytes 589832 | tf_op jit(solution)/shard_map/ppermute | solution.py:40
  378.3 25.9 %collective-permute-start.67 = (bf16[96,1024]{1,0:T(8,128)(2,1)S(1)}, bf16[96,1024]{1,0:T(8,128)(2,1)S(1)}, u32[]{:S(2)}, u32[]{:S(2)}) collective-permute-start(bf16[96,1024]{1,0:T(8,128)(2,1)S(1)} %get-tuple-element.415), channel_id=1, source_target_pairs={{0,4},{2,6},{4,0},{6,2},{1,5},{3,7},{5,1},{7,3},{8,12},{10,14},{12... | collective-permute-start | bytes 589832 | tf_op jit(solution)/shard_map/ppermute | solution.py:40
  380.6 23.6 %collective-permute-start.68 = (bf16[64,1024]{1,0:T(8,128)(2,1)S(1)}, bf16[64,1024]{1,0:T(8,128)(2,1)S(1)}, u32[]{:S(2)}, u32[]{:S(2)}) collective-permute-start(bf16[64,1024]{1,0:T(8,128)(2,1)S(1)} %get-tuple-element.416), channel_id=1, source_target_pairs={{0,4},{2,6},{4,0},{6,2},{1,5},{3,7},{5,1},{7,3},{8,12},{10,14},{12... | collective-permute-start | bytes 393224 | tf_op jit(solution)/shard_map/ppermute | solution.py:40
  406.0 17.9 %collective-permute-start.69 = (bf16[2,2,2,32,1024]{4,3,2,1,0:T(8,128)(2,1)S(1)}, bf16[2,2,2,32,1024]{4,3,2,1,0:T(8,128)(2,1)S(1)}, u32[]{:S(2)}, u32[]{:S(2)}) collective-permute-start(bf16[2,2,2,32,1024]{4,3,2,1,0:T(8,128)(2,1)S(1)} %dynamic-slice_bitcast_fusion.1), channel_id=1, source_target_pairs={{0,1},{1,0},{2,3},{3,2},{4,5},{5,4},{6,7},{7,6},{8,9},{9,8},{10,11... | collective-permute-start | bytes 1572872 | tf_op jit(solution)/shard_map/ppermute | solution.py:40
  408.7 15.3 %collective-permute-start.70 = (bf16[256,1024]{1,0:T(8,128)(2,1)S(1)}, bf16[256,1024]{1,0:T(8,128)(2,1)}, u32[]{:S(2)}, u32[]{:S(2)}) collective-permute-start(bf16[256,1024]{1,0:T(8,128)(2,1)S(1)} %get-tuple-element.541), channel_id=1, source_target_pairs={{0,16},{16,0},{1,17},{17,1},{2,18},{18,2},{3,19},{19,3},{4,20},{20... | collective-permute-start | bytes 1572872 | tf_op jit(solution)/shard_map/ppermute | solution.py:40
  424.7 25.3 %collective-permute-start.71 = (bf16[2,2,2,272,256]{4,3,2,1,0:T(8,128)(2,1)}, bf16[2,2,2,272,256]{4,3,2,1,0:T(8,128)(2,1)S(1)}, u32[]{:S(2)}, u32[]{:S(2)}) collective-permute-start(bf16[2,2,2,272,256]{4,3,2,1,0:T(8,128)(2,1)} %get-tuple-element.446), channel_id=1, source_target_pairs={{0,1},{1,0},{2,3},{3,2},{4,5},{5,4},{6,7},{7,6},{8,9},{9,8},{10,11... | collective-permute-start | bytes 3342344 | tf_op jit(solution)/shard_map/ppermute | solution.py:40
  424.7 23.6 %collective-permute-start.72 = (bf16[2,2,2,256,256]{4,3,2,1,0:T(8,128)(2,1)}, bf16[2,2,2,256,256]{4,3,2,1,0:T(8,128)(2,1)}, u32[]{:S(2)}, u32[]{:S(2)}) collective-permute-start(bf16[2,2,2,256,256]{4,3,2,1,0:T(8,128)(2,1)} %get-tuple-element.447), channel_id=1, source_target_pairs={{0,16},{16,0},{1,17},{17,1},{2,18},{18,2},{3,19},{19,3},{4,20},{20... | collective-permute-start | bytes 3145736 | tf_op jit(solution)/shard_map/ppermute | solution.py:40
  426.0 23.4 %collective-permute-start.73 = (bf16[2,2,2,256,256]{4,3,2,1,0:T(8,128)(2,1)}, bf16[2,2,2,256,256]{4,3,2,1,0:T(8,128)(2,1)}, u32[]{:S(2)}, u32[]{:S(2)}) collective-permute-start(bf16[2,2,2,256,256]{4,3,2,1,0:T(8,128)(2,1)} %get-tuple-element.448), channel_id=1, source_target_pairs={{0,2},{2,0},{4,6},{6,4},{1,3},{3,1},{5,7},{7,5},{8,10},{10,8},{12,... | collective-permute-start | bytes 3145736 | tf_op jit(solution)/shard_map/ppermute | solution.py:40
  431.5 17.9 %collective-permute-start.74 = (bf16[512,1024]{1,0:T(8,128)(2,1)}, bf16[512,1024]{1,0:T(8,128)(2,1)}, u32[]{:S(2)}, u32[]{:S(2)}) collective-permute-start(bf16[512,1024]{1,0:T(8,128)(2,1)} %get-tuple-element.451), channel_id=1, source_target_pairs={{0,8},{8,0},{1,9},{9,1},{2,10},{10,2},{3,11},{11,3},{4,12},{12,4},... | collective-permute-start | bytes 3145736 | tf_op jit(solution)/shard_map/ppermute | solution.py:40
  458.1 18.5 %collective-permute-start.76 = (bf16[2,2,272,256]{3,2,1,0:T(8,128)(2,1)}, bf16[2,2,272,256]{3,2,1,0:T(8,128)(2,1)}, u32[]{:S(2)}, u32[]{:S(2)}) collective-permute-start(bf16[2,2,272,256]{3,2,1,0:T(8,128)(2,1)} %bitcast.118), channel_id=1, source_target_pairs={{0,16},{16,0},{1,17},{17,1},{2,18},{18,2},{3,19},{19,3},{4,20},{20... | collective-permute-start | bytes 1671176 | tf_op jit(solution)/shard_map/ppermute | solution.py:40
  459.3 17.2 %collective-permute-start.77 = (bf16[2,2,256,256]{3,2,1,0:T(8,128)(2,1)}, bf16[2,2,256,256]{3,2,1,0:T(8,128)(2,1)}, u32[]{:S(2)}, u32[]{:S(2)}) collective-permute-start(bf16[2,2,256,256]{3,2,1,0:T(8,128)(2,1)} %bitcast.119), channel_id=1, source_target_pairs={{0,2},{2,0},{4,6},{6,4},{1,3},{3,1},{5,7},{7,5},{8,10},{10,8},{12,... | collective-permute-start | bytes 1572872 | tf_op jit(solution)/shard_map/ppermute | solution.py:40
  459.3 17.2 %collective-permute-start.78 = (bf16[2,2,256,256]{3,2,1,0:T(8,128)(2,1)}, bf16[2,2,256,256]{3,2,1,0:T(8,128)(2,1)}, u32[]{:S(2)}, u32[]{:S(2)}) collective-permute-start(bf16[2,2,256,256]{3,2,1,0:T(8,128)(2,1)} %bitcast.120), channel_id=1, source_target_pairs={{0,1},{1,0},{2,3},{3,2},{4,5},{5,4},{6,7},{7,6},{8,9},{9,8},{10,11... | collective-permute-start | bytes 1572872 | tf_op jit(solution)/shard_map/ppermute | solution.py:40
  459.6 16.9 %collective-permute-start.79 = (bf16[2,2,32,1024]{3,2,1,0:T(8,128)(2,1)S(1)}, bf16[2,2,32,1024]{3,2,1,0:T(8,128)(2,1)}, u32[]{:S(2)}, u32[]{:S(2)}) collective-permute-start(bf16[2,2,32,1024]{3,2,1,0:T(8,128)(2,1)S(1)} %dynamic-slice_bitcast_fusion.2), channel_id=1, source_target_pairs={{0,2},{2,0},{4,6},{6,4},{1,3},{3,1},{5,7},{7,5},{8,10},{10,8},{12,... | collective-permute-start | bytes 786440 | tf_op jit(solution)/shard_map/ppermute | solution.py:40
  462.3 39.2 %collective-permute-start.89 = (bf16[2,256,1024]{2,1,0:T(8,128)(2,1)S(1)}, bf16[2,256,1024]{2,1,0:T(8,128)(2,1)S(1)}, u32[]{:S(2)}, u32[]{:S(2)}) collective-permute-start(bf16[2,256,1024]{2,1,0:T(8,128)(2,1)S(1)} %pad_maximum_fusion.7.p0), channel_id=1, source_target_pairs={{0,8},{8,0},{1,9},{9,1},{2,10},{10,2},{3,11},{11,3},{4,12},{12,4},... | collective-permute-start | bytes 3145736 | tf_op jit(solution)/shard_map/ppermute | solution.py:40
  487.9 31.3 %collective-permute-start.87 = (bf16[512,1024]{1,0:T(8,128)(2,1)}, bf16[512,1024]{1,0:T(8,128)(2,1)}, u32[]{:S(2)}, u32[]{:S(2)}) collective-permute-start(bf16[512,1024]{1,0:T(8,128)(2,1)} %row_back.2), channel_id=1, source_target_pairs={{1,8},{8,1},{3,10},{10,3},{5,12},{12,5},{7,14},{14,7},{17,24},{24,... | collective-permute-start | bytes 3145736 | tf_op jit(solution)/shard_map/ppermute | solution.py:44
  498.9 20.3 %collective-permute-start.84 = (bf16[272,256]{1,0:T(8,128)(2,1)S(1)}, bf16[272,256]{1,0:T(8,128)(2,1)S(1)}, u32[]{:S(2)}, u32[]{:S(2)}) collective-permute-start(bf16[272,256]{1,0:T(8,128)(2,1)S(1)} %get-tuple-element.486), channel_id=1, source_target_pairs={{0,4},{2,6},{4,0},{6,2},{1,5},{3,7},{5,1},{7,3},{8,12},{10,14},{12... | collective-permute-start | bytes 417800 | tf_op jit(solution)/shard_map/ppermute | solution.py:40
  499.0 17.4 %collective-permute-start.85 = (bf16[256,256]{1,0:T(8,128)(2,1)S(1)}, bf16[256,256]{1,0:T(8,128)(2,1)S(1)}, u32[]{:S(2)}, u32[]{:S(2)}) collective-permute-start(bf16[256,256]{1,0:T(8,128)(2,1)S(1)} %get-tuple-element.487), channel_id=1, source_target_pairs={{0,4},{2,6},{4,0},{6,2},{1,5},{3,7},{5,1},{7,3},{8,12},{10,14},{12... | collective-permute-start | bytes 393224 | tf_op jit(solution)/shard_map/ppermute | solution.py:40
  501.3 17.9 %collective-permute-start.86 = (bf16[256,256]{1,0:T(8,128)(2,1)S(1)}, bf16[256,256]{1,0:T(8,128)(2,1)S(1)}, u32[]{:S(2)}, u32[]{:S(2)}) collective-permute-start(bf16[256,256]{1,0:T(8,128)(2,1)S(1)} %get-tuple-element.488), channel_id=1, source_target_pairs={{0,4},{2,6},{4,0},{6,2},{1,5},{3,7},{5,1},{7,3},{8,12},{10,14},{12... | collective-permute-start | bytes 393224 | tf_op jit(solution)/shard_map/ppermute | solution.py:40
  (194 other events, 1649.9 us)

commit v4 on v3

--- a/solution.py
+++ b/solution.py
@@ -450,7 +450,11 @@
         ],
         scratch_shapes=[pltpu.VMEM((BLK, DH), F32)] * 4,
         name="mem_bwd",
-        **params(flops=10 * BLK * 1024 * KEEP, moved=9 * 2**20, trans=HL * BLK * 1024),
+        **params(
+            flops=10 * BLK * 1024 * KEEP,
+            moved=9 * 2**20,
+            vmem=VMEM_GRADS if final else VMEM_MOST,
+        ),
     )(*ops)
 
 
@@ -593,7 +597,11 @@
         out_shape=out_shape + [rel_shape],
         scratch_shapes=[pltpu.VMEM((BLK, DH), F32)] * scratch,
         name="tok_bwd",
-        **params(flops=10 * BLK * 1280 * KEEP, moved=12 * 2**20, trans=HL * BLK * 1024),
+        **params(
+            flops=10 * BLK * 1280 * KEEP,
+            moved=12 * 2**20,
+            vmem=VMEM_GRADS if has_prev else VMEM_MOST,
+        ),
     )(*ops)
 
 

time: 561 us -> 548 us (0.977)
  local copies, waits for them, and re-layouts: 48.8 us -> 37.2 us
    unnamed x338 -> x312, local copies, waits for them, and re-layouts: 38.2 us -> 27 us
  transfers between devices with their start and end apart: 98 -> 98, of which waited for: 33 -> 35; matrix products, arithmetic and copies ran while one was open for 13% -> 13% of each run, Pallas kernels for 31% -> 32%
where the time goes in v4:
time: 548 us; the launch traced here: 540 us
  Pallas kernels  189 us (34%)
  waiting for transfers between devices  129 us (24%)
  starting transfers between devices  115 us (21%)
  other arithmetic  53.5 us (10%)
  local copies, waits for them, and re-layouts  37.2 us (7%)
  matrix products  13.1 us (2%)
    ppermute x77, waiting for transfers between devices, xch(): return lax.ppermute(value, axis, [(i, i ^ mask) for i in range(count)])  97.9 us
    ppermute x77, starting transfers between devices, xch(): return lax.ppermute(value, axis, [(i, i ^ mask) for i in range(count)])  61.3 us
    ppermute x9, starting transfers between devices, diag_send(): return lax.ppermute(value, ('c', 'x'), [(1, 2), (2, 1)])  40.7 us
    pallas_call x1, Pallas kernels, mlp(): pl.pallas_call(mlp_kernel, grid=(4,), in_specs=[act] * 4 + [up, up, down,...  37.4 us
    unnamed x312, local copies, waits for them, and re-layouts  27 us
    pallas_call x2, Pallas kernels, tok_backward(): pl.pallas_call(functools.partial(tok_bwd_kernel, has_prev), grid=(HL,), i...  25.5 us
    pallas_call x2, Pallas kernels, mem_backward(): pl.pallas_call(functools.partial(mem_bwd_kernel, final), grid=(HL,), in_s...  21.6 us
    ppermute x12, waiting for transfers between devices, to_slot(): return lax.ppermute(value, 's', [(i, i ^ k) for i in range(slots)])  16 us
  transfers between devices with their start and end apart: 98, of which 35 were waited for; matrix products, arithmetic and copies ran while one was open for 13% of the time, Pallas kernels for 32%

profile of v4, /device:TPU:1, one launch (start us, length us, event | category | flops | bytes accessed | tf_op | source)
XLA Modules:
  0.0 540.0 jit_solution(15804207130143152064)
XLA Ops:
  0.6 4.5 collective-permute-start.4
  10.1 2.4 collective-permute-start
  14.0 2.4 collective-permute-start.2
  17.3 6.4 %collective-permute-done = bf16[256,256]{1,0:T(8,128)(2,1)S(1)} collective-permute-done((bf16[256,256]{1,0:T(8,128)(2,1)S(1)}, bf16[256,256]{1,0:T(8,128)(2,1)S(1)}, u32[]{:S(2)}, u32[]{:S(2)}) %collective-permute-start) | collective-permute-done | bytes 131104 | tf_op jit(solution)/shard_map/ppermute | solution.py:40
  23.7 2.2 collective-permute-done.1
  35.4 2.6 collective-permute-start.8
  37.9 4.8 collective-permute-start.9
  60.9 7.9 %collective-permute-done.13 = bf16[64,1024]{1,0:T(8,128)(2,1)S(1)} collective-permute-done((bf16[64,1024]{1,0:T(8,128)(2,1)}, bf16[64,1024]{1,0:T(8,128)(2,1)S(1)}, u32[]{:S(2)}, u32[]{:S(2)}) %collective-permute-start.13) | collective-permute-done | bytes 131104 | tf_op jit(solution)/shard_map/ppermute | solution.py:1107
  77.3 2.5 fusion.2
  80.0 2.5 collective-permute-start.20
  85.6 13.4 %collective-permute-done.18 = bf16[64,1024]{1,0:T(8,128)(2,1)S(1)} collective-permute-done((bf16[64,1024]{1,0:T(8,128)(2,1)S(1)}, bf16[64,1024]{1,0:T(8,128)(2,1)S(1)}, u32[]{:S(2)}, u32[]{:S(2)}) %collective-permute-start.18) | collective-permute-done | bytes 131104 | tf_op jit(solution)/shard_map/ppermute | solution.py:40
  101.2 5.2 collective-permute-start.22
  108.9 2.4 collective-permute-start.25
  111.9 3.6 convolution_convert_fusion.ko.vo.refs_0_.refs_3_.refs_4_.refs_6_.refs_7_.refs_8_.refs_9_
  122.2 5.4 %mem_fwd.2 = (bf16[512,512]{1,0:T(8,128)(2,1)S(1)}, f32[512,128]{1,0:T(8,128)S(1)}) custom-call(bf16[512,1536]{1,0:T(8,128)(2,1)S(1)} %convolution_convert_fusion.2.q.ks.vs.refs_1_.refs_2_.refs_0_, bf16[512,1536]{1,0:T(8,128)(2,1)S(1)} %convolution_convert_fusion.2.q.ks.vs.refs_1_.refs_2_.refs_0_, ...), custom_call_target="tpu_custom_call" | custom-call | flops 107374184 | bytes 419430 | tf_op jit(solution)/shard_map/mem_fwd/pallas_call | solution.py:369
  128.4 9.6 %collective-permute-done.25 = bf16[256,1024]{1,0:T(8,128)(2,1)S(1)} collective-permute-done((bf16[256,1024]{1,0:T(8,128)(2,1)S(1)}, bf16[256,1024]{1,0:T(8,128)(2,1)S(1)}, u32[]{:S(2)}, u32[]{:S(2)}) %collective-permute-start.25) | collective-permute-done | bytes 524320 | tf_op jit(solution)/shard_map/ppermute | solution.py:40
  137.9 2.9 collective-permute-done.26
  145.0 5.2 tok_fwd.2
  151.1 2.6 collective-permute-done.32
  153.7 6.5 %collective-permute-done.31 = bf16[2,64,1024]{2,1,0:T(8,128)(2,1)S(1)} collective-permute-done((bf16[2,64,1024]{2,1,0:T(8,128)(2,1)S(1)}, bf16[2,64,1024]{2,1,0:T(8,128)(2,1)S(1)}, u32[]{:S(2)}, u32[]{:S(2)}) %collective-permute-start.31) | collective-permute-done | bytes 262176 | tf_op jit(solution)/shard_map/ppermute | solution.py:40
  160.9 2.4 fusion.57
  167.6 2.8 fusion.53
  175.0 6.8 %tok_fwd.3 = (bf16[512,512]{1,0:T(8,128)(2,1)S(1)}, f32[512,128]{1,0:T(8,128)S(1)}) custom-call(bf16[1024,1536]{1,0:T(8,128)(2,1)S(1)} %convolution_convert_fusion.ko.vo.refs_0_.refs_3_.refs_4_.refs_6_.refs_7_.refs_8_.refs_9_, bf16[512,1536]{1,0:T(8,128)(2,1)S(1)} %convolution_convert_fusion.1.refs_1_.refs_2_.q.ks.vs.refs_0_, ...), custom_call_target="tpu_custom_call" | custom-call | flops 134217728 | bytes 838860 | tf_op jit(solution)/shard_map/tok_fwd/pallas_call | solution.py:337
  181.9 8.7 %collective-permute-done.36.high = bf16[2,2,2,32,1024]{4,3,2,1,0:T(8,128)(2,1)S(1)} collective-permute-done((bf16[2,2,2,32,1024]{4,3,2,1,0:T(8,128)(2,1)S(1)}, bf16[2,2,2,32,1024]{4,3,2,1,0:T(8,128)(2,1)S(1)}, u32[]{:S(2)}, u32[]{:S(2)}) %collective-permute-start.36) | collective-permute-done | bytes 524320 | tf_op jit(solution)/shard_map/ppermute | solution.py:40
  198.5 5.4 %mem_fwd.3 = (bf16[512,512]{1,0:T(8,128)(2,1)S(1)}, f32[512,128]{1,0:T(8,128)S(1)}) custom-call(bf16[512,1536]{1,0:T(8,128)(2,1)S(1)} %convolution_convert_fusion.1.refs_1_.refs_2_.q.ks.vs.refs_0_, bf16[512,1536]{1,0:T(8,128)(2,1)S(1)} %convolution_convert_fusion.1.refs_1_.refs_2_.q.ks.vs.refs_0_, ...), custom_call_target="tpu_custom_call" | custom-call | flops 107374184 | bytes 419430 | tf_op jit(solution)/shard_map/mem_fwd/pallas_call | solution.py:369
  205.4 2.4 collective-permute-start.43
  212.9 9.2 %mem_bwd.2 = (f32[512,1536]{1,0:T(8,128)S(1)}, f32[512,1024]{1,0:T(8,128)S(1)}) custom-call(bf16[512,1536]{1,0:T(8,128)(2,1)S(1)} %convolution_convert_fusion.1.refs_1_.refs_2_.q.ks.vs.refs_0_, bf16[512,1536]{1,0:T(8,128)(2,1)S(1)} %convolution_convert_fusion.1.refs_1_.refs_2_.q.ks.vs.refs_0_, ...), custom_call_target="tpu_custom_call" | custom-call | flops 268435456 | bytes 943718 | tf_op jit(solution)/shard_map/mem_bwd/pallas_call | solution.py:442
  223.6 5.3 collective-permute-done.43
  231.2 2.4 collective-permute-start.48
  234.6 37.4 %mlp.1 = (bf16[2,2,2,96,1024]{4,3,2,1,0:T(8,128)(2,1)}, bf16[2,2,2,96,1024]{4,3,2,1,0:T(8,128)(2,1)}, bf16[2,2,2,96,1024]{4,3,2,1,0:T(8,128)(2,1)}, bf16[2,2,2,9...) custom-call(bf16[512,1024]{1,0:T(8,128)(2,1)S(1)} %multiply_convert_, ...), custom_call_target="tpu_custom_call" | custom-call | flops 2576980480 | bytes 2726297 | tf_op jit(solution)/shard_map/mlp/pallas_call | solution.py:694
  280.5 6.4 %mid_back.1 = (f32[512,1024]{1,0:T(8,128)}, bf16[512,1024]{1,0:T(8,128)(2,1)}, bf16[512,1024]{1,0:T(8,128)(2,1)}, f32[8,1024]{1,0:T(8,128)}) custom-call(f32[512,1024]{1,0:T(8,128)} %copy-done.70, f32[1,1024]{1,0:T(1,128)} %get-tuple-element.591.gain, bf16[512,1024]{1,0:T(8,128)(2,1)} %copy-done.46, bf16[512,1024]{1,0:T(8,128)(2,1)} %copy-done.103, ...), custom_call_target="tpu_custom_call" | custom-call | tf_op jit(solution)/shard_map/mid_back/pallas_call | solution.py:766
  289.9 6.2 %out_back.1 = (bf16[1024,512]{1,0:T(8,128)(2,1)}, bf16[512,1024]{1,0:T(8,128)(2,1)}) custom-call(s32[4]{0:T(128)} %copy-done.62, bf16[512,1024]{1,0:T(8,128)(2,1)} %get-tuple-element.364.own, bf16[512,1024]{1,0:T(8,128)(2,1)} %collective-permute-done.55.oth, bf16[512,1024]{1,0:T(8,128)(2,1)} %copy-done.12, bf16[512,512]{1,0:T(8,128)(2,1)} %copy-done.34, ...), custom_call_target="tpu_custom_call" | custom-call | tf_op jit(solution)/shard_map/out_back/pallas_call | solution.py:792
  296.1 16.1 %tok_bwd.2 = (bf16[512,1536]{1,0:T(8,128)(2,1)}, bf16[512,1536]{1,0:T(8,128)(2,1)}, f32[512,1024]{1,0:T(8,128)}, f32[4,8,512]{2,1,0:T(8,128)}) custom-call(bf16[1024,1536]{1,0:T(8,128)(2,1)} %copy-done, bf16[512,1536]{1,0:T(8,128)(2,1)} %copy-done.2, bf16[512,1536]{1,0:T(8,128)(2,1)} %copy-done.2, bf16[1024,1536]{1,0:T(8,128)(2,1)} %copy-done, ...), custom_call_target="tpu_custom_call" | custom-call | flops 335544320 | bytes 1258291 | tf_op jit(solution)/shard_map/tok_bwd/pallas_call | solution.py:592
  313.3 3.9 halves.6
  318.4 4.1 collective-permute-start.59
  324.0 2.5 proj_one.1.refs_2_
  329.1 6.8 %collective-permute-start.60 = (bf16[4,64,1024]{2,1,0:T(8,128)(2,1)S(1)}, bf16[4,64,1024]{2,1,0:T(8,128)(2,1)S(1)}, u32[]{:S(2)}, u32[]{:S(2)}) collective-permute-start(bf16[4,64,1024]{2,1,0:T(8,128)(2,1)S(1)} %bitcast.298), channel_id=1, source_target_pairs={{1,8},{8,1},{3,10},{10,3},{5,12},{12,5},{7,14},{14,7},{17,24},{24,... | collective-permute-start | bytes 1572872 | tf_op jit(solution)/shard_map/ppermute | solution.py:44
  336.0 9.4 %tok_bwd.3 = (f32[512,1024]{1,0:T(8,128)S(1)}, f32[512,1536]{1,0:T(8,128)S(1)}, f32[4,8,512]{2,1,0:T(8,128)S(1)}) custom-call(bf16[1024,1536]{1,0:T(8,128)(2,1)S(1)} %copy-done.1, bf16[512,1536]{1,0:T(8,128)(2,1)S(1)} %copy-done.4, bf16[512,1536]{1,0:T(8,128)(2,1)S(1)} %copy-done.4, bf16[1024,1536]{1,0:T(8,128)(2,1)S(1)} %copy-done.1, ...), custom_call_target="tpu_custom_call" | custom-call | flops 335544320 | bytes 1258291 | tf_op jit(solution)/shard_map/tok_bwd/pallas_call | solution.py:592
  349.8 11.7 %state_back.1 = (f32[512,1024]{1,0:T(8,128)}, bf16[512,512]{1,0:T(8,128)(2,1)}, bf16[512,1024]{1,0:T(8,128)(2,1)}, f32[8,1024]{1,0:T(8,128)}) custom-call(s32[4]{0:T(128)} %copy-done.62, f32[512,1024]{1,0:T(8,128)} %copy-done.65, f32[1,1024]{1,0:T(1,128)} %get-tuple-element.590.refs_1_.gain, bf16[512,1024]{1,0:T(8,128)(2,1)} %copy-done.26, ...), custom_call_target="tpu_custom_call" | custom-call | tf_op jit(solution)/shard_map/state_back/pallas_call | solution.py:889
  366.8 2.1 collective-permute-start.67
  369.2 12.4 %mem_bwd.3 = (bf16[512,1536]{1,0:T(8,128)(2,1)}, bf16[512,1536]{1,0:T(8,128)(2,1)}) custom-call(bf16[512,1536]{1,0:T(8,128)(2,1)} %copy-done.3, bf16[512,1536]{1,0:T(8,128)(2,1)} %copy-done.3, bf16[512,1536]{1,0:T(8,128)(2,1)} %copy-done.3, bf16[1024,1536]{1,0:T(8,128)(2,1)} %copy-done, bf16[1024,1536]{1,0:T(8,128)(2,1)} %copy-done, ...), custom_call_target="tpu_custom_call" | custom-call | flops 268435456 | bytes 943718 | tf_op jit(solution)/shard_map/mem_bwd/pallas_call | solution.py:442
  381.6 10.3 %collective-permute-done.68 = bf16[64,1024]{1,0:T(8,128)(2,1)S(1)} collective-permute-done((bf16[64,1024]{1,0:T(8,128)(2,1)S(1)}, bf16[64,1024]{1,0:T(8,128)(2,1)S(1)}, u32[]{:S(2)}, u32[]{:S(2)}) %collective-permute-start.68) | collective-permute-done | bytes 131104 | tf_op jit(solution)/shard_map/ppermute | solution.py:40
  397.4 14.2 %proj_grad.1 = (bf16[2,2,2,272,256]{4,3,2,1,0:T(8,128)(2,1)}, bf16[2,2,2,272,256]{4,3,2,1,0:T(8,128)(2,1)}, bf16[2,2,2,256,256]{4,3,2,1,0:T(8,128)(2,1)}, bf16[2...) custom-call(s32[4]{0:T(128)} %copy-done.62, ...), custom_call_target="tpu_custom_call" | custom-call | flops 644245120 | bytes 1677721 | tf_op jit(solution)/shard_map/proj_grad/pallas_call | solution.py:976
  413.7 5.4 %proj_back.2 = (bf16[512,1024]{1,0:T(8,128)(2,1)S(1)}, bf16[512,1024]{1,0:T(8,128)(2,1)}) custom-call(s32[4]{0:T(128)S(1)} %copy-done.63, bf16[512,1536]{1,0:T(8,128)(2,1)S(1)} %copy-done.24, bf16[512,1536]{1,0:T(8,128)(2,1)S(1)} %copy-done.22, bf16[1024,1536]{1,0:T(8,128)(2,1)S(1)} %copy-done.28), custom_call_target="tpu_custom_call" | custom-call | tf_op jit(solution)/shard_map/proj_back/pallas_call | solution.py:835
  419.1 2.2 collective-permute-start.74
  421.3 3.1 proj_back.3
  427.3 8.2 %collective-permute-done.72 = bf16[2,2,2,256,256]{4,3,2,1,0:T(8,128)(2,1)} collective-permute-done((bf16[2,2,2,256,256]{4,3,2,1,0:T(8,128)(2,1)}, bf16[2,2,2,256,256]{4,3,2,1,0:T(8,128)(2,1)}, u32[]{:S(2)}, u32[]{:S(2)}) %collective-permute-start.72) | collective-permute-done | bytes 1048608 | tf_op jit(solution)/shard_map/ppermute | solution.py:40
  439.6 4.3 halves.9
  449.6 4.1 collective-permute-start.89
  454.4 5.8 %row_back.2 = bf16[512,1024]{1,0:T(8,128)(2,1)} custom-call(s32[4]{0:T(128)} %copy-done.62, bf16[512,1024]{1,0:T(8,128)(2,1)} %copy-done.68, f32[1,1024]{1,0:T(1,128)} %get-tuple-element.589.gain, bf16[512,1024]{1,0:T(8,128)(2,1)} %copy-done.42, bf16[512,1024]{1,0:T(8,128)(2,1)} %collective-permute-done.74.got, f32[1,1024]{1,0:T(1,128)} %broadcast.130.scale, ...), custom_call_target="tpu_custom_call" | custom-call | tf_op jit(solution)/shard_map/row_back/pallas_call | solution.py:922
  460.1 3.1 collective-permute-done.79
  468.7 3.6 row_back.3
  474.6 9.0 %collective-permute-start.87 = (bf16[512,1024]{1,0:T(8,128)(2,1)}, bf16[512,1024]{1,0:T(8,128)(2,1)}, u32[]{:S(2)}, u32[]{:S(2)}) collective-permute-start(bf16[512,1024]{1,0:T(8,128)(2,1)} %row_back.2), channel_id=1, source_target_pairs={{1,8},{8,1},{3,10},{10,3},{5,12},{12,5},{7,14},{14,7},{17,24},{24,... | collective-permute-start | bytes 3145736 | tf_op jit(solution)/shard_map/ppermute | solution.py:44
  483.7 2.4 broadcast_select_fusion.2
  486.4 2.4 collective-permute-start.85
  491.2 2.8 place_mlp.1
  494.2 9.6 %collective-permute-done.85 = bf16[256,256]{1,0:T(8,128)(2,1)S(1)} collective-permute-done((bf16[256,256]{1,0:T(8,128)(2,1)S(1)}, bf16[256,256]{1,0:T(8,128)(2,1)S(1)}, u32[]{:S(2)}, u32[]{:S(2)}) %collective-permute-start.85) | collective-permute-done | bytes 131104 | tf_op jit(solution)/shard_map/ppermute | solution.py:40
  503.7 2.8 collective-permute-done.86
  508.4 2.5 collective-permute-start.93
  510.9 2.7 select_convert_fusion.1
  513.6 3.6 collective-permute-done.94
  518.7 2.7 collective-permute-start.97
  525.0 7.2 %collective-permute-done.95 = bf16[4,64,1024]{2,1,0:T(8,128)(2,1)S(1)} collective-permute-done((bf16[4,64,1024]{2,1,0:T(8,128)(2,1)S(1)}, bf16[4,64,1024]{2,1,0:T(8,128)(2,1)S(1)}, u32[]{:S(2)}, u32[]{:S(2)}) %collective-permute-start.95) | collective-permute-done | bytes 524320 | tf_op jit(solution)/shard_map/ppermute | solution.py:44
  533.3 4.4 place_proj.1
  (618 shorter events, 160.7 us)
Async XLA Ops:
  0.6 26.8 %collective-permute-start.4 = (bf16[512,1024]{1,0:T(8,128)(2,1)}, bf16[512,1024]{1,0:T(8,128)(2,1)S(1)}, u32[]{:S(2)}, u32[]{:S(2)}) collective-permute-start(bf16[512,1024]{1,0:T(8,128)(2,1)} %param.16), channel_id=1, source_target_pairs={{1,8},{8,1},{3,10},{10,3},{5,12},{12,5},{7,14},{14,7},{17,24},{24,... | collective-permute-start | bytes 3145736 | tf_op jit(solution)/shard_map/ppermute | solution.py:44
  5.2 22.3 %collective-permute-start.3 = (bf16[4,64,1024]{2,1,0:T(8,128)(2,1)}, bf16[4,64,1024]{2,1,0:T(8,128)(2,1)S(1)}, u32[]{:S(2)}, u32[]{:S(2)}) collective-permute-start(bf16[4,64,1024]{2,1,0:T(8,128)(2,1)} %param.17), channel_id=1, source_target_pairs={{1,8},{8,1},{3,10},{10,3},{5,12},{12,5},{7,14},{14,7},{17,24},{24,... | collective-permute-start | bytes 1572872 | tf_op jit(solution)/shard_map/ppermute | solution.py:44
  10.1 13.6 %collective-permute-start = (bf16[256,256]{1,0:T(8,128)(2,1)S(1)}, bf16[256,256]{1,0:T(8,128)(2,1)S(1)}, u32[]{:S(2)}, u32[]{:S(2)}) collective-permute-start(bf16[256,256]{1,0:T(8,128)(2,1)S(1)} %get-tuple-element.266), channel_id=1, source_target_pairs={{0,4},{2,6},{4,0},{6,2},{1,5},{3,7},{5,1},{7,3},{8,12},{10,14},{12... | collective-permute-start | bytes 393224 | tf_op jit(solution)/shard_map/ppermute | solution.py:40
  27.5 17.8 %collective-permute-start.5 = (bf16[2,272,256]{2,1,0:T(8,128)(2,1)S(1)}, bf16[2,272,256]{2,1,0:T(8,128)(2,1)S(1)}, u32[]{:S(2)}, u32[]{:S(2)}) collective-permute-start(bf16[2,272,256]{2,1,0:T(8,128)(2,1)S(1)} %get-tuple-element.576), channel_id=1, source_target_pairs={{0,2},{2,0},{4,6},{6,4},{1,3},{3,1},{5,7},{7,5},{8,10},{10,8},{12,... | collective-permute-start | bytes 835592 | tf_op jit(solution)/shard_map/ppermute | solution.py:40
  30.4 14.9 %collective-permute-start.6 = (bf16[2,256,256]{2,1,0:T(8,128)(2,1)S(1)}, bf16[2,256,256]{2,1,0:T(8,128)(2,1)S(1)}, u32[]{:S(2)}, u32[]{:S(2)}) collective-permute-start(bf16[2,256,256]{2,1,0:T(8,128)(2,1)S(1)} %get-tuple-element.584), channel_id=1, source_target_pairs={{0,1},{1,0},{2,3},{3,2},{4,5},{5,4},{6,7},{7,6},{8,9},{9,8},{10,11... | collective-permute-start | bytes 786440 | tf_op jit(solution)/shard_map/ppermute | solution.py:40
  47.0 21.8 %collective-permute-start.14 = (bf16[512,1024]{1,0:T(8,128)(2,1)S(1)}, bf16[512,1024]{1,0:T(8,128)(2,1)S(1)}, u32[]{:S(2)}, u32[]{:S(2)}) collective-permute-start(bf16[512,1024]{1,0:T(8,128)(2,1)S(1)} %broadcast_select_fusion.4.values), channel_id=1, source_target_pairs={{0,8},{8,0},{1,9},{9,1},{2,10},{10,2},{3,11},{11,3},{4,12},{12,4},... | collective-permute-start | bytes 3145736 | tf_op jit(solution)/shard_map/ppermute | solution.py:40
  49.1 19.7 %collective-permute-start.10 = (bf16[2,2,272,256]{3,2,1,0:T(8,128)(2,1)}, bf16[2,2,272,256]{3,2,1,0:T(8,128)(2,1)}, u32[]{:S(2)}, u32[]{:S(2)}) collective-permute-start(bf16[2,2,272,256]{3,2,1,0:T(8,128)(2,1)} %get-tuple-element.535), channel_id=1, source_target_pairs={{0,16},{16,0},{1,17},{17,1},{2,18},{18,2},{3,19},{19,3},{4,20},{20... | collective-permute-start | bytes 1671176 | tf_op jit(solution)/shard_map/ppermute | solution.py:40
  51.2 17.6 %collective-permute-start.11 = (bf16[2,2,256,256]{3,2,1,0:T(8,128)(2,1)}, bf16[2,2,256,256]{3,2,1,0:T(8,128)(2,1)}, u32[]{:S(2)}, u32[]{:S(2)}) collective-permute-start(bf16[2,2,256,256]{3,2,1,0:T(8,128)(2,1)} %get-tuple-element.568), channel_id=1, source_target_pairs={{0,2},{2,0},{4,6},{6,4},{1,3},{3,1},{5,7},{7,5},{8,10},{10,8},{12,... | collective-permute-start | bytes 1572872 | tf_op jit(solution)/shard_map/ppermute | solution.py:40
  54.0 14.8 %collective-permute-start.12 = (bf16[2,2,256,256]{3,2,1,0:T(8,128)(2,1)}, bf16[2,2,256,256]{3,2,1,0:T(8,128)(2,1)}, u32[]{:S(2)}, u32[]{:S(2)}) collective-permute-start(bf16[2,2,256,256]{3,2,1,0:T(8,128)(2,1)} %get-tuple-element.566), channel_id=1, source_target_pairs={{0,1},{1,0},{2,3},{3,2},{4,5},{5,4},{6,7},{7,6},{8,9},{9,8},{10,11... | collective-permute-start | bytes 1572872 | tf_op jit(solution)/shard_map/ppermute | solution.py:40
  70.1 30.0 %collective-permute-start.15 = (bf16[2,2,2,272,256]{4,3,2,1,0:T(8,128)(2,1)S(1)}, bf16[2,2,2,272,256]{4,3,2,1,0:T(8,128)(2,1)S(1)}, u32[]{:S(2)}, u32[]{:S(2)}) collective-permute-start(bf16[2,2,2,272,256]{4,3,2,1,0:T(8,128)(2,1)S(1)} %pad_maximum_fusion.3.a0), channel_id=1, source_target_pairs={{0,1},{1,0},{2,3},{3,2},{4,5},{5,4},{6,7},{7,6},{8,9},{9,8},{10,11... | collective-permute-start | bytes 3342344 | tf_op jit(solution)/shard_map/ppermute | solution.py:40
  71.7 27.4 %collective-permute-start.16 = (bf16[2,2,2,256,256]{4,3,2,1,0:T(8,128)(2,1)S(1)}, bf16[2,2,2,256,256]{4,3,2,1,0:T(8,128)(2,1)S(1)}, u32[]{:S(2)}, u32[]{:S(2)}) collective-permute-start(bf16[2,2,2,256,256]{4,3,2,1,0:T(8,128)(2,1)S(1)} %pad_maximum_fusion.4.b0), channel_id=1, source_target_pairs={{0,16},{16,0},{1,17},{17,1},{2,18},{18,2},{3,19},{19,3},{4,20},{20... | collective-permute-start | bytes 3145736 | tf_op jit(solution)/shard_map/ppermute | solution.py:40
  74.1 25.9 %collective-permute-start.17 = (bf16[2,2,2,256,256]{4,3,2,1,0:T(8,128)(2,1)S(1)}, bf16[2,2,2,256,256]{4,3,2,1,0:T(8,128)(2,1)S(1)}, u32[]{:S(2)}, u32[]{:S(2)}) collective-permute-start(bf16[2,2,2,256,256]{4,3,2,1,0:T(8,128)(2,1)S(1)} %pad_maximum_fusion.5.c0), channel_id=1, source_target_pairs={{0,2},{2,0},{4,6},{6,4},{1,3},{3,1},{5,7},{7,5},{8,10},{10,8},{12,... | collective-permute-start | bytes 3145736 | tf_op jit(solution)/shard_map/ppermute | solution.py:40
  75.7 23.4 %collective-permute-start.18 = (bf16[64,1024]{1,0:T(8,128)(2,1)S(1)}, bf16[64,1024]{1,0:T(8,128)(2,1)S(1)}, u32[]{:S(2)}, u32[]{:S(2)}) collective-permute-start(bf16[64,1024]{1,0:T(8,128)(2,1)S(1)} %broadcast_select_fusion.7), channel_id=1, source_target_pairs={{0,4},{2,6},{4,0},{6,2},{1,5},{3,7},{5,1},{7,3},{8,12},{10,14},{12... | collective-permute-start | bytes 393224 | tf_op jit(solution)/shard_map/ppermute | solution.py:40
  100.1 17.7 %collective-permute-start.21 = (bf16[2,64,1024]{2,1,0:T(8,128)(2,1)S(1)}, bf16[2,64,1024]{2,1,0:T(8,128)(2,1)S(1)}, u32[]{:S(2)}, u32[]{:S(2)}) collective-permute-start(bf16[2,64,1024]{2,1,0:T(8,128)(2,1)S(1)} %get-tuple-element.579), channel_id=1, source_target_pairs={{0,1},{1,0},{2,3},{3,2},{4,5},{5,4},{6,7},{7,6},{8,9},{9,8},{10,11... | collective-permute-start | bytes 786440 | tf_op jit(solution)/shard_map/ppermute | solution.py:40
  101.2 16.6 %collective-permute-start.22 = (bf16[4,64,1024]{2,1,0:T(8,128)(2,1)S(1)}, bf16[4,64,1024]{2,1,0:T(8,128)(2,1)S(1)}, u32[]{:S(2)}, u32[]{:S(2)}) collective-permute-start(bf16[4,64,1024]{2,1,0:T(8,128)(2,1)S(1)} %copy-done.116), channel_id=1, source_target_pairs={{1,8},{8,1},{3,10},{10,3},{5,12},{12,5},{7,14},{14,7},{17,24},{24,... | collective-permute-start | bytes 1572872 | tf_op jit(solution)/shard_map/ppermute | solution.py:44
  108.9 29.0 %collective-permute-start.25 = (bf16[256,1024]{1,0:T(8,128)(2,1)S(1)}, bf16[256,1024]{1,0:T(8,128)(2,1)S(1)}, u32[]{:S(2)}, u32[]{:S(2)}) collective-permute-start(bf16[256,1024]{1,0:T(8,128)(2,1)S(1)} %pad_maximum_fusion.14), channel_id=1, source_target_pairs={{0,4},{2,6},{4,0},{6,2},{1,5},{3,7},{5,1},{7,3},{8,12},{10,14},{12... | collective-permute-start | bytes 1572872 | tf_op jit(solution)/shard_map/ppermute | solution.py:40
  117.9 23.0 %collective-permute-start.23 = (bf16[2,2,32,1024]{3,2,1,0:T(8,128)(2,1)S(1)}, bf16[2,2,32,1024]{3,2,1,0:T(8,128)(2,1)S(1)}, u32[]{:S(2)}, u32[]{:S(2)}) collective-permute-start(bf16[2,2,32,1024]{3,2,1,0:T(8,128)(2,1)S(1)} %get-tuple-element.558), channel_id=1, source_target_pairs={{0,2},{2,0},{4,6},{6,4},{1,3},{3,1},{5,7},{7,5},{8,10},{10,8},{12,... | collective-permute-start | bytes 786440 | tf_op jit(solution)/shard_map/ppermute | solution.py:40
  118.4 22.5 %collective-permute-start.24 = (bf16[2,2,32,1024]{3,2,1,0:T(8,128)(2,1)S(1)}, bf16[2,2,32,1024]{3,2,1,0:T(8,128)(2,1)S(1)}, u32[]{:S(2)}, u32[]{:S(2)}) collective-permute-start(bf16[2,2,32,1024]{3,2,1,0:T(8,128)(2,1)S(1)} %get-tuple-element.557), channel_id=1, source_target_pairs={{0,16},{16,0},{1,17},{17,1},{2,18},{18,2},{3,19},{19,3},{4,20},{20... | collective-permute-start | bytes 786440 | tf_op jit(solution)/shard_map/ppermute | solution.py:40
  119.4 21.4 %collective-permute-start.26 = (bf16[64,1024]{1,0:T(8,128)(2,1)S(1)}, bf16[64,1024]{1,0:T(8,128)(2,1)S(1)}, u32[]{:S(2)}, u32[]{:S(2)}) collective-permute-start(bf16[64,1024]{1,0:T(8,128)(2,1)S(1)} %get-tuple-element.555), channel_id=1, source_target_pairs={{0,2},{2,0},{4,6},{6,4},{1,3},{3,1},{5,7},{7,5},{8,10},{10,8},{12,... | collective-permute-start | bytes 393224 | tf_op jit(solution)/shard_map/ppermute | solution.py:1107
  120.4 20.4 %collective-permute-start.27 = (bf16[64,1024]{1,0:T(8,128)(2,1)S(1)}, bf16[64,1024]{1,0:T(8,128)(2,1)S(1)}, u32[]{:S(2)}, u32[]{:S(2)}) collective-permute-start(bf16[64,1024]{1,0:T(8,128)(2,1)S(1)} %get-tuple-element.554), channel_id=1, source_target_pairs={{0,4},{2,6},{4,0},{6,2},{1,5},{3,7},{5,1},{7,3},{8,12},{10,14},{12... | collective-permute-start | bytes 393224 | tf_op jit(solution)/shard_map/ppermute | solution.py:1107
  140.9 19.3 %collective-permute-start.28 = (bf16[2,2,2,32,1024]{4,3,2,1,0:T(8,128)(2,1)S(1)}, bf16[2,2,2,32,1024]{4,3,2,1,0:T(8,128)(2,1)S(1)}, u32[]{:S(2)}, u32[]{:S(2)}) collective-permute-start(bf16[2,2,2,32,1024]{4,3,2,1,0:T(8,128)(2,1)S(1)} %pad_maximum_fusion.17.low), channel_id=1, source_target_pairs={{0,16},{16,0},{1,17},{17,1},{2,18},{18,2},{3,19},{19,3},{4,20},{20... | collective-permute-start | bytes 1572872 | tf_op jit(solution)/shard_map/ppermute | solution.py:40
  142.0 18.2 %collective-permute-start.29 = (bf16[2,96,1024]{2,1,0:T(8,128)(2,1)S(1)}, bf16[2,96,1024]{2,1,0:T(8,128)(2,1)S(1)}, u32[]{:S(2)}, u32[]{:S(2)}) collective-permute-start(bf16[2,96,1024]{2,1,0:T(8,128)(2,1)S(1)} %get-tuple-element.574), channel_id=1, source_target_pairs={{0,2},{2,0},{4,6},{6,4},{1,3},{3,1},{5,7},{7,5},{8,10},{10,8},{12,... | collective-permute-start | bytes 1179656 | tf_op jit(solution)/shard_map/ppermute | solution.py:40
  142.8 17.4 %collective-permute-start.30 = (bf16[2,96,1024]{2,1,0:T(8,128)(2,1)S(1)}, bf16[2,96,1024]{2,1,0:T(8,128)(2,1)S(1)}, u32[]{:S(2)}, u32[]{:S(2)}) collective-permute-start(bf16[2,96,1024]{2,1,0:T(8,128)(2,1)S(1)} %get-tuple-element.572), channel_id=1, source_target_pairs={{0,1},{1,0},{2,3},{3,2},{4,5},{5,4},{6,7},{7,6},{8,9},{9,8},{10,11... | collective-permute-start | bytes 1179656 | tf_op jit(solution)/shard_map/ppermute | solution.py:40
  143.6 16.6 %collective-permute-start.31 = (bf16[2,64,1024]{2,1,0:T(8,128)(2,1)S(1)}, bf16[2,64,1024]{2,1,0:T(8,128)(2,1)S(1)}, u32[]{:S(2)}, u32[]{:S(2)}) collective-permute-start(bf16[2,64,1024]{2,1,0:T(8,128)(2,1)S(1)} %get-tuple-element.578), channel_id=1, source_target_pairs={{0,16},{16,0},{1,17},{17,1},{2,18},{18,2},{3,19},{19,3},{4,20},{20... | collective-permute-start | bytes 786440 | tf_op jit(solution)/shard_map/ppermute | solution.py:40
  165.5 25.1 %collective-permute-start.33 = (bf16[2,2,96,1024]{3,2,1,0:T(8,128)(2,1)S(1)}, bf16[2,2,96,1024]{3,2,1,0:T(8,128)(2,1)S(1)}, u32[]{:S(2)}, u32[]{:S(2)}) collective-permute-start(bf16[2,2,96,1024]{3,2,1,0:T(8,128)(2,1)S(1)} %get-tuple-element.533), channel_id=1, source_target_pairs={{0,1},{1,0},{2,3},{3,2},{4,5},{5,4},{6,7},{7,6},{8,9},{9,8},{10,11... | collective-permute-start | bytes 2359304 | tf_op jit(solution)/shard_map/ppermute | solution.py:40
  165.7 24.9 %collective-permute-start.34 = (bf16[2,2,96,1024]{3,2,1,0:T(8,128)(2,1)S(1)}, bf16[2,2,96,1024]{3,2,1,0:T(8,128)(2,1)S(1)}, u32[]{:S(2)}, u32[]{:S(2)}) collective-permute-start(bf16[2,2,96,1024]{3,2,1,0:T(8,128)(2,1)S(1)} %get-tuple-element.531), channel_id=1, source_target_pairs={{0,16},{16,0},{1,17},{17,1},{2,18},{18,2},{3,19},{19,3},{4,20},{20... | collective-permute-start | bytes 2359304 | tf_op jit(solution)/shard_map/ppermute | solution.py:40
  166.1 15.8 %collective-permute-start.35 = (bf16[2,2,64,1024]{3,2,1,0:T(8,128)(2,1)S(1)}, bf16[2,2,64,1024]{3,2,1,0:T(8,128)(2,1)S(1)}, u32[]{:S(2)}, u32[]{:S(2)}) collective-permute-start(bf16[2,2,64,1024]{3,2,1,0:T(8,128)(2,1)S(1)} %get-tuple-element.549), channel_id=1, source_target_pairs={{0,2},{2,0},{4,6},{6,4},{1,3},{3,1},{5,7},{7,5},{8,10},{10,8},{12,... | collective-permute-start | bytes 1572872 | tf_op jit(solution)/shard_map/ppermute | solution.py:40
  166.6 24.0 %collective-permute-start.36 = (bf16[2,2,2,32,1024]{4,3,2,1,0:T(8,128)(2,1)S(1)}, bf16[2,2,2,32,1024]{4,3,2,1,0:T(8,128)(2,1)S(1)}, u32[]{:S(2)}, u32[]{:S(2)}) collective-permute-start(bf16[2,2,2,32,1024]{4,3,2,1,0:T(8,128)(2,1)S(1)} %copy-done.37), channel_id=1, source_target_pairs={{0,2},{2,0},{4,6},{6,4},{1,3},{3,1},{5,7},{7,5},{8,10},{10,8},{12,... | collective-permute-start | bytes 1572872 | tf_op jit(solution)/shard_map/ppermute | solution.py:40
  190.8 38.2 %collective-permute-start.38 = (bf16[2,2,2,96,1024]{4,3,2,1,0:T(8,128)(2,1)S(1)}, bf16[2,2,2,96,1024]{4,3,2,1,0:T(8,128)(2,1)S(1)}, u32[]{:S(2)}, u32[]{:S(2)}) collective-permute-start(bf16[2,2,2,96,1024]{4,3,2,1,0:T(8,128)(2,1)S(1)} %pad_maximum_fusion.1.u0), channel_id=1, source_target_pairs={{0,16},{16,0},{1,17},{17,1},{2,18},{18,2},{3,19},{19,3},{4,20},{20... | collective-permute-start | bytes 4718600 | tf_op jit(solution)/shard_map/ppermute | solution.py:40
  192.2 36.7 %collective-permute-start.39 = (bf16[2,2,2,96,1024]{4,3,2,1,0:T(8,128)(2,1)S(1)}, bf16[2,2,2,96,1024]{4,3,2,1,0:T(8,128)(2,1)S(1)}, u32[]{:S(2)}, u32[]{:S(2)}) collective-permute-start(bf16[2,2,2,96,1024]{4,3,2,1,0:T(8,128)(2,1)S(1)} %pad_maximum_fusion.2.w0), channel_id=1, source_target_pairs={{0,2},{2,0},{4,6},{6,4},{1,3},{3,1},{5,7},{7,5},{8,10},{10,8},{12,... | collective-permute-start | bytes 4718600 | tf_op jit(solution)/shard_map/ppermute | solution.py:40
  192.8 30.8 %collective-permute-start.40 = (bf16[2,2,2,64,1024]{4,3,2,1,0:T(8,128)(2,1)S(1)}, bf16[2,2,2,64,1024]{4,3,2,1,0:T(8,128)(2,1)S(1)}, u32[]{:S(2)}, u32[]{:S(2)}) collective-permute-start(bf16[2,2,2,64,1024]{4,3,2,1,0:T(8,128)(2,1)S(1)} %pad_maximum_fusion.6.r0), channel_id=1, source_target_pairs={{0,1},{1,0},{2,3},{3,2},{4,5},{5,4},{6,7},{7,6},{8,9},{9,8},{10,11... | collective-permute-start | bytes 3145736 | tf_op jit(solution)/shard_map/ppermute | solution.py:40
  205.4 23.6 %collective-permute-start.43 = (bf16[512,1024]{1,0:T(8,128)(2,1)S(1)}, bf16[512,1024]{1,0:T(8,128)(2,1)S(1)}, u32[]{:S(2)}, u32[]{:S(2)}) collective-permute-start(bf16[512,1024]{1,0:T(8,128)(2,1)S(1)} %copy-done.106), channel_id=1, source_target_pairs={{1,8},{8,1},{3,10},{10,3},{5,12},{12,5},{7,14},{14,7},{17,24},{24,... | collective-permute-start | bytes 3145736 | tf_op jit(solution)/shard_map/ppermute | solution.py:44
  210.0 19.0 %collective-permute-start.42 = (bf16[512,1024]{1,0:T(8,128)(2,1)S(1)}, bf16[512,1024]{1,0:T(8,128)(2,1)S(1)}, u32[]{:S(2)}, u32[]{:S(2)}) collective-permute-start(bf16[512,1024]{1,0:T(8,128)(2,1)S(1)} %multiply_convert_fusion.2.h0), channel_id=1, source_target_pairs={{0,8},{8,0},{1,9},{9,1},{2,10},{10,2},{3,11},{11,3},{4,12},{12,4},... | collective-permute-start | bytes 3145736 | tf_op jit(solution)/shard_map/ppermute | solution.py:40
  230.1 44.9 %collective-permute-start.46 = (bf16[64,1024]{1,0:T(8,128)(2,1)S(1)}, bf16[64,1024]{1,0:T(8,128)(2,1)S(1)}, u32[]{:S(2)}, u32[]{:S(2)}) collective-permute-start(bf16[64,1024]{1,0:T(8,128)(2,1)S(1)} %get-tuple-element.544), channel_id=1, source_target_pairs={{0,2},{2,0},{4,6},{6,4},{1,3},{3,1},{5,7},{7,5},{8,10},{10,8},{12,... | collective-permute-start | bytes 393224 | tf_op jit(solution)/shard_map/ppermute | solution.py:1107
  231.2 43.8 %collective-permute-start.47 = (bf16[64,1024]{1,0:T(8,128)(2,1)S(1)}, bf16[64,1024]{1,0:T(8,128)(2,1)S(1)}, u32[]{:S(2)}, u32[]{:S(2)}) collective-permute-start(bf16[64,1024]{1,0:T(8,128)(2,1)S(1)} %get-tuple-element.543), channel_id=1, source_target_pairs={{0,4},{2,6},{4,0},{6,2},{1,5},{3,7},{5,1},{7,3},{8,12},{10,14},{12... | collective-permute-start | bytes 393224 | tf_op jit(solution)/shard_map/ppermute | solution.py:1107
  231.2 43.8 %collective-permute-start.48 = (bf16[64,1024]{1,0:T(8,128)(2,1)S(1)}, bf16[64,1024]{1,0:T(8,128)(2,1)S(1)}, u32[]{:S(2)}, u32[]{:S(2)}) collective-permute-start(bf16[64,1024]{1,0:T(8,128)(2,1)S(1)} %get-tuple-element.542), channel_id=1, source_target_pairs={{0,6},{2,4},{4,2},{6,0},{1,7},{3,5},{5,3},{7,1},{8,14},{10,12},{12... | collective-permute-start | bytes 393224 | tf_op jit(solution)/shard_map/ppermute | solution.py:1107
  275.8 36.8 %collective-permute-start.50 = (bf16[2,2,2,96,1024]{4,3,2,1,0:T(8,128)(2,1)}, bf16[2,2,2,96,1024]{4,3,2,1,0:T(8,128)(2,1)S(1)}, u32[]{:S(2)}, u32[]{:S(2)}) collective-permute-start(bf16[2,2,2,96,1024]{4,3,2,1,0:T(8,128)(2,1)} %get-tuple-element.357), channel_id=1, source_target_pairs={{0,1},{1,0},{2,3},{3,2},{4,5},{5,4},{6,7},{7,6},{8,9},{9,8},{10,11... | collective-permute-start | bytes 4718600 | tf_op jit(solution)/shard_map/ppermute | solution.py:40
  277.8 35.4 %collective-permute-start.51 = (bf16[2,2,2,96,1024]{4,3,2,1,0:T(8,128)(2,1)}, bf16[2,2,2,96,1024]{4,3,2,1,0:T(8,128)(2,1)S(1)}, u32[]{:S(2)}, u32[]{:S(2)}) collective-permute-start(bf16[2,2,2,96,1024]{4,3,2,1,0:T(8,128)(2,1)} %get-tuple-element.358), channel_id=1, source_target_pairs={{0,16},{16,0},{1,17},{17,1},{2,18},{18,2},{3,19},{19,3},{4,20},{20... | collective-permute-start | bytes 4718600 | tf_op jit(solution)/shard_map/ppermute | solution.py:40
  287.3 24.9 %collective-permute-start.52 = (bf16[2,2,2,64,1024]{4,3,2,1,0:T(8,128)(2,1)}, bf16[2,2,2,64,1024]{4,3,2,1,0:T(8,128)(2,1)}, u32[]{:S(2)}, u32[]{:S(2)}) collective-permute-start(bf16[2,2,2,64,1024]{4,3,2,1,0:T(8,128)(2,1)} %get-tuple-element.359), channel_id=1, source_target_pairs={{0,2},{2,0},{4,6},{6,4},{1,3},{3,1},{5,7},{7,5},{8,10},{10,8},{12,... | collective-permute-start | bytes 3145736 | tf_op jit(solution)/shard_map/ppermute | solution.py:40
  318.4 29.4 %collective-permute-start.59 = (bf16[512,1024]{1,0:T(8,128)(2,1)}, bf16[512,1024]{1,0:T(8,128)(2,1)}, u32[]{:S(2)}, u32[]{:S(2)}) collective-permute-start(bf16[512,1024]{1,0:T(8,128)(2,1)} %get-tuple-element.375), channel_id=1, source_target_pairs={{1,8},{8,1},{3,10},{10,3},{5,12},{12,5},{7,14},{14,7},{17,24},{24,... | collective-permute-start | bytes 3145736 | tf_op jit(solution)/shard_map/ppermute | solution.py:44
  326.5 21.3 %collective-permute-start.61 = (bf16[512,1024]{1,0:T(8,128)(2,1)S(1)}, bf16[512,1024]{1,0:T(8,128)(2,1)S(1)}, u32[]{:S(2)}, u32[]{:S(2)}) collective-permute-start(bf16[512,1024]{1,0:T(8,128)(2,1)S(1)} %proj_one.1.refs_2_), channel_id=1, source_target_pairs={{0,8},{8,0},{1,9},{9,1},{2,10},{10,2},{3,11},{11,3},{4,12},{12,4},... | collective-permute-start | bytes 3145736 | tf_op jit(solution)/shard_map/ppermute | solution.py:40
  326.6 21.2 %collective-permute-start.56 = (bf16[2,2,96,1024]{3,2,1,0:T(8,128)(2,1)S(1)}, bf16[2,2,96,1024]{3,2,1,0:T(8,128)(2,1)S(1)}, u32[]{:S(2)}, u32[]{:S(2)}) collective-permute-start(bf16[2,2,96,1024]{3,2,1,0:T(8,128)(2,1)S(1)} %bitcast.288), channel_id=1, source_target_pairs={{0,16},{16,0},{1,17},{17,1},{2,18},{18,2},{3,19},{19,3},{4,20},{20... | collective-permute-start | bytes 2359304 | tf_op jit(solution)/shard_map/ppermute | solution.py:40
  327.0 20.8 %collective-permute-start.57 = (bf16[2,2,96,1024]{3,2,1,0:T(8,128)(2,1)S(1)}, bf16[2,2,96,1024]{3,2,1,0:T(8,128)(2,1)S(1)}, u32[]{:S(2)}, u32[]{:S(2)}) collective-permute-start(bf16[2,2,96,1024]{3,2,1,0:T(8,128)(2,1)S(1)} %bitcast.287), channel_id=1, source_target_pairs={{0,2},{2,0},{4,6},{6,4},{1,3},{3,1},{5,7},{7,5},{8,10},{10,8},{12,... | collective-permute-start | bytes 2359304 | tf_op jit(solution)/shard_map/ppermute | solution.py:40
  329.1 18.7 %collective-permute-start.60 = (bf16[4,64,1024]{2,1,0:T(8,128)(2,1)S(1)}, bf16[4,64,1024]{2,1,0:T(8,128)(2,1)S(1)}, u32[]{:S(2)}, u32[]{:S(2)}) collective-permute-start(bf16[4,64,1024]{2,1,0:T(8,128)(2,1)S(1)} %bitcast.298), channel_id=1, source_target_pairs={{1,8},{8,1},{3,10},{10,3},{5,12},{12,5},{7,14},{14,7},{17,24},{24,... | collective-permute-start | bytes 1572872 | tf_op jit(solution)/shard_map/ppermute | solution.py:44
  348.9 14.2 %collective-permute-start.62 = (bf16[2,96,1024]{2,1,0:T(8,128)(2,1)S(1)}, bf16[2,96,1024]{2,1,0:T(8,128)(2,1)S(1)}, u32[]{:S(2)}, u32[]{:S(2)}) collective-permute-start(bf16[2,96,1024]{2,1,0:T(8,128)(2,1)S(1)} %bitcast.291), channel_id=1, source_target_pairs={{0,2},{2,0},{4,6},{6,4},{1,3},{3,1},{5,7},{7,5},{8,10},{10,8},{12,... | collective-permute-start | bytes 1179656 | tf_op jit(solution)/shard_map/ppermute | solution.py:40
  364.3 27.6 %collective-permute-start.65 = (bf16[2,2,2,2,32,1024]{5,4,3,2,1,0:T(8,128)(2,1)S(1)}, bf16[2,2,2,2,32,1024]{5,4,3,2,1,0:T(8,128)(2,1)}, u32[]{:S(2)}, u32[]{:S(2)}) collective-permute-start(bf16[2,2,2,2,32,1024]{5,4,3,2,1,0:T(8,128)(2,1)S(1)} %dynamic-slice_bitcast_fusion), channel_id=1, source_target_pairs={{0,16},{16,0},{1,17},{17,1},{2,18},{18,2},{3,19},{19,3},{4,20},{20... | collective-permute-start | bytes 3145736 | tf_op jit(solution)/shard_map/ppermute | solution.py:40
  366.5 25.4 %collective-permute-start.66 = (bf16[96,1024]{1,0:T(8,128)(2,1)S(1)}, bf16[96,1024]{1,0:T(8,128)(2,1)S(1)}, u32[]{:S(2)}, u32[]{:S(2)}) collective-permute-start(bf16[96,1024]{1,0:T(8,128)(2,1)S(1)} %get-tuple-element.414), channel_id=1, source_target_pairs={{0,4},{2,6},{4,0},{6,2},{1,5},{3,7},{5,1},{7,3},{8,12},{10,14},{12... | collective-permute-start | bytes 589832 | tf_op jit(solution)/shard_map/ppermute | solution.py:40
  366.8 25.1 %collective-permute-start.67 = (bf16[96,1024]{1,0:T(8,128)(2,1)S(1)}, bf16[96,1024]{1,0:T(8,128)(2,1)S(1)}, u32[]{:S(2)}, u32[]{:S(2)}) collective-permute-start(bf16[96,1024]{1,0:T(8,128)(2,1)S(1)} %get-tuple-element.415), channel_id=1, source_target_pairs={{0,4},{2,6},{4,0},{6,2},{1,5},{3,7},{5,1},{7,3},{8,12},{10,14},{12... | collective-permute-start | bytes 589832 | tf_op jit(solution)/shard_map/ppermute | solution.py:40
  368.9 23.0 %collective-permute-start.68 = (bf16[64,1024]{1,0:T(8,128)(2,1)S(1)}, bf16[64,1024]{1,0:T(8,128)(2,1)S(1)}, u32[]{:S(2)}, u32[]{:S(2)}) collective-permute-start(bf16[64,1024]{1,0:T(8,128)(2,1)S(1)} %get-tuple-element.416), channel_id=1, source_target_pairs={{0,4},{2,6},{4,0},{6,2},{1,5},{3,7},{5,1},{7,3},{8,12},{10,14},{12... | collective-permute-start | bytes 393224 | tf_op jit(solution)/shard_map/ppermute | solution.py:40
  393.7 18.0 %collective-permute-start.69 = (bf16[2,2,2,32,1024]{4,3,2,1,0:T(8,128)(2,1)S(1)}, bf16[2,2,2,32,1024]{4,3,2,1,0:T(8,128)(2,1)S(1)}, u32[]{:S(2)}, u32[]{:S(2)}) collective-permute-start(bf16[2,2,2,32,1024]{4,3,2,1,0:T(8,128)(2,1)S(1)} %dynamic-slice_bitcast_fusion.1), channel_id=1, source_target_pairs={{0,1},{1,0},{2,3},{3,2},{4,5},{5,4},{6,7},{7,6},{8,9},{9,8},{10,11... | collective-permute-start | bytes 1572872 | tf_op jit(solution)/shard_map/ppermute | solution.py:40
  396.3 15.4 %collective-permute-start.70 = (bf16[256,1024]{1,0:T(8,128)(2,1)S(1)}, bf16[256,1024]{1,0:T(8,128)(2,1)}, u32[]{:S(2)}, u32[]{:S(2)}) collective-permute-start(bf16[256,1024]{1,0:T(8,128)(2,1)S(1)} %get-tuple-element.541), channel_id=1, source_target_pairs={{0,16},{16,0},{1,17},{17,1},{2,18},{18,2},{3,19},{19,3},{4,20},{20... | collective-permute-start | bytes 1572872 | tf_op jit(solution)/shard_map/ppermute | solution.py:40
  412.5 24.7 %collective-permute-start.71 = (bf16[2,2,2,272,256]{4,3,2,1,0:T(8,128)(2,1)}, bf16[2,2,2,272,256]{4,3,2,1,0:T(8,128)(2,1)S(1)}, u32[]{:S(2)}, u32[]{:S(2)}) collective-permute-start(bf16[2,2,2,272,256]{4,3,2,1,0:T(8,128)(2,1)} %get-tuple-element.446), channel_id=1, source_target_pairs={{0,1},{1,0},{2,3},{3,2},{4,5},{5,4},{6,7},{7,6},{8,9},{9,8},{10,11... | collective-permute-start | bytes 3342344 | tf_op jit(solution)/shard_map/ppermute | solution.py:40
  412.5 23.0 %collective-permute-start.72 = (bf16[2,2,2,256,256]{4,3,2,1,0:T(8,128)(2,1)}, bf16[2,2,2,256,256]{4,3,2,1,0:T(8,128)(2,1)}, u32[]{:S(2)}, u32[]{:S(2)}) collective-permute-start(bf16[2,2,2,256,256]{4,3,2,1,0:T(8,128)(2,1)} %get-tuple-element.447), channel_id=1, source_target_pairs={{0,16},{16,0},{1,17},{17,1},{2,18},{18,2},{3,19},{19,3},{4,20},{20... | collective-permute-start | bytes 3145736 | tf_op jit(solution)/shard_map/ppermute | solution.py:40
  413.6 22.7 %collective-permute-start.73 = (bf16[2,2,2,256,256]{4,3,2,1,0:T(8,128)(2,1)}, bf16[2,2,2,256,256]{4,3,2,1,0:T(8,128)(2,1)}, u32[]{:S(2)}, u32[]{:S(2)}) collective-permute-start(bf16[2,2,2,256,256]{4,3,2,1,0:T(8,128)(2,1)} %get-tuple-element.448), channel_id=1, source_target_pairs={{0,2},{2,0},{4,6},{6,4},{1,3},{3,1},{5,7},{7,5},{8,10},{10,8},{12,... | collective-permute-start | bytes 3145736 | tf_op jit(solution)/shard_map/ppermute | solution.py:40
  419.1 17.3 %collective-permute-start.74 = (bf16[512,1024]{1,0:T(8,128)(2,1)}, bf16[512,1024]{1,0:T(8,128)(2,1)}, u32[]{:S(2)}, u32[]{:S(2)}) collective-permute-start(bf16[512,1024]{1,0:T(8,128)(2,1)} %get-tuple-element.451), channel_id=1, source_target_pairs={{0,8},{8,0},{1,9},{9,1},{2,10},{10,2},{3,11},{11,3},{4,12},{12,4},... | collective-permute-start | bytes 3145736 | tf_op jit(solution)/shard_map/ppermute | solution.py:40
  445.5 17.8 %collective-permute-start.76 = (bf16[2,2,272,256]{3,2,1,0:T(8,128)(2,1)}, bf16[2,2,272,256]{3,2,1,0:T(8,128)(2,1)}, u32[]{:S(2)}, u32[]{:S(2)}) collective-permute-start(bf16[2,2,272,256]{3,2,1,0:T(8,128)(2,1)} %bitcast.118), channel_id=1, source_target_pairs={{0,16},{16,0},{1,17},{17,1},{2,18},{18,2},{3,19},{19,3},{4,20},{20... | collective-permute-start | bytes 1671176 | tf_op jit(solution)/shard_map/ppermute | solution.py:40
  446.7 16.6 %collective-permute-start.77 = (bf16[2,2,256,256]{3,2,1,0:T(8,128)(2,1)}, bf16[2,2,256,256]{3,2,1,0:T(8,128)(2,1)}, u32[]{:S(2)}, u32[]{:S(2)}) collective-permute-start(bf16[2,2,256,256]{3,2,1,0:T(8,128)(2,1)} %bitcast.119), channel_id=1, source_target_pairs={{0,2},{2,0},{4,6},{6,4},{1,3},{3,1},{5,7},{7,5},{8,10},{10,8},{12,... | collective-permute-start | bytes 1572872 | tf_op jit(solution)/shard_map/ppermute | solution.py:40
  446.7 16.6 %collective-permute-start.78 = (bf16[2,2,256,256]{3,2,1,0:T(8,128)(2,1)}, bf16[2,2,256,256]{3,2,1,0:T(8,128)(2,1)}, u32[]{:S(2)}, u32[]{:S(2)}) collective-permute-start(bf16[2,2,256,256]{3,2,1,0:T(8,128)(2,1)} %bitcast.120), channel_id=1, source_target_pairs={{0,1},{1,0},{2,3},{3,2},{4,5},{5,4},{6,7},{7,6},{8,9},{9,8},{10,11... | collective-permute-start | bytes 1572872 | tf_op jit(solution)/shard_map/ppermute | solution.py:40
  447.0 16.2 %collective-permute-start.79 = (bf16[2,2,32,1024]{3,2,1,0:T(8,128)(2,1)S(1)}, bf16[2,2,32,1024]{3,2,1,0:T(8,128)(2,1)}, u32[]{:S(2)}, u32[]{:S(2)}) collective-permute-start(bf16[2,2,32,1024]{3,2,1,0:T(8,128)(2,1)S(1)} %dynamic-slice_bitcast_fusion.2), channel_id=1, source_target_pairs={{0,2},{2,0},{4,6},{6,4},{1,3},{3,1},{5,7},{7,5},{8,10},{10,8},{12,... | collective-permute-start | bytes 786440 | tf_op jit(solution)/shard_map/ppermute | solution.py:40
  449.6 39.2 %collective-permute-start.89 = (bf16[2,256,1024]{2,1,0:T(8,128)(2,1)S(1)}, bf16[2,256,1024]{2,1,0:T(8,128)(2,1)S(1)}, u32[]{:S(2)}, u32[]{:S(2)}) collective-permute-start(bf16[2,256,1024]{2,1,0:T(8,128)(2,1)S(1)} %pad_maximum_fusion.7.p0), channel_id=1, source_target_pairs={{0,8},{8,0},{1,9},{9,1},{2,10},{10,2},{3,11},{11,3},{4,12},{12,4},... | collective-permute-start | bytes 3145736 | tf_op jit(solution)/shard_map/ppermute | solution.py:40
  474.6 31.9 %collective-permute-start.87 = (bf16[512,1024]{1,0:T(8,128)(2,1)}, bf16[512,1024]{1,0:T(8,128)(2,1)}, u32[]{:S(2)}, u32[]{:S(2)}) collective-permute-start(bf16[512,1024]{1,0:T(8,128)(2,1)} %row_back.2), channel_id=1, source_target_pairs={{1,8},{8,1},{3,10},{10,3},{5,12},{12,5},{7,14},{14,7},{17,24},{24,... | collective-permute-start | bytes 3145736 | tf_op jit(solution)/shard_map/ppermute | solution.py:44
  486.3 20.2 %collective-permute-start.84 = (bf16[272,256]{1,0:T(8,128)(2,1)S(1)}, bf16[272,256]{1,0:T(8,128)(2,1)S(1)}, u32[]{:S(2)}, u32[]{:S(2)}) collective-permute-start(bf16[272,256]{1,0:T(8,128)(2,1)S(1)} %get-tuple-element.486), channel_id=1, source_target_pairs={{0,4},{2,6},{4,0},{6,2},{1,5},{3,7},{5,1},{7,3},{8,12},{10,14},{12... | collective-permute-start | bytes 417800 | tf_op jit(solution)/shard_map/ppermute | solution.py:40
  486.4 17.4 %collective-permute-start.85 = (bf16[256,256]{1,0:T(8,128)(2,1)S(1)}, bf16[256,256]{1,0:T(8,128)(2,1)S(1)}, u32[]{:S(2)}, u32[]{:S(2)}) collective-permute-start(bf16[256,256]{1,0:T(8,128)(2,1)S(1)} %get-tuple-element.487), channel_id=1, source_target_pairs={{0,4},{2,6},{4,0},{6,2},{1,5},{3,7},{5,1},{7,3},{8,12},{10,14},{12... | collective-permute-start | bytes 393224 | tf_op jit(solution)/shard_map/ppermute | solution.py:40
  488.7 17.8 %collective-permute-start.86 = (bf16[256,256]{1,0:T(8,128)(2,1)S(1)}, bf16[256,256]{1,0:T(8,128)(2,1)S(1)}, u32[]{:S(2)}, u32[]{:S(2)}) collective-permute-start(bf16[256,256]{1,0:T(8,128)(2,1)S(1)} %get-tuple-element.488), channel_id=1, source_target_pairs={{0,4},{2,6},{4,0},{6,2},{1,5},{3,7},{5,1},{7,3},{8,12},{10,14},{12... | collective-permute-start | bytes 393224 | tf_op jit(solution)/shard_map/ppermute | solution.py:40
  (181 other events, 1695.1 us)
